TPU v7x, 32 devices: a whole 2x2x4 slice. The times are simulated.
32 devices in a mesh: grp: 8 (over z, core), ep: 4 (over y, x).
Axes of the slice: x: 2, y: 2, z: 4, core: 2. Of those that a mesh axis runs over, the one named last changes fastest.
Arguments:
- queries: bfloat16 [128, 64, 576], P(('grp', 'ep')), may hold values from -75 to 75
- cache: bfloat16 [128, 256, 576], P(('grp', 'ep')), may hold values from -6 to 6
- lengths: int32 [128], P(('grp', 'ep')), may hold values from 2 to 256, as said below
- live_rows: int32 [32], P(('grp', 'ep')), may hold values from 1 to 4, as said below
- tokens: bfloat16 [512, 3584], P(('grp', 'ep')), may hold values from -6 to 6
- ids: int32 [512, 8], P(('grp', 'ep')), may hold values from 0 to 15, all different within a row; in each aligned block of 16 rows (0 to 15, 16 to 31, ...) at most 16 rows name the same one
- gates: float32 [512, 8], P(('grp', 'ep')), may hold values from 0.1 to 1
- w_gate: bfloat16 [32, 3584, 512], P(('grp', 'ep')), may hold values from -0.09375 to 0.09375
- w_up: bfloat16 [32, 3584, 512], P(('grp', 'ep')), may hold values from -0.09375 to 0.09375
- w_down: bfloat16 [32, 512, 3584], P(('grp', 'ep')), may hold values from -0.1875 to 0.1875
Outputs:
- context: bfloat16 [128, 64, 512], P(('grp', 'ep'))
- mixed: bfloat16 [512, 3584], P(('grp', 'ep'))
Inputs may be any that keep to these rules, and one draw needn't show every extreme that they name: `ids`: each row names 8 different experts; among the rows of one device no expert is named more than 16 times. `lengths`: the first request slot of every device holds 256 positions. `live_rows`: a device's live request slots are its first ones; on a quarter of the grp indices every device holds 2 or fewer, elsewhere exactly 4.
All inputs are finite; a program needn't handle non-finite values.
Results may differ from a plain program's by a relative error of at most 0.012.
Values may be sent and summed in bfloat16 or wider, within the bound.
No kernel may reach another device: no remote copies, remote signals or barrier semaphores. Data moves between devices by JAX's collectives and lax.ppermute only.
A program may use at most 128 MiB of HBM per device.

v0:
```python
from functools import partial

import jax
import jax.numpy as jnp
from jax import lax
from jax.sharding import PartitionSpec as P

TOPK = 8
LAT = 512


score_scale = 192.0 ** (-0.5)
neg_large = -1e30


def attend(queries, cache, lengths, live_count):
    scores = (
        jnp.einsum("rhc,rlc->rhl", queries, cache, preferred_element_type=jnp.float32) * score_scale
    )
    positions = lax.broadcasted_iota(jnp.int32, scores.shape, 2)
    inside = positions < lengths[:, None, None]
    masked = jnp.where(inside, scores, neg_large)
    highest = jnp.max(masked, axis=2, keepdims=True)
    powers = jnp.where(inside, jnp.exp(masked - highest), 0.0)
    totals = jnp.sum(powers, axis=2, keepdims=True)
    weights = (powers / totals).astype(jnp.bfloat16)
    context = jnp.einsum(
        "rhl,rlc->rhc", weights, cache[:, :, :LAT], preferred_element_type=jnp.float32
    ).astype(jnp.bfloat16)
    request_slot = lax.broadcasted_iota(jnp.int32, context.shape, 0)
    return jnp.where(request_slot < live_count, context, jnp.zeros_like(context))


def expert_partial(blocks, w_gate, w_up, w_down):
    layout = blocks.shape
    flat_rows = blocks.reshape(-1, layout[-1])
    gate_part = jnp.dot(flat_rows, w_gate[0], preferred_element_type=jnp.float32)
    up_part = jnp.dot(flat_rows, w_up[0], preferred_element_type=jnp.float32)
    hidden = (jax.nn.silu(gate_part) * up_part).astype(jnp.bfloat16)
    partials = jnp.dot(hidden, w_down[0], preferred_element_type=jnp.float32)
    return partials.reshape(layout[:-1] + (w_down.shape[2],))


def per_device(queries, cache, lengths, live_rows, tokens, ids, gates, w_gate, w_up, w_down):
    context = attend(queries, cache, lengths, live_rows[0])
    group_count = lax.axis_size("grp")
    peer_count = lax.axis_size("ep")
    pair_count = peer_count // 2
    expert_count = group_count * pair_count
    row_count = tokens.shape[0]
    feature = tokens.shape[1]
    capacity = 2 * row_count * TOPK // expert_count
    compute = partial(expert_partial, w_gate=w_gate, w_up=w_up, w_down=w_down)
    chosen_ids = ids.reshape(-1)
    onehot = (chosen_ids[:, None] == jnp.arange(expert_count, dtype=jnp.int32)[None, :]).astype(
        jnp.int32
    )
    earlier = jnp.cumsum(onehot, axis=0) - onehot
    slot_only = jnp.sum(earlier * onehot, axis=1)
    position = chosen_ids * capacity + slot_only
    source_row = jnp.arange(row_count * TOPK, dtype=jnp.int32) // TOPK
    outgoing = (
        jnp.zeros((expert_count * capacity, feature), jnp.bfloat16)
        .at[position]
        .set(tokens[source_row])
    )
    outgoing = outgoing.reshape(group_count, pair_count, capacity, feature)
    arriving = lax.all_to_all(outgoing, "grp", split_axis=0, concat_axis=0, tiled=True)
    doubled = jnp.repeat(arriving, 2, axis=1)
    partials = lax.all_to_all(
        compute(lax.all_to_all(doubled, "ep", split_axis=1, concat_axis=1, tiled=True)).astype(
            jnp.bfloat16
        ),
        "ep",
        split_axis=1,
        concat_axis=1,
        tiled=True,
    ).astype(jnp.float32)
    answered = (
        partials.reshape(group_count, pair_count, 2, capacity, feature)
        .sum(axis=2)
        .astype(jnp.bfloat16)
    )
    homebound = lax.all_to_all(answered, "grp", split_axis=0, concat_axis=0, tiled=True)
    picked = homebound.reshape(expert_count * capacity, feature)[position].reshape(
        row_count, TOPK, feature
    )
    summed = jnp.zeros((row_count, feature), jnp.float32)
    for which_pick in range(TOPK):
        summed = summed + gates[:, which_pick : which_pick + 1] * picked[:, which_pick, :].astype(
            jnp.float32
        )
    mixed = summed.astype(jnp.bfloat16)
    return (context, mixed)


def solution(mesh):
    in_specs = (
        P(("grp", "ep"), None, None),
        P(("grp", "ep"), None, None),
        P(("grp", "ep")),
        P(("grp", "ep")),
        P(("grp", "ep"), None),
        P(("grp", "ep"), None),
        P(("grp", "ep"), None),
        P(("grp", "ep"), None, None),
        P(("grp", "ep"), None, None),
        P(("grp", "ep"), None, None),
    )
    out_specs = (P(("grp", "ep"), None, None), P(("grp", "ep"), None))
    return jax.shard_map(
        per_device, mesh=mesh, in_specs=in_specs, out_specs=out_specs, check_vma=False
    )
```

profile of v0, /device:TPU:0, one launch (start us, length us, event | category | flops | bytes accessed | tf_op | source)
XLA Modules:
  0.0 209.1 jit_solution(11782466007746595629)
XLA Ops:
  0.6 0.8 copy.77
  1.4 0.7 broadcast_multiply_fusion
  2.9 6.1 %scatter_custom_fusion = bf16[256,3584]{1,0:T(8,128)(2,1)S(1)} fusion(s32[128]{0:T(128)S(1)} %fusion.32, bf16[16,3584]{1,0:T(8,128)(2,1)} %param.14, s32[1024]{0:T(1024)S(1)} %pad_clamp_fusion.1, bf16[]{:T(256)} %constant.33.clone.1), kind=kCustom, calls=%fused_computation.21 | custom fusion | bytes 1835520 | tf_op jit(solution)/shard_map/scatter | solution.py:65
  8.9 49.6 %all_to_all.20 = bf16[8,2,16,3584]{3,2,1,0:T(8,128)(2,1)S(1)} all-to-all(bf16[8,2,16,3584]{3,2,1,0:T(8,128)(2,1)S(1)} %bitcast.101), channel_id=1, replica_groups=mesh['grp'=8,'ep'=4] {'grp'}, dimensions={0} | all-to-all | bytes 3670016 | tf_op jit(solution)/shard_map/all_to_all | solution.py:68
  58.6 0.4 broadcast_in_dim.27
  59.1 45.4 %all_to_all.21 = bf16[8,4,16,3584]{3,2,0,1:T(8,128)(2,1)S(1)} all-to-all(bf16[8,4,16,3584]{3,2,0,1:T(8,128)(2,1)S(1)} %bitcast.99), channel_id=1, replica_groups=mesh['grp'=8,'ep'=4] {'ep'}, dimensions={1} | all-to-all | bytes 7340032 | tf_op jit(solution)/shard_map/all_to_all | solution.py:71
  104.4 0.3 copy.79
  104.7 1.7 copy-done.5
  106.5 2.0 fusion.4
  108.6 2.1 %fusion.9 = bf16[512,512]{1,0:T(8,128)(2,1)S(1)} fusion(bf16[512,3584]{1,0:T(8,128)(2,1)S(1)} %bitcast.103, bf16[1,3584,512]{2,1,0:T(8,128)(2,1)S(1)} %copy-done.6, f32[512,512]{1,0:T(8,128)S(1)} %fusion.4), kind=kOutput, calls=%fused_computation.12 | convolution fusion | flops 1880621056 | bytes 8912896 | tf_op jit(solution)/shard_map/dot_general | solution.py:38
  110.7 2.1 convolution_convert_fusion
  112.8 0.3 copy.80
  113.1 42.9 %all_to_all.22 = bf16[8,4,16,3584]{3,2,0,1:T(8,128)(2,1)S(1)} all-to-all(bf16[8,4,16,3584]{3,2,0,1:T(8,128)(2,1)S(1)} %copy.80), channel_id=1, replica_groups=mesh['grp'=8,'ep'=4] {'ep'}, dimensions={1} | all-to-all | bytes 7340032 | tf_op jit(solution)/shard_map/all_to_all | solution.py:70
  156.0 0.7 bitcast_reduce_fusion
  156.7 1.4 copy.81
  158.1 3.9 %all-to-all-start.3 = ((bf16[8,2,16,3584]{3,2,1,0:T(8,128)(2,1)}), bf16[8,2,16,3584]{3,2,1,0:T(8,128)(2,1)S(1)}, u32[]{:S(2)}, u32[]{:S(2)}) async-start(bf16[8,2,16,3584]{3,2,1,0:T(8,128)(2,1)} %copy.81), calls=%async_computation.3 | async-start | bytes 3670016 | tf_op jit(solution)/shard_map/all_to_all | solution.py:84
  162.7 0.3 fusion.13
  163.1 0.7 copy-done.2
  163.8 0.2 fusion.36
  164.1 2.3 %fusion.16 = bf16[4,64,512]{2,1,0:T(8,128)(2,1)} fusion(bf16[4,256,576]{1,2,0:T(8,128)(2,1)S(1)} %copy-done.1, pred[4]{0:T(512)(128)(4,1)S(1)} %iota_compare_fusion.2, f32[4,64]{1,0:T(4,128)S(1)} %fusion.36, f32[4,64,256]{2,1,0:T(8,128)} %copy-done.2, s32[4]{0:T(128)S(1)} %copy-done.4), kind=kOutput, calls=%fused_computation.19 | convolution fusion | flops 67699200 | bytes 1838080 | tf_op jit(solution)/shard_map/rhl,rlc->rhc/dot_general | solution.py:27
  166.3 39.1 %all-to-all-done.3 = bf16[8,2,16,3584]{3,2,1,0:T(8,128)(2,1)S(1)} async-done(((bf16[8,2,16,3584]{3,2,1,0:T(8,128)(2,1)}), bf16[8,2,16,3584]{3,2,1,0:T(8,128)(2,1)S(1)}, u32[]{:S(2)}, u32[]{:S(2)}) %all-to-all-start.3) | async-done | bytes 1835040 | tf_op jit(solution)/shard_map/all_to_all | solution.py:84
  205.5 1.1 gather_fusion
  206.6 1.6 fusion.35
  208.2 0.9 fusion.22
  (27 shorter events, 0.9 us)
Async XLA Ops:
  0.6 162.1 %copy-start = (bf16[4,64,576]{2,1,0:T(8,128)(2,1)S(1)}, bf16[4,64,576]{2,1,0:T(8,128)(2,1)}, u32[]{:S(2)}) copy-start(bf16[4,64,576]{2,1,0:T(8,128)(2,1)} %param.10) | copy-start | bytes 884740
  104.4 2.0 copy-start.5
  106.5 2.1 copy-start.6
  108.5 2.2 %copy-start.7 = (bf16[1,512,3584]{2,1,0:T(8,128)(2,1)S(1)}, bf16[1,512,3584]{2,1,0:T(8,128)(2,1)}, u32[]{:S(2)}) copy-start(bf16[1,512,3584]{2,1,0:T(8,128)(2,1)} %param.19) | copy-start | bytes 11010052
  156.7 6.0 %copy-start.1 = (bf16[4,256,576]{1,2,0:T(8,128)(2,1)S(1)}, bf16[4,256,576]{1,2,0:T(8,128)(2,1)}, u32[]{:S(2)}) copy-start(bf16[4,256,576]{1,2,0:T(8,128)(2,1)} %param.11) | copy-start | bytes 3538948
  156.7 6.0 %copy-start.4 = (s32[4]{0:T(128)S(1)}, s32[4]{0:T(128)}, u32[]{:S(2)}) copy-start(s32[4]{0:T(128)} %param.12) | copy-start | bytes 52
  158.1 5.9 %copy-start.3 = (f32[16,8]{0,1:T(8,128)S(1)}, f32[16,8]{0,1:T(8,128)}, u32[]{:S(2)}) copy-start(f32[16,8]{0,1:T(8,128)} %param.16) | copy-start | bytes 1540
  158.1 47.4 %all-to-all-start.3 = ((bf16[8,2,16,3584]{3,2,1,0:T(8,128)(2,1)}), bf16[8,2,16,3584]{3,2,1,0:T(8,128)(2,1)S(1)}, u32[]{:S(2)}, u32[]{:S(2)}) async-start(bf16[8,2,16,3584]{3,2,1,0:T(8,128)(2,1)} %copy.81), calls=%async_computation.3 | async-start | bytes 3670016 | tf_op jit(solution)/shard_map/all_to_all | solution.py:84
  163.1 0.7 copy-start.2
where the time goes:
time: 210 us; the launch traced here: 209 us
  blocking collectives  138 us (66%)
  waiting for transfers between devices  39.1 us (19%)
  local copies, waits for them, and re-layouts  14.8 us (7%)
  matrix products  8.89 us (4%)
  starting transfers between devices  3.9 us (2%)
  other arithmetic  2.96 us (1%)
    all_to_all x1, blocking collectives, per_device(): lax.all_to_all(outgoing, 'grp', split_axis=0, concat_axis=0, tiled=True)  49.6 us
    all_to_all x1, blocking collectives, per_device(): lax.all_to_all(doubled, 'ep', split_axis=1, concat_axis=1, tiled=True)  45.4 us
    all_to_all x1, blocking collectives, per_device(): lax.all_to_all(compute(lax.all_to_all(doubled, 'ep', split_axis=1, concat...  42.9 us
    all_to_all x1, waiting for transfers between devices, per_device(): lax.all_to_all(answered, 'grp', split_axis=0, concat_axis=0, tiled=True)  39.1 us
    scatter x1, local copies, waits for them, and re-layouts, per_device(): outgoing = jnp.zeros((expert_count * capacity, feature), jnp.bfloat16).at...  6.06 us
  transfers between devices with their start and end apart: 1, of which 1 were waited for; matrix products, arithmetic and copies ran while one was open for 1% of the time, Pallas kernels for 0%

commit v1 on v0

v1 whole, which is shorter than its diff:
```python
import jax
import jax.numpy as jnp
from jax import lax
from jax.sharding import PartitionSpec as P

LAT = 512
AXES = ("grp", "ep")

score_scale = 192.0 ** (-0.5)
neg_large = -1e30


def attend(queries, cache, lengths, live_count):
    scores = (
        jnp.einsum("rhc,rlc->rhl", queries, cache, preferred_element_type=jnp.float32) * score_scale
    )
    positions = lax.broadcasted_iota(jnp.int32, scores.shape, 2)
    inside = positions < lengths[:, None, None]
    masked = jnp.where(inside, scores, neg_large)
    highest = jnp.max(masked, axis=2, keepdims=True)
    powers = jnp.where(inside, jnp.exp(masked - highest), 0.0)
    totals = jnp.sum(powers, axis=2, keepdims=True)
    weights = (powers / totals).astype(jnp.bfloat16)
    context = jnp.einsum(
        "rhl,rlc->rhc", weights, cache[:, :, :LAT], preferred_element_type=jnp.float32
    ).astype(jnp.bfloat16)
    request_slot = lax.broadcasted_iota(jnp.int32, context.shape, 0)
    return jnp.where(request_slot < live_count, context, jnp.zeros_like(context))


def per_device(queries, cache, lengths, live_rows, tokens, ids, gates, w_gate, w_up, w_down):
    me = lax.axis_index("grp") * lax.axis_size("ep") + lax.axis_index("ep")
    expert = me // 2
    all_tokens = lax.all_gather(tokens, AXES, axis=0, tiled=True)
    all_ids = lax.all_gather(ids, AXES, axis=0, tiled=True)
    all_gates = lax.all_gather(gates, AXES, axis=0, tiled=True)
    context = attend(queries, cache, lengths, live_rows[0])
    share = jnp.sum(jnp.where(all_ids == expert, all_gates, 0.0), axis=1, keepdims=True)
    gate_part = jnp.dot(all_tokens, w_gate[0], preferred_element_type=jnp.float32)
    up_part = jnp.dot(all_tokens, w_up[0], preferred_element_type=jnp.float32)
    hidden = (jax.nn.silu(gate_part) * up_part).astype(jnp.bfloat16)
    partial_out = jnp.dot(hidden, w_down[0], preferred_element_type=jnp.float32)
    weighted = (partial_out * share).astype(jnp.bfloat16)
    mixed = lax.psum_scatter(weighted, AXES, scatter_dimension=0, tiled=True)
    return (context, mixed)


def solution(mesh):
    rows3 = P(AXES, None, None)
    rows2 = P(AXES, None)
    rows1 = P(AXES)
    return jax.shard_map(
        per_device,
        mesh=mesh,
        in_specs=(rows3, rows3, rows1, rows1, rows2, rows2, rows2, rows3, rows3, rows3),
        out_specs=(rows3, rows2),
        check_vma=False,
    )
```

time: 210 us -> 304 us (1.45)
  waiting for transfers between devices: 39.1 us -> 136 us
  local copies, waits for them, and re-layouts: 14.8 us -> 0.59 us
  between operations: 1.53 us -> 14.8 us
  matrix products: 8.89 us -> 16.9 us
  starting transfers between devices: 3.9 us -> 0.08 us
    all_to_all x3 -> x0, blocking collectives: 138 us -> none  [the longest x1 49.6 us: per_device(): lax.all_to_all(outgoing, 'grp', split_axis=0, concat_axis=0, tiled=True)]
    all_gather x0 -> x2, blocking collectives: none -> 135 us  [the longest x1 70.9 us: per_device(): all_ids = lax.all_gather(ids, AXES, axis=0, tiled=True)]
    reduce_scatter x0 -> x1, waiting for transfers between devices: none -> 135 us  [per_device(): mixed = lax.psum_scatter(weighted, AXES, scatter_dimension=0, tiled=True)]
    all_to_all x1 -> x0, waiting for transfers between devices: 39.1 us -> none  [per_device(): lax.all_to_all(answered, 'grp', split_axis=0, concat_axis=0, tiled=True)]
    dot_general x3 -> x2, matrix products: 6.27 us -> 15.3 us  [the longest x1 10.1 us: per_device(): partial_out = jnp.dot(hidden, w_down[0], preferred_element_type=jnp.float32)]
    scatter x1 -> x0, local copies, waits for them, and re-layouts: 6.06 us -> none  [per_device(): outgoing = jnp.zeros((expert_count * capacity, feature), jnp.bfloat16).at...]
    all_to_all x1 -> x0, starting transfers between devices: 3.9 us -> none  [per_device(): lax.all_to_all(answered, 'grp', split_axis=0, concat_axis=0, tiled=True)]
  transfers between devices with their start and end apart: 1 -> 2, of which waited for: 1 -> 1; matrix products, arithmetic and copies ran while one was open for 1% -> 1% of each run, Pallas kernels for 0% -> 0%
where the time goes in v1:
time: 304 us
  waiting for transfers between devices  136 us (45%)
  blocking collectives  135 us (44%)
  matrix products  16.9 us (6%)
  between operations  14.8 us (5%)
    reduce_scatter x1, waiting for transfers between devices, per_device(): mixed = lax.psum_scatter(weighted, AXES, scatter_dimension=0, tiled=True)  135 us
    all_gather x1, blocking collectives, per_device(): all_ids = lax.all_gather(ids, AXES, axis=0, tiled=True)  70.9 us
    all_gather x1, blocking collectives, per_device(): all_gates = lax.all_gather(gates, AXES, axis=0, tiled=True)  64.3 us
    dot_general x1, matrix products, per_device(): partial_out = jnp.dot(hidden, w_down[0], preferred_element_type=jnp.float32)  10.1 us
  transfers between devices with their start and end apart: 2, of which 1 were waited for; matrix products, arithmetic and copies ran while one was open for 1% of the time, Pallas kernels for 0%

profile of v1, /device:TPU:0, one launch (start us, length us, event | category | flops | bytes accessed | tf_op | source)
XLA Modules:
  0.0 303.9 jit_solution(15121763508230355719)
XLA Ops:
  7.2 0.0 copy-start
  7.2 0.0 all-gather.4.cloned.1.call-start
  7.2 0.7 all-gather.4.cloned.1.call-update
  7.9 0.0 reduce-scatter.2.cloned.1.call-start
  8.0 70.9 %all-gather = s32[32,16,8]{1,2,0:T(8,128)S(1)} all-gather(s32[1,16,8]{1,2,0:T(8,128)} %bitcast.25), channel_id=1, replica_groups=mesh['grp'=8,'ep'=4] {'grp','ep'}, dimensions={0}, use_global_device_ids=true | all-gather | bytes 16896 | tf_op jit(solution)/shard_map/all_gather | solution.py:35
  78.9 64.3 %all-gather.1 = f32[32,16,8]{1,2,0:T(8,128)S(1)} all-gather(f32[1,16,8]{1,2,0:T(8,128)} %bitcast.26), channel_id=1, replica_groups=mesh['grp'=8,'ep'=4] {'grp','ep'}, dimensions={0}, use_global_device_ids=true | all-gather | bytes 16896 | tf_op jit(solution)/shard_map/all_gather | solution.py:36
  143.3 0.1 reshape.16
  143.4 0.0 all-gather.4.cloned.1.call-done
  143.4 5.2 %fusion.4 = f32[512,512]{1,0:T(8,128)S(1)} fusion(bf16[512,3584]{1,0:T(8,128)(2,1)} %all-gather.4.cloned.1.call-done, bf16[1,3584,512]{2,1,0:T(8,128)(2,1)} %param.17), kind=kOutput, calls=%fused_computation.5 | convolution fusion | flops 1879048192 | bytes 8388608 | tf_op jit(solution)/shard_map/dot_general | solution.py:39
  148.6 10.1 %multiply_convert_fusion = bf16[512,3584]{1,0:T(8,128)(2,1)} fusion(bf16[1,512,3584]{2,1,0:T(8,128)(2,1)} %param.19, f32[512]{0:T(512)S(1)} %reshape.16, bf16[512,3584]{1,0:T(8,128)(2,1)} %all-gather.4.cloned.1.call-done, bf16[1,3584,512]{2,1,0:T(8,128)(2,1)} %param.18, f32[512,512]{1,0:T(8,128)S(1)} %fusion.4), kind=kOutput, calls=%fused_computation.1 | convolution fusion | flops 3763339264 | bytes 15730688 | tf_op jit(solution)/shard_map/dot_general | solution.py:42
  158.7 0.0 copy-start.1
  158.7 0.0 copy-start.2
  158.7 0.0 reduce-scatter.2.cloned.1.call-update
  159.5 0.0 copy-done
  159.5 0.5 copy-done.1
  160.0 0.0 copy-done.2
  160.0 0.3 fusion.13
  160.4 0.2 fusion.25
  160.6 1.3 fusion.16
  161.9 135.2 %reduce-scatter.2.cloned.1.call-done = bf16[16,3584]{1,0:T(8,128)(2,1)} async-done(((bf16[512,3584]{1,0:T(8,128)(2,1)}), bf16[16,3584]{1,0:T(8,128)(2,1)}) %reduce-scatter.2.cloned.1.call-update) | async-done | bytes 114704 | tf_op jit(solution)/shard_map/reduce_scatter | solution.py:44
  (2 shorter events, 0.1 us)
Async XLA Ops:
  7.2 152.3 %copy-start = (bf16[4,64,576]{2,1,0:T(8,128)(2,1)S(1)}, bf16[4,64,576]{2,1,0:T(8,128)(2,1)}, u32[]{:S(2)}) copy-start(bf16[4,64,576]{2,1,0:T(8,128)(2,1)} %param.10) | copy-start | bytes 884740
  7.2 136.2 %all-gather.4.cloned.1.call-start = ((), (), s32[]{:S(2)}) async-start(), calls=%async_computation.1 | async-start | bytes 3784704 | tf_op jit(solution)/shard_map/all_gather | solution.py:34
  7.9 289.1 %reduce-scatter.2.cloned.1.call-start = ((), (), s32[]{:S(2)}) async-start(), calls=%async_computation.2 | async-start | bytes 3784704 | tf_op jit(solution)/shard_map/reduce_scatter | solution.py:44
  158.7 1.3 copy-start.1
  158.7 1.3 copy-start.2
Sparse Core Ops, SparseCore 0:
  10.9 63.3 all-gather.3
  158.9 138.1 reduce-scatter.1

commit v2 on v1

--- a/solution.py
+++ b/solution.py
@@ -28,20 +28,94 @@
     return jnp.where(request_slot < live_count, context, jnp.zeros_like(context))
 
 
+def bits_of(count):
+    return [1 << i for i in range(count.bit_length() - 1)]
+
+
+def swap(value, step):
+    axis, bit = step
+    size = lax.axis_size(axis)
+    return lax.ppermute(value, axis, [(i, i ^ bit) for i in range(size)])
+
+
+def spread(value, steps):
+    for step in steps:
+        value = jnp.concatenate([value, swap(value, step)], axis=0)
+    return value
+
+
+def fold(value, steps):
+    for step in reversed(steps):
+        half = value.shape[0] // 2
+        arrived = swap(value[half:], step)
+        value = (value[:half].astype(jnp.float32) + arrived.astype(jnp.float32)).astype(
+            jnp.bfloat16
+        )
+    return value
+
+
+def pack(tokens, ids, gates):
+    high = lax.reduce_precision(gates, 8, 7)
+    low = gates - high
+    extra = jnp.concatenate([ids.astype(jnp.float32), high, low], axis=1)
+    extra = jnp.pad(extra, ((0, 0), (0, 128 - extra.shape[1]))).astype(jnp.bfloat16)
+    return jnp.concatenate([tokens, extra], axis=1)
+
+
 def per_device(queries, cache, lengths, live_rows, tokens, ids, gates, w_gate, w_up, w_down):
-    me = lax.axis_index("grp") * lax.axis_size("ep") + lax.axis_index("ep")
-    expert = me // 2
-    all_tokens = lax.all_gather(tokens, AXES, axis=0, tiled=True)
-    all_ids = lax.all_gather(ids, AXES, axis=0, tiled=True)
-    all_gates = lax.all_gather(gates, AXES, axis=0, tiled=True)
+    feature = tokens.shape[1]
+    picks = ids.shape[1]
+    grp_bits = bits_of(lax.axis_size("grp"))
+    ep_bits = bits_of(lax.axis_size("ep"))
+    core = ("grp", 1)
+    z_steps = [("grp", bit) for bit in reversed(grp_bits[1:])]
+    x_steps = [("ep", bit) for bit in ep_bits[: len(ep_bits) // 2]]
+    y_steps = [("ep", bit) for bit in ep_bits[len(ep_bits) // 2 :]]
+    expert = (lax.axis_index("grp") * lax.axis_size("ep") + lax.axis_index("ep")) // 2
+
+    def share_of(extra):
+        extra = extra.astype(jnp.float32)
+        named = extra[:, :picks] == expert.astype(jnp.float32)
+        value = extra[:, picks : 2 * picks] + extra[:, 2 * picks : 3 * picks]
+        return jnp.sum(jnp.where(named, value, 0.0), axis=1, keepdims=True)
+
+    def order_rows(value, steps, wanted):
+        row_count = value.shape[0] >> len(steps)
+        cube = value.reshape((2,) * len(steps) + (row_count, value.shape[1]))
+        axes = [len(steps) - 1 - steps.index(step) for step in reversed(wanted)]
+        cube = cube.transpose(axes + [len(steps), len(steps) + 1])
+        return cube.reshape(value.shape)
+
+    packed = pack(tokens, ids, gates)
+    near = spread(packed, z_steps)
+    half_width = feature // 2
+    first = spread(near[:, :half_width], x_steps + y_steps)
+    second = spread(near[:, half_width:], y_steps + x_steps)
+    second = order_rows(second, z_steps + y_steps + x_steps, z_steps + x_steps + y_steps)
+    own = jnp.concatenate([first, second], axis=1)
+    other = swap(own, core)
+
     context = attend(queries, cache, lengths, live_rows[0])
-    share = jnp.sum(jnp.where(all_ids == expert, all_gates, 0.0), axis=1, keepdims=True)
-    gate_part = jnp.dot(all_tokens, w_gate[0], preferred_element_type=jnp.float32)
-    up_part = jnp.dot(all_tokens, w_up[0], preferred_element_type=jnp.float32)
-    hidden = (jax.nn.silu(gate_part) * up_part).astype(jnp.bfloat16)
-    partial_out = jnp.dot(hidden, w_down[0], preferred_element_type=jnp.float32)
-    weighted = (partial_out * share).astype(jnp.bfloat16)
-    mixed = lax.psum_scatter(weighted, AXES, scatter_dimension=0, tiled=True)
+
+    def hidden_of(rows):
+        gate_part = jnp.dot(rows[:, :feature], w_gate[0], preferred_element_type=jnp.float32)
+        up_part = jnp.dot(rows[:, :feature], w_up[0], preferred_element_type=jnp.float32)
+        return (jax.nn.silu(gate_part) * up_part).astype(jnp.bfloat16)
+
+    def partial_of(rows, hidden):
+        product = jnp.dot(hidden, w_down[0], preferred_element_type=jnp.float32)
+        return product * share_of(rows[:, feature:])
+
+    own_hidden = hidden_of(own)
+    other_hidden = hidden_of(other)
+    arrived = swap(partial_of(other, other_hidden).astype(jnp.bfloat16), core)
+    summed = (partial_of(own, own_hidden) + arrived.astype(jnp.float32)).astype(jnp.bfloat16)
+    first = fold(summed[:, :half_width], x_steps + y_steps)
+    second = order_rows(
+        summed[:, half_width:], z_steps + x_steps + y_steps, z_steps + y_steps + x_steps
+    )
+    second = fold(second, y_steps + x_steps)
+    mixed = fold(jnp.concatenate([first, second], axis=1), z_steps)
     return (context, mixed)
 
 

time: 304 us -> 112 us (0.37)
  blocking collectives: 135 us -> 0 us
  waiting for transfers between devices: 136 us -> 53.2 us
  starting transfers between devices: 0.08 us -> 20.1 us
  between operations: 14.8 us -> 1.49 us
  other arithmetic: 0.29 us -> 8.86 us
  matrix products: 16.9 us -> 25 us
    all_gather x2 -> x0, blocking collectives: 135 us -> none  [the longest x1 70.9 us: per_device(): all_ids = lax.all_gather(ids, AXES, axis=0, tiled=True)]
    reduce_scatter x1 -> x0, waiting for transfers between devices: 135 us -> none  [per_device(): mixed = lax.psum_scatter(weighted, AXES, scatter_dimension=0, tiled=True)]
    ppermute x0 -> x14, waiting for transfers between devices: none -> 53.2 us  [swap(): return lax.ppermute(value, axis, [(i, i ^ bit) for i in range(size)])]
    ppermute x0 -> x14, starting transfers between devices: none -> 20.1 us  [swap(): return lax.ppermute(value, axis, [(i, i ^ bit) for i in range(size)])]
    dot_general x2 -> x4, matrix products: 15.3 us -> 22.1 us  [the longest x2 14.4 us: partial_of(): product = jnp.dot(hidden, w_down[0], preferred_element_type=jnp.float32)]
  transfers between devices with their start and end apart: 2 -> 14, of which waited for: 1 -> 12; matrix products, arithmetic and copies ran while one was open for 1% -> 8% of each run, Pallas kernels for 0% -> 0%
where the time goes in v2:
time: 112 us; the launch traced here: 111 us
  waiting for transfers between devices  53.2 us (48%)
  matrix products  25 us (22%)
  starting transfers between devices  20.1 us (18%)
  other arithmetic  8.86 us (8%)
  local copies, waits for them, and re-layouts  2.57 us (2%)
  between operations  1.49 us (1%)
    ppermute x14, waiting for transfers between devices, swap(): return lax.ppermute(value, axis, [(i, i ^ bit) for i in range(size)])  53.2 us
    ppermute x14, starting transfers between devices, swap(): return lax.ppermute(value, axis, [(i, i ^ bit) for i in range(size)])  20.1 us
    dot_general x2, matrix products, partial_of(): product = jnp.dot(hidden, w_down[0], preferred_element_type=jnp.float32)  14.4 us
    dot_general x2, matrix products, hidden_of(): jnp.dot(rows[:, :feature], w_up[0], preferred_element_type=jnp.float32)  7.66 us
  transfers between devices with their start and end apart: 14, of which 12 were waited for; matrix products, arithmetic and copies ran while one was open for 8% of the time, Pallas kernels for 0%

profile of v2, /device:TPU:0, one launch (start us, length us, event | category | flops | bytes accessed | tf_op | source)
XLA Modules:
  0.0 111.2 jit_solution(15108039142211696450)
XLA Ops:
  3.1 4.1 %collective-permute-start = (bf16[16,3712]{1,0:T(8,128)(2,1)S(1)}, bf16[16,3712]{1,0:T(8,128)(2,1)S(1)}, u32[]{:S(2)}, u32[]{:S(2)}) collective-permute-start(bf16[16,3712]{1,0:T(8,128)(2,1)S(1)} %pad_maximum_fusion.10), channel_id=1, source_target_pairs={{0,16},{4,20},{8,24},{12,28},{16,0},{20,4},{24,8},{28,12},{1,17},{... | collective-permute-start | bytes 356360 | tf_op jit(solution)/shard_map/ppermute | solution.py:38
  7.2 5.8 %collective-permute-done = bf16[16,3712]{1,0:T(8,128)(2,1)S(1)} collective-permute-done((bf16[16,3712]{1,0:T(8,128)(2,1)S(1)}, bf16[16,3712]{1,0:T(8,128)(2,1)S(1)}, u32[]{:S(2)}, u32[]{:S(2)}) %collective-permute-start) | collective-permute-done | bytes 118816 | tf_op jit(solution)/shard_map/ppermute | solution.py:38
  14.7 6.2 %collective-permute-done.1 = bf16[32,3712]{1,0:T(8,128)(2,1)S(1)} collective-permute-done((bf16[32,3712]{1,0:T(8,128)(2,1)S(1)}, bf16[32,3712]{1,0:T(8,128)(2,1)S(1)}, u32[]{:S(2)}, u32[]{:S(2)}) %collective-permute-start.1) | collective-permute-done | bytes 237600 | tf_op jit(solution)/shard_map/ppermute | solution.py:38
  21.8 1.3 %collective-permute-start.4 = (bf16[64,1920]{1,0:T(8,128)(2,1)S(1)}, bf16[64,1920]{1,0:T(8,128)(2,1)S(1)}, u32[]{:S(2)}, u32[]{:S(2)}) collective-permute-start(bf16[64,1920]{1,0:T(8,128)(2,1)S(1)} %pad_maximum_fusion.4), channel_id=1, source_target_pairs={{0,2},{1,3},{2,0},{3,1},{4,6},{5,7},{6,4},{7,5},{8,10},{9,11},{10,... | collective-permute-start | bytes 737288 | tf_op jit(solution)/shard_map/ppermute | solution.py:38
  23.9 1.6 %collective-permute-start.2 = (bf16[64,1792]{1,0:T(8,128)(2,1)S(1)}, bf16[64,1792]{1,0:T(8,128)(2,1)S(1)}, u32[]{:S(2)}, u32[]{:S(2)}) collective-permute-start(bf16[64,1792]{1,0:T(8,128)(2,1)S(1)} %pad_maximum_fusion.9), channel_id=1, source_target_pairs={{0,1},{1,0},{2,3},{3,2},{4,5},{5,4},{6,7},{7,6},{8,9},{9,8},{10,11... | collective-permute-start | bytes 688136 | tf_op jit(solution)/shard_map/ppermute | solution.py:38
  25.5 2.6 %collective-permute-done.4 = bf16[64,1920]{1,0:T(8,128)(2,1)S(1)} collective-permute-done((bf16[64,1920]{1,0:T(8,128)(2,1)S(1)}, bf16[64,1920]{1,0:T(8,128)(2,1)S(1)}, u32[]{:S(2)}, u32[]{:S(2)}) %collective-permute-start.4) | collective-permute-done | bytes 245792 | tf_op jit(solution)/shard_map/ppermute | solution.py:38
  28.1 1.3 %collective-permute-start.5 = (bf16[128,1920]{1,0:T(8,128)(2,1)S(1)}, bf16[128,1920]{1,0:T(8,128)(2,1)S(1)}, u32[]{:S(2)}, u32[]{:S(2)}) collective-permute-start(bf16[128,1920]{1,0:T(8,128)(2,1)S(1)} %pad_maximum_fusion.2), channel_id=1, source_target_pairs={{0,1},{1,0},{2,3},{3,2},{4,5},{5,4},{6,7},{7,6},{8,9},{9,8},{10,11... | collective-permute-start | bytes 1474568 | tf_op jit(solution)/shard_map/ppermute | solution.py:38
  29.4 2.8 %collective-permute-done.2 = bf16[64,1792]{1,0:T(8,128)(2,1)S(1)} collective-permute-done((bf16[64,1792]{1,0:T(8,128)(2,1)S(1)}, bf16[64,1792]{1,0:T(8,128)(2,1)S(1)}, u32[]{:S(2)}, u32[]{:S(2)}) %collective-permute-start.2) | collective-permute-done | bytes 229408 | tf_op jit(solution)/shard_map/ppermute | solution.py:38
  32.4 8.1 %collective-permute-done.5 = bf16[128,1920]{1,0:T(8,128)(2,1)S(1)} collective-permute-done((bf16[128,1920]{1,0:T(8,128)(2,1)S(1)}, bf16[128,1920]{1,0:T(8,128)(2,1)S(1)}, u32[]{:S(2)}, u32[]{:S(2)}) %collective-permute-start.5) | collective-permute-done | bytes 491552 | tf_op jit(solution)/shard_map/ppermute | solution.py:38
  41.0 4.0 %collective-permute-done.6 = bf16[256,3712]{1,0:T(8,128)(2,1)} collective-permute-done((bf16[256,3712]{1,0:T(8,128)(2,1)S(1)}, bf16[256,3712]{1,0:T(8,128)(2,1)}, u32[]{:S(2)}, u32[]{:S(2)}) %collective-permute-start.6) | collective-permute-done | bytes 1900576 | tf_op jit(solution)/shard_map/ppermute | solution.py:38
  46.1 4.5 %fusion.4 = f32[256,512]{1,0:T(8,128)} fusion(bf16[1,3584,512]{2,1,0:T(8,128)(2,1)} %param.18, bf16[256,3712]{1,0:T(8,128)(2,1)} %collective-permute-done.6), kind=kOutput, calls=%fused_computation.6 | convolution fusion | flops 939524096 | bytes 6029312 | tf_op jit(solution)/shard_map/dot_general | solution.py:102
  50.6 7.3 %fusion.1 = bf16[256,3584]{1,0:T(8,128)(2,1)} fusion(bf16[1,512,3584]{2,1,0:T(8,128)(2,1)} %param.19, f32[256]{0:T(256)S(1)} %fusion.45, f32[256,512]{1,0:T(8,128)} %fusion.4, bf16[1,3584,512]{2,1,0:T(8,128)(2,1)} %param.17, bf16[256,3712]{1,0:T(8,128)(2,1)} %collective-permute-done.6), kind=kOutput, calls=%fused_computation.3 | convolution fusion | flops 1881669632 | bytes 11535360 | tf_op jit(solution)/shard_map/dot_general | solution.py:106
  58.7 1.6 %fusion.19 = f32[4,64,256]{2,1,0:T(8,128)S(1)} fusion(bf16[4,64,576]{2,1,0:T(8,128)(2,1)S(1)} %copy-done, bf16[4,256,576]{1,2,0:T(8,128)(2,1)} %param.11, s32[4]{0:T(128)S(1)} %copy-done.2), kind=kOutput, calls=%fused_computation.23 | convolution fusion | flops 75694080 | bytes 1736720 | tf_op jit(solution)/shard_map/rhc,rlc->rhl/dot_general | solution.py:15
  60.5 3.2 %fusion.6 = f32[256,512]{1,0:T(8,128)S(1)} fusion(bf16[1,3584,512]{2,1,0:T(8,128)(2,1)} %param.18, bf16[256,3712]{1,0:T(8,128)(2,1)S(1)} %pad_maximum_fusion), kind=kOutput, calls=%fused_computation.8 | convolution fusion | flops 939524096 | bytes 6029312 | tf_op jit(solution)/shard_map/dot_general | solution.py:102
  63.7 7.1 %add_convert_fusion = bf16[256,3584]{1,0:T(8,128)(2,1)} fusion(bf16[256,3584]{1,0:T(8,128)(2,1)} %collective-permute-done.7, f32[256]{0:T(256)S(1)} %fusion.47, bf16[1,512,3584]{2,1,0:T(8,128)(2,1)} %param.19, f32[256,512]{1,0:T(8,128)S(1)} %fusion.6, bf16[1,3584,512]{2,1,0:T(8,128)(2,1)} %param.17, bf16[256,3712]{1,0:T(8,128)(2,1)S(1)} %pad_maximum_fusion), kind=kOutput, calls=%fused_computation.14 | convolution fusion | flops 1883504640 | bytes 13370368 | tf_op jit(solution)/shard_map/dot_general | solution.py:106
  74.0 1.3 %collective-permute-start.10 = (bf16[128,1792]{1,0:T(8,128)(2,1)S(1)}, bf16[128,1792]{1,0:T(8,128)(2,1)S(1)}, u32[]{:S(2)}, u32[]{:S(2)}) collective-permute-start(bf16[128,1792]{1,0:T(8,128)(2,1)S(1)} %bitcast.46), channel_id=1, source_target_pairs={{0,1},{1,0},{2,3},{3,2},{4,5},{5,4},{6,7},{7,6},{8,9},{9,8},{10,11... | collective-permute-start | bytes 1376264 | tf_op jit(solution)/shard_map/ppermute | solution.py:38
  75.3 10.7 %collective-permute-done.8 = bf16[128,1792]{1,0:T(8,128)(2,1)S(1)} collective-permute-done((bf16[128,1792]{1,0:T(8,128)(2,1)S(1)}, bf16[128,1792]{1,0:T(8,128)(2,1)S(1)}, u32[]{:S(2)}, u32[]{:S(2)}) %collective-permute-start.8) | collective-permute-done | bytes 458784 | tf_op jit(solution)/shard_map/ppermute | solution.py:38
  87.1 1.7 %collective-permute-start.9 = (bf16[64,1792]{1,0:T(8,128)(2,1)S(1)}, bf16[64,1792]{1,0:T(8,128)(2,1)S(1)}, u32[]{:S(2)}, u32[]{:S(2)}) collective-permute-start(bf16[64,1792]{1,0:T(8,128)(2,1)S(1)} %slice.127), channel_id=1, source_target_pairs={{0,1},{1,0},{2,3},{3,2},{4,5},{5,4},{6,7},{7,6},{8,9},{9,8},{10,11... | collective-permute-start | bytes 688136 | tf_op jit(solution)/shard_map/ppermute | solution.py:38
  89.4 4.9 %collective-permute-done.9 = bf16[64,1792]{1,0:T(8,128)(2,1)S(1)} collective-permute-done((bf16[64,1792]{1,0:T(8,128)(2,1)S(1)}, bf16[64,1792]{1,0:T(8,128)(2,1)S(1)}, u32[]{:S(2)}, u32[]{:S(2)}) %collective-permute-start.9) | collective-permute-done | bytes 229408 | tf_op jit(solution)/shard_map/ppermute | solution.py:38
  94.3 1.5 %collective-permute-done.11 = bf16[64,1792]{1,0:T(8,128)(2,1)S(1)} collective-permute-done((bf16[64,1792]{1,0:T(8,128)(2,1)S(1)}, bf16[64,1792]{1,0:T(8,128)(2,1)S(1)}, u32[]{:S(2)}, u32[]{:S(2)}) %collective-permute-start.11) | collective-permute-done | bytes 229408 | tf_op jit(solution)/shard_map/ppermute | solution.py:38
  95.9 2.0 %collective-permute-start.12 = (bf16[32,3584]{1,0:T(8,128)(2,1)S(1)}, bf16[32,3584]{1,0:T(8,128)(2,1)S(1)}, u32[]{:S(2)}, u32[]{:S(2)}) collective-permute-start(bf16[32,3584]{1,0:T(8,128)(2,1)S(1)} %pad_maximum_fusion.8), channel_id=1, source_target_pairs={{0,8},{4,12},{8,0},{12,4},{16,24},{20,28},{24,16},{28,20},{1,9},{5... | collective-permute-start | bytes 688136 | tf_op jit(solution)/shard_map/ppermute | solution.py:38
  98.2 3.9 %collective-permute-done.12 = bf16[32,3584]{1,0:T(8,128)(2,1)S(1)} collective-permute-done((bf16[32,3584]{1,0:T(8,128)(2,1)S(1)}, bf16[32,3584]{1,0:T(8,128)(2,1)S(1)}, u32[]{:S(2)}, u32[]{:S(2)}) %collective-permute-start.12) | collective-permute-done | bytes 229408 | tf_op jit(solution)/shard_map/ppermute | solution.py:38
  102.1 4.5 %collective-permute-start.13 = (bf16[16,3584]{1,0:T(8,128)(2,1)S(1)}, bf16[16,3584]{1,0:T(8,128)(2,1)S(1)}, u32[]{:S(2)}, u32[]{:S(2)}) collective-permute-start(bf16[16,3584]{1,0:T(8,128)(2,1)S(1)} %slice.136), channel_id=1, source_target_pairs={{0,16},{4,20},{8,24},{12,28},{16,0},{20,4},{24,8},{28,12},{1,17},{... | collective-permute-start | bytes 344072 | tf_op jit(solution)/shard_map/ppermute | solution.py:38
  107.8 2.8 %collective-permute-done.13 = bf16[16,3584]{1,0:T(8,128)(2,1)S(1)} collective-permute-done((bf16[16,3584]{1,0:T(8,128)(2,1)S(1)}, bf16[16,3584]{1,0:T(8,128)(2,1)S(1)}, u32[]{:S(2)}, u32[]{:S(2)}) %collective-permute-start.13) | collective-permute-done | bytes 114720 | tf_op jit(solution)/shard_map/ppermute | solution.py:38
  (49 shorter events, 15.1 us)
Async XLA Ops:
  0.6 58.0 %copy-start = (bf16[4,64,576]{2,1,0:T(8,128)(2,1)S(1)}, bf16[4,64,576]{2,1,0:T(8,128)(2,1)}, u32[]{:S(2)}) copy-start(bf16[4,64,576]{2,1,0:T(8,128)(2,1)} %param.10) | copy-start | bytes 884740
  3.1 9.9 %collective-permute-start = (bf16[16,3712]{1,0:T(8,128)(2,1)S(1)}, bf16[16,3712]{1,0:T(8,128)(2,1)S(1)}, u32[]{:S(2)}, u32[]{:S(2)}) collective-permute-start(bf16[16,3712]{1,0:T(8,128)(2,1)S(1)} %pad_maximum_fusion.10), channel_id=1, source_target_pairs={{0,16},{4,20},{8,24},{12,28},{16,0},{20,4},{24,8},{28,12},{1,17},{... | collective-permute-start | bytes 356360 | tf_op jit(solution)/shard_map/ppermute | solution.py:38
  13.9 7.0 %collective-permute-start.1 = (bf16[32,3712]{1,0:T(8,128)(2,1)S(1)}, bf16[32,3712]{1,0:T(8,128)(2,1)S(1)}, u32[]{:S(2)}, u32[]{:S(2)}) collective-permute-start(bf16[32,3712]{1,0:T(8,128)(2,1)S(1)} %pad_maximum_fusion.7), channel_id=1, source_target_pairs={{0,8},{4,12},{8,0},{12,4},{16,24},{20,28},{24,16},{28,20},{1,9},{5... | collective-permute-start | bytes 712712 | tf_op jit(solution)/shard_map/ppermute | solution.py:38
  21.8 6.3 %collective-permute-start.4 = (bf16[64,1920]{1,0:T(8,128)(2,1)S(1)}, bf16[64,1920]{1,0:T(8,128)(2,1)S(1)}, u32[]{:S(2)}, u32[]{:S(2)}) collective-permute-start(bf16[64,1920]{1,0:T(8,128)(2,1)S(1)} %pad_maximum_fusion.4), channel_id=1, source_target_pairs={{0,2},{1,3},{2,0},{3,1},{4,6},{5,7},{6,4},{7,5},{8,10},{9,11},{10,... | collective-permute-start | bytes 737288 | tf_op jit(solution)/shard_map/ppermute | solution.py:38
  23.9 8.3 %collective-permute-start.2 = (bf16[64,1792]{1,0:T(8,128)(2,1)S(1)}, bf16[64,1792]{1,0:T(8,128)(2,1)S(1)}, u32[]{:S(2)}, u32[]{:S(2)}) collective-permute-start(bf16[64,1792]{1,0:T(8,128)(2,1)S(1)} %pad_maximum_fusion.9), channel_id=1, source_target_pairs={{0,1},{1,0},{2,3},{3,2},{4,5},{5,4},{6,7},{7,6},{8,9},{9,8},{10,11... | collective-permute-start | bytes 688136 | tf_op jit(solution)/shard_map/ppermute | solution.py:38
  28.1 12.5 %collective-permute-start.5 = (bf16[128,1920]{1,0:T(8,128)(2,1)S(1)}, bf16[128,1920]{1,0:T(8,128)(2,1)S(1)}, u32[]{:S(2)}, u32[]{:S(2)}) collective-permute-start(bf16[128,1920]{1,0:T(8,128)(2,1)S(1)} %pad_maximum_fusion.2), channel_id=1, source_target_pairs={{0,1},{1,0},{2,3},{3,2},{4,5},{5,4},{6,7},{7,6},{8,9},{9,8},{10,11... | collective-permute-start | bytes 1474568 | tf_op jit(solution)/shard_map/ppermute | solution.py:38
  32.2 8.5 %collective-permute-start.3 = (bf16[128,1792]{1,0:T(8,128)(2,1)S(1)}, bf16[128,1792]{1,0:T(8,128)(2,1)S(1)}, u32[]{:S(2)}, u32[]{:S(2)}) collective-permute-start(bf16[128,1792]{1,0:T(8,128)(2,1)S(1)} %pad_maximum_fusion.3), channel_id=1, source_target_pairs={{0,2},{1,3},{2,0},{3,1},{4,6},{5,7},{6,4},{7,5},{8,10},{9,11},{10,... | collective-permute-start | bytes 1376264 | tf_op jit(solution)/shard_map/ppermute | solution.py:38
  40.9 4.1 %collective-permute-start.6 = (bf16[256,3712]{1,0:T(8,128)(2,1)S(1)}, bf16[256,3712]{1,0:T(8,128)(2,1)}, u32[]{:S(2)}, u32[]{:S(2)}) collective-permute-start(bf16[256,3712]{1,0:T(8,128)(2,1)S(1)} %pad_maximum_fusion), channel_id=1, source_target_pairs={{0,4},{4,0},{8,12},{12,8},{16,20},{20,16},{24,28},{28,24},{1,5},{5... | collective-permute-start | bytes 5701640 | tf_op jit(solution)/shard_map/ppermute | solution.py:38
  50.6 8.1 %copy-start.2 = (s32[4]{0:T(128)S(1)}, s32[4]{0:T(128)}, u32[]{:S(2)}) copy-start(s32[4]{0:T(128)} %param.12) | copy-start | bytes 52
  57.9 5.8 %collective-permute-start.7 = (bf16[256,3584]{1,0:T(8,128)(2,1)}, bf16[256,3584]{1,0:T(8,128)(2,1)}, u32[]{:S(2)}, u32[]{:S(2)}) collective-permute-start(bf16[256,3584]{1,0:T(8,128)(2,1)} %fusion.1), channel_id=1, source_target_pairs={{0,4},{4,0},{8,12},{12,8},{16,20},{20,16},{24,28},{28,24},{1,5},{5... | collective-permute-start | bytes 5505032 | tf_op jit(solution)/shard_map/ppermute | solution.py:38
  73.1 12.8 %collective-permute-start.8 = (bf16[128,1792]{1,0:T(8,128)(2,1)S(1)}, bf16[128,1792]{1,0:T(8,128)(2,1)S(1)}, u32[]{:S(2)}, u32[]{:S(2)}) collective-permute-start(bf16[128,1792]{1,0:T(8,128)(2,1)S(1)} %slice.125), channel_id=1, source_target_pairs={{0,2},{1,3},{2,0},{3,1},{4,6},{5,7},{6,4},{7,5},{8,10},{9,11},{10,... | collective-permute-start | bytes 1376264 | tf_op jit(solution)/shard_map/ppermute | solution.py:38
  74.0 14.8 %collective-permute-start.10 = (bf16[128,1792]{1,0:T(8,128)(2,1)S(1)}, bf16[128,1792]{1,0:T(8,128)(2,1)S(1)}, u32[]{:S(2)}, u32[]{:S(2)}) collective-permute-start(bf16[128,1792]{1,0:T(8,128)(2,1)S(1)} %bitcast.46), channel_id=1, source_target_pairs={{0,1},{1,0},{2,3},{3,2},{4,5},{5,4},{6,7},{7,6},{8,9},{9,8},{10,11... | collective-permute-start | bytes 1376264 | tf_op jit(solution)/shard_map/ppermute | solution.py:38
  87.1 7.1 %collective-permute-start.9 = (bf16[64,1792]{1,0:T(8,128)(2,1)S(1)}, bf16[64,1792]{1,0:T(8,128)(2,1)S(1)}, u32[]{:S(2)}, u32[]{:S(2)}) collective-permute-start(bf16[64,1792]{1,0:T(8,128)(2,1)S(1)} %slice.127), channel_id=1, source_target_pairs={{0,1},{1,0},{2,3},{3,2},{4,5},{5,4},{6,7},{7,6},{8,9},{9,8},{10,11... | collective-permute-start | bytes 688136 | tf_op jit(solution)/shard_map/ppermute | solution.py:38
  89.0 17.6 %copy-start.1 = (bf16[4,256,576]{1,2,0:T(8,128)(2,1)S(1)}, bf16[4,256,576]{1,2,0:T(8,128)(2,1)}, u32[]{:S(2)}) copy-start(bf16[4,256,576]{1,2,0:T(8,128)(2,1)} %param.11) | copy-start | bytes 3538948
  89.0 6.9 %collective-permute-start.11 = (bf16[64,1792]{1,0:T(8,128)(2,1)S(1)}, bf16[64,1792]{1,0:T(8,128)(2,1)S(1)}, u32[]{:S(2)}, u32[]{:S(2)}) collective-permute-start(bf16[64,1792]{1,0:T(8,128)(2,1)S(1)} %slice.132), channel_id=1, source_target_pairs={{0,2},{1,3},{2,0},{3,1},{4,6},{5,7},{6,4},{7,5},{8,10},{9,11},{10,... | collective-permute-start | bytes 688136 | tf_op jit(solution)/shard_map/ppermute | solution.py:38
  95.9 6.1 %collective-permute-start.12 = (bf16[32,3584]{1,0:T(8,128)(2,1)S(1)}, bf16[32,3584]{1,0:T(8,128)(2,1)S(1)}, u32[]{:S(2)}, u32[]{:S(2)}) collective-permute-start(bf16[32,3584]{1,0:T(8,128)(2,1)S(1)} %pad_maximum_fusion.8), channel_id=1, source_target_pairs={{0,8},{4,12},{8,0},{12,4},{16,24},{20,28},{24,16},{28,20},{1,9},{5... | collective-permute-start | bytes 688136 | tf_op jit(solution)/shard_map/ppermute | solution.py:38
  102.1 8.5 %collective-permute-start.13 = (bf16[16,3584]{1,0:T(8,128)(2,1)S(1)}, bf16[16,3584]{1,0:T(8,128)(2,1)S(1)}, u32[]{:S(2)}, u32[]{:S(2)}) collective-permute-start(bf16[16,3584]{1,0:T(8,128)(2,1)S(1)} %slice.136), channel_id=1, source_target_pairs={{0,16},{4,20},{8,24},{12,28},{16,0},{20,4},{24,8},{28,12},{1,17},{... | collective-permute-start | bytes 344072 | tf_op jit(solution)/shard_map/ppermute | solution.py:38

commit v3 on v1

v3 whole, which is shorter than its diff:
```python
import functools

import jax
import jax.numpy as jnp
from jax import lax
from jax.experimental import pallas as pl
from jax.experimental.pallas import tpu as pltpu
from jax.sharding import PartitionSpec as P

LAT = 512
AXES = ("grp", "ep")
EXTRA = 128
BLOCKS = 4
VMEM_BYTES = 48 * 1024 * 1024

score_scale = 192.0 ** (-0.5)
neg_large = -1e30


def attend(queries, cache, lengths, live_count):
    scores = (
        jnp.einsum("rhc,rlc->rhl", queries, cache, preferred_element_type=jnp.float32) * score_scale
    )
    positions = lax.broadcasted_iota(jnp.int32, scores.shape, 2)
    inside = positions < lengths[:, None, None]
    masked = jnp.where(inside, scores, neg_large)
    highest = jnp.max(masked, axis=2, keepdims=True)
    powers = jnp.where(inside, jnp.exp(masked - highest), 0.0)
    totals = jnp.sum(powers, axis=2, keepdims=True)
    weights = (powers / totals).astype(jnp.bfloat16)
    context = jnp.einsum(
        "rhl,rlc->rhc", weights, cache[:, :, :LAT], preferred_element_type=jnp.float32
    ).astype(jnp.bfloat16)
    request_slot = lax.broadcasted_iota(jnp.int32, context.shape, 0)
    return jnp.where(request_slot < live_count, context, jnp.zeros_like(context))


def bits_of(count):
    return [1 << i for i in range(count.bit_length() - 1)]


def swap(value, step):
    axis, bit = step
    size = lax.axis_size(axis)
    return lax.ppermute(value, axis, [(i, i ^ bit) for i in range(size)])


def spread(value, steps):
    for step in steps:
        value = jnp.concatenate([value, swap(value, step)], axis=0)
    return value


def others(value, steps):
    if len(steps) == 1:
        return swap(value, steps[0])
    return spread(value, steps)[value.shape[0] :]


def give_back(rest, steps, rows):
    terms = []
    for step in reversed(steps):
        keep = (rest.shape[0] + rows) // 2 - rows
        arrived = swap(rest[keep:], step)
        terms.append(arrived[:rows])
        if keep:
            rest = add_up(rest[:keep], [arrived[rows:]])
    return terms


def add_up(own, terms):
    total = own.astype(jnp.float32)
    for term in terms:
        total = total + term.astype(jnp.float32)
    return total.astype(jnp.bfloat16)


def pack_kernel(tokens, ids, gates, out):
    feature = tokens.shape[1]
    high = gates[...].astype(jnp.bfloat16)
    low = (gates[...] - high.astype(jnp.float32)).astype(jnp.bfloat16)
    named = ids[...].astype(jnp.float32).astype(jnp.bfloat16)
    stacked = jnp.concatenate(
        [named.astype(jnp.float32), high.astype(jnp.float32), low.astype(jnp.float32)], axis=0
    ).astype(jnp.bfloat16)
    row = lax.broadcasted_iota(jnp.int32, (stacked.shape[0], EXTRA), 0)
    column = lax.broadcasted_iota(jnp.int32, (stacked.shape[0], EXTRA), 1)
    place = jnp.where(row == column, 1.0, 0.0).astype(jnp.bfloat16)
    extra = lax.dot_general(
        stacked, place, (((0,), (0,)), ((), ())), preferred_element_type=jnp.float32
    )
    out[:, :feature] = tokens[...]
    out[:, feature:] = extra.astype(jnp.bfloat16)


def pack(tokens, ids, gates):
    return pl.pallas_call(
        pack_kernel,
        out_shape=jax.ShapeDtypeStruct((tokens.shape[0], tokens.shape[1] + EXTRA), jnp.bfloat16),
        in_specs=[pl.BlockSpec(memory_space=pltpu.VMEM)] * 3,
        out_specs=pl.BlockSpec(memory_space=pltpu.VMEM),
        name="pack",
    )(tokens, ids.T, gates.T)


def hidden_kernel(picks, expert, own, other, extra_own, extra_other, w_gate, w_up, h_own, h_other, gate_sum, up_sum):
    step = pl.program_id(0)
    rows = jnp.concatenate([own[...], other[...]], axis=0)
    gate_part = jnp.dot(rows, w_gate[0], preferred_element_type=jnp.float32)
    up_part = jnp.dot(rows, w_up[0], preferred_element_type=jnp.float32)

    @pl.when(step == 0)
    def _():
        gate_sum[...] = gate_part
        up_sum[...] = up_part

    @pl.when(step > 0)
    def _():
        gate_sum[...] += gate_part
        up_sum[...] += up_part

    @pl.when(step == pl.num_programs(0) - 1)
    def _():
        count = own.shape[0]
        wanted = expert[0].astype(jnp.float32)
        for extra, out, at in ((extra_own, h_own, 0), (extra_other, h_other, count)):
            columns = extra[...].astype(jnp.float32)
            value = columns[:, picks : 2 * picks] + columns[:, 2 * picks : 3 * picks]
            share = jnp.sum(
                jnp.where(columns[:, :picks] == wanted, value, 0.0), axis=1, keepdims=True
            )
            gate_all = gate_sum[at : at + count, :]
            up_all = up_sum[at : at + count, :]
            hidden = gate_all / (1.0 + jnp.exp(-gate_all)) * up_all
            out[...] = (hidden * share).astype(jnp.bfloat16)


def hidden_of(expert, own, other, w_gate, w_up, picks):
    count, width = own.shape
    _, feature, half = w_gate.shape
    depth = feature // BLOCKS
    rows_spec = pl.BlockSpec((count, depth), lambda k: (0, k))
    extra_spec = pl.BlockSpec((count, EXTRA), lambda k: (0, feature // EXTRA))
    weight_spec = pl.BlockSpec((1, depth, half), lambda k: (0, k, 0))
    out_spec = pl.BlockSpec((count, half), lambda k: (0, 0))
    return pl.pallas_call(
        functools.partial(hidden_kernel, picks),
        grid=(BLOCKS,),
        out_shape=[jax.ShapeDtypeStruct((count, half), jnp.bfloat16)] * 2,
        in_specs=[pl.BlockSpec(memory_space=pltpu.SMEM), rows_spec, rows_spec, extra_spec, extra_spec]
        + [weight_spec] * 2,
        out_specs=[out_spec] * 2,
        scratch_shapes=[pltpu.VMEM((2 * count, half), jnp.float32)] * 2,
        compiler_params=pltpu.CompilerParams(vmem_limit_bytes=VMEM_BYTES),
        cost_estimate=pl.CostEstimate(
            flops=8 * count * feature * half,
            bytes_accessed=4 * feature * half + 4 * count * width,
            transcendentals=2 * count * half,
        ),
        name="hidden",
    )(expert, own, other, own, other, w_gate, w_up)


def down_kernel(cuts, hidden, w_down, *refs):
    part = jnp.dot(hidden[...], w_down[0], preferred_element_type=jnp.float32)
    if len(refs) > len(cuts):
        part = part + refs[0][...].astype(jnp.float32)
        refs = refs[1:]
    at = 0
    for cut, out in zip(cuts, refs):
        out[...] = part[at : at + cut, :].astype(jnp.bfloat16)
        at += cut


def down_of(hidden, w_down, cuts, arrived=None):
    count, half = hidden.shape
    feature = w_down.shape[2]
    wide = feature // BLOCKS
    operands = [hidden, w_down]
    in_specs = [
        pl.BlockSpec((count, half), lambda n: (0, 0)),
        pl.BlockSpec((1, half, wide), lambda n: (0, 0, n)),
    ]
    if arrived is not None:
        operands.append(arrived)
        in_specs.append(pl.BlockSpec((count, wide), lambda n: (0, n)))
    return pl.pallas_call(
        functools.partial(down_kernel, cuts),
        grid=(BLOCKS,),
        out_shape=[jax.ShapeDtypeStruct((cut, feature), jnp.bfloat16) for cut in cuts],
        in_specs=in_specs,
        out_specs=[pl.BlockSpec((cut, wide), lambda n: (0, n)) for cut in cuts],
        compiler_params=pltpu.CompilerParams(vmem_limit_bytes=VMEM_BYTES),
        cost_estimate=pl.CostEstimate(
            flops=2 * count * feature * half,
            bytes_accessed=2 * feature * half + 4 * count * feature,
            transcendentals=0,
        ),
        name="down",
    )(*operands)


def per_device(queries, cache, lengths, live_rows, tokens, ids, gates, w_gate, w_up, w_down):
    picks = ids.shape[1]
    grp_bits = bits_of(lax.axis_size("grp"))
    ep_bits = bits_of(lax.axis_size("ep"))
    core = ("grp", 1)
    z_near = [("grp", bit) for bit in reversed(grp_bits[1:-1])]
    z_far = ("grp", grp_bits[-1])
    x_steps = [("ep", bit) for bit in ep_bits[: len(ep_bits) // 2]]
    y_steps = [("ep", bit) for bit in ep_bits[len(ep_bits) // 2 :]]
    expert = ((lax.axis_index("grp") * lax.axis_size("ep") + lax.axis_index("ep")) >> 1).reshape(1)

    packed = pack(tokens, ids, gates)
    near = spread(packed, z_near)
    far = spread(swap(packed, z_far), z_near)
    near_x, near_y = others(near, x_steps), others(near, y_steps)
    far_x, far_y = others(far, x_steps), others(far, y_steps)
    near_xy, far_xy = others(near_x, y_steps), others(far_y, x_steps)
    early = [near, near_x, near_y, far, far_x, far_y]
    late = [near_xy, far_xy]
    early_cuts = [group.shape[0] for group in early]
    late_cuts = [group.shape[0] for group in late]
    early_own = jnp.concatenate(early, axis=0)
    late_own = jnp.concatenate(late, axis=0)
    early_other = swap(early_own, core)
    late_other = swap(late_own, core)

    context = attend(queries, cache, lengths, live_rows[0])

    early_h, early_h_other = hidden_of(expert, early_own, early_other, w_gate, w_up, picks)
    late_h, late_h_other = hidden_of(expert, late_own, late_other, w_gate, w_up, picks)

    (late_out,) = down_of(late_h_other, w_down, [late_h_other.shape[0]])
    late_in = swap(late_out, core)
    (early_out,) = down_of(early_h_other, w_down, [early_h_other.shape[0]])
    early_in = swap(early_out, core)
    near_xy, far_xy = down_of(late_h, w_down, late_cuts, late_in)
    near, near_x, near_y, far, far_x, far_y = down_of(early_h, w_down, early_cuts, early_in)
    rows, count = near.shape[0], tokens.shape[0]
    near_x = add_up(near_x, give_back(near_xy, y_steps, near_x.shape[0]))
    far_y = add_up(far_y, give_back(far_xy, x_steps, far_y.shape[0]))
    far = add_up(far, give_back(far_x, x_steps, rows) + give_back(far_y, y_steps, rows))
    near = add_up(near, give_back(near_y, y_steps, rows) + give_back(near_x, x_steps, rows))
    far = add_up(far[:count], give_back(far[count:], z_near, count))
    mixed = add_up(near[:count], give_back(near[count:], z_near, count) + [swap(far, z_far)])
    return (context, mixed)


def solution(mesh):
    rows3 = P(AXES, None, None)
    rows2 = P(AXES, None)
    rows1 = P(AXES)
    return jax.shard_map(
        per_device,
        mesh=mesh,
        in_specs=(rows3, rows3, rows1, rows1, rows2, rows2, rows2, rows3, rows3, rows3),
        out_specs=(rows3, rows2),
        check_vma=False,
    )
```

time: 304 us -> 91.9 us (0.30)
  blocking collectives: 135 us -> 0 us
  waiting for transfers between devices: 136 us -> 37.2 us
  starting transfers between devices: 0.08 us -> 24.5 us
  Pallas kernels: 0 us -> 22.5 us
  matrix products: 16.9 us -> 1.58 us
  between operations: 14.8 us -> 1.52 us
    all_gather x2 -> x0, blocking collectives: 135 us -> none  [the longest x1 70.9 us: per_device(): all_ids = lax.all_gather(ids, AXES, axis=0, tiled=True)]
    reduce_scatter x1 -> x0, waiting for transfers between devices: 135 us -> none  [per_device(): mixed = lax.psum_scatter(weighted, AXES, scatter_dimension=0, tiled=True)]
    ppermute x0 -> x22, waiting for transfers between devices: none -> 37.2 us  [swap(): return lax.ppermute(value, axis, [(i, i ^ bit) for i in range(size)])]
    ppermute x0 -> x22, starting transfers between devices: none -> 24.5 us  [swap(): return lax.ppermute(value, axis, [(i, i ^ bit) for i in range(size)])]
    pallas_call x0 -> x7, Pallas kernels: none -> 22.5 us  [the longest x2 11.8 us: hidden_of(): pl.pallas_call(functools.partial(hidden_kernel, picks), grid=(BLOCKS,), o...]
    dot_general x2 -> x0, matrix products: 15.3 us -> none  [the longest x1 10.1 us: per_device(): partial_out = jnp.dot(hidden, w_down[0], preferred_element_type=jnp.float32)]
  transfers between devices with their start and end apart: 2 -> 22, of which waited for: 1 -> 15; matrix products, arithmetic and copies ran while one was open for 1% -> 6% of each run, Pallas kernels for 0% -> 23%
where the time goes in v3:
time: 91.9 us; the launch traced here: 91.5 us
  waiting for transfers between devices  37.2 us (40%)
  starting transfers between devices  24.5 us (27%)
  Pallas kernels  22.5 us (24%)
  other arithmetic  2.16 us (2%)
  local copies, waits for them, and re-layouts  2.14 us (2%)
  matrix products  1.58 us (2%)
  between operations  1.52 us (2%)
    ppermute x22, waiting for transfers between devices, swap(): return lax.ppermute(value, axis, [(i, i ^ bit) for i in range(size)])  37.2 us
    ppermute x22, starting transfers between devices, swap(): return lax.ppermute(value, axis, [(i, i ^ bit) for i in range(size)])  24.5 us
    pallas_call x2, Pallas kernels, hidden_of(): pl.pallas_call(functools.partial(hidden_kernel, picks), grid=(BLOCKS,), o...  11.8 us
    pallas_call x4, Pallas kernels, down_of(): pl.pallas_call(functools.partial(down_kernel, cuts), grid=(BLOCKS,), out_...  8.94 us
    unnamed x20, local copies, waits for them, and re-layouts  2.07 us
  transfers between devices with their start and end apart: 22, of which 15 were waited for; matrix products, arithmetic and copies ran while one was open for 6% of the time, Pallas kernels for 23%

profile of v3, /device:TPU:0, one launch (start us, length us, event | category | flops | bytes accessed | tf_op | source)
XLA Modules:
  0.0 91.5 jit_solution(15221340493903654820)
XLA Ops:
  0.6 1.8 %pack.1 = bf16[16,3712]{1,0:T(8,128)(2,1)} custom-call(bf16[16,3584]{1,0:T(8,128)(2,1)} %tokens.1, s32[8,16]{1,0:T(8,128)} %bitcast.9, f32[8,16]{1,0:T(8,128)} %bitcast.10), custom_call_target="tpu_custom_call" | custom-call | tf_op jit(solution)/shard_map/pack/pallas_call | solution.py:97
  2.4 3.0 %collective-permute-start = (bf16[16,3712]{1,0:T(8,128)(2,1)}, bf16[16,3712]{1,0:T(8,128)(2,1)S(1)}, u32[]{:S(2)}, u32[]{:S(2)}) collective-permute-start(bf16[16,3712]{1,0:T(8,128)(2,1)} %pack.1), channel_id=1, source_target_pairs={{0,8},{4,12},{8,0},{12,4},{16,24},{20,28},{24,16},{28,20},{1,9},{5... | collective-permute-start | bytes 356360 | tf_op jit(solution)/shard_map/ppermute | solution.py:45
  5.5 2.6 %collective-permute-start.3 = (bf16[16,3712]{1,0:T(8,128)(2,1)}, bf16[16,3712]{1,0:T(8,128)(2,1)S(1)}, u32[]{:S(2)}, u32[]{:S(2)}) collective-permute-start(bf16[16,3712]{1,0:T(8,128)(2,1)} %pack.1), channel_id=1, source_target_pairs={{0,16},{4,20},{8,24},{12,28},{16,0},{20,4},{24,8},{28,12},{1,17},{... | collective-permute-start | bytes 356360 | tf_op jit(solution)/shard_map/ppermute | solution.py:45
  11.1 1.9 %collective-permute-start.1 = (bf16[32,3712]{1,0:T(8,128)(2,1)S(1)}, bf16[32,3712]{1,0:T(8,128)(2,1)S(1)}, u32[]{:S(2)}, u32[]{:S(2)}) collective-permute-start(bf16[32,3712]{1,0:T(8,128)(2,1)S(1)} %pad_maximum_fusion), channel_id=1, source_target_pairs={{0,1},{1,0},{2,3},{3,2},{4,5},{5,4},{6,7},{7,6},{8,9},{9,8},{10,11... | collective-permute-start | bytes 712712 | tf_op jit(solution)/shard_map/ppermute | solution.py:45
  13.0 1.5 %collective-permute-start.2 = (bf16[32,3712]{1,0:T(8,128)(2,1)S(1)}, bf16[32,3712]{1,0:T(8,128)(2,1)S(1)}, u32[]{:S(2)}, u32[]{:S(2)}) collective-permute-start(bf16[32,3712]{1,0:T(8,128)(2,1)S(1)} %pad_maximum_fusion), channel_id=1, source_target_pairs={{0,2},{1,3},{2,0},{3,1},{4,6},{5,7},{6,4},{7,5},{8,10},{9,11},{10,... | collective-permute-start | bytes 712712 | tf_op jit(solution)/shard_map/ppermute | solution.py:45
  14.9 2.4 %collective-permute-done.1 = bf16[32,3712]{1,0:T(8,128)(2,1)S(1)} collective-permute-done((bf16[32,3712]{1,0:T(8,128)(2,1)S(1)}, bf16[32,3712]{1,0:T(8,128)(2,1)S(1)}, u32[]{:S(2)}, u32[]{:S(2)}) %collective-permute-start.1) | collective-permute-done | bytes 237600 | tf_op jit(solution)/shard_map/ppermute | solution.py:45
  17.3 1.8 %collective-permute-done.2 = bf16[32,3712]{1,0:T(8,128)(2,1)S(1)} collective-permute-done((bf16[32,3712]{1,0:T(8,128)(2,1)S(1)}, bf16[32,3712]{1,0:T(8,128)(2,1)S(1)}, u32[]{:S(2)}, u32[]{:S(2)}) %collective-permute-start.2) | collective-permute-done | bytes 237600 | tf_op jit(solution)/shard_map/ppermute | solution.py:45
  20.3 1.5 %collective-permute-start.6 = (bf16[32,3712]{1,0:T(8,128)(2,1)S(1)}, bf16[32,3712]{1,0:T(8,128)(2,1)S(1)}, u32[]{:S(2)}, u32[]{:S(2)}) collective-permute-start(bf16[32,3712]{1,0:T(8,128)(2,1)S(1)} %get-tuple-element.27), channel_id=1, source_target_pairs={{0,2},{1,3},{2,0},{3,1},{4,6},{5,7},{6,4},{7,5},{8,10},{9,11},{10,... | collective-permute-start | bytes 712712 | tf_op jit(solution)/shard_map/ppermute | solution.py:45
  21.8 3.7 %collective-permute-done.5 = bf16[32,3712]{1,0:T(8,128)(2,1)S(1)} collective-permute-done((bf16[32,3712]{1,0:T(8,128)(2,1)S(1)}, bf16[32,3712]{1,0:T(8,128)(2,1)S(1)}, u32[]{:S(2)}, u32[]{:S(2)}) %collective-permute-start.5) | collective-permute-done | bytes 237600 | tf_op jit(solution)/shard_map/ppermute | solution.py:45
  26.5 1.6 %collective-permute-start.10 = (bf16[32,3712]{1,0:T(8,128)(2,1)S(1)}, bf16[32,3712]{1,0:T(8,128)(2,1)}, u32[]{:S(2)}, u32[]{:S(2)}) collective-permute-start(bf16[32,3712]{1,0:T(8,128)(2,1)S(1)} %collective-permute-done.1), channel_id=1, source_target_pairs={{0,2},{1,3},{2,0},{3,1},{4,6},{5,7},{6,4},{7,5},{8,10},{9,11},{10,... | collective-permute-start | bytes 712712 | tf_op jit(solution)/shard_map/ppermute | solution.py:45
  29.1 5.7 %collective-permute-done.10 = bf16[32,3712]{1,0:T(8,128)(2,1)} collective-permute-done((bf16[32,3712]{1,0:T(8,128)(2,1)S(1)}, bf16[32,3712]{1,0:T(8,128)(2,1)}, u32[]{:S(2)}, u32[]{:S(2)}) %collective-permute-start.10) | collective-permute-done | bytes 237600 | tf_op jit(solution)/shard_map/ppermute | solution.py:45
  35.8 7.3 %hidden.2 = (bf16[192,512]{1,0:T(8,128)(2,1)S(1)}, bf16[192,512]{1,0:T(8,128)(2,1)S(1)}) custom-call(s32[1]{0:T(128)} %bitcast.1.expert, bf16[192,3712]{1,0:T(8,128)(2,1)S(1)} %constant_dynamic-update-slice_fusion.2.own.extra_own, bf16[192,3712]{1,0:T(8,128)(2,1)S(1)} %collective-permute-done.7.other.extra_other, ...), custom_call_target="tpu_custom_call" | custom-call | flops 2818572288 | bytes 10190848 | tf_op jit(solution)/shard_map/hidden/pallas_call | solution.py:146
  43.1 2.0 %down.4 = bf16[192,3584]{1,0:T(8,128)(2,1)S(1)} custom-call(bf16[192,512]{1,0:T(8,128)(2,1)S(1)} %get-tuple-element.15.hidden, bf16[1,512,3584]{2,1,0:T(8,128)(2,1)S(1)} %copy-done.1), custom_call_target="tpu_custom_call" | custom-call | flops 704643072 | bytes 6422528 | tf_op jit(solution)/shard_map/down/pallas_call | solution.py:187
  45.8 3.2 %collective-permute-done.12.other.extra_other = bf16[64,3712]{1,0:T(8,128)(2,1)S(1)} collective-permute-done((bf16[64,3712]{1,0:T(8,128)(2,1)S(1)}, bf16[64,3712]{1,0:T(8,128)(2,1)S(1)}, u32[]{:S(2)}, u32[]{:S(2)}) %collective-permute-start.12) | collective-permute-done | bytes 475168 | tf_op jit(solution)/shard_map/ppermute | solution.py:45
  49.0 4.5 %hidden.3 = (bf16[64,512]{1,0:T(8,128)(2,1)S(1)}, bf16[64,512]{1,0:T(8,128)(2,1)S(1)}) custom-call(s32[1]{0:T(128)} %bitcast.1.expert, bf16[64,3712]{1,0:T(8,128)(2,1)S(1)} %constant_dynamic-update-slice_fusion.10.own.extra_own, bf16[64,3712]{1,0:T(8,128)(2,1)S(1)} %collective-permute-done.12.other.extra_other, ...), custom_call_target="tpu_custom_call" | custom-call | flops 939524096 | bytes 8290304 | tf_op jit(solution)/shard_map/hidden/pallas_call | solution.py:146
  53.5 1.6 %down.6 = bf16[64,3584]{1,0:T(8,128)(2,1)S(1)} custom-call(bf16[64,512]{1,0:T(8,128)(2,1)S(1)} %get-tuple-element.20.hidden, bf16[1,512,3584]{2,1,0:T(8,128)(2,1)S(1)} %copy-done.1), custom_call_target="tpu_custom_call" | custom-call | flops 234881024 | bytes 4587520 | tf_op jit(solution)/shard_map/down/pallas_call | solution.py:187
  56.9 1.6 %down.7 = (bf16[32,3584]{1,0:T(8,128)(2,1)S(1)}, bf16[32,3584]{1,0:T(8,128)(2,1)S(1)}) custom-call(bf16[64,512]{1,0:T(8,128)(2,1)S(1)} %get-tuple-element.19.hidden, bf16[1,512,3584]{2,1,0:T(8,128)(2,1)S(1)} %copy-done.1, bf16[64,3584]{1,0:T(8,128)(2,1)S(1)} %collective-permute-done.13.refs_0_), custom_call_target="tpu_custom_call" | custom-call | flops 234881024 | bytes 4587520 | tf_op jit(solution)/shard_map/down/pallas_call | solution.py:187
  61.5 3.8 %down.5 = (bf16[32,3584]{1,0:T(8,128)(2,1)S(1)}, bf16[32,3584]{1,0:T(8,128)(2,1)S(1)}, bf16[32,3584]{1,0:T(8,128)(2,1)S(1)}, bf16[32,3584]{1,0:T(8,128)(2,1)S(1)...) custom-call(bf16[192,512]{1,0:T(8,128)(2,1)S(1)} %get-tuple-element.14.hidden, ...), custom_call_target="tpu_custom_call" | custom-call | flops 704643072 | bytes 6422528 | tf_op jit(solution)/shard_map/down/pallas_call | solution.py:187
  66.3 1.6 %collective-permute-start.19 = (bf16[32,3584]{1,0:T(8,128)(2,1)S(1)}, bf16[32,3584]{1,0:T(8,128)(2,1)S(1)}, u32[]{:S(2)}, u32[]{:S(2)}) collective-permute-start(bf16[32,3584]{1,0:T(8,128)(2,1)S(1)} %add_convert_fusion.1), channel_id=1, source_target_pairs={{0,2},{1,3},{2,0},{3,1},{4,6},{5,7},{6,4},{7,5},{8,10},{9,11},{10,... | collective-permute-start | bytes 688136 | tf_op jit(solution)/shard_map/ppermute | solution.py:45
  70.6 4.4 %collective-permute-done.19 = bf16[32,3584]{1,0:T(8,128)(2,1)S(1)} collective-permute-done((bf16[32,3584]{1,0:T(8,128)(2,1)S(1)}, bf16[32,3584]{1,0:T(8,128)(2,1)S(1)}, u32[]{:S(2)}, u32[]{:S(2)}) %collective-permute-start.19) | collective-permute-done | bytes 229408 | tf_op jit(solution)/shard_map/ppermute | solution.py:45
  74.9 1.5 %collective-permute-done.17 = bf16[32,3584]{1,0:T(8,128)(2,1)S(1)} collective-permute-done((bf16[32,3584]{1,0:T(8,128)(2,1)S(1)}, bf16[32,3584]{1,0:T(8,128)(2,1)S(1)}, u32[]{:S(2)}, u32[]{:S(2)}) %collective-permute-start.17) | collective-permute-done | bytes 229408 | tf_op jit(solution)/shard_map/ppermute | solution.py:45
  77.1 2.3 %collective-permute-done.15 = bf16[32,3584]{1,0:T(8,128)(2,1)S(1)} collective-permute-done((bf16[32,3584]{1,0:T(8,128)(2,1)S(1)}, bf16[32,3584]{1,0:T(8,128)(2,1)S(1)}, u32[]{:S(2)}, u32[]{:S(2)}) %collective-permute-start.15) | collective-permute-done | bytes 229408 | tf_op jit(solution)/shard_map/ppermute | solution.py:45
  80.0 3.8 %collective-permute-done.20 = bf16[16,3584]{1,0:T(8,128)(2,1)S(1)} collective-permute-done((bf16[16,3584]{1,0:T(8,128)(2,1)S(1)}, bf16[16,3584]{1,0:T(8,128)(2,1)S(1)}, u32[]{:S(2)}, u32[]{:S(2)}) %collective-permute-start.20) | collective-permute-done | bytes 114720 | tf_op jit(solution)/shard_map/ppermute | solution.py:45
  86.5 4.3 %collective-permute-done.21 = bf16[16,3584]{1,0:T(8,128)(2,1)S(1)} collective-permute-done((bf16[16,3584]{1,0:T(8,128)(2,1)S(1)}, bf16[16,3584]{1,0:T(8,128)(2,1)S(1)}, u32[]{:S(2)}, u32[]{:S(2)}) %collective-permute-start.21) | collective-permute-done | bytes 114720 | tf_op jit(solution)/shard_map/ppermute | solution.py:45
  (62 shorter events, 20.6 us)
Async XLA Ops:
  0.6 55.3 %copy-start = (bf16[4,64,576]{2,1,0:T(8,128)(2,1)S(1)}, bf16[4,64,576]{2,1,0:T(8,128)(2,1)}, u32[]{:S(2)}) copy-start(bf16[4,64,576]{2,1,0:T(8,128)(2,1)} %param.10) | copy-start | bytes 884740
  2.4 7.7 %collective-permute-start = (bf16[16,3712]{1,0:T(8,128)(2,1)}, bf16[16,3712]{1,0:T(8,128)(2,1)S(1)}, u32[]{:S(2)}, u32[]{:S(2)}) collective-permute-start(bf16[16,3712]{1,0:T(8,128)(2,1)} %pack.1), channel_id=1, source_target_pairs={{0,8},{4,12},{8,0},{12,4},{16,24},{20,28},{24,16},{28,20},{1,9},{5... | collective-permute-start | bytes 356360 | tf_op jit(solution)/shard_map/ppermute | solution.py:45
  5.5 9.1 %collective-permute-start.3 = (bf16[16,3712]{1,0:T(8,128)(2,1)}, bf16[16,3712]{1,0:T(8,128)(2,1)S(1)}, u32[]{:S(2)}, u32[]{:S(2)}) collective-permute-start(bf16[16,3712]{1,0:T(8,128)(2,1)} %pack.1), channel_id=1, source_target_pairs={{0,16},{4,20},{8,24},{12,28},{16,0},{20,4},{24,8},{28,12},{1,17},{... | collective-permute-start | bytes 356360 | tf_op jit(solution)/shard_map/ppermute | solution.py:45
  11.1 6.2 %collective-permute-start.1 = (bf16[32,3712]{1,0:T(8,128)(2,1)S(1)}, bf16[32,3712]{1,0:T(8,128)(2,1)S(1)}, u32[]{:S(2)}, u32[]{:S(2)}) collective-permute-start(bf16[32,3712]{1,0:T(8,128)(2,1)S(1)} %pad_maximum_fusion), channel_id=1, source_target_pairs={{0,1},{1,0},{2,3},{3,2},{4,5},{5,4},{6,7},{7,6},{8,9},{9,8},{10,11... | collective-permute-start | bytes 712712 | tf_op jit(solution)/shard_map/ppermute | solution.py:45
  13.0 6.1 %collective-permute-start.2 = (bf16[32,3712]{1,0:T(8,128)(2,1)S(1)}, bf16[32,3712]{1,0:T(8,128)(2,1)S(1)}, u32[]{:S(2)}, u32[]{:S(2)}) collective-permute-start(bf16[32,3712]{1,0:T(8,128)(2,1)S(1)} %pad_maximum_fusion), channel_id=1, source_target_pairs={{0,2},{1,3},{2,0},{3,1},{4,6},{5,7},{6,4},{7,5},{8,10},{9,11},{10,... | collective-permute-start | bytes 712712 | tf_op jit(solution)/shard_map/ppermute | solution.py:45
  14.5 4.8 %collective-permute-start.4 = (bf16[16,3712]{1,0:T(8,128)(2,1)S(1)}, bf16[16,3712]{1,0:T(8,128)(2,1)S(1)}, u32[]{:S(2)}, u32[]{:S(2)}) collective-permute-start(bf16[16,3712]{1,0:T(8,128)(2,1)S(1)} %collective-permute-done.3), channel_id=1, source_target_pairs={{0,8},{4,12},{8,0},{12,4},{16,24},{20,28},{24,16},{28,20},{1,9},{5... | collective-permute-start | bytes 356360 | tf_op jit(solution)/shard_map/ppermute | solution.py:45
  19.4 6.2 %collective-permute-start.5 = (bf16[32,3712]{1,0:T(8,128)(2,1)S(1)}, bf16[32,3712]{1,0:T(8,128)(2,1)S(1)}, u32[]{:S(2)}, u32[]{:S(2)}) collective-permute-start(bf16[32,3712]{1,0:T(8,128)(2,1)S(1)} %get-tuple-element.27), channel_id=1, source_target_pairs={{0,1},{1,0},{2,3},{3,2},{4,5},{5,4},{6,7},{7,6},{8,9},{9,8},{10,11... | collective-permute-start | bytes 712712 | tf_op jit(solution)/shard_map/ppermute | solution.py:45
  20.3 6.1 %collective-permute-start.6 = (bf16[32,3712]{1,0:T(8,128)(2,1)S(1)}, bf16[32,3712]{1,0:T(8,128)(2,1)S(1)}, u32[]{:S(2)}, u32[]{:S(2)}) collective-permute-start(bf16[32,3712]{1,0:T(8,128)(2,1)S(1)} %get-tuple-element.27), channel_id=1, source_target_pairs={{0,2},{1,3},{2,0},{3,1},{4,6},{5,7},{6,4},{7,5},{8,10},{9,11},{10,... | collective-permute-start | bytes 712712 | tf_op jit(solution)/shard_map/ppermute | solution.py:45
  26.4 9.3 %collective-permute-start.7 = (bf16[192,3712]{1,0:T(8,128)(2,1)S(1)}, bf16[192,3712]{1,0:T(8,128)(2,1)S(1)}, u32[]{:S(2)}, u32[]{:S(2)}) collective-permute-start(bf16[192,3712]{1,0:T(8,128)(2,1)S(1)} %constant_dynamic-update-slice_fusion.2.own.extra_own), channel_id=1, source_target_pairs={{0,4},{4,0},{8,12},{12,8},{16,20},{20,16},{24,28},{28,24},{1,5},{5... | collective-permute-start | bytes 4276232 | tf_op jit(solution)/shard_map/ppermute | solution.py:45
  26.5 8.3 %collective-permute-start.10 = (bf16[32,3712]{1,0:T(8,128)(2,1)S(1)}, bf16[32,3712]{1,0:T(8,128)(2,1)}, u32[]{:S(2)}, u32[]{:S(2)}) collective-permute-start(bf16[32,3712]{1,0:T(8,128)(2,1)S(1)} %collective-permute-done.1), channel_id=1, source_target_pairs={{0,2},{1,3},{2,0},{3,1},{4,6},{5,7},{6,4},{7,5},{8,10},{9,11},{10,... | collective-permute-start | bytes 712712 | tf_op jit(solution)/shard_map/ppermute | solution.py:45
  28.1 17.1 %collective-permute-start.11 = (bf16[32,3712]{1,0:T(8,128)(2,1)}, bf16[32,3712]{1,0:T(8,128)(2,1)S(1)}, u32[]{:S(2)}, u32[]{:S(2)}) collective-permute-start(bf16[32,3712]{1,0:T(8,128)(2,1)} %copy-done.4), channel_id=1, source_target_pairs={{0,1},{1,0},{2,3},{3,2},{4,5},{5,4},{6,7},{7,6},{8,9},{9,8},{10,11... | collective-permute-start | bytes 712712 | tf_op jit(solution)/shard_map/ppermute | solution.py:45
  35.8 7.3 %copy-start.1 = (bf16[1,512,3584]{2,1,0:T(8,128)(2,1)S(1)}, bf16[1,512,3584]{2,1,0:T(8,128)(2,1)}, u32[]{:S(2)}) copy-start(bf16[1,512,3584]{2,1,0:T(8,128)(2,1)} %w_down.7) | copy-start | bytes 11010052
  45.1 16.4 %collective-permute-start.8 = (bf16[192,3584]{1,0:T(8,128)(2,1)S(1)}, bf16[192,3584]{1,0:T(8,128)(2,1)S(1)}, u32[]{:S(2)}, u32[]{:S(2)}) collective-permute-start(bf16[192,3584]{1,0:T(8,128)(2,1)S(1)} %down.4), channel_id=1, source_target_pairs={{0,4},{4,0},{8,12},{12,8},{16,20},{20,16},{24,28},{28,24},{1,5},{5... | collective-permute-start | bytes 4128776 | tf_op jit(solution)/shard_map/ppermute | solution.py:45
  45.2 3.8 %collective-permute-start.12 = (bf16[64,3712]{1,0:T(8,128)(2,1)S(1)}, bf16[64,3712]{1,0:T(8,128)(2,1)S(1)}, u32[]{:S(2)}, u32[]{:S(2)}) collective-permute-start(bf16[64,3712]{1,0:T(8,128)(2,1)S(1)} %constant_dynamic-update-slice_fusion.10.own.extra_own), channel_id=1, source_target_pairs={{0,4},{4,0},{8,12},{12,8},{16,20},{20,16},{24,28},{28,24},{1,5},{5... | collective-permute-start | bytes 1425416 | tf_op jit(solution)/shard_map/ppermute | solution.py:45
  55.0 1.9 %collective-permute-start.13 = (bf16[64,3584]{1,0:T(8,128)(2,1)S(1)}, bf16[64,3584]{1,0:T(8,128)(2,1)S(1)}, u32[]{:S(2)}, u32[]{:S(2)}) collective-permute-start(bf16[64,3584]{1,0:T(8,128)(2,1)S(1)} %down.6), channel_id=1, source_target_pairs={{0,4},{4,0},{8,12},{12,8},{16,20},{20,16},{24,28},{28,24},{1,5},{5... | collective-permute-start | bytes 1376264 | tf_op jit(solution)/shard_map/ppermute | solution.py:45
  58.6 7.7 %collective-permute-start.18 = (bf16[32,3584]{1,0:T(8,128)(2,1)S(1)}, bf16[32,3584]{1,0:T(8,128)(2,1)S(1)}, u32[]{:S(2)}, u32[]{:S(2)}) collective-permute-start(bf16[32,3584]{1,0:T(8,128)(2,1)S(1)} %get-tuple-element.25), channel_id=1, source_target_pairs={{0,1},{1,0},{2,3},{3,2},{4,5},{5,4},{6,7},{7,6},{8,9},{9,8},{10,11... | collective-permute-start | bytes 688136 | tf_op jit(solution)/shard_map/ppermute | solution.py:45
  60.1 8.9 %collective-permute-start.14 = (bf16[32,3584]{1,0:T(8,128)(2,1)S(1)}, bf16[32,3584]{1,0:T(8,128)(2,1)S(1)}, u32[]{:S(2)}, u32[]{:S(2)}) collective-permute-start(bf16[32,3584]{1,0:T(8,128)(2,1)S(1)} %get-tuple-element.21), channel_id=1, source_target_pairs={{0,2},{1,3},{2,0},{3,1},{4,6},{5,7},{6,4},{7,5},{8,10},{9,11},{10,... | collective-permute-start | bytes 688136 | tf_op jit(solution)/shard_map/ppermute | solution.py:45
  66.3 8.6 %collective-permute-start.19 = (bf16[32,3584]{1,0:T(8,128)(2,1)S(1)}, bf16[32,3584]{1,0:T(8,128)(2,1)S(1)}, u32[]{:S(2)}, u32[]{:S(2)}) collective-permute-start(bf16[32,3584]{1,0:T(8,128)(2,1)S(1)} %add_convert_fusion.1), channel_id=1, source_target_pairs={{0,2},{1,3},{2,0},{3,1},{4,6},{5,7},{6,4},{7,5},{8,10},{9,11},{10,... | collective-permute-start | bytes 688136 | tf_op jit(solution)/shard_map/ppermute | solution.py:45
  67.9 8.5 %collective-permute-start.17 = (bf16[32,3584]{1,0:T(8,128)(2,1)S(1)}, bf16[32,3584]{1,0:T(8,128)(2,1)S(1)}, u32[]{:S(2)}, u32[]{:S(2)}) collective-permute-start(bf16[32,3584]{1,0:T(8,128)(2,1)S(1)} %get-tuple-element.23), channel_id=1, source_target_pairs={{0,1},{1,0},{2,3},{3,2},{4,5},{5,4},{6,7},{7,6},{8,9},{9,8},{10,11... | collective-permute-start | bytes 688136 | tf_op jit(solution)/shard_map/ppermute | solution.py:45
  69.0 10.4 %collective-permute-start.15 = (bf16[32,3584]{1,0:T(8,128)(2,1)S(1)}, bf16[32,3584]{1,0:T(8,128)(2,1)S(1)}, u32[]{:S(2)}, u32[]{:S(2)}) collective-permute-start(bf16[32,3584]{1,0:T(8,128)(2,1)S(1)} %add_convert_fusion.3), channel_id=1, source_target_pairs={{0,1},{1,0},{2,3},{3,2},{4,5},{5,4},{6,7},{7,6},{8,9},{9,8},{10,11... | collective-permute-start | bytes 688136 | tf_op jit(solution)/shard_map/ppermute | solution.py:45
  70.1 9.3 %collective-permute-start.9 = (bf16[32,3584]{1,0:T(8,128)(2,1)S(1)}, bf16[32,3584]{1,0:T(8,128)(2,1)S(1)}, u32[]{:S(2)}, u32[]{:S(2)}) collective-permute-start(bf16[32,3584]{1,0:T(8,128)(2,1)S(1)} %get-tuple-element.17), channel_id=1, source_target_pairs={{0,2},{1,3},{2,0},{3,1},{4,6},{5,7},{6,4},{7,5},{8,10},{9,11},{10,... | collective-permute-start | bytes 688136 | tf_op jit(solution)/shard_map/ppermute | solution.py:45
  76.6 7.3 %collective-permute-start.20 = (bf16[16,3584]{1,0:T(8,128)(2,1)S(1)}, bf16[16,3584]{1,0:T(8,128)(2,1)S(1)}, u32[]{:S(2)}, u32[]{:S(2)}) collective-permute-start(bf16[16,3584]{1,0:T(8,128)(2,1)S(1)} %slice.23), channel_id=1, source_target_pairs={{0,8},{4,12},{8,0},{12,4},{16,24},{20,28},{24,16},{28,20},{1,9},{5... | collective-permute-start | bytes 344072 | tf_op jit(solution)/shard_map/ppermute | solution.py:45
  79.5 7.0 %collective-permute-start.16 = (bf16[16,3584]{1,0:T(8,128)(2,1)S(1)}, bf16[16,3584]{1,0:T(8,128)(2,1)S(1)}, u32[]{:S(2)}, u32[]{:S(2)}) collective-permute-start(bf16[16,3584]{1,0:T(8,128)(2,1)S(1)} %slice.21), channel_id=1, source_target_pairs={{0,8},{4,12},{8,0},{12,4},{16,24},{20,28},{24,16},{28,20},{1,9},{5... | collective-permute-start | bytes 344072 | tf_op jit(solution)/shard_map/ppermute | solution.py:45
  83.9 7.0 %collective-permute-start.21 = (bf16[16,3584]{1,0:T(8,128)(2,1)S(1)}, bf16[16,3584]{1,0:T(8,128)(2,1)S(1)}, u32[]{:S(2)}, u32[]{:S(2)}) collective-permute-start(bf16[16,3584]{1,0:T(8,128)(2,1)S(1)} %add_convert_fusion.5), channel_id=1, source_target_pairs={{0,16},{4,20},{8,24},{12,28},{16,0},{20,4},{24,8},{28,12},{1,17},{... | collective-permute-start | bytes 344072 | tf_op jit(solution)/shard_map/ppermute | solution.py:45
  (4 other events, 12.5 us)

commit v4 on v3

--- a/solution.py
+++ b/solution.py
@@ -11,7 +11,12 @@
 AXES = ("grp", "ep")
 EXTRA = 128
 BLOCKS = 4
+TILE = 256
+RESIDENT_ROWS = 256
 VMEM_BYTES = 48 * 1024 * 1024
+LARGE_BYTES = 16 * 1024 * 1024
+SMALL_BYTES = 8 * 1024 * 1024
+whole = pl.BlockSpec(memory_space=pltpu.VMEM)
 
 score_scale = 192.0 ** (-0.5)
 neg_large = -1e30
@@ -200,6 +205,112 @@
     )(*operands)
 
 
+def join_kernel(count, *refs):
+    out, at = refs[-1], 0
+    for group in refs[:count]:
+        out[at : at + group.shape[0], :] = group[...]
+        at += group.shape[0]
+
+
+def join(groups, after=()):
+    rows = sum(group.shape[0] for group in groups)
+    return pl.pallas_call(
+        functools.partial(join_kernel, len(groups)),
+        out_shape=jax.ShapeDtypeStruct((rows, groups[0].shape[1]), groups[0].dtype),
+        in_specs=[whole] * len(groups) + [pl.BlockSpec(memory_space=pl.ANY)] * len(after),
+        out_specs=whole,
+        compiler_params=pltpu.CompilerParams(vmem_limit_bytes=SMALL_BYTES),
+        name="join",
+    )(*groups, *after)
+
+
+def expert_kernel(picks, own, other, w_gate, w_up, w_down, expert, *refs):
+    h_own, out, rows, hidden = refs[-4:]
+    count, feature, half = own.shape[0], w_gate.shape[1], w_gate.shape[2]
+    wanted = expert[0].astype(jnp.float32)
+    shares = []
+    for ref, at in ((own, 0), (other, count)):
+        rows[at : at + count, :] = ref[:, :feature]
+        columns = ref[:, feature:].astype(jnp.float32)
+        value = columns[:, picks : 2 * picks] + columns[:, 2 * picks : 3 * picks]
+        named = columns[:, :picks] == wanted
+        shares.append(jnp.sum(jnp.where(named, value, 0.0), axis=1, keepdims=True))
+    share = jnp.concatenate(shares, axis=0)
+    for at in range(0, half, TILE):
+        gate_part = jnp.dot(
+            rows[...], w_gate[0, :, at : at + TILE], preferred_element_type=jnp.float32
+        )
+        up_part = jnp.dot(
+            rows[...], w_up[0, :, at : at + TILE], preferred_element_type=jnp.float32
+        )
+        product = gate_part / (1.0 + jnp.exp(-gate_part)) * up_part * share
+        hidden[:, at : at + TILE] = product.astype(jnp.bfloat16)
+    h_own[...] = hidden[:count, :]
+    for at in range(0, feature, 2 * TILE):
+        out[:, at : at + 2 * TILE] = jnp.dot(
+            hidden[count:, :],
+            w_down[0, :, at : at + 2 * TILE],
+            preferred_element_type=jnp.float32,
+        ).astype(jnp.bfloat16)
+
+
+def expert_of(expert, own, other, w_gate, w_up, w_down, picks, after=()):
+    count = own.shape[0]
+    _, feature, half = w_gate.shape
+    return pl.pallas_call(
+        functools.partial(expert_kernel, picks),
+        out_shape=[
+            jax.ShapeDtypeStruct((count, half), jnp.bfloat16),
+            jax.ShapeDtypeStruct((count, feature), jnp.bfloat16),
+        ],
+        in_specs=[whole] * 5
+        + [pl.BlockSpec(memory_space=pltpu.SMEM)]
+        + [pl.BlockSpec(memory_space=pl.ANY)] * len(after),
+        out_specs=[whole] * 2,
+        scratch_shapes=[
+            pltpu.VMEM((2 * count, feature), jnp.bfloat16),
+            pltpu.VMEM((2 * count, half), jnp.bfloat16),
+        ],
+        compiler_params=pltpu.CompilerParams(vmem_limit_bytes=LARGE_BYTES),
+        cost_estimate=pl.CostEstimate(
+            flops=10 * count * feature * half,
+            bytes_accessed=2 * count * feature,
+            transcendentals=2 * count * half,
+        ),
+        name="expert",
+    )(own, other, w_gate, w_up, w_down, expert, *after)
+
+
+def sums_kernel(cuts, hidden, w_down, arrived, *outs):
+    feature = w_down.shape[2]
+    for column in range(0, feature, 2 * TILE):
+        span = slice(column, column + 2 * TILE)
+        part = jnp.dot(hidden[...], w_down[0, :, span], preferred_element_type=jnp.float32)
+        part = part + arrived[:, span].astype(jnp.float32)
+        at = 0
+        for cut, out in zip(cuts, outs):
+            out[:, span] = part[at : at + cut, :].astype(jnp.bfloat16)
+            at += cut
+
+
+def sums_of(hidden, w_down, cuts, arrived):
+    count, half = hidden.shape
+    feature = w_down.shape[2]
+    return pl.pallas_call(
+        functools.partial(sums_kernel, cuts),
+        out_shape=[jax.ShapeDtypeStruct((cut, feature), jnp.bfloat16) for cut in cuts],
+        in_specs=[whole] * 3,
+        out_specs=[whole] * len(cuts),
+        compiler_params=pltpu.CompilerParams(vmem_limit_bytes=SMALL_BYTES),
+        cost_estimate=pl.CostEstimate(
+            flops=2 * count * feature * half,
+            bytes_accessed=2 * count * feature,
+            transcendentals=0,
+        ),
+        name="sums",
+    )(hidden, w_down, arrived)
+
+
 def per_device(queries, cache, lengths, live_rows, tokens, ids, gates, w_gate, w_up, w_down):
     picks = ids.shape[1]
     grp_bits = bits_of(lax.axis_size("grp"))
@@ -221,22 +332,32 @@
     late = [near_xy, far_xy]
     early_cuts = [group.shape[0] for group in early]
     late_cuts = [group.shape[0] for group in late]
-    early_own = jnp.concatenate(early, axis=0)
-    late_own = jnp.concatenate(late, axis=0)
-    early_other = swap(early_own, core)
-    late_other = swap(late_own, core)
-
     context = attend(queries, cache, lengths, live_rows[0])
 
-    early_h, early_h_other = hidden_of(expert, early_own, early_other, w_gate, w_up, picks)
-    late_h, late_h_other = hidden_of(expert, late_own, late_other, w_gate, w_up, picks)
-
-    (late_out,) = down_of(late_h_other, w_down, [late_h_other.shape[0]])
-    late_in = swap(late_out, core)
-    (early_out,) = down_of(early_h_other, w_down, [early_h_other.shape[0]])
-    early_in = swap(early_out, core)
-    near_xy, far_xy = down_of(late_h, w_down, late_cuts, late_in)
-    near, near_x, near_y, far, far_x, far_y = down_of(early_h, w_down, early_cuts, early_in)
+    if sum(early_cuts) <= RESIDENT_ROWS:
+        early_own = join(early)
+        early_other = swap(early_own, core)
+        early_h, early_out = expert_of(expert, early_own, early_other, w_gate, w_up, w_down, picks)
+        early_in = swap(early_out, core)
+        late_own = join(late, [early_out])
+        late_other = swap(late_own, core)
+        near, near_x, near_y, far, far_x, far_y = sums_of(early_h, w_down, early_cuts, early_in)
+        late_h, late_out = expert_of(
+            expert, late_own, late_other, w_gate, w_up, w_down, picks, [near]
+        )
+        near_xy, far_xy = sums_of(late_h, w_down, late_cuts, swap(late_out, core))
+    else:
+        early_own, late_own = jnp.concatenate(early, axis=0), jnp.concatenate(late, axis=0)
+        early_other, late_other = swap(early_own, core), swap(late_own, core)
+        early_h, early_h_other = hidden_of(expert, early_own, early_other, w_gate, w_up, picks)
+        late_h, late_h_other = hidden_of(expert, late_own, late_other, w_gate, w_up, picks)
+        (late_out,) = down_of(late_h_other, w_down, [late_h_other.shape[0]])
+        late_in = swap(late_out, core)
+        (early_out,) = down_of(early_h_other, w_down, [early_h_other.shape[0]])
+        early_in = swap(early_out, core)
+        near_xy, far_xy = down_of(late_h, w_down, late_cuts, late_in)
+        near, near_x, near_y, far, far_x, far_y = down_of(early_h, w_down, early_cuts, early_in)
+
     rows, count = near.shape[0], tokens.shape[0]
     near_x = add_up(near_x, give_back(near_xy, y_steps, near_x.shape[0]))
     far_y = add_up(far_y, give_back(far_xy, x_steps, far_y.shape[0]))

time: 91.9 us -> 88.4 us (0.962)
  Pallas kernels: 22.5 us -> 9.21 us
  local copies, waits for them, and re-layouts: 2.14 us -> 7.43 us
  waiting for transfers between devices: 37.2 us -> 42 us
    pallas_call x6, Pallas kernels: 20.7 us -> 7.42 us  [the longest x2 5.66 us: expert_of(): pl.pallas_call(functools.partial(expert_kernel, picks), out_shape=[jax.Sh...]
    unnamed x20 -> x21, local copies, waits for them, and re-layouts: 2.07 us -> 7.4 us
    ppermute x22, waiting for transfers between devices: 37.2 us -> 42 us  [swap(): return lax.ppermute(value, axis, [(i, i ^ bit) for i in range(size)])]
  transfers between devices with their start and end apart: 22 -> 22, of which waited for: 15 -> 15; matrix products, arithmetic and copies ran while one was open for 6% -> 4% of each run, Pallas kernels for 23% -> 1%
where the time goes in v4:
time: 88.4 us; the launch traced here: 88.1 us
  waiting for transfers between devices  42 us (48%)
  starting transfers between devices  24.3 us (27%)
  Pallas kernels  9.21 us (10%)
  local copies, waits for them, and re-layouts  7.43 us (8%)
  other arithmetic  2.17 us (2%)
  matrix products  1.58 us (2%)
  between operations  1.47 us (2%)
    ppermute x22, waiting for transfers between devices, swap(): return lax.ppermute(value, axis, [(i, i ^ bit) for i in range(size)])  42 us
    ppermute x22, starting transfers between devices, swap(): return lax.ppermute(value, axis, [(i, i ^ bit) for i in range(size)])  24.3 us
    unnamed x21, local copies, waits for them, and re-layouts  7.4 us
    pallas_call x2, Pallas kernels, expert_of(): pl.pallas_call(functools.partial(expert_kernel, picks), out_shape=[jax.Sh...  5.66 us
    pallas_call x1, Pallas kernels, pack(): pl.pallas_call(pack_kernel, out_shape=jax.ShapeDtypeStruct((tokens.shape[...  1.78 us
  transfers between devices with their start and end apart: 22, of which 15 were waited for; matrix products, arithmetic and copies ran while one was open for 4% of the time, Pallas kernels for 1%

profile of v4, /device:TPU:0, one launch (start us, length us, event | category | flops | bytes accessed | tf_op | source)
XLA Modules:
  0.0 88.1 jit_solution(2197646952879306266)
XLA Ops:
  0.6 1.8 %pack.1 = bf16[16,3712]{1,0:T(8,128)(2,1)} custom-call(bf16[16,3584]{1,0:T(8,128)(2,1)} %tokens.1, s32[8,16]{1,0:T(8,128)} %bitcast.9, f32[8,16]{1,0:T(8,128)} %bitcast.10), custom_call_target="tpu_custom_call" | custom-call | tf_op jit(solution)/shard_map/pack/pallas_call | solution.py:102
  2.4 3.0 %collective-permute-start = (bf16[16,3712]{1,0:T(8,128)(2,1)}, bf16[16,3712]{1,0:T(8,128)(2,1)S(1)}, u32[]{:S(2)}, u32[]{:S(2)}) collective-permute-start(bf16[16,3712]{1,0:T(8,128)(2,1)} %pack.1), channel_id=1, source_target_pairs={{0,8},{4,12},{8,0},{12,4},{16,24},{20,28},{24,16},{28,20},{1,9},{5... | collective-permute-start | bytes 356360 | tf_op jit(solution)/shard_map/ppermute | solution.py:50
  5.5 2.6 %collective-permute-start.3 = (bf16[16,3712]{1,0:T(8,128)(2,1)}, bf16[16,3712]{1,0:T(8,128)(2,1)S(1)}, u32[]{:S(2)}, u32[]{:S(2)}) collective-permute-start(bf16[16,3712]{1,0:T(8,128)(2,1)} %pack.1), channel_id=1, source_target_pairs={{0,16},{4,20},{8,24},{12,28},{16,0},{20,4},{24,8},{28,12},{1,17},{... | collective-permute-start | bytes 356360 | tf_op jit(solution)/shard_map/ppermute | solution.py:50
  8.0 2.1 %collective-permute-done = bf16[16,3712]{1,0:T(8,128)(2,1)S(1)} collective-permute-done((bf16[16,3712]{1,0:T(8,128)(2,1)}, bf16[16,3712]{1,0:T(8,128)(2,1)S(1)}, u32[]{:S(2)}, u32[]{:S(2)}) %collective-permute-start) | collective-permute-done | bytes 118816 | tf_op jit(solution)/shard_map/ppermute | solution.py:50
  11.1 1.9 %collective-permute-start.1 = (bf16[32,3712]{1,0:T(8,128)(2,1)S(1)}, bf16[32,3712]{1,0:T(8,128)(2,1)S(1)}, u32[]{:S(2)}, u32[]{:S(2)}) collective-permute-start(bf16[32,3712]{1,0:T(8,128)(2,1)S(1)} %pad_maximum_fusion.refs_0_), channel_id=1, source_target_pairs={{0,1},{1,0},{2,3},{3,2},{4,5},{5,4},{6,7},{7,6},{8,9},{9,8},{10,11... | collective-permute-start | bytes 712712 | tf_op jit(solution)/shard_map/ppermute | solution.py:50
  13.0 1.5 %collective-permute-start.2 = (bf16[32,3712]{1,0:T(8,128)(2,1)S(1)}, bf16[32,3712]{1,0:T(8,128)(2,1)S(1)}, u32[]{:S(2)}, u32[]{:S(2)}) collective-permute-start(bf16[32,3712]{1,0:T(8,128)(2,1)S(1)} %pad_maximum_fusion.refs_0_), channel_id=1, source_target_pairs={{0,2},{1,3},{2,0},{3,1},{4,6},{5,7},{6,4},{7,5},{8,10},{9,11},{10,... | collective-permute-start | bytes 712712 | tf_op jit(solution)/shard_map/ppermute | solution.py:50
  14.9 4.5 %collective-permute-done.4 = bf16[16,3712]{1,0:T(8,128)(2,1)S(1)} collective-permute-done((bf16[16,3712]{1,0:T(8,128)(2,1)S(1)}, bf16[16,3712]{1,0:T(8,128)(2,1)S(1)}, u32[]{:S(2)}, u32[]{:S(2)}) %collective-permute-start.4) | collective-permute-done | bytes 118816 | tf_op jit(solution)/shard_map/ppermute | solution.py:50
  20.3 1.5 %collective-permute-start.5 = (bf16[32,3712]{1,0:T(8,128)(2,1)S(1)}, bf16[32,3712]{1,0:T(8,128)(2,1)S(1)}, u32[]{:S(2)}, u32[]{:S(2)}) collective-permute-start(bf16[32,3712]{1,0:T(8,128)(2,1)S(1)} %constant_dynamic-update-slice_fusion.refs_3_), channel_id=1, source_target_pairs={{0,1},{1,0},{2,3},{3,2},{4,5},{5,4},{6,7},{7,6},{8,9},{9,8},{10,11... | collective-permute-start | bytes 712712 | tf_op jit(solution)/shard_map/ppermute | solution.py:50
  21.8 3.7 %collective-permute-done.6.refs_5_ = bf16[32,3712]{1,0:T(8,128)(2,1)S(1)} collective-permute-done((bf16[32,3712]{1,0:T(8,128)(2,1)S(1)}, bf16[32,3712]{1,0:T(8,128)(2,1)S(1)}, u32[]{:S(2)}, u32[]{:S(2)}) %collective-permute-start.6) | collective-permute-done | bytes 237600 | tf_op jit(solution)/shard_map/ppermute | solution.py:50
  26.6 3.2 %collective-permute-done.7.other = bf16[192,3712]{1,0:T(8,128)(2,1)S(1)} collective-permute-done((bf16[192,3712]{1,0:T(8,128)(2,1)S(1)}, bf16[192,3712]{1,0:T(8,128)(2,1)S(1)}, u32[]{:S(2)}, u32[]{:S(2)}) %collective-permute-start.7) | collective-permute-done | bytes 1425440 | tf_op jit(solution)/shard_map/ppermute | solution.py:50
  29.8 2.0 %copy-done.1 = bf16[1,512,3584]{2,1,0:T(8,128)(2,1)S(1)} copy-done((bf16[1,512,3584]{2,1,0:T(8,128)(2,1)S(1)}, bf16[1,512,3584]{2,1,0:T(8,128)(2,1)}, u32[]{:S(2)}) %copy-start.1) | copy-done | bytes 3670040
  31.8 2.0 %copy-done.3 = bf16[1,3584,512]{2,1,0:T(8,128)(2,1)S(1)} copy-done((bf16[1,3584,512]{2,1,0:T(8,128)(2,1)S(1)}, bf16[1,3584,512]{2,1,0:T(8,128)(2,1)}, u32[]{:S(2)}) %copy-start.3) | copy-done | bytes 3670040
  33.9 2.0 %copy-done.5 = bf16[1,3584,512]{2,1,0:T(8,128)(2,1)S(1)} copy-done((bf16[1,3584,512]{2,1,0:T(8,128)(2,1)S(1)}, bf16[1,3584,512]{2,1,0:T(8,128)(2,1)}, u32[]{:S(2)}) %copy-start.5) | copy-done | bytes 3670040
  35.9 3.8 %expert.2 = (bf16[192,512]{1,0:T(8,128)(2,1)S(1)}, bf16[192,3584]{1,0:T(8,128)(2,1)S(1)}) custom-call(bf16[192,3712]{1,0:T(8,128)(2,1)S(1)} %join.2.own, bf16[192,3712]{1,0:T(8,128)(2,1)S(1)} %collective-permute-done.7.other, bf16[1,3584,512]{2,1,0:T(8,128)(2,1)S(1)} %copy-done.3, bf16[1,3584,512]{2,1,0:T(8,128)(2,1)S(1)} %copy-done.5, ...), custom_call_target="tpu_custom_call" | custom-call | flops 3523215360 | bytes 1376256 | tf_op jit(solution)/shard_map/expert/pallas_call | solution.py:260
  42.0 6.0 %collective-permute-done.10.refs_0_ = bf16[32,3712]{1,0:T(8,128)(2,1)S(1)} collective-permute-done((bf16[32,3712]{1,0:T(8,128)(2,1)S(1)}, bf16[32,3712]{1,0:T(8,128)(2,1)S(1)}, u32[]{:S(2)}, u32[]{:S(2)}) %collective-permute-start.10) | collective-permute-done | bytes 237600 | tf_op jit(solution)/shard_map/ppermute | solution.py:50
  52.1 1.8 %expert.3 = (bf16[64,512]{1,0:T(8,128)(2,1)S(1)}, bf16[64,3584]{1,0:T(8,128)(2,1)S(1)}) custom-call(bf16[64,3712]{1,0:T(8,128)(2,1)S(1)} %join.3.own, bf16[64,3712]{1,0:T(8,128)(2,1)S(1)} %collective-permute-done.12.other, bf16[1,3584,512]{2,1,0:T(8,128)(2,1)S(1)} %copy-done.4, bf16[1,3584,512]{2,1,0:T(8,128)(2,1)S(1)} %copy-done.5, ...), custom_call_target="tpu_custom_call" | custom-call | flops 1174405120 | bytes 458752 | tf_op jit(solution)/shard_map/expert/pallas_call | solution.py:260
  57.7 1.6 %collective-permute-start.9 = (bf16[32,3584]{1,0:T(8,128)(2,1)S(1)}, bf16[32,3584]{1,0:T(8,128)(2,1)S(1)}, u32[]{:S(2)}, u32[]{:S(2)}) collective-permute-start(bf16[32,3584]{1,0:T(8,128)(2,1)S(1)} %get-tuple-element.17), channel_id=1, source_target_pairs={{0,2},{1,3},{2,0},{3,1},{4,6},{5,7},{6,4},{7,5},{8,10},{9,11},{10,... | collective-permute-start | bytes 688136 | tf_op jit(solution)/shard_map/ppermute | solution.py:50
  61.0 4.1 %collective-permute-done.18 = bf16[32,3584]{1,0:T(8,128)(2,1)S(1)} collective-permute-done((bf16[32,3584]{1,0:T(8,128)(2,1)S(1)}, bf16[32,3584]{1,0:T(8,128)(2,1)S(1)}, u32[]{:S(2)}, u32[]{:S(2)}) %collective-permute-start.18) | collective-permute-done | bytes 229408 | tf_op jit(solution)/shard_map/ppermute | solution.py:50
  66.1 5.1 %collective-permute-done.14 = bf16[32,3584]{1,0:T(8,128)(2,1)S(1)} collective-permute-done((bf16[32,3584]{1,0:T(8,128)(2,1)S(1)}, bf16[32,3584]{1,0:T(8,128)(2,1)S(1)}, u32[]{:S(2)}, u32[]{:S(2)}) %collective-permute-start.14) | collective-permute-done | bytes 229408 | tf_op jit(solution)/shard_map/ppermute | solution.py:50
  72.5 2.5 %collective-permute-done.19 = bf16[32,3584]{1,0:T(8,128)(2,1)S(1)} collective-permute-done((bf16[32,3584]{1,0:T(8,128)(2,1)S(1)}, bf16[32,3584]{1,0:T(8,128)(2,1)S(1)}, u32[]{:S(2)}, u32[]{:S(2)}) %collective-permute-start.19) | collective-permute-done | bytes 229408 | tf_op jit(solution)/shard_map/ppermute | solution.py:50
  75.6 1.8 %collective-permute-done.15 = bf16[32,3584]{1,0:T(8,128)(2,1)S(1)} collective-permute-done((bf16[32,3584]{1,0:T(8,128)(2,1)S(1)}, bf16[32,3584]{1,0:T(8,128)(2,1)S(1)}, u32[]{:S(2)}, u32[]{:S(2)}) %collective-permute-start.15) | collective-permute-done | bytes 229408 | tf_op jit(solution)/shard_map/ppermute | solution.py:50
  77.9 2.5 %collective-permute-done.20 = bf16[16,3584]{1,0:T(8,128)(2,1)S(1)} collective-permute-done((bf16[16,3584]{1,0:T(8,128)(2,1)S(1)}, bf16[16,3584]{1,0:T(8,128)(2,1)S(1)}, u32[]{:S(2)}, u32[]{:S(2)}) %collective-permute-start.20) | collective-permute-done | bytes 114720 | tf_op jit(solution)/shard_map/ppermute | solution.py:50
  80.4 2.7 %collective-permute-start.21 = (bf16[16,3584]{1,0:T(8,128)(2,1)S(1)}, bf16[16,3584]{1,0:T(8,128)(2,1)S(1)}, u32[]{:S(2)}, u32[]{:S(2)}) collective-permute-start(bf16[16,3584]{1,0:T(8,128)(2,1)S(1)} %add_convert_fusion.5), channel_id=1, source_target_pairs={{0,16},{4,20},{8,24},{12,28},{16,0},{20,4},{24,8},{28,12},{1,17},{... | collective-permute-start | bytes 344072 | tf_op jit(solution)/shard_map/ppermute | solution.py:50
  84.4 3.0 %collective-permute-done.21 = bf16[16,3584]{1,0:T(8,128)(2,1)S(1)} collective-permute-done((bf16[16,3584]{1,0:T(8,128)(2,1)S(1)}, bf16[16,3584]{1,0:T(8,128)(2,1)S(1)}, u32[]{:S(2)}, u32[]{:S(2)}) %collective-permute-start.21) | collective-permute-done | bytes 114720 | tf_op jit(solution)/shard_map/ppermute | solution.py:50
  (62 shorter events, 19.8 us)
Async XLA Ops:
  0.6 54.0 %copy-start = (bf16[4,64,576]{2,1,0:T(8,128)(2,1)S(1)}, bf16[4,64,576]{2,1,0:T(8,128)(2,1)}, u32[]{:S(2)}) copy-start(bf16[4,64,576]{2,1,0:T(8,128)(2,1)} %param.10) | copy-start | bytes 884740
  2.4 7.7 %collective-permute-start = (bf16[16,3712]{1,0:T(8,128)(2,1)}, bf16[16,3712]{1,0:T(8,128)(2,1)S(1)}, u32[]{:S(2)}, u32[]{:S(2)}) collective-permute-start(bf16[16,3712]{1,0:T(8,128)(2,1)} %pack.1), channel_id=1, source_target_pairs={{0,8},{4,12},{8,0},{12,4},{16,24},{20,28},{24,16},{28,20},{1,9},{5... | collective-permute-start | bytes 356360 | tf_op jit(solution)/shard_map/ppermute | solution.py:50
  5.5 9.1 %collective-permute-start.3 = (bf16[16,3712]{1,0:T(8,128)(2,1)}, bf16[16,3712]{1,0:T(8,128)(2,1)S(1)}, u32[]{:S(2)}, u32[]{:S(2)}) collective-permute-start(bf16[16,3712]{1,0:T(8,128)(2,1)} %pack.1), channel_id=1, source_target_pairs={{0,16},{4,20},{8,24},{12,28},{16,0},{20,4},{24,8},{28,12},{1,17},{... | collective-permute-start | bytes 356360 | tf_op jit(solution)/shard_map/ppermute | solution.py:50
  11.1 10.7 %collective-permute-start.1 = (bf16[32,3712]{1,0:T(8,128)(2,1)S(1)}, bf16[32,3712]{1,0:T(8,128)(2,1)S(1)}, u32[]{:S(2)}, u32[]{:S(2)}) collective-permute-start(bf16[32,3712]{1,0:T(8,128)(2,1)S(1)} %pad_maximum_fusion.refs_0_), channel_id=1, source_target_pairs={{0,1},{1,0},{2,3},{3,2},{4,5},{5,4},{6,7},{7,6},{8,9},{9,8},{10,11... | collective-permute-start | bytes 712712 | tf_op jit(solution)/shard_map/ppermute | solution.py:50
  13.0 8.8 %collective-permute-start.2 = (bf16[32,3712]{1,0:T(8,128)(2,1)S(1)}, bf16[32,3712]{1,0:T(8,128)(2,1)S(1)}, u32[]{:S(2)}, u32[]{:S(2)}) collective-permute-start(bf16[32,3712]{1,0:T(8,128)(2,1)S(1)} %pad_maximum_fusion.refs_0_), channel_id=1, source_target_pairs={{0,2},{1,3},{2,0},{3,1},{4,6},{5,7},{6,4},{7,5},{8,10},{9,11},{10,... | collective-permute-start | bytes 712712 | tf_op jit(solution)/shard_map/ppermute | solution.py:50
  14.5 4.8 %collective-permute-start.4 = (bf16[16,3712]{1,0:T(8,128)(2,1)S(1)}, bf16[16,3712]{1,0:T(8,128)(2,1)S(1)}, u32[]{:S(2)}, u32[]{:S(2)}) collective-permute-start(bf16[16,3712]{1,0:T(8,128)(2,1)S(1)} %collective-permute-done.3), channel_id=1, source_target_pairs={{0,8},{4,12},{8,0},{12,4},{16,24},{20,28},{24,16},{28,20},{1,9},{5... | collective-permute-start | bytes 356360 | tf_op jit(solution)/shard_map/ppermute | solution.py:50
  19.4 6.2 %collective-permute-start.6 = (bf16[32,3712]{1,0:T(8,128)(2,1)S(1)}, bf16[32,3712]{1,0:T(8,128)(2,1)S(1)}, u32[]{:S(2)}, u32[]{:S(2)}) collective-permute-start(bf16[32,3712]{1,0:T(8,128)(2,1)S(1)} %constant_dynamic-update-slice_fusion.refs_3_), channel_id=1, source_target_pairs={{0,2},{1,3},{2,0},{3,1},{4,6},{5,7},{6,4},{7,5},{8,10},{9,11},{10,... | collective-permute-start | bytes 712712 | tf_op jit(solution)/shard_map/ppermute | solution.py:50
  20.3 6.1 %collective-permute-start.5 = (bf16[32,3712]{1,0:T(8,128)(2,1)S(1)}, bf16[32,3712]{1,0:T(8,128)(2,1)S(1)}, u32[]{:S(2)}, u32[]{:S(2)}) collective-permute-start(bf16[32,3712]{1,0:T(8,128)(2,1)S(1)} %constant_dynamic-update-slice_fusion.refs_3_), channel_id=1, source_target_pairs={{0,1},{1,0},{2,3},{3,2},{4,5},{5,4},{6,7},{7,6},{8,9},{9,8},{10,11... | collective-permute-start | bytes 712712 | tf_op jit(solution)/shard_map/ppermute | solution.py:50
  26.5 3.3 %collective-permute-start.7 = (bf16[192,3712]{1,0:T(8,128)(2,1)S(1)}, bf16[192,3712]{1,0:T(8,128)(2,1)S(1)}, u32[]{:S(2)}, u32[]{:S(2)}) collective-permute-start(bf16[192,3712]{1,0:T(8,128)(2,1)S(1)} %join.2.own), channel_id=1, source_target_pairs={{0,4},{4,0},{8,12},{12,8},{16,20},{20,16},{24,28},{28,24},{1,5},{5... | collective-permute-start | bytes 4276232 | tf_op jit(solution)/shard_map/ppermute | solution.py:50
  35.9 5.2 %copy-start.7 = (bf16[32,3712]{1,0:T(8,128)(2,1)S(1)}, bf16[32,3712]{1,0:T(8,128)(2,1)}, u32[]{:S(2)}) copy-start(bf16[32,3712]{1,0:T(8,128)(2,1)} %copy-done.6) | copy-start | bytes 712708
  39.8 9.3 %collective-permute-start.8 = (bf16[192,3584]{1,0:T(8,128)(2,1)S(1)}, bf16[192,3584]{1,0:T(8,128)(2,1)S(1)}, u32[]{:S(2)}, u32[]{:S(2)}) collective-permute-start(bf16[192,3584]{1,0:T(8,128)(2,1)S(1)} %get-tuple-element.15.refs_2_), channel_id=1, source_target_pairs={{0,4},{4,0},{8,12},{12,8},{16,20},{20,16},{24,28},{28,24},{1,5},{5... | collective-permute-start | bytes 4128776 | tf_op jit(solution)/shard_map/ppermute | solution.py:50
  40.0 8.1 %collective-permute-start.10 = (bf16[32,3712]{1,0:T(8,128)(2,1)S(1)}, bf16[32,3712]{1,0:T(8,128)(2,1)S(1)}, u32[]{:S(2)}, u32[]{:S(2)}) collective-permute-start(bf16[32,3712]{1,0:T(8,128)(2,1)S(1)} %collective-permute-done.1.refs_1_), channel_id=1, source_target_pairs={{0,2},{1,3},{2,0},{3,1},{4,6},{5,7},{6,4},{7,5},{8,10},{9,11},{10,... | collective-permute-start | bytes 712712 | tf_op jit(solution)/shard_map/ppermute | solution.py:50
  41.1 7.8 %collective-permute-start.11 = (bf16[32,3712]{1,0:T(8,128)(2,1)S(1)}, bf16[32,3712]{1,0:T(8,128)(2,1)S(1)}, u32[]{:S(2)}, u32[]{:S(2)}) collective-permute-start(bf16[32,3712]{1,0:T(8,128)(2,1)S(1)} %copy-done.7), channel_id=1, source_target_pairs={{0,1},{1,0},{2,3},{3,2},{4,5},{5,4},{6,7},{7,6},{8,9},{9,8},{10,11... | collective-permute-start | bytes 712712 | tf_op jit(solution)/shard_map/ppermute | solution.py:50
  48.9 1.9 %collective-permute-start.12 = (bf16[64,3712]{1,0:T(8,128)(2,1)S(1)}, bf16[64,3712]{1,0:T(8,128)(2,1)S(1)}, u32[]{:S(2)}, u32[]{:S(2)}) collective-permute-start(bf16[64,3712]{1,0:T(8,128)(2,1)S(1)} %join.3.own), channel_id=1, source_target_pairs={{0,4},{4,0},{8,12},{12,8},{16,20},{20,16},{24,28},{28,24},{1,5},{5... | collective-permute-start | bytes 1425416 | tf_op jit(solution)/shard_map/ppermute | solution.py:50
  53.9 1.9 %collective-permute-start.13 = (bf16[64,3584]{1,0:T(8,128)(2,1)S(1)}, bf16[64,3584]{1,0:T(8,128)(2,1)S(1)}, u32[]{:S(2)}, u32[]{:S(2)}) collective-permute-start(bf16[64,3584]{1,0:T(8,128)(2,1)S(1)} %get-tuple-element.20), channel_id=1, source_target_pairs={{0,4},{4,0},{8,12},{12,8},{16,20},{20,16},{24,28},{28,24},{1,5},{5... | collective-permute-start | bytes 1376264 | tf_op jit(solution)/shard_map/ppermute | solution.py:50
  56.5 8.5 %collective-permute-start.18 = (bf16[32,3584]{1,0:T(8,128)(2,1)S(1)}, bf16[32,3584]{1,0:T(8,128)(2,1)S(1)}, u32[]{:S(2)}, u32[]{:S(2)}) collective-permute-start(bf16[32,3584]{1,0:T(8,128)(2,1)S(1)} %get-tuple-element.25), channel_id=1, source_target_pairs={{0,1},{1,0},{2,3},{3,2},{4,5},{5,4},{6,7},{7,6},{8,9},{9,8},{10,11... | collective-permute-start | bytes 688136 | tf_op jit(solution)/shard_map/ppermute | solution.py:50
  57.7 17.9 %collective-permute-start.9 = (bf16[32,3584]{1,0:T(8,128)(2,1)S(1)}, bf16[32,3584]{1,0:T(8,128)(2,1)S(1)}, u32[]{:S(2)}, u32[]{:S(2)}) collective-permute-start(bf16[32,3584]{1,0:T(8,128)(2,1)S(1)} %get-tuple-element.17), channel_id=1, source_target_pairs={{0,2},{1,3},{2,0},{3,1},{4,6},{5,7},{6,4},{7,5},{8,10},{9,11},{10,... | collective-permute-start | bytes 688136 | tf_op jit(solution)/shard_map/ppermute | solution.py:50
  59.3 13.2 %collective-permute-start.17 = (bf16[32,3584]{1,0:T(8,128)(2,1)S(1)}, bf16[32,3584]{1,0:T(8,128)(2,1)S(1)}, u32[]{:S(2)}, u32[]{:S(2)}) collective-permute-start(bf16[32,3584]{1,0:T(8,128)(2,1)S(1)} %get-tuple-element.23), channel_id=1, source_target_pairs={{0,1},{1,0},{2,3},{3,2},{4,5},{5,4},{6,7},{7,6},{8,9},{9,8},{10,11... | collective-permute-start | bytes 688136 | tf_op jit(solution)/shard_map/ppermute | solution.py:50
  59.8 11.4 %collective-permute-start.14 = (bf16[32,3584]{1,0:T(8,128)(2,1)S(1)}, bf16[32,3584]{1,0:T(8,128)(2,1)S(1)}, u32[]{:S(2)}, u32[]{:S(2)}) collective-permute-start(bf16[32,3584]{1,0:T(8,128)(2,1)S(1)} %get-tuple-element.21), channel_id=1, source_target_pairs={{0,2},{1,3},{2,0},{3,1},{4,6},{5,7},{6,4},{7,5},{8,10},{9,11},{10,... | collective-permute-start | bytes 688136 | tf_op jit(solution)/shard_map/ppermute | solution.py:50
  65.1 9.8 %collective-permute-start.19 = (bf16[32,3584]{1,0:T(8,128)(2,1)S(1)}, bf16[32,3584]{1,0:T(8,128)(2,1)S(1)}, u32[]{:S(2)}, u32[]{:S(2)}) collective-permute-start(bf16[32,3584]{1,0:T(8,128)(2,1)S(1)} %add_convert_fusion.1), channel_id=1, source_target_pairs={{0,2},{1,3},{2,0},{3,1},{4,6},{5,7},{6,4},{7,5},{8,10},{9,11},{10,... | collective-permute-start | bytes 688136 | tf_op jit(solution)/shard_map/ppermute | solution.py:50
  71.2 6.1 %collective-permute-start.15 = (bf16[32,3584]{1,0:T(8,128)(2,1)S(1)}, bf16[32,3584]{1,0:T(8,128)(2,1)S(1)}, u32[]{:S(2)}, u32[]{:S(2)}) collective-permute-start(bf16[32,3584]{1,0:T(8,128)(2,1)S(1)} %add_convert_fusion.3), channel_id=1, source_target_pairs={{0,1},{1,0},{2,3},{3,2},{4,5},{5,4},{6,7},{7,6},{8,9},{9,8},{10,11... | collective-permute-start | bytes 688136 | tf_op jit(solution)/shard_map/ppermute | solution.py:50
  75.1 5.3 %collective-permute-start.20 = (bf16[16,3584]{1,0:T(8,128)(2,1)S(1)}, bf16[16,3584]{1,0:T(8,128)(2,1)S(1)}, u32[]{:S(2)}, u32[]{:S(2)}) collective-permute-start(bf16[16,3584]{1,0:T(8,128)(2,1)S(1)} %slice.23), channel_id=1, source_target_pairs={{0,8},{4,12},{8,0},{12,4},{16,24},{20,28},{24,16},{28,20},{1,9},{5... | collective-permute-start | bytes 344072 | tf_op jit(solution)/shard_map/ppermute | solution.py:50
  77.4 6.9 %collective-permute-start.16 = (bf16[16,3584]{1,0:T(8,128)(2,1)S(1)}, bf16[16,3584]{1,0:T(8,128)(2,1)S(1)}, u32[]{:S(2)}, u32[]{:S(2)}) collective-permute-start(bf16[16,3584]{1,0:T(8,128)(2,1)S(1)} %slice.21), channel_id=1, source_target_pairs={{0,8},{4,12},{8,0},{12,4},{16,24},{20,28},{24,16},{28,20},{1,9},{5... | collective-permute-start | bytes 344072 | tf_op jit(solution)/shard_map/ppermute | solution.py:50
  80.4 7.0 %collective-permute-start.21 = (bf16[16,3584]{1,0:T(8,128)(2,1)S(1)}, bf16[16,3584]{1,0:T(8,128)(2,1)S(1)}, u32[]{:S(2)}, u32[]{:S(2)}) collective-permute-start(bf16[16,3584]{1,0:T(8,128)(2,1)S(1)} %add_convert_fusion.5), channel_id=1, source_target_pairs={{0,16},{4,20},{8,24},{12,28},{16,0},{20,4},{24,8},{28,12},{1,17},{... | collective-permute-start | bytes 344072 | tf_op jit(solution)/shard_map/ppermute | solution.py:50
  (8 other events, 17.3 us)

commit v5 on v4

--- a/solution.py
+++ b/solution.py
@@ -12,7 +12,7 @@
 EXTRA = 128
 BLOCKS = 4
 TILE = 256
-RESIDENT_ROWS = 256
+WIDE = 512
 VMEM_BYTES = 48 * 1024 * 1024
 LARGE_BYTES = 16 * 1024 * 1024
 SMALL_BYTES = 8 * 1024 * 1024
@@ -205,23 +205,70 @@
     )(*operands)
 
 
-def join_kernel(count, *refs):
-    out, at = refs[-1], 0
-    for group in refs[:count]:
-        out[at : at + group.shape[0], :] = group[...]
-        at += group.shape[0]
-
-
-def join(groups, after=()):
-    rows = sum(group.shape[0] for group in groups)
-    return pl.pallas_call(
-        functools.partial(join_kernel, len(groups)),
-        out_shape=jax.ShapeDtypeStruct((rows, groups[0].shape[1]), groups[0].dtype),
-        in_specs=[whole] * len(groups) + [pl.BlockSpec(memory_space=pl.ANY)] * len(after),
+def combine_kernel(count, plans, *refs):
+    outs = refs[len(refs) - len(plans) :]
+    width = outs[0].shape[1]
+    for plan, out in zip(plans, outs):
+        at = 0
+        for rows, terms in plan:
+            if len(terms) == 1:
+                index, start = terms[0]
+                out[at : at + rows, :] = refs[index][start : start + rows, :]
+            else:
+                for left in range(0, width, WIDE):
+                    span = slice(left, left + WIDE)
+                    total = sum(
+                        refs[index][start : start + rows, span].astype(jnp.float32)
+                        for index, start in terms
+                    )
+                    out[at : at + rows, span] = total.astype(out.dtype)
+            at += rows
+
+
+def combine(inputs, plans, after=()):
+    width = inputs[0].shape[1]
+    return pl.pallas_call(
+        functools.partial(combine_kernel, len(inputs), plans),
+        out_shape=[
+            jax.ShapeDtypeStruct((sum(rows for rows, _ in plan), width), jnp.bfloat16)
+            for plan in plans
+        ],
+        in_specs=[whole] * len(inputs) + [pl.BlockSpec(memory_space=pl.ANY)] * len(after),
+        out_specs=[whole] * len(plans),
+        compiler_params=pltpu.CompilerParams(vmem_limit_bytes=SMALL_BYTES),
+        name="combine",
+    )(*inputs, *after)
+
+
+def hold_kernel(parts, *refs):
+    weight, out, sems = refs[0], refs[-2], refs[-1]
+    depth = weight.shape[1] // parts
+    copies = [
+        pltpu.make_async_copy(
+            weight.at[:, pl.ds(part * depth, depth), :],
+            out.at[:, pl.ds(part * depth, depth), :],
+            sems.at[part],
+        )
+        for part in range(parts)
+    ]
+    for copy in copies:
+        copy.start()
+    for copy in copies:
+        copy.wait()
+
+
+def hold(weight, after):
+    parts = 8
+    return pl.pallas_call(
+        functools.partial(hold_kernel, parts),
+        out_shape=jax.ShapeDtypeStruct(weight.shape, weight.dtype),
+        in_specs=[pl.BlockSpec(memory_space=pltpu.HBM)]
+        + [pl.BlockSpec(memory_space=pl.ANY)] * len(after),
         out_specs=whole,
+        scratch_shapes=[pltpu.SemaphoreType.DMA((parts,))],
         compiler_params=pltpu.CompilerParams(vmem_limit_bytes=SMALL_BYTES),
-        name="join",
-    )(*groups, *after)
+        name="hold",
+    )(weight, *after)
 
 
 def expert_kernel(picks, own, other, w_gate, w_up, w_down, expert, *refs):
@@ -281,7 +328,8 @@
     )(own, other, w_gate, w_up, w_down, expert, *after)
 
 
-def sums_kernel(cuts, hidden, w_down, arrived, *outs):
+def sums_kernel(cuts, hidden, w_down, arrived, *refs):
+    outs = refs[len(refs) - len(cuts) :]
     feature = w_down.shape[2]
     for column in range(0, feature, 2 * TILE):
         span = slice(column, column + 2 * TILE)
@@ -293,13 +341,13 @@
             at += cut
 
 
-def sums_of(hidden, w_down, cuts, arrived):
+def sums_of(hidden, w_down, cuts, arrived, after=()):
     count, half = hidden.shape
     feature = w_down.shape[2]
     return pl.pallas_call(
         functools.partial(sums_kernel, cuts),
         out_shape=[jax.ShapeDtypeStruct((cut, feature), jnp.bfloat16) for cut in cuts],
-        in_specs=[whole] * 3,
+        in_specs=[whole] * 3 + [pl.BlockSpec(memory_space=pl.ANY)] * len(after),
         out_specs=[whole] * len(cuts),
         compiler_params=pltpu.CompilerParams(vmem_limit_bytes=SMALL_BYTES),
         cost_estimate=pl.CostEstimate(
@@ -308,7 +356,118 @@
             transcendentals=0,
         ),
         name="sums",
-    )(hidden, w_down, arrived)
+    )(hidden, w_down, arrived, *after)
+
+
+def mix_large(packed, weights, expert, picks, steps):
+    w_gate, w_up, w_down = weights
+    z_near, z_far, x_steps, y_steps, core = steps
+    near = spread(packed, z_near)
+    far = spread(swap(packed, z_far), z_near)
+    near_x, near_y = others(near, x_steps), others(near, y_steps)
+    far_x, far_y = others(far, x_steps), others(far, y_steps)
+    near_xy, far_xy = others(near_x, y_steps), others(far_y, x_steps)
+    early = [near, near_x, near_y, far, far_x, far_y]
+    late = [near_xy, far_xy]
+    early_cuts = [group.shape[0] for group in early]
+    late_cuts = [group.shape[0] for group in late]
+    early_own, late_own = jnp.concatenate(early, axis=0), jnp.concatenate(late, axis=0)
+    early_other, late_other = swap(early_own, core), swap(late_own, core)
+    early_h, early_h_other = hidden_of(expert, early_own, early_other, w_gate, w_up, picks)
+    late_h, late_h_other = hidden_of(expert, late_own, late_other, w_gate, w_up, picks)
+    (late_out,) = down_of(late_h_other, w_down, [late_h_other.shape[0]])
+    late_in = swap(late_out, core)
+    (early_out,) = down_of(early_h_other, w_down, [early_h_other.shape[0]])
+    early_in = swap(early_out, core)
+    near_xy, far_xy = down_of(late_h, w_down, late_cuts, late_in)
+    near, near_x, near_y, far, far_x, far_y = down_of(early_h, w_down, early_cuts, early_in)
+    rows, count = near.shape[0], packed.shape[0]
+    near_x = add_up(near_x, give_back(near_xy, y_steps, near_x.shape[0]))
+    far_y = add_up(far_y, give_back(far_xy, x_steps, far_y.shape[0]))
+    far = add_up(far, give_back(far_x, x_steps, rows) + give_back(far_y, y_steps, rows))
+    near = add_up(near, give_back(near_y, y_steps, rows) + give_back(near_x, x_steps, rows))
+    far = add_up(far[:count], give_back(far[count:], z_near, count))
+    return add_up(near[:count], give_back(near[count:], z_near, count) + [swap(far, z_far)])
+
+
+def mix_small(packed, weights, expert, picks, steps):
+    w_gate, w_up, w_down = weights
+    z_near, z_far, x, y, core = steps
+    n = packed.shape[0]
+
+    def rows_of(*segments):
+        return [(count, [(index, start)]) for index, start, count in segments]
+
+    from_near = swap(packed, z_near)
+    from_far = swap(packed, z_far)
+    w_down = hold(w_down, [packed])
+    (near,) = combine([packed, from_near], [rows_of((0, 0, n), (1, 0, n))], [w_down])
+    near_x, near_y = swap(near, x), swap(near, y)
+    from_both = swap(from_far, z_near)
+    w_gate = hold(w_gate, [near])
+    first_own, far, half_x, half_y = combine(
+        [near, near_x, near_y, from_far, from_both],
+        [
+            rows_of((0, 0, 2 * n), (1, 0, 2 * n), (2, 0, 2 * n)),
+            rows_of((3, 0, n), (4, 0, n)),
+            rows_of((1, 0, n)),
+            rows_of((2, n, n)),
+        ],
+        [w_gate],
+    )
+    first_other = swap(first_own, core)
+    far_x, far_y = swap(far, x), swap(far, y)
+    near_xy_top, near_xy_low = swap(half_x, y), swap(half_y, x)
+    w_up = hold(w_up, [far])
+    held = (w_gate, w_up, w_down)
+    first_h, first_out = expert_of(expert, first_own, first_other, *held, picks)
+    second_own, half_x, half_y = combine(
+        [near_xy_top, near_xy_low, far, far_x, far_y],
+        [
+            rows_of((0, 0, n), (1, 0, n), (2, 0, 2 * n), (3, 0, 2 * n), (4, 0, 2 * n)),
+            rows_of((3, 0, n)),
+            rows_of((4, n, n)),
+        ],
+        [first_out],
+    )
+    far_xy_top, far_xy_low = swap(half_x, y), swap(half_y, x)
+    second_other = swap(second_own, core)
+    first_in = swap(first_out, core)
+    near, near_x, near_y = sums_of(first_h, w_down, [2 * n] * 3, first_in)
+    (third_own,) = combine([far_xy_top, far_xy_low], [rows_of((0, 0, n), (1, 0, n))], [near])
+    third_other = swap(third_own, core)
+    second_h, second_out = expert_of(
+        expert, second_own, second_other, *held, picks, [third_own]
+    )
+    second_in = swap(second_out, core)
+    third_h, third_out = expert_of(expert, third_own, third_other, *held, picks, [second_out])
+    near_xy_top, near_xy_low, far, far_x, far_y = sums_of(
+        second_h, w_down, [n, n, 2 * n, 2 * n, 2 * n], second_in, [third_out]
+    )
+    third_in = swap(third_out, core)
+    far_xy_top, far_xy_low = sums_of(third_h, w_down, [n, n], third_in)
+
+    to_near_x, to_near_y = swap(near_xy_top, y), swap(near_xy_low, x)
+    to_far_x, to_far_y = swap(far_xy_top, y), swap(far_xy_low, x)
+    far_x, far_y, near_x, near_y = combine(
+        [far_x, far_y, near_x, near_y, to_far_x, to_far_y, to_near_x, to_near_y],
+        [
+            [(n, [(0, 0), (4, 0)]), (n, [(0, n)])],
+            [(n, [(1, 0)]), (n, [(1, n), (5, 0)])],
+            [(n, [(2, 0), (6, 0)]), (n, [(2, n)])],
+            [(n, [(3, 0)]), (n, [(3, n), (7, 0)])],
+        ],
+    )
+    to_far = [swap(far_x, x), swap(far_y, y)]
+    to_near = [swap(near_x, x), swap(near_y, y)]
+    both = lambda start: [(n, [(0, start), (1, start), (2, start)])]
+    far_sum, both_sum = combine([far, *to_far], [both(0), both(n)])
+    own_sum, near_sum = combine([near, *to_near], [both(0), both(n)], [far_sum])
+    size = lax.axis_size(z_far[0])
+    direct = [(i, i ^ z_far[1] ^ z_near[1]) for i in range(size)]
+    terms = [swap(far_sum, z_far), lax.ppermute(both_sum, z_far[0], direct), swap(near_sum, z_near)]
+    (mixed,) = combine([own_sum, *terms], [[(n, [(0, 0), (1, 0), (2, 0), (3, 0)])]])
+    return mixed
 
 
 def per_device(queries, cache, lengths, live_rows, tokens, ids, gates, w_gate, w_up, w_down):
@@ -322,49 +481,15 @@
     y_steps = [("ep", bit) for bit in ep_bits[len(ep_bits) // 2 :]]
     expert = ((lax.axis_index("grp") * lax.axis_size("ep") + lax.axis_index("ep")) >> 1).reshape(1)
 
+    context = attend(queries, cache, lengths, live_rows[0])
     packed = pack(tokens, ids, gates)
-    near = spread(packed, z_near)
-    far = spread(swap(packed, z_far), z_near)
-    near_x, near_y = others(near, x_steps), others(near, y_steps)
-    far_x, far_y = others(far, x_steps), others(far, y_steps)
-    near_xy, far_xy = others(near_x, y_steps), others(far_y, x_steps)
-    early = [near, near_x, near_y, far, far_x, far_y]
-    late = [near_xy, far_xy]
-    early_cuts = [group.shape[0] for group in early]
-    late_cuts = [group.shape[0] for group in late]
-    context = attend(queries, cache, lengths, live_rows[0])
-
-    if sum(early_cuts) <= RESIDENT_ROWS:
-        early_own = join(early)
-        early_other = swap(early_own, core)
-        early_h, early_out = expert_of(expert, early_own, early_other, w_gate, w_up, w_down, picks)
-        early_in = swap(early_out, core)
-        late_own = join(late, [early_out])
-        late_other = swap(late_own, core)
-        near, near_x, near_y, far, far_x, far_y = sums_of(early_h, w_down, early_cuts, early_in)
-        late_h, late_out = expert_of(
-            expert, late_own, late_other, w_gate, w_up, w_down, picks, [near]
-        )
-        near_xy, far_xy = sums_of(late_h, w_down, late_cuts, swap(late_out, core))
+    weights = (w_gate, w_up, w_down)
+    if len(z_near) == len(x_steps) == len(y_steps) == 1:
+        steps = (z_near[0], z_far, x_steps[0], y_steps[0], core)
+        mixed = mix_small(packed, weights, expert, picks, steps)
     else:
-        early_own, late_own = jnp.concatenate(early, axis=0), jnp.concatenate(late, axis=0)
-        early_other, late_other = swap(early_own, core), swap(late_own, core)
-        early_h, early_h_other = hidden_of(expert, early_own, early_other, w_gate, w_up, picks)
-        late_h, late_h_other = hidden_of(expert, late_own, late_other, w_gate, w_up, picks)
-        (late_out,) = down_of(late_h_other, w_down, [late_h_other.shape[0]])
-        late_in = swap(late_out, core)
-        (early_out,) = down_of(early_h_other, w_down, [early_h_other.shape[0]])
-        early_in = swap(early_out, core)
-        near_xy, far_xy = down_of(late_h, w_down, late_cuts, late_in)
-        near, near_x, near_y, far, far_x, far_y = down_of(early_h, w_down, early_cuts, early_in)
-
-    rows, count = near.shape[0], tokens.shape[0]
-    near_x = add_up(near_x, give_back(near_xy, y_steps, near_x.shape[0]))
-    far_y = add_up(far_y, give_back(far_xy, x_steps, far_y.shape[0]))
-    far = add_up(far, give_back(far_x, x_steps, rows) + give_back(far_y, y_steps, rows))
-    near = add_up(near, give_back(near_y, y_steps, rows) + give_back(near_x, x_steps, rows))
-    far = add_up(far[:count], give_back(far[count:], z_near, count))
-    mixed = add_up(near[:count], give_back(near[count:], z_near, count) + [swap(far, z_far)])
+        steps = (z_near, z_far, x_steps, y_steps, core)
+        mixed = mix_large(packed, weights, expert, picks, steps)
     return (context, mixed)
 
 

time: 88.4 us -> 83.8 us (0.948)
  waiting for transfers between devices: 42 us -> 24.6 us
  Pallas kernels: 9.21 us -> 18.9 us
  starting transfers between devices: 24.3 us -> 28.1 us
  other arithmetic: 2.17 us -> 0.24 us
  local copies, waits for them, and re-layouts: 7.43 us -> 8.66 us
    ppermute x22 -> x27, waiting for transfers between devices: 42 us -> 24.6 us  [swap(): return lax.ppermute(value, axis, [(i, i ^ bit) for i in range(size)])]
    pallas_call x2 -> x11, Pallas kernels: 0.13 us -> 7.93 us  [the longest x3 6.73 us: hold(): pl.pallas_call(functools.partial(hold_kernel, parts), out_shape=jax.Shape...]
    ppermute x22 -> x27, starting transfers between devices: 24.3 us -> 26.5 us  [swap(): return lax.ppermute(value, axis, [(i, i ^ bit) for i in range(size)])]
    ppermute x0 -> x1, starting transfers between devices: none -> 1.64 us  [mix_small(): lax.ppermute(both_sum, z_far[0], direct)]
    pallas_call x2 -> x3, Pallas kernels: 5.66 us -> 7.03 us  [expert_of(): pl.pallas_call(functools.partial(expert_kernel, picks), out_shape=[jax.Sh...]
    unnamed x21 -> x24, local copies, waits for them, and re-layouts: 7.4 us -> 8.66 us
    convert_element_type x6 -> x0, other arithmetic: 1.01 us -> none  [add_up(): return total.astype(jnp.bfloat16)]
    concatenate x1 -> x0, other arithmetic: 0.92 us -> none  [spread(): value = jnp.concatenate([value, swap(value, step)], axis=0)]
  transfers between devices with their start and end apart: 22 -> 28, of which waited for: 15 -> 16; matrix products, arithmetic and copies ran while one was open for 4% -> 2% of each run, Pallas kernels for 1% -> 16%
where the time goes in v5:
time: 83.8 us; the launch traced here: 83.6 us
  starting transfers between devices  28.1 us (34%)
  waiting for transfers between devices  24.6 us (29%)
  Pallas kernels  18.9 us (23%)
  local copies, waits for them, and re-layouts  8.66 us (10%)
  matrix products  1.58 us (2%)
  between operations  1.49 us (2%)
    ppermute x27, starting transfers between devices, swap(): return lax.ppermute(value, axis, [(i, i ^ bit) for i in range(size)])  26.5 us
    ppermute x27, waiting for transfers between devices, swap(): return lax.ppermute(value, axis, [(i, i ^ bit) for i in range(size)])  24.6 us
    unnamed x24, local copies, waits for them, and re-layouts  8.66 us
    pallas_call x3, Pallas kernels, expert_of(): pl.pallas_call(functools.partial(expert_kernel, picks), out_shape=[jax.Sh...  7.03 us
    pallas_call x3, Pallas kernels, hold(): pl.pallas_call(functools.partial(hold_kernel, parts), out_shape=jax.Shape...  6.73 us
    pallas_call x3, Pallas kernels, sums_of(): pl.pallas_call(functools.partial(sums_kernel, cuts), out_shape=[jax.Shape...  2.12 us
    pallas_call x1, Pallas kernels, pack(): pl.pallas_call(pack_kernel, out_shape=jax.ShapeDtypeStruct((tokens.shape[...  1.78 us
  transfers between devices with their start and end apart: 28, of which 16 were waited for; matrix products, arithmetic and copies ran while one was open for 2% of the time, Pallas kernels for 16%

profile of v5, /device:TPU:0, one launch (start us, length us, event | category | flops | bytes accessed | tf_op | source)
XLA Modules:
  0.0 83.6 jit_solution(15017842494260544418)
XLA Ops:
  0.6 1.8 %pack.1.refs_1_.refs_0_ = bf16[16,3712]{1,0:T(8,128)(2,1)} custom-call(bf16[16,3584]{1,0:T(8,128)(2,1)} %tokens.1, s32[8,16]{1,0:T(8,128)} %bitcast.9, f32[8,16]{1,0:T(8,128)} %bitcast.10), custom_call_target="tpu_custom_call" | custom-call | tf_op jit(solution)/shard_map/pack/pallas_call | solution.py:102
  2.4 3.0 %collective-permute-start = (bf16[16,3712]{1,0:T(8,128)(2,1)}, bf16[16,3712]{1,0:T(8,128)(2,1)S(1)}, u32[]{:S(2)}, u32[]{:S(2)}) collective-permute-start(bf16[16,3712]{1,0:T(8,128)(2,1)} %pack.1.refs_1_.refs_0_), channel_id=1, source_target_pairs={{0,8},{4,12},{8,0},{12,4},{16,24},{20,28},{24,16},{28,20},{1,9},{5... | collective-permute-start | bytes 356360 | tf_op jit(solution)/shard_map/ppermute | solution.py:50
  5.5 2.6 %collective-permute-start.3 = (bf16[16,3712]{1,0:T(8,128)(2,1)}, bf16[16,3712]{1,0:T(8,128)(2,1)S(1)}, u32[]{:S(2)}, u32[]{:S(2)}) collective-permute-start(bf16[16,3712]{1,0:T(8,128)(2,1)} %pack.1.refs_1_.refs_0_), channel_id=1, source_target_pairs={{0,16},{4,20},{8,24},{12,28},{16,0},{20,4},{24,8},{28,12},{1,17},{... | collective-permute-start | bytes 356360 | tf_op jit(solution)/shard_map/ppermute | solution.py:50
  8.0 2.0 %copy-done.5 = bf16[1,512,3584]{2,1,0:T(8,128)(2,1)S(1)} copy-done((bf16[1,512,3584]{2,1,0:T(8,128)(2,1)S(1)}, bf16[1,512,3584]{2,1,0:T(8,128)(2,1)}, u32[]{:S(2)}) %copy-start.5) | copy-done | bytes 3670040
  11.0 2.2 %hold.3.refs_2_.w_down = bf16[1,512,3584]{2,1,0:T(8,128)(2,1)S(1)} custom-call(bf16[1,512,3584]{2,1,0:T(8,128)(2,1)S(1)} %copy-done.5, bf16[16,3712]{1,0:T(8,128)(2,1)S(1)} %copy-done.8), custom_call_target="tpu_custom_call" | custom-call | tf_op jit(solution)/shard_map/hold/pallas_call | solution.py:262
  13.3 1.9 %copy-done.1 = bf16[1,512,3584]{2,1,0:T(8,128)(2,1)} copy-done((bf16[1,512,3584]{2,1,0:T(8,128)(2,1)}, bf16[1,512,3584]{2,1,0:T(8,128)(2,1)S(1)}, u32[]{:S(2)}) %copy-start.1) | copy-done | bytes 3670040
  16.7 1.5 %collective-permute-start.2 = (bf16[32,3712]{1,0:T(8,128)(2,1)S(1)}, bf16[32,3712]{1,0:T(8,128)(2,1)S(1)}, u32[]{:S(2)}, u32[]{:S(2)}) collective-permute-start(bf16[32,3712]{1,0:T(8,128)(2,1)S(1)} %combine.8.refs_1_.refs_0_), channel_id=1, source_target_pairs={{0,2},{1,3},{2,0},{3,1},{4,6},{5,7},{6,4},{7,5},{8,10},{9,11},{10,... | collective-permute-start | bytes 712712 | tf_op jit(solution)/shard_map/ppermute | solution.py:50
  18.6 2.2 %hold.4.refs_5_.w_gate = bf16[1,3584,512]{2,1,0:T(8,128)(2,1)S(1)} custom-call(bf16[1,3584,512]{2,1,0:T(8,128)(2,1)S(1)} %copy-done.6, bf16[32,3712]{1,0:T(8,128)(2,1)S(1)} %combine.8.refs_1_.refs_0_), custom_call_target="tpu_custom_call" | custom-call | tf_op jit(solution)/shard_map/hold/pallas_call | solution.py:262
  20.9 2.1 %collective-permute-done.4.refs_4_ = bf16[16,3712]{1,0:T(8,128)(2,1)S(1)} collective-permute-done((bf16[16,3712]{1,0:T(8,128)(2,1)S(1)}, bf16[16,3712]{1,0:T(8,128)(2,1)S(1)}, u32[]{:S(2)}, u32[]{:S(2)}) %collective-permute-start.4) | collective-permute-done | bytes 118816 | tf_op jit(solution)/shard_map/ppermute | solution.py:50
  23.4 1.8 %copy-done.3 = bf16[1,3584,512]{2,1,0:T(8,128)(2,1)} copy-done((bf16[1,3584,512]{2,1,0:T(8,128)(2,1)}, bf16[1,3584,512]{2,1,0:T(8,128)(2,1)S(1)}, u32[]{:S(2)}) %copy-start.3) | copy-done | bytes 3670040
  25.2 1.5 %collective-permute-start.10 = (bf16[32,3712]{1,0:T(8,128)(2,1)S(1)}, bf16[32,3712]{1,0:T(8,128)(2,1)S(1)}, u32[]{:S(2)}, u32[]{:S(2)}) collective-permute-start(bf16[32,3712]{1,0:T(8,128)(2,1)S(1)} %get-tuple-element.34.refs_1_.refs_2_), channel_id=1, source_target_pairs={{0,2},{1,3},{2,0},{3,1},{4,6},{5,7},{6,4},{7,5},{8,10},{9,11},{10,... | collective-permute-start | bytes 712712 | tf_op jit(solution)/shard_map/ppermute | solution.py:50
  27.3 2.0 %copy-done.7 = bf16[1,3584,512]{2,1,0:T(8,128)(2,1)S(1)} copy-done((bf16[1,3584,512]{2,1,0:T(8,128)(2,1)S(1)}, bf16[1,3584,512]{2,1,0:T(8,128)(2,1)}, u32[]{:S(2)}) %copy-start.7) | copy-done | bytes 3670040
  29.3 2.2 %hold.5.w_up = bf16[1,3584,512]{2,1,0:T(8,128)(2,1)S(1)} custom-call(bf16[1,3584,512]{2,1,0:T(8,128)(2,1)S(1)} %copy-done.7, bf16[32,3712]{1,0:T(8,128)(2,1)S(1)} %get-tuple-element.34.refs_1_.refs_2_), custom_call_target="tpu_custom_call" | custom-call | tf_op jit(solution)/shard_map/hold/pallas_call | solution.py:262
  33.6 2.3 %expert.3 = (bf16[96,512]{1,0:T(8,128)(2,1)S(1)}, bf16[96,3584]{1,0:T(8,128)(2,1)S(1)}) custom-call(bf16[96,3712]{1,0:T(8,128)(2,1)S(1)} %get-tuple-element.33.own, bf16[96,3712]{1,0:T(8,128)(2,1)S(1)} %collective-permute-done.5.other, bf16[1,3584,512]{2,1,0:T(8,128)(2,1)S(1)} %copy-done.4, bf16[1,3584,512]{2,1,0:T(8,128)(2,1)S(1)} %hold.5.w_up, ...), custom_call_target="tpu_custom_call" | custom-call | flops 1761607680 | bytes 688128 | tf_op jit(solution)/shard_map/expert/pallas_call | solution.py:307
  41.6 1.5 %collective-permute-done.12.refs_0_ = bf16[16,3712]{1,0:T(8,128)(2,1)S(1)} collective-permute-done((bf16[16,3712]{1,0:T(8,128)(2,1)S(1)}, bf16[16,3712]{1,0:T(8,128)(2,1)S(1)}, u32[]{:S(2)}, u32[]{:S(2)}) %collective-permute-start.12) | collective-permute-done | bytes 118816 | tf_op jit(solution)/shard_map/ppermute | solution.py:50
  44.1 2.7 %expert.4 = (bf16[128,512]{1,0:T(8,128)(2,1)S(1)}, bf16[128,3584]{1,0:T(8,128)(2,1)S(1)}) custom-call(bf16[128,3712]{1,0:T(8,128)(2,1)S(1)} %get-tuple-element.40.own, bf16[128,3712]{1,0:T(8,128)(2,1)S(1)} %collective-permute-done.11.other, bf16[1,3584,512]{2,1,0:T(8,128)(2,1)S(1)} %copy-done.4, bf16[1,3584,512]{2,1,0:T(8,128)(2,1)S(1)} %hold.5.w_up, ...), custom_call_target="tpu_custom_call" | custom-call | flops 2348810240 | bytes 917504 | tf_op jit(solution)/shard_map/expert/pallas_call | solution.py:307
  47.4 2.3 %collective-permute-done.15.other = bf16[32,3712]{1,0:T(8,128)(2,1)S(1)} collective-permute-done((bf16[32,3712]{1,0:T(8,128)(2,1)S(1)}, bf16[32,3712]{1,0:T(8,128)(2,1)S(1)}, u32[]{:S(2)}, u32[]{:S(2)}) %collective-permute-start.15) | collective-permute-done | bytes 237600 | tf_op jit(solution)/shard_map/ppermute | solution.py:50
  49.7 2.1 %expert.5 = (bf16[32,512]{1,0:T(8,128)(2,1)S(1)}, bf16[32,3584]{1,0:T(8,128)(2,1)S(1)}) custom-call(bf16[32,3712]{1,0:T(8,128)(2,1)S(1)} %combine.11.refs_0_.own, bf16[32,3712]{1,0:T(8,128)(2,1)S(1)} %collective-permute-done.15.other, bf16[1,3584,512]{2,1,0:T(8,128)(2,1)S(1)} %copy-done.4, bf16[1,3584,512]{2,1,0:T(8,128)(2,1)S(1)} %hold.5.w_up, ...), custom_call_target="tpu_custom_call" | custom-call | flops 587202560 | bytes 229376 | tf_op jit(solution)/shard_map/expert/pallas_call | solution.py:307
  56.7 1.6 %collective-permute-start.19 = (bf16[16,3584]{1,0:T(8,128)(2,1)S(1)}, bf16[16,3584]{1,0:T(8,128)(2,1)S(1)}, u32[]{:S(2)}, u32[]{:S(2)}) collective-permute-start(bf16[16,3584]{1,0:T(8,128)(2,1)S(1)} %get-tuple-element.53), channel_id=1, source_target_pairs={{0,2},{1,3},{2,0},{3,1},{4,6},{5,7},{6,4},{7,5},{8,10},{9,11},{10,... | collective-permute-start | bytes 344072 | tf_op jit(solution)/shard_map/ppermute | solution.py:50
  59.9 1.8 %collective-permute-done.19.refs_6_ = bf16[16,3584]{1,0:T(8,128)(2,1)S(1)} collective-permute-done((bf16[16,3584]{1,0:T(8,128)(2,1)S(1)}, bf16[16,3584]{1,0:T(8,128)(2,1)S(1)}, u32[]{:S(2)}, u32[]{:S(2)}) %collective-permute-start.19) | collective-permute-done | bytes 114720 | tf_op jit(solution)/shard_map/ppermute | solution.py:50
  65.8 1.5 %collective-permute-start.22 = (bf16[32,3584]{1,0:T(8,128)(2,1)S(1)}, bf16[32,3584]{1,0:T(8,128)(2,1)S(1)}, u32[]{:S(2)}, u32[]{:S(2)}) collective-permute-start(bf16[32,3584]{1,0:T(8,128)(2,1)S(1)} %get-tuple-element.56), channel_id=1, source_target_pairs={{0,2},{1,3},{2,0},{3,1},{4,6},{5,7},{6,4},{7,5},{8,10},{9,11},{10,... | collective-permute-start | bytes 688136 | tf_op jit(solution)/shard_map/ppermute | solution.py:50
  67.6 4.1 %collective-permute-done.23.refs_1_ = bf16[32,3584]{1,0:T(8,128)(2,1)S(1)} collective-permute-done((bf16[32,3584]{1,0:T(8,128)(2,1)S(1)}, bf16[32,3584]{1,0:T(8,128)(2,1)S(1)}, u32[]{:S(2)}, u32[]{:S(2)}) %collective-permute-start.23) | collective-permute-done | bytes 229408 | tf_op jit(solution)/shard_map/ppermute | solution.py:50
  75.4 1.6 %collective-permute-start.26 = (bf16[16,3584]{1,0:T(8,128)(2,1)S(1)}, bf16[16,3584]{1,0:T(8,128)(2,1)S(1)}, u32[]{:S(2)}, u32[]{:S(2)}) collective-permute-start(bf16[16,3584]{1,0:T(8,128)(2,1)S(1)} %get-tuple-element.62), channel_id=1, source_target_pairs={{0,24},{4,28},{8,16},{12,20},{16,8},{20,12},{24,0},{28,4},{1,25},{... | collective-permute-start | bytes 344072 | tf_op jit(solution)/shard_map/ppermute | solution.py:468
  78.3 4.5 %collective-permute-done.27.refs_3_ = bf16[16,3584]{1,0:T(8,128)(2,1)S(1)} collective-permute-done((bf16[16,3584]{1,0:T(8,128)(2,1)S(1)}, bf16[16,3584]{1,0:T(8,128)(2,1)S(1)}, u32[]{:S(2)}, u32[]{:S(2)}) %collective-permute-start.27) | collective-permute-done | bytes 114720 | tf_op jit(solution)/shard_map/ppermute | solution.py:50
  (78 shorter events, 29.0 us)
Async XLA Ops:
  2.4 10.8 %collective-permute-start = (bf16[16,3712]{1,0:T(8,128)(2,1)}, bf16[16,3712]{1,0:T(8,128)(2,1)S(1)}, u32[]{:S(2)}, u32[]{:S(2)}) collective-permute-start(bf16[16,3712]{1,0:T(8,128)(2,1)} %pack.1.refs_1_.refs_0_), channel_id=1, source_target_pairs={{0,8},{4,12},{8,0},{12,4},{16,24},{20,28},{24,16},{28,20},{1,9},{5... | collective-permute-start | bytes 356360 | tf_op jit(solution)/shard_map/ppermute | solution.py:50
  5.5 12.7 %collective-permute-start.3 = (bf16[16,3712]{1,0:T(8,128)(2,1)}, bf16[16,3712]{1,0:T(8,128)(2,1)S(1)}, u32[]{:S(2)}, u32[]{:S(2)}) collective-permute-start(bf16[16,3712]{1,0:T(8,128)(2,1)} %pack.1.refs_1_.refs_0_), channel_id=1, source_target_pairs={{0,16},{4,20},{8,24},{12,28},{16,0},{20,4},{24,8},{28,12},{1,17},{... | collective-permute-start | bytes 356360 | tf_op jit(solution)/shard_map/ppermute | solution.py:50
  15.2 7.9 %collective-permute-start.1 = (bf16[32,3712]{1,0:T(8,128)(2,1)S(1)}, bf16[32,3712]{1,0:T(8,128)(2,1)S(1)}, u32[]{:S(2)}, u32[]{:S(2)}) collective-permute-start(bf16[32,3712]{1,0:T(8,128)(2,1)S(1)} %combine.8.refs_1_.refs_0_), channel_id=1, source_target_pairs={{0,1},{1,0},{2,3},{3,2},{4,5},{5,4},{6,7},{7,6},{8,9},{9,8},{10,11... | collective-permute-start | bytes 712712 | tf_op jit(solution)/shard_map/ppermute | solution.py:50
  16.7 6.7 %collective-permute-start.2 = (bf16[32,3712]{1,0:T(8,128)(2,1)S(1)}, bf16[32,3712]{1,0:T(8,128)(2,1)S(1)}, u32[]{:S(2)}, u32[]{:S(2)}) collective-permute-start(bf16[32,3712]{1,0:T(8,128)(2,1)S(1)} %combine.8.refs_1_.refs_0_), channel_id=1, source_target_pairs={{0,2},{1,3},{2,0},{3,1},{4,6},{5,7},{6,4},{7,5},{8,10},{9,11},{10,... | collective-permute-start | bytes 712712 | tf_op jit(solution)/shard_map/ppermute | solution.py:50
  18.2 4.8 %collective-permute-start.4 = (bf16[16,3712]{1,0:T(8,128)(2,1)S(1)}, bf16[16,3712]{1,0:T(8,128)(2,1)S(1)}, u32[]{:S(2)}, u32[]{:S(2)}) collective-permute-start(bf16[16,3712]{1,0:T(8,128)(2,1)S(1)} %collective-permute-done.3.refs_3_), channel_id=1, source_target_pairs={{0,8},{4,12},{8,0},{12,4},{16,24},{20,28},{24,16},{28,20},{1,9},{5... | collective-permute-start | bytes 356360 | tf_op jit(solution)/shard_map/ppermute | solution.py:50
  25.2 8.4 %collective-permute-start.5 = (bf16[96,3712]{1,0:T(8,128)(2,1)S(1)}, bf16[96,3712]{1,0:T(8,128)(2,1)S(1)}, u32[]{:S(2)}, u32[]{:S(2)}) collective-permute-start(bf16[96,3712]{1,0:T(8,128)(2,1)S(1)} %get-tuple-element.33.own), channel_id=1, source_target_pairs={{0,4},{4,0},{8,12},{12,8},{16,20},{20,16},{24,28},{28,24},{1,5},{5... | collective-permute-start | bytes 2138120 | tf_op jit(solution)/shard_map/ppermute | solution.py:50
  25.2 12.0 %collective-permute-start.10 = (bf16[32,3712]{1,0:T(8,128)(2,1)S(1)}, bf16[32,3712]{1,0:T(8,128)(2,1)S(1)}, u32[]{:S(2)}, u32[]{:S(2)}) collective-permute-start(bf16[32,3712]{1,0:T(8,128)(2,1)S(1)} %get-tuple-element.34.refs_1_.refs_2_), channel_id=1, source_target_pairs={{0,2},{1,3},{2,0},{3,1},{4,6},{5,7},{6,4},{7,5},{8,10},{9,11},{10,... | collective-permute-start | bytes 712712 | tf_op jit(solution)/shard_map/ppermute | solution.py:50
  26.7 10.5 %collective-permute-start.9 = (bf16[32,3712]{1,0:T(8,128)(2,1)S(1)}, bf16[32,3712]{1,0:T(8,128)(2,1)S(1)}, u32[]{:S(2)}, u32[]{:S(2)}) collective-permute-start(bf16[32,3712]{1,0:T(8,128)(2,1)S(1)} %get-tuple-element.34.refs_1_.refs_2_), channel_id=1, source_target_pairs={{0,1},{1,0},{2,3},{3,2},{4,5},{5,4},{6,7},{7,6},{8,9},{9,8},{10,11... | collective-permute-start | bytes 712712 | tf_op jit(solution)/shard_map/ppermute | solution.py:50
  31.6 5.2 %collective-permute-start.7 = (bf16[16,3712]{1,0:T(8,128)(2,1)S(1)}, bf16[16,3712]{1,0:T(8,128)(2,1)S(1)}, u32[]{:S(2)}, u32[]{:S(2)}) collective-permute-start(bf16[16,3712]{1,0:T(8,128)(2,1)S(1)} %get-tuple-element.38), channel_id=1, source_target_pairs={{0,2},{1,3},{2,0},{3,1},{4,6},{5,7},{6,4},{7,5},{8,10},{9,11},{10,... | collective-permute-start | bytes 356360 | tf_op jit(solution)/shard_map/ppermute | solution.py:50
  32.1 5.1 %collective-permute-start.8 = (bf16[16,3712]{1,0:T(8,128)(2,1)S(1)}, bf16[16,3712]{1,0:T(8,128)(2,1)S(1)}, u32[]{:S(2)}, u32[]{:S(2)}) collective-permute-start(bf16[16,3712]{1,0:T(8,128)(2,1)S(1)} %get-tuple-element.39), channel_id=1, source_target_pairs={{0,1},{1,0},{2,3},{3,2},{4,5},{5,4},{6,7},{7,6},{8,9},{9,8},{10,11... | collective-permute-start | bytes 356360 | tf_op jit(solution)/shard_map/ppermute | solution.py:50
  37.3 6.8 %collective-permute-start.11 = (bf16[128,3712]{1,0:T(8,128)(2,1)S(1)}, bf16[128,3712]{1,0:T(8,128)(2,1)S(1)}, u32[]{:S(2)}, u32[]{:S(2)}) collective-permute-start(bf16[128,3712]{1,0:T(8,128)(2,1)S(1)} %get-tuple-element.40.own), channel_id=1, source_target_pairs={{0,4},{4,0},{8,12},{12,8},{16,20},{20,16},{24,28},{28,24},{1,5},{5... | collective-permute-start | bytes 2850824 | tf_op jit(solution)/shard_map/ppermute | solution.py:50
  37.9 5.2 %collective-permute-start.12 = (bf16[16,3712]{1,0:T(8,128)(2,1)S(1)}, bf16[16,3712]{1,0:T(8,128)(2,1)S(1)}, u32[]{:S(2)}, u32[]{:S(2)}) collective-permute-start(bf16[16,3712]{1,0:T(8,128)(2,1)S(1)} %get-tuple-element.41), channel_id=1, source_target_pairs={{0,2},{1,3},{2,0},{3,1},{4,6},{5,7},{6,4},{7,5},{8,10},{9,11},{10,... | collective-permute-start | bytes 356360 | tf_op jit(solution)/shard_map/ppermute | solution.py:50
  39.2 4.9 %collective-permute-start.13 = (bf16[16,3712]{1,0:T(8,128)(2,1)S(1)}, bf16[16,3712]{1,0:T(8,128)(2,1)S(1)}, u32[]{:S(2)}, u32[]{:S(2)}) collective-permute-start(bf16[16,3712]{1,0:T(8,128)(2,1)S(1)} %get-tuple-element.42), channel_id=1, source_target_pairs={{0,1},{1,0},{2,3},{3,2},{4,5},{5,4},{6,7},{7,6},{8,9},{9,8},{10,11... | collective-permute-start | bytes 356360 | tf_op jit(solution)/shard_map/ppermute | solution.py:50
  46.8 9.2 %collective-permute-start.14 = (bf16[128,3584]{1,0:T(8,128)(2,1)S(1)}, bf16[128,3584]{1,0:T(8,128)(2,1)S(1)}, u32[]{:S(2)}, u32[]{:S(2)}) collective-permute-start(bf16[128,3584]{1,0:T(8,128)(2,1)S(1)} %get-tuple-element.44.refs_0_), channel_id=1, source_target_pairs={{0,4},{4,0},{8,12},{12,8},{16,20},{20,16},{24,28},{28,24},{1,5},{5... | collective-permute-start | bytes 2752520 | tf_op jit(solution)/shard_map/ppermute | solution.py:50
  54.0 5.8 %collective-permute-start.17 = (bf16[16,3584]{1,0:T(8,128)(2,1)S(1)}, bf16[16,3584]{1,0:T(8,128)(2,1)S(1)}, u32[]{:S(2)}, u32[]{:S(2)}) collective-permute-start(bf16[16,3584]{1,0:T(8,128)(2,1)S(1)} %get-tuple-element.51), channel_id=1, source_target_pairs={{0,2},{1,3},{2,0},{3,1},{4,6},{5,7},{6,4},{7,5},{8,10},{9,11},{10,... | collective-permute-start | bytes 344072 | tf_op jit(solution)/shard_map/ppermute | solution.py:50
  54.8 5.1 %collective-permute-start.18 = (bf16[16,3584]{1,0:T(8,128)(2,1)S(1)}, bf16[16,3584]{1,0:T(8,128)(2,1)S(1)}, u32[]{:S(2)}, u32[]{:S(2)}) collective-permute-start(bf16[16,3584]{1,0:T(8,128)(2,1)S(1)} %get-tuple-element.52), channel_id=1, source_target_pairs={{0,1},{1,0},{2,3},{3,2},{4,5},{5,4},{6,7},{7,6},{8,9},{9,8},{10,11... | collective-permute-start | bytes 344072 | tf_op jit(solution)/shard_map/ppermute | solution.py:50
  56.7 5.0 %collective-permute-start.19 = (bf16[16,3584]{1,0:T(8,128)(2,1)S(1)}, bf16[16,3584]{1,0:T(8,128)(2,1)S(1)}, u32[]{:S(2)}, u32[]{:S(2)}) collective-permute-start(bf16[16,3584]{1,0:T(8,128)(2,1)S(1)} %get-tuple-element.53), channel_id=1, source_target_pairs={{0,2},{1,3},{2,0},{3,1},{4,6},{5,7},{6,4},{7,5},{8,10},{9,11},{10,... | collective-permute-start | bytes 344072 | tf_op jit(solution)/shard_map/ppermute | solution.py:50
  63.2 8.5 %collective-permute-start.23 = (bf16[32,3584]{1,0:T(8,128)(2,1)S(1)}, bf16[32,3584]{1,0:T(8,128)(2,1)S(1)}, u32[]{:S(2)}, u32[]{:S(2)}) collective-permute-start(bf16[32,3584]{1,0:T(8,128)(2,1)S(1)} %get-tuple-element.58), channel_id=1, source_target_pairs={{0,1},{1,0},{2,3},{3,2},{4,5},{5,4},{6,7},{7,6},{8,9},{9,8},{10,11... | collective-permute-start | bytes 688136 | tf_op jit(solution)/shard_map/ppermute | solution.py:50
  63.8 8.5 %collective-permute-start.24 = (bf16[32,3584]{1,0:T(8,128)(2,1)S(1)}, bf16[32,3584]{1,0:T(8,128)(2,1)S(1)}, u32[]{:S(2)}, u32[]{:S(2)}) collective-permute-start(bf16[32,3584]{1,0:T(8,128)(2,1)S(1)} %get-tuple-element.59), channel_id=1, source_target_pairs={{0,2},{1,3},{2,0},{3,1},{4,6},{5,7},{6,4},{7,5},{8,10},{9,11},{10,... | collective-permute-start | bytes 688136 | tf_op jit(solution)/shard_map/ppermute | solution.py:50
  65.1 9.0 %collective-permute-start.21 = (bf16[32,3584]{1,0:T(8,128)(2,1)S(1)}, bf16[32,3584]{1,0:T(8,128)(2,1)S(1)}, u32[]{:S(2)}, u32[]{:S(2)}) collective-permute-start(bf16[32,3584]{1,0:T(8,128)(2,1)S(1)} %get-tuple-element.55), channel_id=1, source_target_pairs={{0,1},{1,0},{2,3},{3,2},{4,5},{5,4},{6,7},{7,6},{8,9},{9,8},{10,11... | collective-permute-start | bytes 688136 | tf_op jit(solution)/shard_map/ppermute | solution.py:50
  65.8 9.0 %collective-permute-start.22 = (bf16[32,3584]{1,0:T(8,128)(2,1)S(1)}, bf16[32,3584]{1,0:T(8,128)(2,1)S(1)}, u32[]{:S(2)}, u32[]{:S(2)}) collective-permute-start(bf16[32,3584]{1,0:T(8,128)(2,1)S(1)} %get-tuple-element.56), channel_id=1, source_target_pairs={{0,2},{1,3},{2,0},{3,1},{4,6},{5,7},{6,4},{7,5},{8,10},{9,11},{10,... | collective-permute-start | bytes 688136 | tf_op jit(solution)/shard_map/ppermute | solution.py:50
  72.5 10.4 %collective-permute-start.25 = (bf16[16,3584]{1,0:T(8,128)(2,1)S(1)}, bf16[16,3584]{1,0:T(8,128)(2,1)S(1)}, u32[]{:S(2)}, u32[]{:S(2)}) collective-permute-start(bf16[16,3584]{1,0:T(8,128)(2,1)S(1)} %get-tuple-element.60.refs_3_), channel_id=1, source_target_pairs={{0,16},{4,20},{8,24},{12,28},{16,0},{20,4},{24,8},{28,12},{1,17},{... | collective-permute-start | bytes 344072 | tf_op jit(solution)/shard_map/ppermute | solution.py:50
  74.9 7.9 %collective-permute-start.27 = (bf16[16,3584]{1,0:T(8,128)(2,1)S(1)}, bf16[16,3584]{1,0:T(8,128)(2,1)S(1)}, u32[]{:S(2)}, u32[]{:S(2)}) collective-permute-start(bf16[16,3584]{1,0:T(8,128)(2,1)S(1)} %get-tuple-element.63), channel_id=1, source_target_pairs={{0,8},{4,12},{8,0},{12,4},{16,24},{20,28},{24,16},{28,20},{1,9},{5... | collective-permute-start | bytes 344072 | tf_op jit(solution)/shard_map/ppermute | solution.py:50
  75.4 7.4 %collective-permute-start.26 = (bf16[16,3584]{1,0:T(8,128)(2,1)S(1)}, bf16[16,3584]{1,0:T(8,128)(2,1)S(1)}, u32[]{:S(2)}, u32[]{:S(2)}) collective-permute-start(bf16[16,3584]{1,0:T(8,128)(2,1)S(1)} %get-tuple-element.62), channel_id=1, source_target_pairs={{0,24},{4,28},{8,16},{12,20},{16,8},{20,12},{24,0},{28,4},{1,25},{... | collective-permute-start | bytes 344072 | tf_op jit(solution)/shard_map/ppermute | solution.py:468
  (16 other events, 106.9 us)

commit v6 on v5

--- a/solution.py
+++ b/solution.py
@@ -16,28 +16,67 @@
 VMEM_BYTES = 48 * 1024 * 1024
 LARGE_BYTES = 16 * 1024 * 1024
 SMALL_BYTES = 8 * 1024 * 1024
+FIRST_BYTES = 39 * 1024 * 1024
 whole = pl.BlockSpec(memory_space=pltpu.VMEM)
 
 score_scale = 192.0 ** (-0.5)
 neg_large = -1e30
 
 
-def attend(queries, cache, lengths, live_count):
-    scores = (
-        jnp.einsum("rhc,rlc->rhl", queries, cache, preferred_element_type=jnp.float32) * score_scale
-    )
-    positions = lax.broadcasted_iota(jnp.int32, scores.shape, 2)
-    inside = positions < lengths[:, None, None]
+def attend_kernel(lengths, live_rows, queries, channels, out):
+    request = pl.program_id(0)
+    scores = jnp.dot(queries[0], channels[0], preferred_element_type=jnp.float32) * score_scale
+    positions = lax.broadcasted_iota(jnp.int32, scores.shape, 1)
+    inside = positions < lengths[request]
     masked = jnp.where(inside, scores, neg_large)
-    highest = jnp.max(masked, axis=2, keepdims=True)
+    highest = jnp.max(masked, axis=1, keepdims=True)
     powers = jnp.where(inside, jnp.exp(masked - highest), 0.0)
-    totals = jnp.sum(powers, axis=2, keepdims=True)
+    totals = jnp.sum(powers, axis=1, keepdims=True)
     weights = (powers / totals).astype(jnp.bfloat16)
-    context = jnp.einsum(
-        "rhl,rlc->rhc", weights, cache[:, :, :LAT], preferred_element_type=jnp.float32
-    ).astype(jnp.bfloat16)
-    request_slot = lax.broadcasted_iota(jnp.int32, context.shape, 0)
-    return jnp.where(request_slot < live_count, context, jnp.zeros_like(context))
+    context = lax.dot_general(
+        weights,
+        channels[0, :LAT, :],
+        (((1,), (1,)), ((), ())),
+        preferred_element_type=jnp.float32,
+    )
+    out[0] = jnp.where(request < live_rows[0], context, 0.0).astype(jnp.bfloat16)
+
+
+def attend(queries, cache, lengths, live_rows, after=()):
+    count, heads, width = queries.shape
+    positions = cache.shape[1]
+    scalars = pl.BlockSpec(memory_space=pltpu.SMEM)
+
+    def kernel(*refs):
+        attend_kernel(*refs[:4], refs[-2])
+        refs[-1][...] = jnp.zeros_like(refs[-1])
+
+    return pl.pallas_call(
+        kernel,
+        grid=(count,),
+        out_shape=[
+            jax.ShapeDtypeStruct((count, heads, LAT), jnp.bfloat16),
+            jax.ShapeDtypeStruct((8, 128), jnp.float32),
+        ],
+        in_specs=[
+            scalars,
+            scalars,
+            pl.BlockSpec((1, heads, width), lambda r: (r, 0, 0)),
+            pl.BlockSpec((1, width, positions), lambda r: (r, 0, 0)),
+        ]
+        + [pl.BlockSpec(memory_space=pl.ANY)] * len(after),
+        out_specs=[
+            pl.BlockSpec((1, heads, LAT), lambda r: (r, 0, 0)),
+            pl.BlockSpec((8, 128), lambda r: (0, 0)),
+        ],
+        compiler_params=pltpu.CompilerParams(vmem_limit_bytes=SMALL_BYTES),
+        cost_estimate=pl.CostEstimate(
+            flops=4 * count * heads * width * positions,
+            bytes_accessed=2 * count * positions * width,
+            transcendentals=count * heads * positions,
+        ),
+        name="attend",
+    )(lengths, live_rows, queries, jnp.swapaxes(cache, 1, 2), *after)
 
 
 def bits_of(count):
@@ -104,11 +143,16 @@
         out_shape=jax.ShapeDtypeStruct((tokens.shape[0], tokens.shape[1] + EXTRA), jnp.bfloat16),
         in_specs=[pl.BlockSpec(memory_space=pltpu.VMEM)] * 3,
         out_specs=pl.BlockSpec(memory_space=pltpu.VMEM),
+        compiler_params=pltpu.CompilerParams(vmem_limit_bytes=SMALL_BYTES),
         name="pack",
     )(tokens, ids.T, gates.T)
 
 
-def hidden_kernel(picks, expert, own, other, extra_own, extra_other, w_gate, w_up, h_own, h_other, gate_sum, up_sum):
+def expert_index():
+    return (lax.axis_index("grp") * lax.axis_size("ep") + lax.axis_index("ep")) // 2
+
+
+def hidden_kernel(picks, own, other, extra_own, extra_other, w_gate, w_up, h_own, h_other, gate_sum, up_sum):
     step = pl.program_id(0)
     rows = jnp.concatenate([own[...], other[...]], axis=0)
     gate_part = jnp.dot(rows, w_gate[0], preferred_element_type=jnp.float32)
@@ -127,7 +171,7 @@
     @pl.when(step == pl.num_programs(0) - 1)
     def _():
         count = own.shape[0]
-        wanted = expert[0].astype(jnp.float32)
+        wanted = expert_index().astype(jnp.float32)
         for extra, out, at in ((extra_own, h_own, 0), (extra_other, h_other, count)):
             columns = extra[...].astype(jnp.float32)
             value = columns[:, picks : 2 * picks] + columns[:, 2 * picks : 3 * picks]
@@ -140,7 +184,7 @@
             out[...] = (hidden * share).astype(jnp.bfloat16)
 
 
-def hidden_of(expert, own, other, w_gate, w_up, picks):
+def hidden_of(own, other, w_gate, w_up, picks):
     count, width = own.shape
     _, feature, half = w_gate.shape
     depth = feature // BLOCKS
@@ -152,8 +196,7 @@
         functools.partial(hidden_kernel, picks),
         grid=(BLOCKS,),
         out_shape=[jax.ShapeDtypeStruct((count, half), jnp.bfloat16)] * 2,
-        in_specs=[pl.BlockSpec(memory_space=pltpu.SMEM), rows_spec, rows_spec, extra_spec, extra_spec]
-        + [weight_spec] * 2,
+        in_specs=[rows_spec] * 2 + [extra_spec] * 2 + [weight_spec] * 2,
         out_specs=[out_spec] * 2,
         scratch_shapes=[pltpu.VMEM((2 * count, half), jnp.float32)] * 2,
         compiler_params=pltpu.CompilerParams(vmem_limit_bytes=VMEM_BYTES),
@@ -163,7 +206,7 @@
             transcendentals=2 * count * half,
         ),
         name="hidden",
-    )(expert, own, other, own, other, w_gate, w_up)
+    )(own, other, own, other, w_gate, w_up)
 
 
 def down_kernel(cuts, hidden, w_down, *refs):
@@ -240,41 +283,15 @@
     )(*inputs, *after)
 
 
-def hold_kernel(parts, *refs):
-    weight, out, sems = refs[0], refs[-2], refs[-1]
-    depth = weight.shape[1] // parts
-    copies = [
-        pltpu.make_async_copy(
-            weight.at[:, pl.ds(part * depth, depth), :],
-            out.at[:, pl.ds(part * depth, depth), :],
-            sems.at[part],
-        )
-        for part in range(parts)
-    ]
-    for copy in copies:
-        copy.start()
-    for copy in copies:
-        copy.wait()
-
-
-def hold(weight, after):
-    parts = 8
-    return pl.pallas_call(
-        functools.partial(hold_kernel, parts),
-        out_shape=jax.ShapeDtypeStruct(weight.shape, weight.dtype),
-        in_specs=[pl.BlockSpec(memory_space=pltpu.HBM)]
-        + [pl.BlockSpec(memory_space=pl.ANY)] * len(after),
-        out_specs=whole,
-        scratch_shapes=[pltpu.SemaphoreType.DMA((parts,))],
-        compiler_params=pltpu.CompilerParams(vmem_limit_bytes=SMALL_BYTES),
-        name="hold",
-    )(weight, *after)
-
-
-def expert_kernel(picks, own, other, w_gate, w_up, w_down, expert, *refs):
-    h_own, out, rows, hidden = refs[-4:]
+def expert_kernel(picks, own, other, w_gate, w_up, w_down, *refs):
+    expert_body(picks, own, other, w_gate, w_up, w_down, *refs[-4:])
+
+
+def expert_body(
+    picks, own, other, w_gate, w_up, w_down, h_own, out, rows, hidden, ready=lambda number: None
+):
     count, feature, half = own.shape[0], w_gate.shape[1], w_gate.shape[2]
-    wanted = expert[0].astype(jnp.float32)
+    wanted = expert_index().astype(jnp.float32)
     shares = []
     for ref, at in ((own, 0), (other, count)):
         rows[at : at + count, :] = ref[:, :feature]
@@ -284,24 +301,85 @@
         shares.append(jnp.sum(jnp.where(named, value, 0.0), axis=1, keepdims=True))
     share = jnp.concatenate(shares, axis=0)
     for at in range(0, half, TILE):
+        ready(at // TILE * 2)
         gate_part = jnp.dot(
             rows[...], w_gate[0, :, at : at + TILE], preferred_element_type=jnp.float32
         )
+        ready(at // TILE * 2 + 1)
         up_part = jnp.dot(
             rows[...], w_up[0, :, at : at + TILE], preferred_element_type=jnp.float32
         )
         product = gate_part / (1.0 + jnp.exp(-gate_part)) * up_part * share
         hidden[:, at : at + TILE] = product.astype(jnp.bfloat16)
     h_own[...] = hidden[:count, :]
-    for at in range(0, feature, 2 * TILE):
-        out[:, at : at + 2 * TILE] = jnp.dot(
-            hidden[count:, :],
-            w_down[0, :, at : at + 2 * TILE],
-            preferred_element_type=jnp.float32,
+    wide = feature // BLOCKS
+    for at in range(0, feature, wide):
+        ready(half // TILE * 2 + at // wide)
+        out[:, at : at + wide] = jnp.dot(
+            hidden[count:, :], w_down[0, :, at : at + wide], preferred_element_type=jnp.float32
         ).astype(jnp.bfloat16)
 
 
-def expert_of(expert, own, other, w_gate, w_up, w_down, picks, after=()):
+def first_kernel(picks, own, other, gate_far, up_far, down_far, *refs):
+    h_own, out, w_gate, w_up, w_down, rows, hidden, sems = refs
+    feature, half = w_gate.shape[1], w_gate.shape[2]
+    depth = feature // BLOCKS
+    groups = []
+
+    def begin(pairs):
+        copies = []
+        for source, target, index in pairs:
+            at = len(copies) + sum(len(group) for group in groups)
+            copies.append(pltpu.make_async_copy(source.at[index], target.at[index], sems.at[at]))
+        for copy in copies:
+            copy.start()
+        groups.append(copies)
+
+    for left in range(0, half, TILE):
+        for source, target in ((gate_far, w_gate), (up_far, w_up)):
+            begin(
+                (source, target, (0, pl.ds(top, depth), pl.ds(left, TILE)))
+                for top in range(0, feature, depth)
+            )
+    for left in range(0, feature, feature // BLOCKS):
+        begin([(down_far, w_down, (0, slice(None), pl.ds(left, feature // BLOCKS)))])
+
+    def ready(number):
+        for copy in groups[number]:
+            copy.wait()
+
+    expert_body(picks, own, other, w_gate, w_up, w_down, h_own, out, rows, hidden, ready)
+
+
+def first_of(own, other, w_gate, w_up, w_down, picks, after=()):
+    count = own.shape[0]
+    _, feature, half = w_gate.shape
+    copies = 2 * (half // TILE) * BLOCKS + BLOCKS
+    return pl.pallas_call(
+        functools.partial(first_kernel, picks),
+        out_shape=[
+            jax.ShapeDtypeStruct((count, half), jnp.bfloat16),
+            jax.ShapeDtypeStruct((count, feature), jnp.bfloat16),
+        ]
+        + [jax.ShapeDtypeStruct(w.shape, w.dtype) for w in (w_gate, w_up, w_down)],
+        in_specs=[whole] * 2 + [pl.BlockSpec(memory_space=pl.ANY)] * 3,
+        out_specs=[whole] * 5,
+        scratch_shapes=[
+            pltpu.VMEM((2 * count, feature), jnp.bfloat16),
+            pltpu.VMEM((2 * count, half), jnp.bfloat16),
+            pltpu.SemaphoreType.DMA((copies,)),
+        ],
+        compiler_params=pltpu.CompilerParams(vmem_limit_bytes=FIRST_BYTES),
+        cost_estimate=pl.CostEstimate(
+            flops=10 * count * feature * half,
+            bytes_accessed=6 * feature * half,
+            transcendentals=2 * count * half,
+        ),
+        name="first",
+    )(own, other, w_gate, w_up, w_down)
+
+
+def expert_of(own, other, w_gate, w_up, w_down, picks, after=()):
     count = own.shape[0]
     _, feature, half = w_gate.shape
     return pl.pallas_call(
@@ -310,9 +388,7 @@
             jax.ShapeDtypeStruct((count, half), jnp.bfloat16),
             jax.ShapeDtypeStruct((count, feature), jnp.bfloat16),
         ],
-        in_specs=[whole] * 5
-        + [pl.BlockSpec(memory_space=pltpu.SMEM)]
-        + [pl.BlockSpec(memory_space=pl.ANY)] * len(after),
+        in_specs=[whole] * 5 + [pl.BlockSpec(memory_space=pl.ANY)] * len(after),
         out_specs=[whole] * 2,
         scratch_shapes=[
             pltpu.VMEM((2 * count, feature), jnp.bfloat16),
@@ -325,7 +401,7 @@
             transcendentals=2 * count * half,
         ),
         name="expert",
-    )(own, other, w_gate, w_up, w_down, expert, *after)
+    )(own, other, w_gate, w_up, w_down, *after)
 
 
 def sums_kernel(cuts, hidden, w_down, arrived, *refs):
@@ -359,7 +435,7 @@
     )(hidden, w_down, arrived, *after)
 
 
-def mix_large(packed, weights, expert, picks, steps):
+def mix_large(packed, weights, picks, steps):
     w_gate, w_up, w_down = weights
     z_near, z_far, x_steps, y_steps, core = steps
     near = spread(packed, z_near)
@@ -373,8 +449,8 @@
     late_cuts = [group.shape[0] for group in late]
     early_own, late_own = jnp.concatenate(early, axis=0), jnp.concatenate(late, axis=0)
     early_other, late_other = swap(early_own, core), swap(late_own, core)
-    early_h, early_h_other = hidden_of(expert, early_own, early_other, w_gate, w_up, picks)
-    late_h, late_h_other = hidden_of(expert, late_own, late_other, w_gate, w_up, picks)
+    early_h, early_h_other = hidden_of(early_own, early_other, w_gate, w_up, picks)
+    late_h, late_h_other = hidden_of(late_own, late_other, w_gate, w_up, picks)
     (late_out,) = down_of(late_h_other, w_down, [late_h_other.shape[0]])
     late_in = swap(late_out, core)
     (early_out,) = down_of(early_h_other, w_down, [early_h_other.shape[0]])
@@ -390,8 +466,7 @@
     return add_up(near[:count], give_back(near[count:], z_near, count) + [swap(far, z_far)])
 
 
-def mix_small(packed, weights, expert, picks, steps):
-    w_gate, w_up, w_down = weights
+def mix_small(packed, weights, picks, steps, attention):
     z_near, z_far, x, y, core = steps
     n = packed.shape[0]
 
@@ -400,11 +475,10 @@
 
     from_near = swap(packed, z_near)
     from_far = swap(packed, z_far)
-    w_down = hold(w_down, [packed])
-    (near,) = combine([packed, from_near], [rows_of((0, 0, n), (1, 0, n))], [w_down])
+    (near,) = combine([packed, from_near], [rows_of((0, 0, n), (1, 0, n))])
     near_x, near_y = swap(near, x), swap(near, y)
     from_both = swap(from_far, z_near)
-    w_gate = hold(w_gate, [near])
+    context, done = attention([near])
     first_own, far, half_x, half_y = combine(
         [near, near_x, near_y, from_far, from_both],
         [
@@ -413,14 +487,13 @@
             rows_of((1, 0, n)),
             rows_of((2, n, n)),
         ],
-        [w_gate],
+        [done],
     )
     first_other = swap(first_own, core)
     far_x, far_y = swap(far, x), swap(far, y)
     near_xy_top, near_xy_low = swap(half_x, y), swap(half_y, x)
-    w_up = hold(w_up, [far])
-    held = (w_gate, w_up, w_down)
-    first_h, first_out = expert_of(expert, first_own, first_other, *held, picks)
+    first_h, first_out, *weights = first_of(first_own, first_other, *weights, picks)
+    w_down = weights[2]
     second_own, half_x, half_y = combine(
         [near_xy_top, near_xy_low, far, far_x, far_y],
         [
@@ -437,10 +510,10 @@
     (third_own,) = combine([far_xy_top, far_xy_low], [rows_of((0, 0, n), (1, 0, n))], [near])
     third_other = swap(third_own, core)
     second_h, second_out = expert_of(
-        expert, second_own, second_other, *held, picks, [third_own]
+        second_own, second_other, *weights, picks, [third_own]
     )
     second_in = swap(second_out, core)
-    third_h, third_out = expert_of(expert, third_own, third_other, *held, picks, [second_out])
+    third_h, third_out = expert_of(third_own, third_other, *weights, picks, [second_out])
     near_xy_top, near_xy_low, far, far_x, far_y = sums_of(
         second_h, w_down, [n, n, 2 * n, 2 * n, 2 * n], second_in, [third_out]
     )
@@ -467,7 +540,7 @@
     direct = [(i, i ^ z_far[1] ^ z_near[1]) for i in range(size)]
     terms = [swap(far_sum, z_far), lax.ppermute(both_sum, z_far[0], direct), swap(near_sum, z_near)]
     (mixed,) = combine([own_sum, *terms], [[(n, [(0, 0), (1, 0), (2, 0), (3, 0)])]])
-    return mixed
+    return mixed, context
 
 
 def per_device(queries, cache, lengths, live_rows, tokens, ids, gates, w_gate, w_up, w_down):
@@ -479,17 +552,17 @@
     z_far = ("grp", grp_bits[-1])
     x_steps = [("ep", bit) for bit in ep_bits[: len(ep_bits) // 2]]
     y_steps = [("ep", bit) for bit in ep_bits[len(ep_bits) // 2 :]]
-    expert = ((lax.axis_index("grp") * lax.axis_size("ep") + lax.axis_index("ep")) >> 1).reshape(1)
-
-    context = attend(queries, cache, lengths, live_rows[0])
+
     packed = pack(tokens, ids, gates)
     weights = (w_gate, w_up, w_down)
     if len(z_near) == len(x_steps) == len(y_steps) == 1:
         steps = (z_near[0], z_far, x_steps[0], y_steps[0], core)
-        mixed = mix_small(packed, weights, expert, picks, steps)
+        attention = functools.partial(attend, queries, cache, lengths, live_rows)
+        mixed, context = mix_small(packed, weights, picks, steps, attention)
     else:
         steps = (z_near, z_far, x_steps, y_steps, core)
-        mixed = mix_large(packed, weights, expert, picks, steps)
+        mixed = mix_large(packed, weights, picks, steps)
+        context, _ = attend(queries, cache, lengths, live_rows)
     return (context, mixed)
 
 

time: 83.8 us -> 80.3 us (0.958)
  local copies, waits for them, and re-layouts: 8.66 us -> 5.16 us
  matrix products: 1.58 us -> 0 us
  starting transfers between devices: 28.1 us -> 29.4 us
  waiting for transfers between devices: 24.6 us -> 25.8 us
    ppermute x1, waiting for transfers between devices: 0.01 us -> 3.55 us  [mix_small(): lax.ppermute(both_sum, z_far[0], direct)]
    unnamed x24 -> x12, local copies, waits for them, and re-layouts: 8.66 us -> 5.16 us
    pallas_call x3 -> x2, Pallas kernels: 6.73 us -> 10 us  [the longest x1 6.38 us: first_of(): pl.pallas_call(functools.partial(first_kernel, picks), out_shape=[jax.Sha...]
    ppermute x27, waiting for transfers between devices: 24.6 us -> 22.3 us  [swap(): return lax.ppermute(value, axis, [(i, i ^ bit) for i in range(size)])]
    pallas_call x3 -> x2, Pallas kernels: 7.03 us -> 4.72 us  [expert_of(): pl.pallas_call(functools.partial(expert_kernel, picks), out_shape=[jax.Sh...]
    pallas_call x1, Pallas kernels: 1.78 us -> 0.17 us  [pack(): pl.pallas_call(pack_kernel, out_shape=jax.ShapeDtypeStruct((tokens.shape[...]
    dot_general x2 -> x0, matrix products: 1.58 us -> none  [the longest x1 1.24 us: attend(): jnp.einsum('rhl,rlc->rhc', weights, cache[:, :, :LAT], preferred_element_...]
    ppermute x27, starting transfers between devices: 26.5 us -> 28.1 us  [swap(): return lax.ppermute(value, axis, [(i, i ^ bit) for i in range(size)])]
  transfers between devices with their start and end apart: 28 -> 28, of which waited for: 16 -> 16; matrix products, arithmetic and copies ran while one was open for 2% -> 0% of each run, Pallas kernels for 16% -> 18%
where the time goes in v6:
time: 80.3 us; the launch traced here: 80 us
  starting transfers between devices  29.4 us (37%)
  waiting for transfers between devices  25.8 us (32%)
  Pallas kernels  18.2 us (23%)
  local copies, waits for them, and re-layouts  5.16 us (6%)
  between operations  1.44 us (2%)
    ppermute x27, starting transfers between devices, swap(): return lax.ppermute(value, axis, [(i, i ^ bit) for i in range(size)])  28.1 us
    ppermute x27, waiting for transfers between devices, swap(): return lax.ppermute(value, axis, [(i, i ^ bit) for i in range(size)])  22.3 us
    pallas_call x1, Pallas kernels, first_of(): pl.pallas_call(functools.partial(first_kernel, picks), out_shape=[jax.Sha...  6.38 us
    unnamed x12, local copies, waits for them, and re-layouts  5.16 us
    pallas_call x2, Pallas kernels, expert_of(): pl.pallas_call(functools.partial(expert_kernel, picks), out_shape=[jax.Sh...  4.72 us
    pallas_call x1, Pallas kernels, attend(): pl.pallas_call(kernel, grid=(count,), out_shape=[jax.ShapeDtypeStruct((co...  3.66 us
    ppermute x1, waiting for transfers between devices, mix_small(): lax.ppermute(both_sum, z_far[0], direct)  3.55 us
    pallas_call x3, Pallas kernels, sums_of(): pl.pallas_call(functools.partial(sums_kernel, cuts), out_shape=[jax.Shape...  2.08 us
  transfers between devices with their start and end apart: 28, of which 16 were waited for; matrix products, arithmetic and copies ran while one was open for 0% of the time, Pallas kernels for 18%

profile of v6, /device:TPU:0, one launch (start us, length us, event | category | flops | bytes accessed | tf_op | source)
XLA Modules:
  0.0 80.0 jit_solution(2366682090460671153)
XLA Ops:
  3.1 3.0 %collective-permute-start = (bf16[16,3712]{1,0:T(8,128)(2,1)S(1)}, bf16[16,3712]{1,0:T(8,128)(2,1)S(1)}, u32[]{:S(2)}, u32[]{:S(2)}) collective-permute-start(bf16[16,3712]{1,0:T(8,128)(2,1)S(1)} %pack.1.refs_0_), channel_id=1, source_target_pairs={{0,8},{4,12},{8,0},{12,4},{16,24},{20,28},{24,16},{28,20},{1,9},{5... | collective-permute-start | bytes 356360 | tf_op jit(solution)/shard_map/ppermute | solution.py:89
  6.1 2.6 %collective-permute-start.3 = (bf16[16,3712]{1,0:T(8,128)(2,1)S(1)}, bf16[16,3712]{1,0:T(8,128)(2,1)S(1)}, u32[]{:S(2)}, u32[]{:S(2)}) collective-permute-start(bf16[16,3712]{1,0:T(8,128)(2,1)S(1)} %pack.1.refs_0_), channel_id=1, source_target_pairs={{0,16},{4,20},{8,24},{12,28},{16,0},{20,4},{24,8},{28,12},{1,17},{... | collective-permute-start | bytes 356360 | tf_op jit(solution)/shard_map/ppermute | solution.py:89
  8.7 1.9 %collective-permute-done.refs_1_ = bf16[16,3712]{1,0:T(8,128)(2,1)S(1)} collective-permute-done((bf16[16,3712]{1,0:T(8,128)(2,1)S(1)}, bf16[16,3712]{1,0:T(8,128)(2,1)S(1)}, u32[]{:S(2)}, u32[]{:S(2)}) %collective-permute-start) | collective-permute-done | bytes 118816 | tf_op jit(solution)/shard_map/ppermute | solution.py:89
  10.7 1.9 %collective-permute-start.1 = (bf16[32,3712]{1,0:T(8,128)(2,1)S(1)}, bf16[32,3712]{1,0:T(8,128)(2,1)S(1)}, u32[]{:S(2)}, u32[]{:S(2)}) collective-permute-start(bf16[32,3712]{1,0:T(8,128)(2,1)S(1)} %combine.8.refs_4_.refs_0_), channel_id=1, source_target_pairs={{0,1},{1,0},{2,3},{3,2},{4,5},{5,4},{6,7},{7,6},{8,9},{9,8},{10,11... | collective-permute-start | bytes 712712 | tf_op jit(solution)/shard_map/ppermute | solution.py:89
  12.5 1.5 %collective-permute-start.2 = (bf16[32,3712]{1,0:T(8,128)(2,1)S(1)}, bf16[32,3712]{1,0:T(8,128)(2,1)S(1)}, u32[]{:S(2)}, u32[]{:S(2)}) collective-permute-start(bf16[32,3712]{1,0:T(8,128)(2,1)S(1)} %combine.8.refs_4_.refs_0_), channel_id=1, source_target_pairs={{0,2},{1,3},{2,0},{3,1},{4,6},{5,7},{6,4},{7,5},{8,10},{9,11},{10,... | collective-permute-start | bytes 712712 | tf_op jit(solution)/shard_map/ppermute | solution.py:89
  18.3 3.7 %attend.1 = (bf16[4,64,512]{2,1,0:T(8,128)(2,1)}, f32[8,128]{1,0:T(8,128)S(1)}) custom-call(s32[4]{0:T(128)S(1)} %copy-done.5, s32[1]{0:T(128)S(6)} %copy.12.refs_1_, bf16[4,64,576]{2,1,0:T(8,128)(2,1)S(1)} %copy-done.1, bf16[4,576,256]{2,1,0:T(8,128)(2,1)S(1)} %bitcast.3, bf16[32,3712]{1,0:T(8,128)(2,1)S(1)} %combine.8.refs_4_.refs_0_), custom_call_target="tpu_custom_call" | custom-call | flops 150994944 | bytes 1179648 | tf_op jit(solution)/shard_map/attend/pallas_call | solution.py:54
  22.1 1.6 %collective-permute-start.9 = (bf16[32,3712]{1,0:T(8,128)(2,1)S(1)}, bf16[32,3712]{1,0:T(8,128)(2,1)S(1)}, u32[]{:S(2)}, u32[]{:S(2)}) collective-permute-start(bf16[32,3712]{1,0:T(8,128)(2,1)S(1)} %get-tuple-element.47.refs_2_), channel_id=1, source_target_pairs={{0,1},{1,0},{2,3},{3,2},{4,5},{5,4},{6,7},{7,6},{8,9},{9,8},{10,11... | collective-permute-start | bytes 712712 | tf_op jit(solution)/shard_map/ppermute | solution.py:89
  23.7 1.6 %collective-permute-start.10 = (bf16[32,3712]{1,0:T(8,128)(2,1)S(1)}, bf16[32,3712]{1,0:T(8,128)(2,1)S(1)}, u32[]{:S(2)}, u32[]{:S(2)}) collective-permute-start(bf16[32,3712]{1,0:T(8,128)(2,1)S(1)} %get-tuple-element.47.refs_2_), channel_id=1, source_target_pairs={{0,2},{1,3},{2,0},{3,1},{4,6},{5,7},{6,4},{7,5},{8,10},{9,11},{10,... | collective-permute-start | bytes 712712 | tf_op jit(solution)/shard_map/ppermute | solution.py:89
  26.3 6.4 %first.1 = (bf16[96,512]{1,0:T(8,128)(2,1)S(1)}, bf16[96,3584]{1,0:T(8,128)(2,1)S(1)}, bf16[1,3584,512]{2,1,0:T(8,128)(2,1)S(1)}, bf16[1,3584,512]{2,1,0:T(8,128)(2,1)S(1)}, bf16[1,512,3584]{2,1,0:T(8,128)(2,1)S(1)}) custom-call(bf16[96,3712]{1,0:T(8,128)(2,1)S(1)} %get-tuple-element.40.own, bf16[96,3712]{1,0:T(8,128)(2,1)S(1)} %collective-permute-done.5.other, ...), custom_call_target="tpu_custom_call" | custom-call | flops 1761607680 | bytes 11010048 | tf_op jit(solution)/shard_map/first/pallas_call | solution.py:358
  32.7 1.4 %collective-permute-done.7.refs_0_ = bf16[16,3712]{1,0:T(8,128)(2,1)S(1)} collective-permute-done((bf16[16,3712]{1,0:T(8,128)(2,1)S(1)}, bf16[16,3712]{1,0:T(8,128)(2,1)S(1)}, u32[]{:S(2)}, u32[]{:S(2)}) %collective-permute-start.7) | collective-permute-done | bytes 118816 | tf_op jit(solution)/shard_map/ppermute | solution.py:89
  34.8 1.5 %collective-permute-start.12 = (bf16[16,3712]{1,0:T(8,128)(2,1)S(1)}, bf16[16,3712]{1,0:T(8,128)(2,1)S(1)}, u32[]{:S(2)}, u32[]{:S(2)}) collective-permute-start(bf16[16,3712]{1,0:T(8,128)(2,1)S(1)} %get-tuple-element.51), channel_id=1, source_target_pairs={{0,2},{1,3},{2,0},{3,1},{4,6},{5,7},{6,4},{7,5},{8,10},{9,11},{10,... | collective-permute-start | bytes 356360 | tf_op jit(solution)/shard_map/ppermute | solution.py:89
  38.5 1.5 %collective-permute-done.12.refs_0_ = bf16[16,3712]{1,0:T(8,128)(2,1)S(1)} collective-permute-done((bf16[16,3712]{1,0:T(8,128)(2,1)S(1)}, bf16[16,3712]{1,0:T(8,128)(2,1)S(1)}, u32[]{:S(2)}, u32[]{:S(2)}) %collective-permute-start.12) | collective-permute-done | bytes 118816 | tf_op jit(solution)/shard_map/ppermute | solution.py:89
  41.3 2.7 %expert.2 = (bf16[128,512]{1,0:T(8,128)(2,1)S(1)}, bf16[128,3584]{1,0:T(8,128)(2,1)S(1)}) custom-call(bf16[128,3712]{1,0:T(8,128)(2,1)S(1)} %get-tuple-element.48.own, bf16[128,3712]{1,0:T(8,128)(2,1)S(1)} %collective-permute-done.11.other, bf16[1,3584,512]{2,1,0:T(8,128)(2,1)S(1)} %get-tuple-element.49.w_gate, ...), custom_call_target="tpu_custom_call" | custom-call | flops 2348810240 | bytes 917504 | tf_op jit(solution)/shard_map/expert/pallas_call | solution.py:385
  44.5 2.3 %collective-permute-done.15.other = bf16[32,3712]{1,0:T(8,128)(2,1)S(1)} collective-permute-done((bf16[32,3712]{1,0:T(8,128)(2,1)S(1)}, bf16[32,3712]{1,0:T(8,128)(2,1)S(1)}, u32[]{:S(2)}, u32[]{:S(2)}) %collective-permute-start.15) | collective-permute-done | bytes 237600 | tf_op jit(solution)/shard_map/ppermute | solution.py:89
  46.8 2.0 %expert.3 = (bf16[32,512]{1,0:T(8,128)(2,1)S(1)}, bf16[32,3584]{1,0:T(8,128)(2,1)S(1)}) custom-call(bf16[32,3712]{1,0:T(8,128)(2,1)S(1)} %combine.11.refs_0_.own, bf16[32,3712]{1,0:T(8,128)(2,1)S(1)} %collective-permute-done.15.other, bf16[1,3584,512]{2,1,0:T(8,128)(2,1)S(1)} %get-tuple-element.49.w_gate, bf16[1,3584,512]{2,1,0:T(8,128)(2,1)S(1)} %get-tuple-element.50.w_up, ...), custom_call_target="tpu_custom_call" | custom-call | flops 587202560 | bytes 229376 | tf_op jit(solution)/shard_map/expert/pallas_call | solution.py:385
  49.1 1.4 %collective-permute-done.16.arrived = bf16[32,3584]{1,0:T(8,128)(2,1)S(1)} collective-permute-done((bf16[32,3584]{1,0:T(8,128)(2,1)S(1)}, bf16[32,3584]{1,0:T(8,128)(2,1)S(1)}, u32[]{:S(2)}, u32[]{:S(2)}) %collective-permute-start.16) | collective-permute-done | bytes 229408 | tf_op jit(solution)/shard_map/ppermute | solution.py:89
  52.9 1.6 %collective-permute-start.19 = (bf16[16,3584]{1,0:T(8,128)(2,1)S(1)}, bf16[16,3584]{1,0:T(8,128)(2,1)S(1)}, u32[]{:S(2)}, u32[]{:S(2)}) collective-permute-start(bf16[16,3584]{1,0:T(8,128)(2,1)S(1)} %get-tuple-element.63), channel_id=1, source_target_pairs={{0,2},{1,3},{2,0},{3,1},{4,6},{5,7},{6,4},{7,5},{8,10},{9,11},{10,... | collective-permute-start | bytes 344072 | tf_op jit(solution)/shard_map/ppermute | solution.py:89
  54.5 1.5 %collective-permute-start.20 = (bf16[16,3584]{1,0:T(8,128)(2,1)S(1)}, bf16[16,3584]{1,0:T(8,128)(2,1)S(1)}, u32[]{:S(2)}, u32[]{:S(2)}) collective-permute-start(bf16[16,3584]{1,0:T(8,128)(2,1)S(1)} %get-tuple-element.64), channel_id=1, source_target_pairs={{0,1},{1,0},{2,3},{3,2},{4,5},{5,4},{6,7},{7,6},{8,9},{9,8},{10,11... | collective-permute-start | bytes 344072 | tf_op jit(solution)/shard_map/ppermute | solution.py:89
  57.2 1.7 %collective-permute-done.19.refs_6_ = bf16[16,3584]{1,0:T(8,128)(2,1)S(1)} collective-permute-done((bf16[16,3584]{1,0:T(8,128)(2,1)S(1)}, bf16[16,3584]{1,0:T(8,128)(2,1)S(1)}, u32[]{:S(2)}, u32[]{:S(2)}) %collective-permute-start.19) | collective-permute-done | bytes 114720 | tf_op jit(solution)/shard_map/ppermute | solution.py:89
  59.4 1.6 %collective-permute-start.23 = (bf16[32,3584]{1,0:T(8,128)(2,1)S(1)}, bf16[32,3584]{1,0:T(8,128)(2,1)S(1)}, u32[]{:S(2)}, u32[]{:S(2)}) collective-permute-start(bf16[32,3584]{1,0:T(8,128)(2,1)S(1)} %get-tuple-element.68), channel_id=1, source_target_pairs={{0,1},{1,0},{2,3},{3,2},{4,5},{5,4},{6,7},{7,6},{8,9},{9,8},{10,11... | collective-permute-start | bytes 688136 | tf_op jit(solution)/shard_map/ppermute | solution.py:89
  63.5 4.5 %collective-permute-done.23.refs_1_ = bf16[32,3584]{1,0:T(8,128)(2,1)S(1)} collective-permute-done((bf16[32,3584]{1,0:T(8,128)(2,1)S(1)}, bf16[32,3584]{1,0:T(8,128)(2,1)S(1)}, u32[]{:S(2)}, u32[]{:S(2)}) %collective-permute-start.23) | collective-permute-done | bytes 229408 | tf_op jit(solution)/shard_map/ppermute | solution.py:89
  69.1 2.7 %collective-permute-start.25 = (bf16[16,3584]{1,0:T(8,128)(2,1)S(1)}, bf16[16,3584]{1,0:T(8,128)(2,1)S(1)}, u32[]{:S(2)}, u32[]{:S(2)}) collective-permute-start(bf16[16,3584]{1,0:T(8,128)(2,1)S(1)} %get-tuple-element.70.refs_3_), channel_id=1, source_target_pairs={{0,16},{4,20},{8,24},{12,28},{16,0},{20,4},{24,8},{28,12},{1,17},{... | collective-permute-start | bytes 344072 | tf_op jit(solution)/shard_map/ppermute | solution.py:89
  73.3 1.7 %collective-permute-done.25.refs_1_ = bf16[16,3584]{1,0:T(8,128)(2,1)S(1)} collective-permute-done((bf16[16,3584]{1,0:T(8,128)(2,1)S(1)}, bf16[16,3584]{1,0:T(8,128)(2,1)S(1)}, u32[]{:S(2)}, u32[]{:S(2)}) %collective-permute-start.25) | collective-permute-done | bytes 114720 | tf_op jit(solution)/shard_map/ppermute | solution.py:89
  75.0 3.5 %collective-permute-done.26.refs_2_ = bf16[16,3584]{1,0:T(8,128)(2,1)S(1)} collective-permute-done((bf16[16,3584]{1,0:T(8,128)(2,1)S(1)}, bf16[16,3584]{1,0:T(8,128)(2,1)S(1)}, u32[]{:S(2)}, u32[]{:S(2)}) %collective-permute-start.26) | collective-permute-done | bytes 114720 | tf_op jit(solution)/shard_map/ppermute | solution.py:541
  (60 shorter events, 22.9 us)
Async XLA Ops:
  3.1 7.6 %collective-permute-start = (bf16[16,3712]{1,0:T(8,128)(2,1)S(1)}, bf16[16,3712]{1,0:T(8,128)(2,1)S(1)}, u32[]{:S(2)}, u32[]{:S(2)}) collective-permute-start(bf16[16,3712]{1,0:T(8,128)(2,1)S(1)} %pack.1.refs_0_), channel_id=1, source_target_pairs={{0,8},{4,12},{8,0},{12,4},{16,24},{20,28},{24,16},{28,20},{1,9},{5... | collective-permute-start | bytes 356360 | tf_op jit(solution)/shard_map/ppermute | solution.py:89
  6.1 8.2 %collective-permute-start.3 = (bf16[16,3712]{1,0:T(8,128)(2,1)S(1)}, bf16[16,3712]{1,0:T(8,128)(2,1)S(1)}, u32[]{:S(2)}, u32[]{:S(2)}) collective-permute-start(bf16[16,3712]{1,0:T(8,128)(2,1)S(1)} %pack.1.refs_0_), channel_id=1, source_target_pairs={{0,16},{4,20},{8,24},{12,28},{16,0},{20,4},{24,8},{28,12},{1,17},{... | collective-permute-start | bytes 356360 | tf_op jit(solution)/shard_map/ppermute | solution.py:89
  10.7 11.3 %collective-permute-start.1 = (bf16[32,3712]{1,0:T(8,128)(2,1)S(1)}, bf16[32,3712]{1,0:T(8,128)(2,1)S(1)}, u32[]{:S(2)}, u32[]{:S(2)}) collective-permute-start(bf16[32,3712]{1,0:T(8,128)(2,1)S(1)} %combine.8.refs_4_.refs_0_), channel_id=1, source_target_pairs={{0,1},{1,0},{2,3},{3,2},{4,5},{5,4},{6,7},{7,6},{8,9},{9,8},{10,11... | collective-permute-start | bytes 712712 | tf_op jit(solution)/shard_map/ppermute | solution.py:89
  12.5 9.4 %collective-permute-start.2 = (bf16[32,3712]{1,0:T(8,128)(2,1)S(1)}, bf16[32,3712]{1,0:T(8,128)(2,1)S(1)}, u32[]{:S(2)}, u32[]{:S(2)}) collective-permute-start(bf16[32,3712]{1,0:T(8,128)(2,1)S(1)} %combine.8.refs_4_.refs_0_), channel_id=1, source_target_pairs={{0,2},{1,3},{2,0},{3,1},{4,6},{5,7},{6,4},{7,5},{8,10},{9,11},{10,... | collective-permute-start | bytes 712712 | tf_op jit(solution)/shard_map/ppermute | solution.py:89
  14.3 7.7 %collective-permute-start.4 = (bf16[16,3712]{1,0:T(8,128)(2,1)S(1)}, bf16[16,3712]{1,0:T(8,128)(2,1)S(1)}, u32[]{:S(2)}, u32[]{:S(2)}) collective-permute-start(bf16[16,3712]{1,0:T(8,128)(2,1)S(1)} %collective-permute-done.3.refs_3_), channel_id=1, source_target_pairs={{0,8},{4,12},{8,0},{12,4},{16,24},{20,28},{24,16},{28,20},{1,9},{5... | collective-permute-start | bytes 356360 | tf_op jit(solution)/shard_map/ppermute | solution.py:89
  22.1 12.0 %collective-permute-start.9 = (bf16[32,3712]{1,0:T(8,128)(2,1)S(1)}, bf16[32,3712]{1,0:T(8,128)(2,1)S(1)}, u32[]{:S(2)}, u32[]{:S(2)}) collective-permute-start(bf16[32,3712]{1,0:T(8,128)(2,1)S(1)} %get-tuple-element.47.refs_2_), channel_id=1, source_target_pairs={{0,1},{1,0},{2,3},{3,2},{4,5},{5,4},{6,7},{7,6},{8,9},{9,8},{10,11... | collective-permute-start | bytes 712712 | tf_op jit(solution)/shard_map/ppermute | solution.py:89
  23.7 10.4 %collective-permute-start.10 = (bf16[32,3712]{1,0:T(8,128)(2,1)S(1)}, bf16[32,3712]{1,0:T(8,128)(2,1)S(1)}, u32[]{:S(2)}, u32[]{:S(2)}) collective-permute-start(bf16[32,3712]{1,0:T(8,128)(2,1)S(1)} %get-tuple-element.47.refs_2_), channel_id=1, source_target_pairs={{0,2},{1,3},{2,0},{3,1},{4,6},{5,7},{6,4},{7,5},{8,10},{9,11},{10,... | collective-permute-start | bytes 712712 | tf_op jit(solution)/shard_map/ppermute | solution.py:89
  25.2 8.8 %collective-permute-start.7 = (bf16[16,3712]{1,0:T(8,128)(2,1)S(1)}, bf16[16,3712]{1,0:T(8,128)(2,1)S(1)}, u32[]{:S(2)}, u32[]{:S(2)}) collective-permute-start(bf16[16,3712]{1,0:T(8,128)(2,1)S(1)} %get-tuple-element.45), channel_id=1, source_target_pairs={{0,2},{1,3},{2,0},{3,1},{4,6},{5,7},{6,4},{7,5},{8,10},{9,11},{10,... | collective-permute-start | bytes 356360 | tf_op jit(solution)/shard_map/ppermute | solution.py:89
  25.7 8.4 %collective-permute-start.8 = (bf16[16,3712]{1,0:T(8,128)(2,1)S(1)}, bf16[16,3712]{1,0:T(8,128)(2,1)S(1)}, u32[]{:S(2)}, u32[]{:S(2)}) collective-permute-start(bf16[16,3712]{1,0:T(8,128)(2,1)S(1)} %get-tuple-element.46), channel_id=1, source_target_pairs={{0,1},{1,0},{2,3},{3,2},{4,5},{5,4},{6,7},{7,6},{8,9},{9,8},{10,11... | collective-permute-start | bytes 356360 | tf_op jit(solution)/shard_map/ppermute | solution.py:89
  34.2 7.1 %collective-permute-start.11 = (bf16[128,3712]{1,0:T(8,128)(2,1)S(1)}, bf16[128,3712]{1,0:T(8,128)(2,1)S(1)}, u32[]{:S(2)}, u32[]{:S(2)}) collective-permute-start(bf16[128,3712]{1,0:T(8,128)(2,1)S(1)} %get-tuple-element.48.own), channel_id=1, source_target_pairs={{0,4},{4,0},{8,12},{12,8},{16,20},{20,16},{24,28},{28,24},{1,5},{5... | collective-permute-start | bytes 2850824 | tf_op jit(solution)/shard_map/ppermute | solution.py:89
  34.8 5.2 %collective-permute-start.12 = (bf16[16,3712]{1,0:T(8,128)(2,1)S(1)}, bf16[16,3712]{1,0:T(8,128)(2,1)S(1)}, u32[]{:S(2)}, u32[]{:S(2)}) collective-permute-start(bf16[16,3712]{1,0:T(8,128)(2,1)S(1)} %get-tuple-element.51), channel_id=1, source_target_pairs={{0,2},{1,3},{2,0},{3,1},{4,6},{5,7},{6,4},{7,5},{8,10},{9,11},{10,... | collective-permute-start | bytes 356360 | tf_op jit(solution)/shard_map/ppermute | solution.py:89
  36.3 4.9 %collective-permute-start.13 = (bf16[16,3712]{1,0:T(8,128)(2,1)S(1)}, bf16[16,3712]{1,0:T(8,128)(2,1)S(1)}, u32[]{:S(2)}, u32[]{:S(2)}) collective-permute-start(bf16[16,3712]{1,0:T(8,128)(2,1)S(1)} %get-tuple-element.52), channel_id=1, source_target_pairs={{0,1},{1,0},{2,3},{3,2},{4,5},{5,4},{6,7},{7,6},{8,9},{9,8},{10,11... | collective-permute-start | bytes 356360 | tf_op jit(solution)/shard_map/ppermute | solution.py:89
  44.0 8.3 %collective-permute-start.14 = (bf16[128,3584]{1,0:T(8,128)(2,1)S(1)}, bf16[128,3584]{1,0:T(8,128)(2,1)S(1)}, u32[]{:S(2)}, u32[]{:S(2)}) collective-permute-start(bf16[128,3584]{1,0:T(8,128)(2,1)S(1)} %get-tuple-element.54.refs_0_), channel_id=1, source_target_pairs={{0,4},{4,0},{8,12},{12,8},{16,20},{20,16},{24,28},{28,24},{1,5},{5... | collective-permute-start | bytes 2752520 | tf_op jit(solution)/shard_map/ppermute | solution.py:89
  51.2 6.0 %collective-permute-start.17 = (bf16[16,3584]{1,0:T(8,128)(2,1)S(1)}, bf16[16,3584]{1,0:T(8,128)(2,1)S(1)}, u32[]{:S(2)}, u32[]{:S(2)}) collective-permute-start(bf16[16,3584]{1,0:T(8,128)(2,1)S(1)} %get-tuple-element.61), channel_id=1, source_target_pairs={{0,2},{1,3},{2,0},{3,1},{4,6},{5,7},{6,4},{7,5},{8,10},{9,11},{10,... | collective-permute-start | bytes 344072 | tf_op jit(solution)/shard_map/ppermute | solution.py:89
  51.7 5.5 %collective-permute-start.18 = (bf16[16,3584]{1,0:T(8,128)(2,1)S(1)}, bf16[16,3584]{1,0:T(8,128)(2,1)S(1)}, u32[]{:S(2)}, u32[]{:S(2)}) collective-permute-start(bf16[16,3584]{1,0:T(8,128)(2,1)S(1)} %get-tuple-element.62), channel_id=1, source_target_pairs={{0,1},{1,0},{2,3},{3,2},{4,5},{5,4},{6,7},{7,6},{8,9},{9,8},{10,11... | collective-permute-start | bytes 344072 | tf_op jit(solution)/shard_map/ppermute | solution.py:89
  52.9 5.9 %collective-permute-start.19 = (bf16[16,3584]{1,0:T(8,128)(2,1)S(1)}, bf16[16,3584]{1,0:T(8,128)(2,1)S(1)}, u32[]{:S(2)}, u32[]{:S(2)}) collective-permute-start(bf16[16,3584]{1,0:T(8,128)(2,1)S(1)} %get-tuple-element.63), channel_id=1, source_target_pairs={{0,2},{1,3},{2,0},{3,1},{4,6},{5,7},{6,4},{7,5},{8,10},{9,11},{10,... | collective-permute-start | bytes 344072 | tf_op jit(solution)/shard_map/ppermute | solution.py:89
  54.5 4.8 %collective-permute-start.20 = (bf16[16,3584]{1,0:T(8,128)(2,1)S(1)}, bf16[16,3584]{1,0:T(8,128)(2,1)S(1)}, u32[]{:S(2)}, u32[]{:S(2)}) collective-permute-start(bf16[16,3584]{1,0:T(8,128)(2,1)S(1)} %get-tuple-element.64), channel_id=1, source_target_pairs={{0,1},{1,0},{2,3},{3,2},{4,5},{5,4},{6,7},{7,6},{8,9},{9,8},{10,11... | collective-permute-start | bytes 344072 | tf_op jit(solution)/shard_map/ppermute | solution.py:89
  59.4 8.6 %collective-permute-start.23 = (bf16[32,3584]{1,0:T(8,128)(2,1)S(1)}, bf16[32,3584]{1,0:T(8,128)(2,1)S(1)}, u32[]{:S(2)}, u32[]{:S(2)}) collective-permute-start(bf16[32,3584]{1,0:T(8,128)(2,1)S(1)} %get-tuple-element.68), channel_id=1, source_target_pairs={{0,1},{1,0},{2,3},{3,2},{4,5},{5,4},{6,7},{7,6},{8,9},{9,8},{10,11... | collective-permute-start | bytes 688136 | tf_op jit(solution)/shard_map/ppermute | solution.py:89
  60.9 8.1 %collective-permute-start.24 = (bf16[32,3584]{1,0:T(8,128)(2,1)S(1)}, bf16[32,3584]{1,0:T(8,128)(2,1)S(1)}, u32[]{:S(2)}, u32[]{:S(2)}) collective-permute-start(bf16[32,3584]{1,0:T(8,128)(2,1)S(1)} %get-tuple-element.69), channel_id=1, source_target_pairs={{0,2},{1,3},{2,0},{3,1},{4,6},{5,7},{6,4},{7,5},{8,10},{9,11},{10,... | collective-permute-start | bytes 688136 | tf_op jit(solution)/shard_map/ppermute | solution.py:89
  61.4 11.7 %collective-permute-start.21 = (bf16[32,3584]{1,0:T(8,128)(2,1)S(1)}, bf16[32,3584]{1,0:T(8,128)(2,1)S(1)}, u32[]{:S(2)}, u32[]{:S(2)}) collective-permute-start(bf16[32,3584]{1,0:T(8,128)(2,1)S(1)} %get-tuple-element.65), channel_id=1, source_target_pairs={{0,1},{1,0},{2,3},{3,2},{4,5},{5,4},{6,7},{7,6},{8,9},{9,8},{10,11... | collective-permute-start | bytes 688136 | tf_op jit(solution)/shard_map/ppermute | solution.py:89
  62.8 10.4 %collective-permute-start.22 = (bf16[32,3584]{1,0:T(8,128)(2,1)S(1)}, bf16[32,3584]{1,0:T(8,128)(2,1)S(1)}, u32[]{:S(2)}, u32[]{:S(2)}) collective-permute-start(bf16[32,3584]{1,0:T(8,128)(2,1)S(1)} %get-tuple-element.66), channel_id=1, source_target_pairs={{0,2},{1,3},{2,0},{3,1},{4,6},{5,7},{6,4},{7,5},{8,10},{9,11},{10,... | collective-permute-start | bytes 688136 | tf_op jit(solution)/shard_map/ppermute | solution.py:89
  69.1 5.9 %collective-permute-start.25 = (bf16[16,3584]{1,0:T(8,128)(2,1)S(1)}, bf16[16,3584]{1,0:T(8,128)(2,1)S(1)}, u32[]{:S(2)}, u32[]{:S(2)}) collective-permute-start(bf16[16,3584]{1,0:T(8,128)(2,1)S(1)} %get-tuple-element.70.refs_3_), channel_id=1, source_target_pairs={{0,16},{4,20},{8,24},{12,28},{16,0},{20,4},{24,8},{28,12},{1,17},{... | collective-permute-start | bytes 344072 | tf_op jit(solution)/shard_map/ppermute | solution.py:89
  71.8 6.8 %collective-permute-start.26 = (bf16[16,3584]{1,0:T(8,128)(2,1)S(1)}, bf16[16,3584]{1,0:T(8,128)(2,1)S(1)}, u32[]{:S(2)}, u32[]{:S(2)}) collective-permute-start(bf16[16,3584]{1,0:T(8,128)(2,1)S(1)} %get-tuple-element.72), channel_id=1, source_target_pairs={{0,24},{4,28},{8,16},{12,20},{16,8},{20,12},{24,0},{28,4},{1,25},{... | collective-permute-start | bytes 344072 | tf_op jit(solution)/shard_map/ppermute | solution.py:541
  73.2 6.1 %collective-permute-start.27 = (bf16[16,3584]{1,0:T(8,128)(2,1)S(1)}, bf16[16,3584]{1,0:T(8,128)(2,1)S(1)}, u32[]{:S(2)}, u32[]{:S(2)}) collective-permute-start(bf16[16,3584]{1,0:T(8,128)(2,1)S(1)} %get-tuple-element.73), channel_id=1, source_target_pairs={{0,8},{4,12},{8,0},{12,4},{16,24},{20,28},{24,16},{28,20},{1,9},{5... | collective-permute-start | bytes 344072 | tf_op jit(solution)/shard_map/ppermute | solution.py:89
  (10 other events, 17.2 us)

commit v7 on v6

--- a/solution.py
+++ b/solution.py
@@ -23,52 +23,43 @@
 neg_large = -1e30
 
 
-def attend_kernel(lengths, live_rows, queries, channels, out):
-    request = pl.program_id(0)
-    scores = jnp.dot(queries[0], channels[0], preferred_element_type=jnp.float32) * score_scale
-    positions = lax.broadcasted_iota(jnp.int32, scores.shape, 1)
-    inside = positions < lengths[request]
-    masked = jnp.where(inside, scores, neg_large)
-    highest = jnp.max(masked, axis=1, keepdims=True)
-    powers = jnp.where(inside, jnp.exp(masked - highest), 0.0)
-    totals = jnp.sum(powers, axis=1, keepdims=True)
-    weights = (powers / totals).astype(jnp.bfloat16)
-    context = lax.dot_general(
-        weights,
-        channels[0, :LAT, :],
-        (((1,), (1,)), ((), ())),
-        preferred_element_type=jnp.float32,
-    )
-    out[0] = jnp.where(request < live_rows[0], context, 0.0).astype(jnp.bfloat16)
+def attend_kernel(lengths, live_rows, queries, channels, *refs):
+    out, done = refs[-2:]
+    count, heads, _ = queries.shape
+    positions = lax.broadcasted_iota(jnp.int32, (heads, channels.shape[2]), 1)
+    for request in range(count):
+        scores = jnp.dot(
+            queries[request], channels[request], preferred_element_type=jnp.float32
+        )
+        inside = positions < lengths[request]
+        masked = jnp.where(inside, scores * score_scale, neg_large)
+        highest = jnp.max(masked, axis=1, keepdims=True)
+        powers = jnp.where(inside, jnp.exp(masked - highest), 0.0)
+        totals = jnp.sum(powers, axis=1, keepdims=True)
+        weights = (powers / totals).astype(jnp.bfloat16)
+        context = lax.dot_general(
+            weights,
+            channels[request, :LAT, :],
+            (((1,), (1,)), ((), ())),
+            preferred_element_type=jnp.float32,
+        )
+        out[request] = jnp.where(request < live_rows[0], context, 0.0).astype(jnp.bfloat16)
+    done[...] = jnp.zeros_like(done)
 
 
 def attend(queries, cache, lengths, live_rows, after=()):
     count, heads, width = queries.shape
     positions = cache.shape[1]
-    scalars = pl.BlockSpec(memory_space=pltpu.SMEM)
-
-    def kernel(*refs):
-        attend_kernel(*refs[:4], refs[-2])
-        refs[-1][...] = jnp.zeros_like(refs[-1])
-
-    return pl.pallas_call(
-        kernel,
-        grid=(count,),
+    return pl.pallas_call(
+        attend_kernel,
         out_shape=[
             jax.ShapeDtypeStruct((count, heads, LAT), jnp.bfloat16),
             jax.ShapeDtypeStruct((8, 128), jnp.float32),
         ],
-        in_specs=[
-            scalars,
-            scalars,
-            pl.BlockSpec((1, heads, width), lambda r: (r, 0, 0)),
-            pl.BlockSpec((1, width, positions), lambda r: (r, 0, 0)),
-        ]
+        in_specs=[pl.BlockSpec(memory_space=pltpu.SMEM)] * 2
+        + [whole] * 2
         + [pl.BlockSpec(memory_space=pl.ANY)] * len(after),
-        out_specs=[
-            pl.BlockSpec((1, heads, LAT), lambda r: (r, 0, 0)),
-            pl.BlockSpec((8, 128), lambda r: (0, 0)),
-        ],
+        out_specs=[whole] * 2,
         compiler_params=pltpu.CompilerParams(vmem_limit_bytes=SMALL_BYTES),
         cost_estimate=pl.CostEstimate(
             flops=4 * count * heads * width * positions,
@@ -87,6 +78,12 @@
     axis, bit = step
     size = lax.axis_size(axis)
     return lax.ppermute(value, axis, [(i, i ^ bit) for i in range(size)])
+
+
+def across(value, first, second):
+    axis = first[0]
+    size = lax.axis_size(axis)
+    return lax.ppermute(value, axis, [(i, i ^ first[1] ^ second[1]) for i in range(size)])
 
 
 def spread(value, steps):
@@ -119,31 +116,47 @@
     return total.astype(jnp.bfloat16)
 
 
-def pack_kernel(tokens, ids, gates, out):
+def pack_kernel(tokens, ids, gates, out, ids_here, gates_here, extra, sems):
     feature = tokens.shape[1]
-    high = gates[...].astype(jnp.bfloat16)
-    low = (gates[...] - high.astype(jnp.float32)).astype(jnp.bfloat16)
-    named = ids[...].astype(jnp.float32).astype(jnp.bfloat16)
-    stacked = jnp.concatenate(
-        [named.astype(jnp.float32), high.astype(jnp.float32), low.astype(jnp.float32)], axis=0
-    ).astype(jnp.bfloat16)
+    copies = [
+        pltpu.make_async_copy(ids, ids_here, sems.at[0]),
+        pltpu.make_async_copy(gates, gates_here, sems.at[1]),
+        pltpu.make_async_copy(tokens, out.at[:, pl.ds(0, feature)], sems.at[2]),
+    ]
+    for copy in copies:
+        copy.start()
+    copies[0].wait()
+    copies[1].wait()
+    high = gates_here[...].astype(jnp.bfloat16).astype(jnp.float32)
+    low = gates_here[...] - high
+    stacked = jnp.concatenate([ids_here[...].astype(jnp.float32), high, low], axis=0)
+    stacked = stacked.astype(jnp.bfloat16)
     row = lax.broadcasted_iota(jnp.int32, (stacked.shape[0], EXTRA), 0)
     column = lax.broadcasted_iota(jnp.int32, (stacked.shape[0], EXTRA), 1)
     place = jnp.where(row == column, 1.0, 0.0).astype(jnp.bfloat16)
-    extra = lax.dot_general(
+    extra[...] = lax.dot_general(
         stacked, place, (((0,), (0,)), ((), ())), preferred_element_type=jnp.float32
-    )
-    out[:, :feature] = tokens[...]
-    out[:, feature:] = extra.astype(jnp.bfloat16)
+    ).astype(jnp.bfloat16)
+    last = pltpu.make_async_copy(extra, out.at[:, pl.ds(feature, EXTRA)], sems.at[3])
+    last.start()
+    copies[2].wait()
+    last.wait()
 
 
 def pack(tokens, ids, gates):
+    rows, feature = tokens.shape
+    picks = ids.shape[1]
     return pl.pallas_call(
         pack_kernel,
-        out_shape=jax.ShapeDtypeStruct((tokens.shape[0], tokens.shape[1] + EXTRA), jnp.bfloat16),
-        in_specs=[pl.BlockSpec(memory_space=pltpu.VMEM)] * 3,
-        out_specs=pl.BlockSpec(memory_space=pltpu.VMEM),
-        compiler_params=pltpu.CompilerParams(vmem_limit_bytes=SMALL_BYTES),
+        out_shape=jax.ShapeDtypeStruct((rows, feature + EXTRA), jnp.bfloat16),
+        in_specs=[pl.BlockSpec(memory_space=pl.ANY)] * 3,
+        out_specs=pl.BlockSpec(memory_space=pl.ANY),
+        scratch_shapes=[
+            pltpu.VMEM((picks, rows), jnp.int32),
+            pltpu.VMEM((picks, rows), jnp.float32),
+            pltpu.VMEM((rows, EXTRA), jnp.bfloat16),
+            pltpu.SemaphoreType.DMA((4,)),
+        ],
         name="pack",
     )(tokens, ids.T, gates.T)
 
@@ -478,68 +491,58 @@
     (near,) = combine([packed, from_near], [rows_of((0, 0, n), (1, 0, n))])
     near_x, near_y = swap(near, x), swap(near, y)
     from_both = swap(from_far, z_near)
-    context, done = attention([near])
     first_own, far, half_x, half_y = combine(
         [near, near_x, near_y, from_far, from_both],
         [
-            rows_of((0, 0, 2 * n), (1, 0, 2 * n), (2, 0, 2 * n)),
+            rows_of((0, 0, 2 * n), (1, 0, 2 * n), (2, 0, 2 * n), (3, 0, n), (4, 0, n)),
             rows_of((3, 0, n), (4, 0, n)),
             rows_of((1, 0, n)),
             rows_of((2, n, n)),
         ],
+    )
+    far_x, far_y, far_xy = swap(far, x), swap(far, y), across(far, x, y)
+    near_xy_top, near_xy_low = swap(half_x, y), swap(half_y, x)
+    first_other = swap(first_own, core)
+    first_h, first_out, *weights = first_of(first_own, first_other, *weights, picks)
+    w_down = weights[2]
+    (second_own,) = combine(
+        [far_x, far_y, far_xy, near_xy_top, near_xy_low],
+        [
+            rows_of(
+                (0, 0, 2 * n), (1, 0, 2 * n), (2, 0, 2 * n), (3, 0, n), (4, 0, n)
+            )
+        ],
+        [first_out],
+    )
+    second_other = swap(second_own, core)
+    first_in = swap(first_out, core)
+    near, near_x, near_y, far = sums_of(first_h, w_down, [2 * n] * 4, first_in)
+    second_h, second_out = expert_of(second_own, second_other, *weights, picks, [near])
+    second_in = swap(second_out, core)
+    far_x, far_y, far_xy, near_xy_top, near_xy_low = sums_of(
+        second_h, w_down, [2 * n] * 3 + [n] * 2, second_in
+    )
+
+    to_far = [swap(far_x, x), swap(far_y, y), across(far_xy, x, y)]
+    to_near_x, to_near_y = swap(near_xy_top, y), swap(near_xy_low, x)
+    context, done = attention([far_x])
+    near_x, near_y = combine(
+        [near_x, near_y, to_near_x, to_near_y],
+        [
+            [(n, [(0, 0), (2, 0)]), (n, [(0, n)])],
+            [(n, [(1, 0)]), (n, [(1, n), (3, 0)])],
+        ],
         [done],
     )
-    first_other = swap(first_own, core)
-    far_x, far_y = swap(far, x), swap(far, y)
-    near_xy_top, near_xy_low = swap(half_x, y), swap(half_y, x)
-    first_h, first_out, *weights = first_of(first_own, first_other, *weights, picks)
-    w_down = weights[2]
-    second_own, half_x, half_y = combine(
-        [near_xy_top, near_xy_low, far, far_x, far_y],
-        [
-            rows_of((0, 0, n), (1, 0, n), (2, 0, 2 * n), (3, 0, 2 * n), (4, 0, 2 * n)),
-            rows_of((3, 0, n)),
-            rows_of((4, n, n)),
-        ],
-        [first_out],
-    )
-    far_xy_top, far_xy_low = swap(half_x, y), swap(half_y, x)
-    second_other = swap(second_own, core)
-    first_in = swap(first_out, core)
-    near, near_x, near_y = sums_of(first_h, w_down, [2 * n] * 3, first_in)
-    (third_own,) = combine([far_xy_top, far_xy_low], [rows_of((0, 0, n), (1, 0, n))], [near])
-    third_other = swap(third_own, core)
-    second_h, second_out = expert_of(
-        second_own, second_other, *weights, picks, [third_own]
-    )
-    second_in = swap(second_out, core)
-    third_h, third_out = expert_of(third_own, third_other, *weights, picks, [second_out])
-    near_xy_top, near_xy_low, far, far_x, far_y = sums_of(
-        second_h, w_down, [n, n, 2 * n, 2 * n, 2 * n], second_in, [third_out]
-    )
-    third_in = swap(third_out, core)
-    far_xy_top, far_xy_low = sums_of(third_h, w_down, [n, n], third_in)
-
-    to_near_x, to_near_y = swap(near_xy_top, y), swap(near_xy_low, x)
-    to_far_x, to_far_y = swap(far_xy_top, y), swap(far_xy_low, x)
-    far_x, far_y, near_x, near_y = combine(
-        [far_x, far_y, near_x, near_y, to_far_x, to_far_y, to_near_x, to_near_y],
-        [
-            [(n, [(0, 0), (4, 0)]), (n, [(0, n)])],
-            [(n, [(1, 0)]), (n, [(1, n), (5, 0)])],
-            [(n, [(2, 0), (6, 0)]), (n, [(2, n)])],
-            [(n, [(3, 0)]), (n, [(3, n), (7, 0)])],
-        ],
-    )
-    to_far = [swap(far_x, x), swap(far_y, y)]
     to_near = [swap(near_x, x), swap(near_y, y)]
-    both = lambda start: [(n, [(0, start), (1, start), (2, start)])]
-    far_sum, both_sum = combine([far, *to_far], [both(0), both(n)])
-    own_sum, near_sum = combine([near, *to_near], [both(0), both(n)], [far_sum])
-    size = lax.axis_size(z_far[0])
-    direct = [(i, i ^ z_far[1] ^ z_near[1]) for i in range(size)]
-    terms = [swap(far_sum, z_far), lax.ppermute(both_sum, z_far[0], direct), swap(near_sum, z_near)]
-    (mixed,) = combine([own_sum, *terms], [[(n, [(0, 0), (1, 0), (2, 0), (3, 0)])]])
+
+    def all_of(terms, start):
+        return [(n, [(index, start) for index in range(terms)])]
+
+    far_sum, both_sum = combine([far, *to_far], [all_of(4, 0), all_of(4, n)], [near_x])
+    own_sum, near_sum = combine([near, *to_near], [all_of(3, 0), all_of(3, n)], [far_sum])
+    terms = [swap(far_sum, z_far), across(both_sum, z_far, z_near), swap(near_sum, z_near)]
+    (mixed,) = combine([own_sum, *terms], [all_of(4, 0)])
     return mixed, context
 
 

time: 80.3 us -> 78.2 us (0.974)
  local copies, waits for them, and re-layouts: 5.16 us -> 0.92 us
  waiting for transfers between devices: 25.8 us -> 28 us
  Pallas kernels: 18.2 us -> 19.8 us
  starting transfers between devices: 29.4 us -> 27.8 us
    ppermute x27 -> x21, starting transfers between devices: 28.1 us -> 23.5 us  [swap(): return lax.ppermute(value, axis, [(i, i ^ bit) for i in range(size)])]
    unnamed x12 -> x8, local copies, waits for them, and re-layouts: 5.16 us -> 0.92 us
    pallas_call x2, Pallas kernels: 3.84 us -> 7.31 us  [the longest x1 4.62 us: pack(): pl.pallas_call(pack_kernel, out_shape=jax.ShapeDtypeStruct((rows, feature...]
    ppermute x1 -> x3, starting transfers between devices: 1.32 us -> 4.26 us  [across(): lax.ppermute(value, axis, [(i, i ^ first[1] ^ second[1]) for i in range(s...]
    pallas_call x2 -> x1, Pallas kernels: 4.72 us -> 2.7 us  [expert_of(): pl.pallas_call(functools.partial(expert_kernel, picks), out_shape=[jax.Sh...]
    ppermute x1 -> x3, waiting for transfers between devices: 3.55 us -> 4.69 us  [across(): lax.ppermute(value, axis, [(i, i ^ first[1] ^ second[1]) for i in range(s...]
    ppermute x27 -> x21, waiting for transfers between devices: 22.3 us -> 23.3 us  [swap(): return lax.ppermute(value, axis, [(i, i ^ bit) for i in range(size)])]
    pallas_call x1, Pallas kernels: 6.38 us -> 7.4 us  [first_of(): pl.pallas_call(functools.partial(first_kernel, picks), out_shape=[jax.Sha...]
  transfers between devices with their start and end apart: 28 -> 24, of which waited for: 16 -> 11; matrix products, arithmetic and copies ran while one was open for 0% -> 0% of each run, Pallas kernels for 18% -> 14%
where the time goes in v7:
time: 78.2 us; the launch traced here: 78 us
  waiting for transfers between devices  28 us (36%)
  starting transfers between devices  27.8 us (36%)
  Pallas kernels  19.8 us (25%)
  between operations  1.42 us (2%)
  local copies, waits for them, and re-layouts  0.92 us (1%)
    ppermute x21, starting transfers between devices, swap(): return lax.ppermute(value, axis, [(i, i ^ bit) for i in range(size)])  23.5 us
    ppermute x21, waiting for transfers between devices, swap(): return lax.ppermute(value, axis, [(i, i ^ bit) for i in range(size)])  23.3 us
    pallas_call x1, Pallas kernels, first_of(): pl.pallas_call(functools.partial(first_kernel, picks), out_shape=[jax.Sha...  7.4 us
    ppermute x3, waiting for transfers between devices, across(): lax.ppermute(value, axis, [(i, i ^ first[1] ^ second[1]) for i in range(s...  4.69 us
    pallas_call x1, Pallas kernels, pack(): pl.pallas_call(pack_kernel, out_shape=jax.ShapeDtypeStruct((rows, feature...  4.62 us
    ppermute x3, starting transfers between devices, across(): lax.ppermute(value, axis, [(i, i ^ first[1] ^ second[1]) for i in range(s...  4.26 us
    pallas_call x1, Pallas kernels, attend(): pl.pallas_call(attend_kernel, out_shape=[jax.ShapeDtypeStruct((count, hea...  2.7 us
    pallas_call x1, Pallas kernels, expert_of(): pl.pallas_call(functools.partial(expert_kernel, picks), out_shape=[jax.Sh...  2.7 us
  transfers between devices with their start and end apart: 24, of which 11 were waited for; matrix products, arithmetic and copies ran while one was open for 0% of the time, Pallas kernels for 14%

profile of v7, /device:TPU:0, one launch (start us, length us, event | category | flops | bytes accessed | tf_op | source)
XLA Modules:
  0.0 78.0 jit_solution(17768015626518997271)
XLA Ops:
  0.6 4.6 %pack.1.refs_0_ = bf16[16,3712]{1,0:T(8,128)(2,1)} custom-call(bf16[16,3584]{1,0:T(8,128)(2,1)} %tokens.1, s32[8,16]{1,0:T(8,128)} %bitcast.4, f32[8,16]{1,0:T(8,128)} %bitcast.5), custom_call_target="tpu_custom_call" | custom-call | tf_op jit(solution)/shard_map/pack/pallas_call | solution.py:149
  5.3 3.1 %collective-permute-start = (bf16[16,3712]{1,0:T(8,128)(2,1)}, bf16[16,3712]{1,0:T(8,128)(2,1)S(1)}, u32[]{:S(2)}, u32[]{:S(2)}) collective-permute-start(bf16[16,3712]{1,0:T(8,128)(2,1)} %pack.1.refs_0_), channel_id=1, source_target_pairs={{0,8},{4,12},{8,0},{12,4},{16,24},{20,28},{24,16},{28,20},{1,9},{5... | collective-permute-start | bytes 356360 | tf_op jit(solution)/shard_map/ppermute | solution.py:80
  8.3 2.6 %collective-permute-start.3 = (bf16[16,3712]{1,0:T(8,128)(2,1)}, bf16[16,3712]{1,0:T(8,128)(2,1)S(1)}, u32[]{:S(2)}, u32[]{:S(2)}) collective-permute-start(bf16[16,3712]{1,0:T(8,128)(2,1)} %pack.1.refs_0_), channel_id=1, source_target_pairs={{0,16},{4,20},{8,24},{12,28},{16,0},{20,4},{24,8},{28,12},{1,17},{... | collective-permute-start | bytes 356360 | tf_op jit(solution)/shard_map/ppermute | solution.py:80
  10.9 2.1 %collective-permute-done.refs_1_ = bf16[16,3712]{1,0:T(8,128)(2,1)S(1)} collective-permute-done((bf16[16,3712]{1,0:T(8,128)(2,1)}, bf16[16,3712]{1,0:T(8,128)(2,1)S(1)}, u32[]{:S(2)}, u32[]{:S(2)}) %collective-permute-start) | collective-permute-done | bytes 118816 | tf_op jit(solution)/shard_map/ppermute | solution.py:80
  14.0 1.9 %collective-permute-start.1 = (bf16[32,3712]{1,0:T(8,128)(2,1)S(1)}, bf16[32,3712]{1,0:T(8,128)(2,1)S(1)}, u32[]{:S(2)}, u32[]{:S(2)}) collective-permute-start(bf16[32,3712]{1,0:T(8,128)(2,1)S(1)} %combine.7.refs_0_), channel_id=1, source_target_pairs={{0,1},{1,0},{2,3},{3,2},{4,5},{5,4},{6,7},{7,6},{8,9},{9,8},{10,11... | collective-permute-start | bytes 712712 | tf_op jit(solution)/shard_map/ppermute | solution.py:80
  15.9 1.5 %collective-permute-start.2 = (bf16[32,3712]{1,0:T(8,128)(2,1)S(1)}, bf16[32,3712]{1,0:T(8,128)(2,1)S(1)}, u32[]{:S(2)}, u32[]{:S(2)}) collective-permute-start(bf16[32,3712]{1,0:T(8,128)(2,1)S(1)} %combine.7.refs_0_), channel_id=1, source_target_pairs={{0,2},{1,3},{2,0},{3,1},{4,6},{5,7},{6,4},{7,5},{8,10},{9,11},{10,... | collective-permute-start | bytes 712712 | tf_op jit(solution)/shard_map/ppermute | solution.py:80
  17.7 4.5 %collective-permute-done.4.refs_4_ = bf16[16,3712]{1,0:T(8,128)(2,1)S(1)} collective-permute-done((bf16[16,3712]{1,0:T(8,128)(2,1)S(1)}, bf16[16,3712]{1,0:T(8,128)(2,1)S(1)}, u32[]{:S(2)}, u32[]{:S(2)}) %collective-permute-start.4) | collective-permute-done | bytes 118816 | tf_op jit(solution)/shard_map/ppermute | solution.py:80
  23.3 1.5 %collective-permute-start.6 = (bf16[32,3712]{1,0:T(8,128)(2,1)S(1)}, bf16[32,3712]{1,0:T(8,128)(2,1)S(1)}, u32[]{:S(2)}, u32[]{:S(2)}) collective-permute-start(bf16[32,3712]{1,0:T(8,128)(2,1)S(1)} %get-tuple-element.30), channel_id=1, source_target_pairs={{0,2},{1,3},{2,0},{3,1},{4,6},{5,7},{6,4},{7,5},{8,10},{9,11},{10,... | collective-permute-start | bytes 712712 | tf_op jit(solution)/shard_map/ppermute | solution.py:80
  26.0 1.3 %collective-permute-start.8 = (bf16[16,3712]{1,0:T(8,128)(2,1)S(1)}, bf16[16,3712]{1,0:T(8,128)(2,1)S(1)}, u32[]{:S(2)}, u32[]{:S(2)}) collective-permute-start(bf16[16,3712]{1,0:T(8,128)(2,1)S(1)} %get-tuple-element.31), channel_id=1, source_target_pairs={{0,2},{1,3},{2,0},{3,1},{4,6},{5,7},{6,4},{7,5},{8,10},{9,11},{10,... | collective-permute-start | bytes 356360 | tf_op jit(solution)/shard_map/ppermute | solution.py:80
  28.4 7.4 %first.1 = (bf16[128,512]{1,0:T(8,128)(2,1)S(1)}, bf16[128,3584]{1,0:T(8,128)(2,1)S(1)}, bf16[1,3584,512]{2,1,0:T(8,128)(2,1)S(1)}, bf16[1,3584,512]{2,1,0:T(8,128)(2,1)S(1)}, bf16[1,512,3584]{2,1,0:T(8,128)(2,1)S(1)}) custom-call(bf16[128,3712]{1,0:T(8,128)(2,1)S(1)} %get-tuple-element.33.own, bf16[128,3712]{1,0:T(8,128)(2,1)S(1)} %collective-permute-done.10.other, ...), custom_call_target="tpu_custom_call" | custom-call | flops 2348810240 | bytes 11010048 | tf_op jit(solution)/shard_map/first/pallas_call | solution.py:371
  35.8 3.1 %collective-permute-done.8.refs_3_ = bf16[16,3712]{1,0:T(8,128)(2,1)S(1)} collective-permute-done((bf16[16,3712]{1,0:T(8,128)(2,1)S(1)}, bf16[16,3712]{1,0:T(8,128)(2,1)S(1)}, u32[]{:S(2)}, u32[]{:S(2)}) %collective-permute-start.8) | collective-permute-done | bytes 118816 | tf_op jit(solution)/shard_map/ppermute | solution.py:80
  39.5 1.8 %collective-permute-done.12.arrived = bf16[128,3584]{1,0:T(8,128)(2,1)S(1)} collective-permute-done((bf16[128,3584]{1,0:T(8,128)(2,1)S(1)}, bf16[128,3584]{1,0:T(8,128)(2,1)S(1)}, u32[]{:S(2)}, u32[]{:S(2)}) %collective-permute-start.12) | collective-permute-done | bytes 917536 | tf_op jit(solution)/shard_map/ppermute | solution.py:80
  42.7 2.7 %expert.1 = (bf16[128,512]{1,0:T(8,128)(2,1)S(1)}, bf16[128,3584]{1,0:T(8,128)(2,1)S(1)}) custom-call(bf16[128,3712]{1,0:T(8,128)(2,1)S(1)} %combine.9.own, bf16[128,3712]{1,0:T(8,128)(2,1)S(1)} %collective-permute-done.11.other, bf16[1,3584,512]{2,1,0:T(8,128)(2,1)S(1)} %get-tuple-element.35.w_gate, bf16[1,3584,512]{2,1,0:T(8,128)(2,1)S(1)} %get-tuple-element.36.w_up, ...), custom_call_target="tpu_custom_call" | custom-call | flops 2348810240 | bytes 917504 | tf_op jit(solution)/shard_map/expert/pallas_call | solution.py:398
  45.6 2.3 %collective-permute-done.13.arrived = bf16[128,3584]{1,0:T(8,128)(2,1)S(1)} collective-permute-done((bf16[128,3584]{1,0:T(8,128)(2,1)S(1)}, bf16[128,3584]{1,0:T(8,128)(2,1)S(1)}, u32[]{:S(2)}, u32[]{:S(2)}) %collective-permute-start.13) | collective-permute-done | bytes 917536 | tf_op jit(solution)/shard_map/ppermute | solution.py:80
  48.6 1.6 %collective-permute-start.14 = (bf16[16,3584]{1,0:T(8,128)(2,1)S(1)}, bf16[16,3584]{1,0:T(8,128)(2,1)S(1)}, u32[]{:S(2)}, u32[]{:S(2)}) collective-permute-start(bf16[16,3584]{1,0:T(8,128)(2,1)S(1)} %get-tuple-element.46), channel_id=1, source_target_pairs={{0,2},{1,3},{2,0},{3,1},{4,6},{5,7},{6,4},{7,5},{8,10},{9,11},{10,... | collective-permute-start | bytes 344072 | tf_op jit(solution)/shard_map/ppermute | solution.py:80
  51.7 1.2 %collective-permute-start.18 = (bf16[32,3584]{1,0:T(8,128)(2,1)S(1)}, bf16[32,3584]{1,0:T(8,128)(2,1)S(1)}, u32[]{:S(2)}, u32[]{:S(2)}) collective-permute-start(bf16[32,3584]{1,0:T(8,128)(2,1)S(1)} %get-tuple-element.42.refs_0_), channel_id=1, source_target_pairs={{0,1},{1,0},{2,3},{3,2},{4,5},{5,4},{6,7},{7,6},{8,9},{9,8},{10,11... | collective-permute-start | bytes 688136 | tf_op jit(solution)/shard_map/ppermute | solution.py:80
  53.4 1.9 %collective-permute-start.20 = (bf16[32,3584]{1,0:T(8,128)(2,1)S(1)}, bf16[32,3584]{1,0:T(8,128)(2,1)S(1)}, u32[]{:S(2)}, u32[]{:S(2)}) collective-permute-start(bf16[32,3584]{1,0:T(8,128)(2,1)S(1)} %get-tuple-element.53), channel_id=1, source_target_pairs={{0,3},{1,2},{2,1},{3,0},{4,7},{5,6},{6,5},{7,4},{8,11},{9,10},{10,... | collective-permute-start | bytes 688136 | tf_op jit(solution)/shard_map/ppermute | solution.py:86
  55.3 2.7 %attend.1 = (bf16[4,64,512]{2,1,0:T(8,128)(2,1)}, f32[8,128]{1,0:T(8,128)S(1)}) custom-call(s32[4]{0:T(128)S(1)} %copy-done.3, s32[1]{0:T(128)S(6)} %copy.12.live_rows, bf16[4,64,576]{2,1,0:T(8,128)(2,1)S(1)} %copy-done.2, bf16[4,576,256]{2,1,0:T(8,128)(2,1)S(1)} %bitcast.3, bf16[32,3584]{1,0:T(8,128)(2,1)S(1)} %get-tuple-element.42.refs_0_), custom_call_target="tpu_custom_call" | custom-call | flops 150994944 | bytes 1179648 | tf_op jit(solution)/shard_map/attend/pallas_call | solution.py:53
  58.1 1.2 %collective-permute-start.16 = (bf16[32,3584]{1,0:T(8,128)(2,1)S(1)}, bf16[32,3584]{1,0:T(8,128)(2,1)S(1)}, u32[]{:S(2)}, u32[]{:S(2)}) collective-permute-start(bf16[32,3584]{1,0:T(8,128)(2,1)S(1)} %get-tuple-element.49.refs_4_), channel_id=1, source_target_pairs={{0,1},{1,0},{2,3},{3,2},{4,5},{5,4},{6,7},{7,6},{8,9},{9,8},{10,11... | collective-permute-start | bytes 688136 | tf_op jit(solution)/shard_map/ppermute | solution.py:80
  59.8 1.3 %collective-permute-done.18.refs_1_ = bf16[32,3584]{1,0:T(8,128)(2,1)S(1)} collective-permute-done((bf16[32,3584]{1,0:T(8,128)(2,1)S(1)}, bf16[32,3584]{1,0:T(8,128)(2,1)S(1)}, u32[]{:S(2)}, u32[]{:S(2)}) %collective-permute-start.18) | collective-permute-done | bytes 229408 | tf_op jit(solution)/shard_map/ppermute | solution.py:80
  61.1 4.7 %collective-permute-done.20.refs_3_ = bf16[32,3584]{1,0:T(8,128)(2,1)S(1)} collective-permute-done((bf16[32,3584]{1,0:T(8,128)(2,1)S(1)}, bf16[32,3584]{1,0:T(8,128)(2,1)S(1)}, u32[]{:S(2)}, u32[]{:S(2)}) %collective-permute-start.20) | collective-permute-done | bytes 229408 | tf_op jit(solution)/shard_map/ppermute | solution.py:86
  65.9 2.1 %collective-permute-start.21 = (bf16[16,3584]{1,0:T(8,128)(2,1)S(1)}, bf16[16,3584]{1,0:T(8,128)(2,1)S(1)}, u32[]{:S(2)}, u32[]{:S(2)}) collective-permute-start(bf16[16,3584]{1,0:T(8,128)(2,1)S(1)} %get-tuple-element.54.refs_3_), channel_id=1, source_target_pairs={{0,16},{4,20},{8,24},{12,28},{16,0},{20,4},{24,8},{28,12},{1,17},{... | collective-permute-start | bytes 344072 | tf_op jit(solution)/shard_map/ppermute | solution.py:80
  68.0 1.3 %collective-permute-start.22 = (bf16[16,3584]{1,0:T(8,128)(2,1)S(1)}, bf16[16,3584]{1,0:T(8,128)(2,1)S(1)}, u32[]{:S(2)}, u32[]{:S(2)}) collective-permute-start(bf16[16,3584]{1,0:T(8,128)(2,1)S(1)} %get-tuple-element.56), channel_id=1, source_target_pairs={{0,24},{4,28},{8,16},{12,20},{16,8},{20,12},{24,0},{28,4},{1,25},{... | collective-permute-start | bytes 344072 | tf_op jit(solution)/shard_map/ppermute | solution.py:86
  70.5 6.0 %collective-permute-done.21.refs_1_ = bf16[16,3584]{1,0:T(8,128)(2,1)S(1)} collective-permute-done((bf16[16,3584]{1,0:T(8,128)(2,1)S(1)}, bf16[16,3584]{1,0:T(8,128)(2,1)S(1)}, u32[]{:S(2)}, u32[]{:S(2)}) %collective-permute-start.21) | collective-permute-done | bytes 114720 | tf_op jit(solution)/shard_map/ppermute | solution.py:80
  (45 shorter events, 12.3 us)
Async XLA Ops:
  5.3 7.8 %collective-permute-start = (bf16[16,3712]{1,0:T(8,128)(2,1)}, bf16[16,3712]{1,0:T(8,128)(2,1)S(1)}, u32[]{:S(2)}, u32[]{:S(2)}) collective-permute-start(bf16[16,3712]{1,0:T(8,128)(2,1)} %pack.1.refs_0_), channel_id=1, source_target_pairs={{0,8},{4,12},{8,0},{12,4},{16,24},{20,28},{24,16},{28,20},{1,9},{5... | collective-permute-start | bytes 356360 | tf_op jit(solution)/shard_map/ppermute | solution.py:80
  8.3 9.1 %collective-permute-start.3 = (bf16[16,3712]{1,0:T(8,128)(2,1)}, bf16[16,3712]{1,0:T(8,128)(2,1)S(1)}, u32[]{:S(2)}, u32[]{:S(2)}) collective-permute-start(bf16[16,3712]{1,0:T(8,128)(2,1)} %pack.1.refs_0_), channel_id=1, source_target_pairs={{0,16},{4,20},{8,24},{12,28},{16,0},{20,4},{24,8},{28,12},{1,17},{... | collective-permute-start | bytes 356360 | tf_op jit(solution)/shard_map/ppermute | solution.py:80
  14.0 8.2 %collective-permute-start.1 = (bf16[32,3712]{1,0:T(8,128)(2,1)S(1)}, bf16[32,3712]{1,0:T(8,128)(2,1)S(1)}, u32[]{:S(2)}, u32[]{:S(2)}) collective-permute-start(bf16[32,3712]{1,0:T(8,128)(2,1)S(1)} %combine.7.refs_0_), channel_id=1, source_target_pairs={{0,1},{1,0},{2,3},{3,2},{4,5},{5,4},{6,7},{7,6},{8,9},{9,8},{10,11... | collective-permute-start | bytes 712712 | tf_op jit(solution)/shard_map/ppermute | solution.py:80
  15.9 6.4 %collective-permute-start.2 = (bf16[32,3712]{1,0:T(8,128)(2,1)S(1)}, bf16[32,3712]{1,0:T(8,128)(2,1)S(1)}, u32[]{:S(2)}, u32[]{:S(2)}) collective-permute-start(bf16[32,3712]{1,0:T(8,128)(2,1)S(1)} %combine.7.refs_0_), channel_id=1, source_target_pairs={{0,2},{1,3},{2,0},{3,1},{4,6},{5,7},{6,4},{7,5},{8,10},{9,11},{10,... | collective-permute-start | bytes 712712 | tf_op jit(solution)/shard_map/ppermute | solution.py:80
  17.4 4.8 %collective-permute-start.4 = (bf16[16,3712]{1,0:T(8,128)(2,1)S(1)}, bf16[16,3712]{1,0:T(8,128)(2,1)S(1)}, u32[]{:S(2)}, u32[]{:S(2)}) collective-permute-start(bf16[16,3712]{1,0:T(8,128)(2,1)S(1)} %collective-permute-done.3.refs_3_), channel_id=1, source_target_pairs={{0,8},{4,12},{8,0},{12,4},{16,24},{20,28},{24,16},{28,20},{1,9},{5... | collective-permute-start | bytes 356360 | tf_op jit(solution)/shard_map/ppermute | solution.py:80
  22.3 4.9 %collective-permute-start.10 = (bf16[128,3712]{1,0:T(8,128)(2,1)S(1)}, bf16[128,3712]{1,0:T(8,128)(2,1)S(1)}, u32[]{:S(2)}, u32[]{:S(2)}) collective-permute-start(bf16[128,3712]{1,0:T(8,128)(2,1)S(1)} %get-tuple-element.33.own), channel_id=1, source_target_pairs={{0,4},{4,0},{8,12},{12,8},{16,20},{20,16},{24,28},{28,24},{1,5},{5... | collective-permute-start | bytes 2850824 | tf_op jit(solution)/shard_map/ppermute | solution.py:80
  22.4 16.4 %collective-permute-start.5 = (bf16[32,3712]{1,0:T(8,128)(2,1)S(1)}, bf16[32,3712]{1,0:T(8,128)(2,1)S(1)}, u32[]{:S(2)}, u32[]{:S(2)}) collective-permute-start(bf16[32,3712]{1,0:T(8,128)(2,1)S(1)} %get-tuple-element.30), channel_id=1, source_target_pairs={{0,1},{1,0},{2,3},{3,2},{4,5},{5,4},{6,7},{7,6},{8,9},{9,8},{10,11... | collective-permute-start | bytes 712712 | tf_op jit(solution)/shard_map/ppermute | solution.py:80
  23.3 15.5 %collective-permute-start.6 = (bf16[32,3712]{1,0:T(8,128)(2,1)S(1)}, bf16[32,3712]{1,0:T(8,128)(2,1)S(1)}, u32[]{:S(2)}, u32[]{:S(2)}) collective-permute-start(bf16[32,3712]{1,0:T(8,128)(2,1)S(1)} %get-tuple-element.30), channel_id=1, source_target_pairs={{0,2},{1,3},{2,0},{3,1},{4,6},{5,7},{6,4},{7,5},{8,10},{9,11},{10,... | collective-permute-start | bytes 712712 | tf_op jit(solution)/shard_map/ppermute | solution.py:80
  24.9 14.0 %collective-permute-start.7 = (bf16[32,3712]{1,0:T(8,128)(2,1)S(1)}, bf16[32,3712]{1,0:T(8,128)(2,1)S(1)}, u32[]{:S(2)}, u32[]{:S(2)}) collective-permute-start(bf16[32,3712]{1,0:T(8,128)(2,1)S(1)} %get-tuple-element.30), channel_id=1, source_target_pairs={{0,3},{1,2},{2,1},{3,0},{4,7},{5,6},{6,5},{7,4},{8,11},{9,10},{10,... | collective-permute-start | bytes 712712 | tf_op jit(solution)/shard_map/ppermute | solution.py:86
  26.0 12.8 %collective-permute-start.8 = (bf16[16,3712]{1,0:T(8,128)(2,1)S(1)}, bf16[16,3712]{1,0:T(8,128)(2,1)S(1)}, u32[]{:S(2)}, u32[]{:S(2)}) collective-permute-start(bf16[16,3712]{1,0:T(8,128)(2,1)S(1)} %get-tuple-element.31), channel_id=1, source_target_pairs={{0,2},{1,3},{2,0},{3,1},{4,6},{5,7},{6,4},{7,5},{8,10},{9,11},{10,... | collective-permute-start | bytes 356360 | tf_op jit(solution)/shard_map/ppermute | solution.py:80
  27.2 11.6 %collective-permute-start.9 = (bf16[16,3712]{1,0:T(8,128)(2,1)S(1)}, bf16[16,3712]{1,0:T(8,128)(2,1)S(1)}, u32[]{:S(2)}, u32[]{:S(2)}) collective-permute-start(bf16[16,3712]{1,0:T(8,128)(2,1)S(1)} %get-tuple-element.32), channel_id=1, source_target_pairs={{0,1},{1,0},{2,3},{3,2},{4,5},{5,4},{6,7},{7,6},{8,9},{9,8},{10,11... | collective-permute-start | bytes 356360 | tf_op jit(solution)/shard_map/ppermute | solution.py:80
  38.8 2.5 %collective-permute-start.12 = (bf16[128,3584]{1,0:T(8,128)(2,1)S(1)}, bf16[128,3584]{1,0:T(8,128)(2,1)S(1)}, u32[]{:S(2)}, u32[]{:S(2)}) collective-permute-start(bf16[128,3584]{1,0:T(8,128)(2,1)S(1)} %get-tuple-element.34.refs_5_), channel_id=1, source_target_pairs={{0,4},{4,0},{8,12},{12,8},{16,20},{20,16},{24,28},{28,24},{1,5},{5... | collective-permute-start | bytes 2752520 | tf_op jit(solution)/shard_map/ppermute | solution.py:80
  38.9 3.7 %collective-permute-start.11 = (bf16[128,3712]{1,0:T(8,128)(2,1)S(1)}, bf16[128,3712]{1,0:T(8,128)(2,1)S(1)}, u32[]{:S(2)}, u32[]{:S(2)}) collective-permute-start(bf16[128,3712]{1,0:T(8,128)(2,1)S(1)} %combine.9.own), channel_id=1, source_target_pairs={{0,4},{4,0},{8,12},{12,8},{16,20},{20,16},{24,28},{28,24},{1,5},{5... | collective-permute-start | bytes 2850824 | tf_op jit(solution)/shard_map/ppermute | solution.py:80
  45.4 2.5 %collective-permute-start.13 = (bf16[128,3584]{1,0:T(8,128)(2,1)S(1)}, bf16[128,3584]{1,0:T(8,128)(2,1)S(1)}, u32[]{:S(2)}, u32[]{:S(2)}) collective-permute-start(bf16[128,3584]{1,0:T(8,128)(2,1)S(1)} %get-tuple-element.41), channel_id=1, source_target_pairs={{0,4},{4,0},{8,12},{12,8},{16,20},{20,16},{24,28},{28,24},{1,5},{5... | collective-permute-start | bytes 2752520 | tf_op jit(solution)/shard_map/ppermute | solution.py:80
  48.6 9.4 %collective-permute-start.14 = (bf16[16,3584]{1,0:T(8,128)(2,1)S(1)}, bf16[16,3584]{1,0:T(8,128)(2,1)S(1)}, u32[]{:S(2)}, u32[]{:S(2)}) collective-permute-start(bf16[16,3584]{1,0:T(8,128)(2,1)S(1)} %get-tuple-element.46), channel_id=1, source_target_pairs={{0,2},{1,3},{2,0},{3,1},{4,6},{5,7},{6,4},{7,5},{8,10},{9,11},{10,... | collective-permute-start | bytes 344072 | tf_op jit(solution)/shard_map/ppermute | solution.py:80
  50.2 7.8 %collective-permute-start.15 = (bf16[16,3584]{1,0:T(8,128)(2,1)S(1)}, bf16[16,3584]{1,0:T(8,128)(2,1)S(1)}, u32[]{:S(2)}, u32[]{:S(2)}) collective-permute-start(bf16[16,3584]{1,0:T(8,128)(2,1)S(1)} %get-tuple-element.47), channel_id=1, source_target_pairs={{0,1},{1,0},{2,3},{3,2},{4,5},{5,4},{6,7},{7,6},{8,9},{9,8},{10,11... | collective-permute-start | bytes 344072 | tf_op jit(solution)/shard_map/ppermute | solution.py:80
  51.7 9.4 %collective-permute-start.18 = (bf16[32,3584]{1,0:T(8,128)(2,1)S(1)}, bf16[32,3584]{1,0:T(8,128)(2,1)S(1)}, u32[]{:S(2)}, u32[]{:S(2)}) collective-permute-start(bf16[32,3584]{1,0:T(8,128)(2,1)S(1)} %get-tuple-element.42.refs_0_), channel_id=1, source_target_pairs={{0,1},{1,0},{2,3},{3,2},{4,5},{5,4},{6,7},{7,6},{8,9},{9,8},{10,11... | collective-permute-start | bytes 688136 | tf_op jit(solution)/shard_map/ppermute | solution.py:80
  52.9 8.2 %collective-permute-start.19 = (bf16[32,3584]{1,0:T(8,128)(2,1)S(1)}, bf16[32,3584]{1,0:T(8,128)(2,1)S(1)}, u32[]{:S(2)}, u32[]{:S(2)}) collective-permute-start(bf16[32,3584]{1,0:T(8,128)(2,1)S(1)} %get-tuple-element.52), channel_id=1, source_target_pairs={{0,2},{1,3},{2,0},{3,1},{4,6},{5,7},{6,4},{7,5},{8,10},{9,11},{10,... | collective-permute-start | bytes 688136 | tf_op jit(solution)/shard_map/ppermute | solution.py:80
  53.4 12.4 %collective-permute-start.20 = (bf16[32,3584]{1,0:T(8,128)(2,1)S(1)}, bf16[32,3584]{1,0:T(8,128)(2,1)S(1)}, u32[]{:S(2)}, u32[]{:S(2)}) collective-permute-start(bf16[32,3584]{1,0:T(8,128)(2,1)S(1)} %get-tuple-element.53), channel_id=1, source_target_pairs={{0,3},{1,2},{2,1},{3,0},{4,7},{5,6},{6,5},{7,4},{8,11},{9,10},{10,... | collective-permute-start | bytes 688136 | tf_op jit(solution)/shard_map/ppermute | solution.py:86
  58.1 11.8 %collective-permute-start.16 = (bf16[32,3584]{1,0:T(8,128)(2,1)S(1)}, bf16[32,3584]{1,0:T(8,128)(2,1)S(1)}, u32[]{:S(2)}, u32[]{:S(2)}) collective-permute-start(bf16[32,3584]{1,0:T(8,128)(2,1)S(1)} %get-tuple-element.49.refs_4_), channel_id=1, source_target_pairs={{0,1},{1,0},{2,3},{3,2},{4,5},{5,4},{6,7},{7,6},{8,9},{9,8},{10,11... | collective-permute-start | bytes 688136 | tf_op jit(solution)/shard_map/ppermute | solution.py:80
  59.3 10.6 %collective-permute-start.17 = (bf16[32,3584]{1,0:T(8,128)(2,1)S(1)}, bf16[32,3584]{1,0:T(8,128)(2,1)S(1)}, u32[]{:S(2)}, u32[]{:S(2)}) collective-permute-start(bf16[32,3584]{1,0:T(8,128)(2,1)S(1)} %get-tuple-element.50), channel_id=1, source_target_pairs={{0,2},{1,3},{2,0},{3,1},{4,6},{5,7},{6,4},{7,5},{8,10},{9,11},{10,... | collective-permute-start | bytes 688136 | tf_op jit(solution)/shard_map/ppermute | solution.py:80
  65.9 10.5 %collective-permute-start.21 = (bf16[16,3584]{1,0:T(8,128)(2,1)S(1)}, bf16[16,3584]{1,0:T(8,128)(2,1)S(1)}, u32[]{:S(2)}, u32[]{:S(2)}) collective-permute-start(bf16[16,3584]{1,0:T(8,128)(2,1)S(1)} %get-tuple-element.54.refs_3_), channel_id=1, source_target_pairs={{0,16},{4,20},{8,24},{12,28},{16,0},{20,4},{24,8},{28,12},{1,17},{... | collective-permute-start | bytes 344072 | tf_op jit(solution)/shard_map/ppermute | solution.py:80
  68.0 8.4 %collective-permute-start.22 = (bf16[16,3584]{1,0:T(8,128)(2,1)S(1)}, bf16[16,3584]{1,0:T(8,128)(2,1)S(1)}, u32[]{:S(2)}, u32[]{:S(2)}) collective-permute-start(bf16[16,3584]{1,0:T(8,128)(2,1)S(1)} %get-tuple-element.56), channel_id=1, source_target_pairs={{0,24},{4,28},{8,16},{12,20},{16,8},{20,12},{24,0},{28,4},{1,25},{... | collective-permute-start | bytes 344072 | tf_op jit(solution)/shard_map/ppermute | solution.py:86
  70.0 7.3 %collective-permute-start.23 = (bf16[16,3584]{1,0:T(8,128)(2,1)S(1)}, bf16[16,3584]{1,0:T(8,128)(2,1)S(1)}, u32[]{:S(2)}, u32[]{:S(2)}) collective-permute-start(bf16[16,3584]{1,0:T(8,128)(2,1)S(1)} %get-tuple-element.57), channel_id=1, source_target_pairs={{0,8},{4,12},{8,0},{12,4},{16,24},{20,28},{24,16},{28,20},{1,9},{5... | collective-permute-start | bytes 344072 | tf_op jit(solution)/shard_map/ppermute | solution.py:80
  (4 other events, 30.7 us)

commit v8 on v7

--- a/solution.py
+++ b/solution.py
@@ -13,6 +13,8 @@
 BLOCKS = 4
 TILE = 256
 WIDE = 512
+GROUPS = 4
+NEAR_FLOPS = 4 * 10**9
 VMEM_BYTES = 48 * 1024 * 1024
 LARGE_BYTES = 16 * 1024 * 1024
 SMALL_BYTES = 8 * 1024 * 1024
@@ -116,47 +118,29 @@
     return total.astype(jnp.bfloat16)
 
 
-def pack_kernel(tokens, ids, gates, out, ids_here, gates_here, extra, sems):
+def pack_kernel(tokens, ids, gates, out):
     feature = tokens.shape[1]
-    copies = [
-        pltpu.make_async_copy(ids, ids_here, sems.at[0]),
-        pltpu.make_async_copy(gates, gates_here, sems.at[1]),
-        pltpu.make_async_copy(tokens, out.at[:, pl.ds(0, feature)], sems.at[2]),
-    ]
-    for copy in copies:
-        copy.start()
-    copies[0].wait()
-    copies[1].wait()
-    high = gates_here[...].astype(jnp.bfloat16).astype(jnp.float32)
-    low = gates_here[...] - high
-    stacked = jnp.concatenate([ids_here[...].astype(jnp.float32), high, low], axis=0)
+    high = gates[...].astype(jnp.bfloat16).astype(jnp.float32)
+    low = gates[...] - high
+    stacked = jnp.concatenate([ids[...].astype(jnp.float32), high, low], axis=0)
     stacked = stacked.astype(jnp.bfloat16)
     row = lax.broadcasted_iota(jnp.int32, (stacked.shape[0], EXTRA), 0)
     column = lax.broadcasted_iota(jnp.int32, (stacked.shape[0], EXTRA), 1)
     place = jnp.where(row == column, 1.0, 0.0).astype(jnp.bfloat16)
-    extra[...] = lax.dot_general(
+    extra = lax.dot_general(
         stacked, place, (((0,), (0,)), ((), ())), preferred_element_type=jnp.float32
-    ).astype(jnp.bfloat16)
-    last = pltpu.make_async_copy(extra, out.at[:, pl.ds(feature, EXTRA)], sems.at[3])
-    last.start()
-    copies[2].wait()
-    last.wait()
+    )
+    out[:, :feature] = tokens[...]
+    out[:, feature:] = extra.astype(jnp.bfloat16)
 
 
 def pack(tokens, ids, gates):
-    rows, feature = tokens.shape
-    picks = ids.shape[1]
     return pl.pallas_call(
         pack_kernel,
-        out_shape=jax.ShapeDtypeStruct((rows, feature + EXTRA), jnp.bfloat16),
-        in_specs=[pl.BlockSpec(memory_space=pl.ANY)] * 3,
-        out_specs=pl.BlockSpec(memory_space=pl.ANY),
-        scratch_shapes=[
-            pltpu.VMEM((picks, rows), jnp.int32),
-            pltpu.VMEM((picks, rows), jnp.float32),
-            pltpu.VMEM((rows, EXTRA), jnp.bfloat16),
-            pltpu.SemaphoreType.DMA((4,)),
-        ],
+        out_shape=jax.ShapeDtypeStruct((tokens.shape[0], tokens.shape[1] + EXTRA), jnp.bfloat16),
+        in_specs=[whole] * 3,
+        out_specs=whole,
+        compiler_params=pltpu.CompilerParams(vmem_limit_bytes=SMALL_BYTES),
         name="pack",
     )(tokens, ids.T, gates.T)
 
@@ -281,7 +265,7 @@
             at += rows
 
 
-def combine(inputs, plans, after=()):
+def combine(inputs, plans, after=(), flops=0):
     width = inputs[0].shape[1]
     return pl.pallas_call(
         functools.partial(combine_kernel, len(inputs), plans),
@@ -292,17 +276,22 @@
         in_specs=[whole] * len(inputs) + [pl.BlockSpec(memory_space=pl.ANY)] * len(after),
         out_specs=[whole] * len(plans),
         compiler_params=pltpu.CompilerParams(vmem_limit_bytes=SMALL_BYTES),
+        cost_estimate=pl.CostEstimate(
+            flops=flops, bytes_accessed=4 * width * inputs[0].shape[0], transcendentals=0
+        ),
         name="combine",
     )(*inputs, *after)
 
 
-def expert_kernel(picks, own, other, w_gate, w_up, w_down, *refs):
-    expert_body(picks, own, other, w_gate, w_up, w_down, *refs[-4:])
+def expert_kernel(picks, after, own, other, w_gate, w_up, w_down, *refs):
+    *outs, rows, hidden = refs[after:]
+    expert_body(picks, own, other, w_gate, w_up, w_down, outs, rows, hidden)
 
 
 def expert_body(
-    picks, own, other, w_gate, w_up, w_down, h_own, out, rows, hidden, ready=lambda number: None
+    picks, own, other, w_gate, w_up, w_down, outs, rows, hidden, ready=lambda number: None
 ):
+    h_own, *outs = outs
     count, feature, half = own.shape[0], w_gate.shape[1], w_gate.shape[2]
     wanted = expert_index().astype(jnp.float32)
     shares = []
@@ -328,13 +317,17 @@
     wide = feature // BLOCKS
     for at in range(0, feature, wide):
         ready(half // TILE * 2 + at // wide)
-        out[:, at : at + wide] = jnp.dot(
+        part = jnp.dot(
             hidden[count:, :], w_down[0, :, at : at + wide], preferred_element_type=jnp.float32
         ).astype(jnp.bfloat16)
+        top = 0
+        for out in outs:
+            out[:, at : at + wide] = part[top : top + out.shape[0], :]
+            top += out.shape[0]
 
 
 def first_kernel(picks, own, other, gate_far, up_far, down_far, *refs):
-    h_own, out, w_gate, w_up, w_down, rows, hidden, sems = refs
+    outs, (w_gate, w_up, w_down, rows, hidden, sems) = refs[:-6], refs[-6:]
     feature, half = w_gate.shape[1], w_gate.shape[2]
     depth = feature // BLOCKS
     groups = []
@@ -361,22 +354,20 @@
         for copy in groups[number]:
             copy.wait()
 
-    expert_body(picks, own, other, w_gate, w_up, w_down, h_own, out, rows, hidden, ready)
-
-
-def first_of(own, other, w_gate, w_up, w_down, picks, after=()):
+    expert_body(picks, own, other, w_gate, w_up, w_down, outs, rows, hidden, ready)
+
+
+def first_of(own, other, w_gate, w_up, w_down, picks, cuts):
     count = own.shape[0]
     _, feature, half = w_gate.shape
     copies = 2 * (half // TILE) * BLOCKS + BLOCKS
     return pl.pallas_call(
         functools.partial(first_kernel, picks),
-        out_shape=[
-            jax.ShapeDtypeStruct((count, half), jnp.bfloat16),
-            jax.ShapeDtypeStruct((count, feature), jnp.bfloat16),
-        ]
+        out_shape=[jax.ShapeDtypeStruct((count, half), jnp.bfloat16)]
+        + [jax.ShapeDtypeStruct((cut, feature), jnp.bfloat16) for cut in cuts]
         + [jax.ShapeDtypeStruct(w.shape, w.dtype) for w in (w_gate, w_up, w_down)],
         in_specs=[whole] * 2 + [pl.BlockSpec(memory_space=pl.ANY)] * 3,
-        out_specs=[whole] * 5,
+        out_specs=[whole] * (len(cuts) + 4),
         scratch_shapes=[
             pltpu.VMEM((2 * count, feature), jnp.bfloat16),
             pltpu.VMEM((2 * count, half), jnp.bfloat16),
@@ -392,17 +383,15 @@
     )(own, other, w_gate, w_up, w_down)
 
 
-def expert_of(own, other, w_gate, w_up, w_down, picks, after=()):
+def expert_of(own, other, w_gate, w_up, w_down, picks, cuts, after=()):
     count = own.shape[0]
     _, feature, half = w_gate.shape
     return pl.pallas_call(
-        functools.partial(expert_kernel, picks),
-        out_shape=[
-            jax.ShapeDtypeStruct((count, half), jnp.bfloat16),
-            jax.ShapeDtypeStruct((count, feature), jnp.bfloat16),
-        ],
+        functools.partial(expert_kernel, picks, len(after)),
+        out_shape=[jax.ShapeDtypeStruct((count, half), jnp.bfloat16)]
+        + [jax.ShapeDtypeStruct((cut, feature), jnp.bfloat16) for cut in cuts],
         in_specs=[whole] * 5 + [pl.BlockSpec(memory_space=pl.ANY)] * len(after),
-        out_specs=[whole] * 2,
+        out_specs=[whole] * (len(cuts) + 1),
         scratch_shapes=[
             pltpu.VMEM((2 * count, feature), jnp.bfloat16),
             pltpu.VMEM((2 * count, half), jnp.bfloat16),
@@ -417,27 +406,30 @@
     )(own, other, w_gate, w_up, w_down, *after)
 
 
-def sums_kernel(cuts, hidden, w_down, arrived, *refs):
-    outs = refs[len(refs) - len(cuts) :]
+def sums_kernel(parts, hidden, w_down, *refs):
+    arrived, outs = refs[:parts], refs[len(refs) - GROUPS :]
     feature = w_down.shape[2]
+    cut = hidden.shape[0] // GROUPS
+    places = [
+        (term, top) for term in arrived for top in range(0, term.shape[0], cut)
+    ]
     for column in range(0, feature, 2 * TILE):
         span = slice(column, column + 2 * TILE)
         part = jnp.dot(hidden[...], w_down[0, :, span], preferred_element_type=jnp.float32)
-        part = part + arrived[:, span].astype(jnp.float32)
-        at = 0
-        for cut, out in zip(cuts, outs):
-            out[:, span] = part[at : at + cut, :].astype(jnp.bfloat16)
-            at += cut
-
-
-def sums_of(hidden, w_down, cuts, arrived, after=()):
+        for number, ((term, top), out) in enumerate(zip(places, outs)):
+            own = part[number * cut : (number + 1) * cut, :]
+            other = term[top : top + cut, span].astype(jnp.float32)
+            out[:, span] = (own + other).astype(jnp.bfloat16)
+
+
+def sums_of(hidden, w_down, arrived, after=()):
     count, half = hidden.shape
     feature = w_down.shape[2]
     return pl.pallas_call(
-        functools.partial(sums_kernel, cuts),
-        out_shape=[jax.ShapeDtypeStruct((cut, feature), jnp.bfloat16) for cut in cuts],
-        in_specs=[whole] * 3 + [pl.BlockSpec(memory_space=pl.ANY)] * len(after),
-        out_specs=[whole] * len(cuts),
+        functools.partial(sums_kernel, len(arrived)),
+        out_shape=[jax.ShapeDtypeStruct((count // GROUPS, feature), jnp.bfloat16)] * GROUPS,
+        in_specs=[whole] * (2 + len(arrived)) + [pl.BlockSpec(memory_space=pl.ANY)] * len(after),
+        out_specs=[whole] * GROUPS,
         compiler_params=pltpu.CompilerParams(vmem_limit_bytes=SMALL_BYTES),
         cost_estimate=pl.CostEstimate(
             flops=2 * count * feature * half,
@@ -445,7 +437,7 @@
             transcendentals=0,
         ),
         name="sums",
-    )(hidden, w_down, arrived, *after)
+    )(hidden, w_down, *arrived, *after)
 
 
 def mix_large(packed, weights, picks, steps):
@@ -491,56 +483,44 @@
     (near,) = combine([packed, from_near], [rows_of((0, 0, n), (1, 0, n))])
     near_x, near_y = swap(near, x), swap(near, y)
     from_both = swap(from_far, z_near)
-    first_own, far, half_x, half_y = combine(
+    first_own, far, way_x, way_y = combine(
         [near, near_x, near_y, from_far, from_both],
         [
             rows_of((0, 0, 2 * n), (1, 0, 2 * n), (2, 0, 2 * n), (3, 0, n), (4, 0, n)),
             rows_of((3, 0, n), (4, 0, n)),
-            rows_of((1, 0, n)),
-            rows_of((2, n, n)),
+            rows_of((3, 0, n), (4, 0, n), (2, n, n)),
+            rows_of((3, 0, n), (4, 0, n), (1, 0, n)),
         ],
     )
-    far_x, far_y, far_xy = swap(far, x), swap(far, y), across(far, x, y)
-    near_xy_top, near_xy_low = swap(half_x, y), swap(half_y, x)
     first_other = swap(first_own, core)
-    first_h, first_out, *weights = first_of(first_own, first_other, *weights, picks)
+    far_x, far_y, far_xy = swap(way_x, x), swap(way_y, y), across(far, x, y)
+    first_h, first_out, *weights = first_of(first_own, first_other, *weights, picks, [8 * n])
     w_down = weights[2]
+    first_in = swap(first_out, core)
     (second_own,) = combine(
-        [far_x, far_y, far_xy, near_xy_top, near_xy_low],
-        [
-            rows_of(
-                (0, 0, 2 * n), (1, 0, 2 * n), (2, 0, 2 * n), (3, 0, n), (4, 0, n)
-            )
-        ],
+        [far_x, far_y, far_xy],
+        [rows_of((0, 0, 2 * n), (1, 0, 2 * n), (2, 0, 2 * n), (1, 2 * n, n), (0, 2 * n, n))],
         [first_out],
     )
     second_other = swap(second_own, core)
-    first_in = swap(first_out, core)
-    near, near_x, near_y, far = sums_of(first_h, w_down, [2 * n] * 4, first_in)
-    second_h, second_out = expert_of(second_own, second_other, *weights, picks, [near])
-    second_in = swap(second_out, core)
-    far_x, far_y, far_xy, near_xy_top, near_xy_low = sums_of(
-        second_h, w_down, [2 * n] * 3 + [n] * 2, second_in
+    near, near_x, near_y, far = sums_of(first_h, w_down, [first_in])
+    to_near = [swap(near_x, x), swap(near_y, y)]
+    second_h, *second_out = expert_of(
+        second_own, second_other, *weights, picks, [2 * n, 2 * n, 4 * n], [near]
     )
+    second_in = [swap(part, core) for part in second_out]
+
+    def all_of(terms, start, count=n):
+        return [(count, [(index, start) for index in range(terms)])]
+
+    (near,) = combine([near, *to_near], [all_of(3, 0, 2 * n)], flops=NEAR_FLOPS)
+    far_x, far_y, far_xy, near_xy = sums_of(second_h, w_down, second_in, [near])
 
     to_far = [swap(far_x, x), swap(far_y, y), across(far_xy, x, y)]
-    to_near_x, to_near_y = swap(near_xy_top, y), swap(near_xy_low, x)
+    to_near = across(near_xy, x, y)
     context, done = attention([far_x])
-    near_x, near_y = combine(
-        [near_x, near_y, to_near_x, to_near_y],
-        [
-            [(n, [(0, 0), (2, 0)]), (n, [(0, n)])],
-            [(n, [(1, 0)]), (n, [(1, n), (3, 0)])],
-        ],
-        [done],
-    )
-    to_near = [swap(near_x, x), swap(near_y, y)]
-
-    def all_of(terms, start):
-        return [(n, [(index, start) for index in range(terms)])]
-
-    far_sum, both_sum = combine([far, *to_far], [all_of(4, 0), all_of(4, n)], [near_x])
-    own_sum, near_sum = combine([near, *to_near], [all_of(3, 0), all_of(3, n)], [far_sum])
+    far_sum, both_sum = combine([far, *to_far], [all_of(4, 0), all_of(4, n)], [done])
+    own_sum, near_sum = combine([near, to_near], [all_of(2, 0), all_of(2, n)], [far_sum])
     terms = [swap(far_sum, z_far), across(both_sum, z_far, z_near), swap(near_sum, z_near)]
     (mixed,) = combine([own_sum, *terms], [all_of(4, 0)])
     return mixed, context

time: 78.2 us -> 74.4 us (0.951)
  Pallas kernels: 19.8 us -> 15.4 us
  starting transfers between devices: 27.8 us -> 25.8 us
  local copies, waits for them, and re-layouts: 0.92 us -> 2.28 us
  waiting for transfers between devices: 28 us -> 29.1 us
    pallas_call x4, Pallas kernels: 8.6 us -> 4.17 us  [the longest x1 2.7 us: expert_of(): pl.pallas_call(functools.partial(expert_kernel, picks, len(after)), out_s...]
    ppermute x21 -> x19, starting transfers between devices: 23.5 us -> 20.1 us  [swap(): return lax.ppermute(value, axis, [(i, i ^ bit) for i in range(size)])]
    ppermute x3 -> x4, waiting for transfers between devices: 4.69 us -> 7.34 us  [across(): lax.ppermute(value, axis, [(i, i ^ first[1] ^ second[1]) for i in range(s...]
    ppermute x21 -> x19, waiting for transfers between devices: 23.3 us -> 21.8 us  [swap(): return lax.ppermute(value, axis, [(i, i ^ bit) for i in range(size)])]
    ppermute x3 -> x4, starting transfers between devices: 4.26 us -> 5.69 us  [across(): lax.ppermute(value, axis, [(i, i ^ first[1] ^ second[1]) for i in range(s...]
    unnamed x8 -> x12, local copies, waits for them, and re-layouts: 0.92 us -> 2.28 us
  transfers between devices with their start and end apart: 24 -> 23, of which waited for: 11 -> 11; matrix products, arithmetic and copies ran while one was open for 0% -> 0% of each run, Pallas kernels for 14% -> 19%
where the time goes in v8:
time: 74.4 us; the launch traced here: 74.1 us
  waiting for transfers between devices  29.1 us (39%)
  starting transfers between devices  25.8 us (35%)
  Pallas kernels  15.4 us (21%)
  local copies, waits for them, and re-layouts  2.28 us (3%)
  between operations  1.49 us (2%)
    ppermute x19, waiting for transfers between devices, swap(): return lax.ppermute(value, axis, [(i, i ^ bit) for i in range(size)])  21.8 us
    ppermute x19, starting transfers between devices, swap(): return lax.ppermute(value, axis, [(i, i ^ bit) for i in range(size)])  20.1 us
    pallas_call x1, Pallas kernels, first_of(): pl.pallas_call(functools.partial(first_kernel, picks), out_shape=[jax.Sha...  7.4 us
    ppermute x4, waiting for transfers between devices, across(): lax.ppermute(value, axis, [(i, i ^ first[1] ^ second[1]) for i in range(s...  7.34 us
    ppermute x4, starting transfers between devices, across(): lax.ppermute(value, axis, [(i, i ^ first[1] ^ second[1]) for i in range(s...  5.69 us
    pallas_call x1, Pallas kernels, attend(): pl.pallas_call(attend_kernel, out_shape=[jax.ShapeDtypeStruct((count, hea...  2.71 us
    pallas_call x1, Pallas kernels, expert_of(): pl.pallas_call(functools.partial(expert_kernel, picks, len(after)), out_s...  2.7 us
    unnamed x12, local copies, waits for them, and re-layouts  2.28 us
  transfers between devices with their start and end apart: 23, of which 11 were waited for; matrix products, arithmetic and copies ran while one was open for 0% of the time, Pallas kernels for 19%

profile of v8, /device:TPU:0, one launch (start us, length us, event | category | flops | bytes accessed | tf_op | source)
XLA Modules:
  0.0 74.1 jit_solution(2104477508514729770)
XLA Ops:
  3.1 3.0 %collective-permute-start = (bf16[16,3712]{1,0:T(8,128)(2,1)S(1)}, bf16[16,3712]{1,0:T(8,128)(2,1)S(1)}, u32[]{:S(2)}, u32[]{:S(2)}) collective-permute-start(bf16[16,3712]{1,0:T(8,128)(2,1)S(1)} %pack.1.refs_0_), channel_id=1, source_target_pairs={{0,8},{4,12},{8,0},{12,4},{16,24},{20,28},{24,16},{28,20},{1,9},{5... | collective-permute-start | bytes 356360 | tf_op jit(solution)/shard_map/ppermute | solution.py:82
  6.1 2.6 %collective-permute-start.3 = (bf16[16,3712]{1,0:T(8,128)(2,1)S(1)}, bf16[16,3712]{1,0:T(8,128)(2,1)S(1)}, u32[]{:S(2)}, u32[]{:S(2)}) collective-permute-start(bf16[16,3712]{1,0:T(8,128)(2,1)S(1)} %pack.1.refs_0_), channel_id=1, source_target_pairs={{0,16},{4,20},{8,24},{12,28},{16,0},{20,4},{24,8},{28,12},{1,17},{... | collective-permute-start | bytes 356360 | tf_op jit(solution)/shard_map/ppermute | solution.py:82
  8.7 1.9 %collective-permute-done.refs_1_ = bf16[16,3712]{1,0:T(8,128)(2,1)S(1)} collective-permute-done((bf16[16,3712]{1,0:T(8,128)(2,1)S(1)}, bf16[16,3712]{1,0:T(8,128)(2,1)S(1)}, u32[]{:S(2)}, u32[]{:S(2)}) %collective-permute-start) | collective-permute-done | bytes 118816 | tf_op jit(solution)/shard_map/ppermute | solution.py:82
  10.7 1.9 %collective-permute-start.1 = (bf16[32,3712]{1,0:T(8,128)(2,1)S(1)}, bf16[32,3712]{1,0:T(8,128)(2,1)S(1)}, u32[]{:S(2)}, u32[]{:S(2)}) collective-permute-start(bf16[32,3712]{1,0:T(8,128)(2,1)S(1)} %combine.7.refs_0_), channel_id=1, source_target_pairs={{0,1},{1,0},{2,3},{3,2},{4,5},{5,4},{6,7},{7,6},{8,9},{9,8},{10,11... | collective-permute-start | bytes 712712 | tf_op jit(solution)/shard_map/ppermute | solution.py:82
  12.5 1.5 %collective-permute-start.2 = (bf16[32,3712]{1,0:T(8,128)(2,1)S(1)}, bf16[32,3712]{1,0:T(8,128)(2,1)S(1)}, u32[]{:S(2)}, u32[]{:S(2)}) collective-permute-start(bf16[32,3712]{1,0:T(8,128)(2,1)S(1)} %combine.7.refs_0_), channel_id=1, source_target_pairs={{0,2},{1,3},{2,0},{3,1},{4,6},{5,7},{6,4},{7,5},{8,10},{9,11},{10,... | collective-permute-start | bytes 712712 | tf_op jit(solution)/shard_map/ppermute | solution.py:82
  14.7 4.4 %collective-permute-done.4.refs_4_ = bf16[16,3712]{1,0:T(8,128)(2,1)S(1)} collective-permute-done((bf16[16,3712]{1,0:T(8,128)(2,1)S(1)}, bf16[16,3712]{1,0:T(8,128)(2,1)S(1)}, u32[]{:S(2)}, u32[]{:S(2)}) %collective-permute-start.4) | collective-permute-done | bytes 118816 | tf_op jit(solution)/shard_map/ppermute | solution.py:82
  19.3 1.6 %collective-permute-start.5 = (bf16[48,3712]{1,0:T(8,128)(2,1)S(1)}, bf16[48,3712]{1,0:T(8,128)(2,1)S(1)}, u32[]{:S(2)}, u32[]{:S(2)}) collective-permute-start(bf16[48,3712]{1,0:T(8,128)(2,1)S(1)} %get-tuple-element.29), channel_id=1, source_target_pairs={{0,1},{1,0},{2,3},{3,2},{4,5},{5,4},{6,7},{7,6},{8,9},{9,8},{10,11... | collective-permute-start | bytes 1069064 | tf_op jit(solution)/shard_map/ppermute | solution.py:82
  20.9 1.5 %collective-permute-start.6 = (bf16[48,3712]{1,0:T(8,128)(2,1)S(1)}, bf16[48,3712]{1,0:T(8,128)(2,1)S(1)}, u32[]{:S(2)}, u32[]{:S(2)}) collective-permute-start(bf16[48,3712]{1,0:T(8,128)(2,1)S(1)} %get-tuple-element.30), channel_id=1, source_target_pairs={{0,2},{1,3},{2,0},{3,1},{4,6},{5,7},{6,4},{7,5},{8,10},{9,11},{10,... | collective-permute-start | bytes 1069064 | tf_op jit(solution)/shard_map/ppermute | solution.py:82
  22.9 7.4 %first.1 = (bf16[128,512]{1,0:T(8,128)(2,1)S(1)}, bf16[128,3584]{1,0:T(8,128)(2,1)S(1)}, bf16[1,3584,512]{2,1,0:T(8,128)(2,1)S(1)}, bf16[1,3584,512]{2,1,0:T(8,128)(2,1)S(1)}, bf16[1,512,3584]{2,1,0:T(8,128)(2,1)S(1)}) custom-call(bf16[128,3712]{1,0:T(8,128)(2,1)S(1)} %get-tuple-element.32.own, bf16[128,3712]{1,0:T(8,128)(2,1)S(1)} %collective-permute-done.8.other, ...), custom_call_target="tpu_custom_call" | custom-call | flops 2348810240 | bytes 11010048 | tf_op jit(solution)/shard_map/first/pallas_call | solution.py:364
  30.4 5.9 %collective-permute-done.7.refs_2_ = bf16[32,3712]{1,0:T(8,128)(2,1)S(1)} collective-permute-done((bf16[32,3712]{1,0:T(8,128)(2,1)S(1)}, bf16[32,3712]{1,0:T(8,128)(2,1)S(1)}, u32[]{:S(2)}, u32[]{:S(2)}) %collective-permute-start.7) | collective-permute-done | bytes 237600 | tf_op jit(solution)/shard_map/ppermute | solution.py:88
  37.2 1.3 %collective-permute-start.14 = (bf16[32,3584]{1,0:T(8,128)(2,1)S(1)}, bf16[32,3584]{1,0:T(8,128)(2,1)S(1)}, u32[]{:S(2)}, u32[]{:S(2)}) collective-permute-start(bf16[32,3584]{1,0:T(8,128)(2,1)S(1)} %get-tuple-element.43), channel_id=1, source_target_pairs={{0,1},{1,0},{2,3},{3,2},{4,5},{5,4},{6,7},{7,6},{8,9},{9,8},{10,11... | collective-permute-start | bytes 688136 | tf_op jit(solution)/shard_map/ppermute | solution.py:82
  39.3 2.7 %expert.1 = (bf16[128,512]{1,0:T(8,128)(2,1)S(1)}, bf16[32,3584]{1,0:T(8,128)(2,1)S(1)}, bf16[32,3584]{1,0:T(8,128)(2,1)S(1)}, bf16[64,3584]{1,0:T(8,128)(2,1)S(1)}) custom-call(bf16[128,3712]{1,0:T(8,128)(2,1)S(1)} %combine.9.own, bf16[128,3712]{1,0:T(8,128)(2,1)S(1)} %collective-permute-done.9.other, bf16[1,3584,512]{2,1,0:T(8,128)(2,1)S(1)} %get-tuple-element.34.w_gate, ...), custom_call_target="tpu_custom_call" | custom-call | flops 2348810240 | bytes 917504 | tf_op jit(solution)/shard_map/expert/pallas_call | solution.py:389
  42.7 2.6 %collective-permute-done.14.refs_1_ = bf16[32,3584]{1,0:T(8,128)(2,1)S(1)} collective-permute-done((bf16[32,3584]{1,0:T(8,128)(2,1)S(1)}, bf16[32,3584]{1,0:T(8,128)(2,1)S(1)}, u32[]{:S(2)}, u32[]{:S(2)}) %collective-permute-start.14) | collective-permute-done | bytes 229408 | tf_op jit(solution)/shard_map/ppermute | solution.py:82
  45.3 1.0 %collective-permute-done.15.refs_2_ = bf16[32,3584]{1,0:T(8,128)(2,1)S(1)} collective-permute-done((bf16[32,3584]{1,0:T(8,128)(2,1)S(1)}, bf16[32,3584]{1,0:T(8,128)(2,1)S(1)}, u32[]{:S(2)}, u32[]{:S(2)}) %collective-permute-start.15) | collective-permute-done | bytes 229408 | tf_op jit(solution)/shard_map/ppermute | solution.py:82
  47.9 1.5 %collective-permute-start.18 = (bf16[32,3584]{1,0:T(8,128)(2,1)S(1)}, bf16[32,3584]{1,0:T(8,128)(2,1)S(1)}, u32[]{:S(2)}, u32[]{:S(2)}) collective-permute-start(bf16[32,3584]{1,0:T(8,128)(2,1)S(1)} %get-tuple-element.49), channel_id=1, source_target_pairs={{0,2},{1,3},{2,0},{3,1},{4,6},{5,7},{6,4},{7,5},{8,10},{9,11},{10,... | collective-permute-start | bytes 688136 | tf_op jit(solution)/shard_map/ppermute | solution.py:82
  49.4 1.2 %collective-permute-start.19 = (bf16[32,3584]{1,0:T(8,128)(2,1)S(1)}, bf16[32,3584]{1,0:T(8,128)(2,1)S(1)}, u32[]{:S(2)}, u32[]{:S(2)}) collective-permute-start(bf16[32,3584]{1,0:T(8,128)(2,1)S(1)} %get-tuple-element.50), channel_id=1, source_target_pairs={{0,3},{1,2},{2,1},{3,0},{4,7},{5,6},{6,5},{7,4},{8,11},{9,10},{10,... | collective-permute-start | bytes 688136 | tf_op jit(solution)/shard_map/ppermute | solution.py:88
  50.6 1.7 %collective-permute-start.16 = (bf16[32,3584]{1,0:T(8,128)(2,1)S(1)}, bf16[32,3584]{1,0:T(8,128)(2,1)S(1)}, u32[]{:S(2)}, u32[]{:S(2)}) collective-permute-start(bf16[32,3584]{1,0:T(8,128)(2,1)S(1)} %get-tuple-element.47), channel_id=1, source_target_pairs={{0,3},{1,2},{2,1},{3,0},{4,7},{5,6},{6,5},{7,4},{8,11},{9,10},{10,... | collective-permute-start | bytes 688136 | tf_op jit(solution)/shard_map/ppermute | solution.py:88
  53.0 2.7 %attend.1 = (bf16[4,64,512]{2,1,0:T(8,128)(2,1)}, f32[8,128]{1,0:T(8,128)S(1)}) custom-call(s32[4]{0:T(128)S(1)} %copy-done.5, s32[1]{0:T(128)S(6)} %copy.12.live_rows, bf16[4,64,576]{2,1,0:T(8,128)(2,1)S(1)} %copy-done.1, bf16[4,576,256]{2,1,0:T(8,128)(2,1)S(1)} %bitcast.3, bf16[32,3584]{1,0:T(8,128)(2,1)S(1)} %get-tuple-element.45.refs_0_), custom_call_target="tpu_custom_call" | custom-call | flops 150994944 | bytes 1179648 | tf_op jit(solution)/shard_map/attend/pallas_call | solution.py:55
  55.7 8.6 %collective-permute-done.18.refs_2_ = bf16[32,3584]{1,0:T(8,128)(2,1)S(1)} collective-permute-done((bf16[32,3584]{1,0:T(8,128)(2,1)S(1)}, bf16[32,3584]{1,0:T(8,128)(2,1)S(1)}, u32[]{:S(2)}, u32[]{:S(2)}) %collective-permute-start.18) | collective-permute-done | bytes 229408 | tf_op jit(solution)/shard_map/ppermute | solution.py:82
  64.6 2.1 %collective-permute-start.22 = (bf16[16,3584]{1,0:T(8,128)(2,1)S(1)}, bf16[16,3584]{1,0:T(8,128)(2,1)S(1)}, u32[]{:S(2)}, u32[]{:S(2)}) collective-permute-start(bf16[16,3584]{1,0:T(8,128)(2,1)S(1)} %get-tuple-element.55), channel_id=1, source_target_pairs={{0,8},{4,12},{8,0},{12,4},{16,24},{20,28},{24,16},{28,20},{1,9},{5... | collective-permute-start | bytes 344072 | tf_op jit(solution)/shard_map/ppermute | solution.py:82
  66.7 2.3 %collective-permute-start.21 = (bf16[16,3584]{1,0:T(8,128)(2,1)S(1)}, bf16[16,3584]{1,0:T(8,128)(2,1)S(1)}, u32[]{:S(2)}, u32[]{:S(2)}) collective-permute-start(bf16[16,3584]{1,0:T(8,128)(2,1)S(1)} %get-tuple-element.54), channel_id=1, source_target_pairs={{0,24},{4,28},{8,16},{12,20},{16,8},{20,12},{24,0},{28,4},{1,25},{... | collective-permute-start | bytes 344072 | tf_op jit(solution)/shard_map/ppermute | solution.py:88
  69.0 1.5 %collective-permute-done.22.refs_3_ = bf16[16,3584]{1,0:T(8,128)(2,1)S(1)} collective-permute-done((bf16[16,3584]{1,0:T(8,128)(2,1)S(1)}, bf16[16,3584]{1,0:T(8,128)(2,1)S(1)}, u32[]{:S(2)}, u32[]{:S(2)}) %collective-permute-start.22) | collective-permute-done | bytes 114720 | tf_op jit(solution)/shard_map/ppermute | solution.py:82
  70.5 1.4 %collective-permute-done.20.refs_1_ = bf16[16,3584]{1,0:T(8,128)(2,1)S(1)} collective-permute-done((bf16[16,3584]{1,0:T(8,128)(2,1)S(1)}, bf16[16,3584]{1,0:T(8,128)(2,1)S(1)}, u32[]{:S(2)}, u32[]{:S(2)}) %collective-permute-start.20) | collective-permute-done | bytes 114720 | tf_op jit(solution)/shard_map/ppermute | solution.py:82
  72.0 1.5 %collective-permute-done.21.refs_2_ = bf16[16,3584]{1,0:T(8,128)(2,1)S(1)} collective-permute-done((bf16[16,3584]{1,0:T(8,128)(2,1)S(1)}, bf16[16,3584]{1,0:T(8,128)(2,1)S(1)}, u32[]{:S(2)}, u32[]{:S(2)}) %collective-permute-start.21) | collective-permute-done | bytes 114720 | tf_op jit(solution)/shard_map/ppermute | solution.py:88
  (47 shorter events, 8.8 us)
Async XLA Ops:
  3.1 7.6 %collective-permute-start = (bf16[16,3712]{1,0:T(8,128)(2,1)S(1)}, bf16[16,3712]{1,0:T(8,128)(2,1)S(1)}, u32[]{:S(2)}, u32[]{:S(2)}) collective-permute-start(bf16[16,3712]{1,0:T(8,128)(2,1)S(1)} %pack.1.refs_0_), channel_id=1, source_target_pairs={{0,8},{4,12},{8,0},{12,4},{16,24},{20,28},{24,16},{28,20},{1,9},{5... | collective-permute-start | bytes 356360 | tf_op jit(solution)/shard_map/ppermute | solution.py:82
  6.1 8.2 %collective-permute-start.3 = (bf16[16,3712]{1,0:T(8,128)(2,1)S(1)}, bf16[16,3712]{1,0:T(8,128)(2,1)S(1)}, u32[]{:S(2)}, u32[]{:S(2)}) collective-permute-start(bf16[16,3712]{1,0:T(8,128)(2,1)S(1)} %pack.1.refs_0_), channel_id=1, source_target_pairs={{0,16},{4,20},{8,24},{12,28},{16,0},{20,4},{24,8},{28,12},{1,17},{... | collective-permute-start | bytes 356360 | tf_op jit(solution)/shard_map/ppermute | solution.py:82
  10.7 8.5 %collective-permute-start.1 = (bf16[32,3712]{1,0:T(8,128)(2,1)S(1)}, bf16[32,3712]{1,0:T(8,128)(2,1)S(1)}, u32[]{:S(2)}, u32[]{:S(2)}) collective-permute-start(bf16[32,3712]{1,0:T(8,128)(2,1)S(1)} %combine.7.refs_0_), channel_id=1, source_target_pairs={{0,1},{1,0},{2,3},{3,2},{4,5},{5,4},{6,7},{7,6},{8,9},{9,8},{10,11... | collective-permute-start | bytes 712712 | tf_op jit(solution)/shard_map/ppermute | solution.py:82
  12.5 6.6 %collective-permute-start.2 = (bf16[32,3712]{1,0:T(8,128)(2,1)S(1)}, bf16[32,3712]{1,0:T(8,128)(2,1)S(1)}, u32[]{:S(2)}, u32[]{:S(2)}) collective-permute-start(bf16[32,3712]{1,0:T(8,128)(2,1)S(1)} %combine.7.refs_0_), channel_id=1, source_target_pairs={{0,2},{1,3},{2,0},{3,1},{4,6},{5,7},{6,4},{7,5},{8,10},{9,11},{10,... | collective-permute-start | bytes 712712 | tf_op jit(solution)/shard_map/ppermute | solution.py:82
  14.3 4.8 %collective-permute-start.4 = (bf16[16,3712]{1,0:T(8,128)(2,1)S(1)}, bf16[16,3712]{1,0:T(8,128)(2,1)S(1)}, u32[]{:S(2)}, u32[]{:S(2)}) collective-permute-start(bf16[16,3712]{1,0:T(8,128)(2,1)S(1)} %collective-permute-done.3.refs_3_), channel_id=1, source_target_pairs={{0,8},{4,12},{8,0},{12,4},{16,24},{20,28},{24,16},{28,20},{1,9},{5... | collective-permute-start | bytes 356360 | tf_op jit(solution)/shard_map/ppermute | solution.py:82
  19.3 3.6 %collective-permute-start.8 = (bf16[128,3712]{1,0:T(8,128)(2,1)S(1)}, bf16[128,3712]{1,0:T(8,128)(2,1)S(1)}, u32[]{:S(2)}, u32[]{:S(2)}) collective-permute-start(bf16[128,3712]{1,0:T(8,128)(2,1)S(1)} %get-tuple-element.32.own), channel_id=1, source_target_pairs={{0,4},{4,0},{8,12},{12,8},{16,20},{20,16},{24,28},{28,24},{1,5},{5... | collective-permute-start | bytes 2850824 | tf_op jit(solution)/shard_map/ppermute | solution.py:82
  19.3 16.9 %collective-permute-start.5 = (bf16[48,3712]{1,0:T(8,128)(2,1)S(1)}, bf16[48,3712]{1,0:T(8,128)(2,1)S(1)}, u32[]{:S(2)}, u32[]{:S(2)}) collective-permute-start(bf16[48,3712]{1,0:T(8,128)(2,1)S(1)} %get-tuple-element.29), channel_id=1, source_target_pairs={{0,1},{1,0},{2,3},{3,2},{4,5},{5,4},{6,7},{7,6},{8,9},{9,8},{10,11... | collective-permute-start | bytes 1069064 | tf_op jit(solution)/shard_map/ppermute | solution.py:82
  20.9 15.5 %collective-permute-start.6 = (bf16[48,3712]{1,0:T(8,128)(2,1)S(1)}, bf16[48,3712]{1,0:T(8,128)(2,1)S(1)}, u32[]{:S(2)}, u32[]{:S(2)}) collective-permute-start(bf16[48,3712]{1,0:T(8,128)(2,1)S(1)} %get-tuple-element.30), channel_id=1, source_target_pairs={{0,2},{1,3},{2,0},{3,1},{4,6},{5,7},{6,4},{7,5},{8,10},{9,11},{10,... | collective-permute-start | bytes 1069064 | tf_op jit(solution)/shard_map/ppermute | solution.py:82
  22.4 13.8 %collective-permute-start.7 = (bf16[32,3712]{1,0:T(8,128)(2,1)S(1)}, bf16[32,3712]{1,0:T(8,128)(2,1)S(1)}, u32[]{:S(2)}, u32[]{:S(2)}) collective-permute-start(bf16[32,3712]{1,0:T(8,128)(2,1)S(1)} %get-tuple-element.31), channel_id=1, source_target_pairs={{0,3},{1,2},{2,1},{3,0},{4,7},{5,6},{6,5},{7,4},{8,11},{9,10},{10,... | collective-permute-start | bytes 712712 | tf_op jit(solution)/shard_map/ppermute | solution.py:88
  30.3 6.2 %collective-permute-start.10 = (bf16[128,3584]{1,0:T(8,128)(2,1)S(1)}, bf16[128,3584]{1,0:T(8,128)(2,1)S(1)}, u32[]{:S(2)}, u32[]{:S(2)}) collective-permute-start(bf16[128,3584]{1,0:T(8,128)(2,1)S(1)} %get-tuple-element.33.refs_3_), channel_id=1, source_target_pairs={{0,4},{4,0},{8,12},{12,8},{16,20},{20,16},{24,28},{28,24},{1,5},{5... | collective-permute-start | bytes 2752520 | tf_op jit(solution)/shard_map/ppermute | solution.py:82
  36.5 2.9 %collective-permute-start.9 = (bf16[128,3712]{1,0:T(8,128)(2,1)S(1)}, bf16[128,3712]{1,0:T(8,128)(2,1)S(1)}, u32[]{:S(2)}, u32[]{:S(2)}) collective-permute-start(bf16[128,3712]{1,0:T(8,128)(2,1)S(1)} %combine.9.own), channel_id=1, source_target_pairs={{0,4},{4,0},{8,12},{12,8},{16,20},{20,16},{24,28},{28,24},{1,5},{5... | collective-permute-start | bytes 2850824 | tf_op jit(solution)/shard_map/ppermute | solution.py:82
  37.2 8.1 %collective-permute-start.14 = (bf16[32,3584]{1,0:T(8,128)(2,1)S(1)}, bf16[32,3584]{1,0:T(8,128)(2,1)S(1)}, u32[]{:S(2)}, u32[]{:S(2)}) collective-permute-start(bf16[32,3584]{1,0:T(8,128)(2,1)S(1)} %get-tuple-element.43), channel_id=1, source_target_pairs={{0,1},{1,0},{2,3},{3,2},{4,5},{5,4},{6,7},{7,6},{8,9},{9,8},{10,11... | collective-permute-start | bytes 688136 | tf_op jit(solution)/shard_map/ppermute | solution.py:82
  38.5 7.7 %collective-permute-start.15 = (bf16[32,3584]{1,0:T(8,128)(2,1)S(1)}, bf16[32,3584]{1,0:T(8,128)(2,1)S(1)}, u32[]{:S(2)}, u32[]{:S(2)}) collective-permute-start(bf16[32,3584]{1,0:T(8,128)(2,1)S(1)} %get-tuple-element.44), channel_id=1, source_target_pairs={{0,2},{1,3},{2,0},{3,1},{4,6},{5,7},{6,4},{7,5},{8,10},{9,11},{10,... | collective-permute-start | bytes 688136 | tf_op jit(solution)/shard_map/ppermute | solution.py:82
  42.0 4.3 %collective-permute-start.13 = (bf16[64,3584]{1,0:T(8,128)(2,1)S(1)}, bf16[64,3584]{1,0:T(8,128)(2,1)S(1)}, u32[]{:S(2)}, u32[]{:S(2)}) collective-permute-start(bf16[64,3584]{1,0:T(8,128)(2,1)S(1)} %get-tuple-element.42), channel_id=1, source_target_pairs={{0,4},{4,0},{8,12},{12,8},{16,20},{20,16},{24,28},{28,24},{1,5},{5... | collective-permute-start | bytes 1376264 | tf_op jit(solution)/shard_map/ppermute | solution.py:82
  42.1 4.2 %collective-permute-start.11 = (bf16[32,3584]{1,0:T(8,128)(2,1)S(1)}, bf16[32,3584]{1,0:T(8,128)(2,1)S(1)}, u32[]{:S(2)}, u32[]{:S(2)}) collective-permute-start(bf16[32,3584]{1,0:T(8,128)(2,1)S(1)} %get-tuple-element.40), channel_id=1, source_target_pairs={{0,4},{4,0},{8,12},{12,8},{16,20},{20,16},{24,28},{28,24},{1,5},{5... | collective-permute-start | bytes 688136 | tf_op jit(solution)/shard_map/ppermute | solution.py:82
  42.6 3.8 %collective-permute-start.12 = (bf16[32,3584]{1,0:T(8,128)(2,1)S(1)}, bf16[32,3584]{1,0:T(8,128)(2,1)S(1)}, u32[]{:S(2)}, u32[]{:S(2)}) collective-permute-start(bf16[32,3584]{1,0:T(8,128)(2,1)S(1)} %get-tuple-element.41), channel_id=1, source_target_pairs={{0,4},{4,0},{8,12},{12,8},{16,20},{20,16},{24,28},{28,24},{1,5},{5... | collective-permute-start | bytes 688136 | tf_op jit(solution)/shard_map/ppermute | solution.py:82
  46.3 6.7 %copy-start = (bf16[4,256,576]{1,2,0:T(8,128)(2,1)S(1)}, bf16[4,256,576]{1,2,0:T(8,128)(2,1)}, u32[]{:S(2)}) copy-start(bf16[4,256,576]{1,2,0:T(8,128)(2,1)} %param.11) | copy-start | bytes 3538948
  47.0 8.7 %collective-permute-start.17 = (bf16[32,3584]{1,0:T(8,128)(2,1)S(1)}, bf16[32,3584]{1,0:T(8,128)(2,1)S(1)}, u32[]{:S(2)}, u32[]{:S(2)}) collective-permute-start(bf16[32,3584]{1,0:T(8,128)(2,1)S(1)} %get-tuple-element.45.refs_0_), channel_id=1, source_target_pairs={{0,1},{1,0},{2,3},{3,2},{4,5},{5,4},{6,7},{7,6},{8,9},{9,8},{10,11... | collective-permute-start | bytes 688136 | tf_op jit(solution)/shard_map/ppermute | solution.py:82
  47.9 16.4 %collective-permute-start.18 = (bf16[32,3584]{1,0:T(8,128)(2,1)S(1)}, bf16[32,3584]{1,0:T(8,128)(2,1)S(1)}, u32[]{:S(2)}, u32[]{:S(2)}) collective-permute-start(bf16[32,3584]{1,0:T(8,128)(2,1)S(1)} %get-tuple-element.49), channel_id=1, source_target_pairs={{0,2},{1,3},{2,0},{3,1},{4,6},{5,7},{6,4},{7,5},{8,10},{9,11},{10,... | collective-permute-start | bytes 688136 | tf_op jit(solution)/shard_map/ppermute | solution.py:82
  49.4 14.9 %collective-permute-start.19 = (bf16[32,3584]{1,0:T(8,128)(2,1)S(1)}, bf16[32,3584]{1,0:T(8,128)(2,1)S(1)}, u32[]{:S(2)}, u32[]{:S(2)}) collective-permute-start(bf16[32,3584]{1,0:T(8,128)(2,1)S(1)} %get-tuple-element.50), channel_id=1, source_target_pairs={{0,3},{1,2},{2,1},{3,0},{4,7},{5,6},{6,5},{7,4},{8,11},{9,10},{10,... | collective-permute-start | bytes 688136 | tf_op jit(solution)/shard_map/ppermute | solution.py:88
  50.6 13.9 %collective-permute-start.16 = (bf16[32,3584]{1,0:T(8,128)(2,1)S(1)}, bf16[32,3584]{1,0:T(8,128)(2,1)S(1)}, u32[]{:S(2)}, u32[]{:S(2)}) collective-permute-start(bf16[32,3584]{1,0:T(8,128)(2,1)S(1)} %get-tuple-element.47), channel_id=1, source_target_pairs={{0,3},{1,2},{2,1},{3,0},{4,7},{5,6},{6,5},{7,4},{8,11},{9,10},{10,... | collective-permute-start | bytes 688136 | tf_op jit(solution)/shard_map/ppermute | solution.py:88
  64.5 7.5 %collective-permute-start.20 = (bf16[16,3584]{1,0:T(8,128)(2,1)S(1)}, bf16[16,3584]{1,0:T(8,128)(2,1)S(1)}, u32[]{:S(2)}, u32[]{:S(2)}) collective-permute-start(bf16[16,3584]{1,0:T(8,128)(2,1)S(1)} %get-tuple-element.52.refs_2_), channel_id=1, source_target_pairs={{0,16},{4,20},{8,24},{12,28},{16,0},{20,4},{24,8},{28,12},{1,17},{... | collective-permute-start | bytes 344072 | tf_op jit(solution)/shard_map/ppermute | solution.py:82
  64.6 5.9 %collective-permute-start.22 = (bf16[16,3584]{1,0:T(8,128)(2,1)S(1)}, bf16[16,3584]{1,0:T(8,128)(2,1)S(1)}, u32[]{:S(2)}, u32[]{:S(2)}) collective-permute-start(bf16[16,3584]{1,0:T(8,128)(2,1)S(1)} %get-tuple-element.55), channel_id=1, source_target_pairs={{0,8},{4,12},{8,0},{12,4},{16,24},{20,28},{24,16},{28,20},{1,9},{5... | collective-permute-start | bytes 344072 | tf_op jit(solution)/shard_map/ppermute | solution.py:82
  66.7 6.7 %collective-permute-start.21 = (bf16[16,3584]{1,0:T(8,128)(2,1)S(1)}, bf16[16,3584]{1,0:T(8,128)(2,1)S(1)}, u32[]{:S(2)}, u32[]{:S(2)}) collective-permute-start(bf16[16,3584]{1,0:T(8,128)(2,1)S(1)} %get-tuple-element.54), channel_id=1, source_target_pairs={{0,24},{4,28},{8,16},{12,20},{16,8},{20,12},{24,0},{28,4},{1,25},{... | collective-permute-start | bytes 344072 | tf_op jit(solution)/shard_map/ppermute | solution.py:88
  (5 other events, 15.6 us)

commit v9 on v8

--- a/solution.py
+++ b/solution.py
@@ -13,8 +13,8 @@
 BLOCKS = 4
 TILE = 256
 WIDE = 512
-GROUPS = 4
 NEAR_FLOPS = 4 * 10**9
+FAR_FLOPS = 4 * 10**9
 VMEM_BYTES = 48 * 1024 * 1024
 LARGE_BYTES = 16 * 1024 * 1024
 SMALL_BYTES = 8 * 1024 * 1024
@@ -118,11 +118,12 @@
     return total.astype(jnp.bfloat16)
 
 
-def pack_kernel(tokens, ids, gates, out):
+def pack_kernel(tokens, chosen, out):
     feature = tokens.shape[1]
-    high = gates[...].astype(jnp.bfloat16).astype(jnp.float32)
-    low = gates[...] - high
-    stacked = jnp.concatenate([ids[...].astype(jnp.float32), high, low], axis=0)
+    picks = chosen.shape[0] // 2
+    gates = chosen[picks:, :]
+    high = gates.astype(jnp.bfloat16).astype(jnp.float32)
+    stacked = jnp.concatenate([chosen[:picks, :], high, gates - high], axis=0)
     stacked = stacked.astype(jnp.bfloat16)
     row = lax.broadcasted_iota(jnp.int32, (stacked.shape[0], EXTRA), 0)
     column = lax.broadcasted_iota(jnp.int32, (stacked.shape[0], EXTRA), 1)
@@ -138,11 +139,11 @@
     return pl.pallas_call(
         pack_kernel,
         out_shape=jax.ShapeDtypeStruct((tokens.shape[0], tokens.shape[1] + EXTRA), jnp.bfloat16),
-        in_specs=[whole] * 3,
+        in_specs=[whole] * 2,
         out_specs=whole,
         compiler_params=pltpu.CompilerParams(vmem_limit_bytes=SMALL_BYTES),
         name="pack",
-    )(tokens, ids.T, gates.T)
+    )(tokens, jnp.concatenate([ids.T.astype(jnp.float32), gates.T], axis=0))
 
 
 def expert_index():
@@ -406,13 +407,11 @@
     )(own, other, w_gate, w_up, w_down, *after)
 
 
-def sums_kernel(parts, hidden, w_down, *refs):
-    arrived, outs = refs[:parts], refs[len(refs) - GROUPS :]
+def sums_kernel(parts, groups, hidden, w_down, *refs):
+    arrived, outs = refs[:parts], refs[len(refs) - groups :]
     feature = w_down.shape[2]
-    cut = hidden.shape[0] // GROUPS
-    places = [
-        (term, top) for term in arrived for top in range(0, term.shape[0], cut)
-    ]
+    cut = hidden.shape[0] // groups
+    places = [(term, top) for term in arrived for top in range(0, term.shape[0], cut)]
     for column in range(0, feature, 2 * TILE):
         span = slice(column, column + 2 * TILE)
         part = jnp.dot(hidden[...], w_down[0, :, span], preferred_element_type=jnp.float32)
@@ -422,14 +421,15 @@
             out[:, span] = (own + other).astype(jnp.bfloat16)
 
 
-def sums_of(hidden, w_down, arrived, after=()):
+def sums_of(hidden, w_down, arrived, cut, after=()):
     count, half = hidden.shape
     feature = w_down.shape[2]
-    return pl.pallas_call(
-        functools.partial(sums_kernel, len(arrived)),
-        out_shape=[jax.ShapeDtypeStruct((count // GROUPS, feature), jnp.bfloat16)] * GROUPS,
+    groups = count // cut
+    return pl.pallas_call(
+        functools.partial(sums_kernel, len(arrived), groups),
+        out_shape=[jax.ShapeDtypeStruct((cut, feature), jnp.bfloat16)] * groups,
         in_specs=[whole] * (2 + len(arrived)) + [pl.BlockSpec(memory_space=pl.ANY)] * len(after),
-        out_specs=[whole] * GROUPS,
+        out_specs=[whole] * groups,
         compiler_params=pltpu.CompilerParams(vmem_limit_bytes=SMALL_BYTES),
         cost_estimate=pl.CostEstimate(
             flops=2 * count * feature * half,
@@ -493,7 +493,7 @@
         ],
     )
     first_other = swap(first_own, core)
-    far_x, far_y, far_xy = swap(way_x, x), swap(way_y, y), across(far, x, y)
+    far_xy, far_x, far_y = across(far, x, y), swap(way_x, x), swap(way_y, y)
     first_h, first_out, *weights = first_of(first_own, first_other, *weights, picks, [8 * n])
     w_down = weights[2]
     first_in = swap(first_out, core)
@@ -503,7 +503,7 @@
         [first_out],
     )
     second_other = swap(second_own, core)
-    near, near_x, near_y, far = sums_of(first_h, w_down, [first_in])
+    near, near_x, near_y, far = sums_of(first_h, w_down, [first_in], 2 * n)
     to_near = [swap(near_x, x), swap(near_y, y)]
     second_h, *second_out = expert_of(
         second_own, second_other, *weights, picks, [2 * n, 2 * n, 4 * n], [near]
@@ -514,15 +514,18 @@
         return [(count, [(index, start) for index in range(terms)])]
 
     (near,) = combine([near, *to_near], [all_of(3, 0, 2 * n)], flops=NEAR_FLOPS)
-    far_x, far_y, far_xy, near_xy = sums_of(second_h, w_down, second_in, [near])
-
-    to_far = [swap(far_x, x), swap(far_y, y), across(far_xy, x, y)]
+    far_x, far_y, far_xy, near_xy = sums_of(second_h, w_down, second_in, 2 * n, [near])
+
+    to_far = [across(far_xy, x, y), swap(far_x, x), swap(far_y, y)]
+    context, done = attention([far_x])
+    (near_xy,) = combine([near_xy], [rows_of((0, 0, 2 * n))], [done])
     to_near = across(near_xy, x, y)
-    context, done = attention([far_x])
-    far_sum, both_sum = combine([far, *to_far], [all_of(4, 0), all_of(4, n)], [done])
+    far_sum, both_sum = combine([far, *to_far], [all_of(4, 0), all_of(4, n)], [near_xy])
     own_sum, near_sum = combine([near, to_near], [all_of(2, 0), all_of(2, n)], [far_sum])
-    terms = [swap(far_sum, z_far), across(both_sum, z_far, z_near), swap(near_sum, z_near)]
-    (mixed,) = combine([own_sum, *terms], [all_of(4, 0)])
+    (far_sum,) = combine(
+        [swap(far_sum, z_far), across(both_sum, z_far, z_near)], [all_of(2, 0)], flops=FAR_FLOPS
+    )
+    (mixed,) = combine([own_sum, far_sum, swap(near_sum, z_near)], [all_of(3, 0)])
     return mixed, context
 
 

time: 74.4 us -> 74.7 us (level)
  waiting for transfers between devices: 29.1 us -> 30.5 us
  other arithmetic: 0 us -> 1.38 us
  local copies, waits for them, and re-layouts: 2.28 us -> 0.92 us
  starting transfers between devices: 25.8 us -> 24.7 us
    ppermute x19, waiting for transfers between devices: 21.8 us -> 23.5 us  [swap(): return lax.ppermute(value, axis, [(i, i ^ bit) for i in range(size)])]
    unnamed x12 -> x8, local copies, waits for them, and re-layouts: 2.28 us -> 0.92 us
    ppermute x19, starting transfers between devices: 20.1 us -> 19.2 us  [swap(): return lax.ppermute(value, axis, [(i, i ^ bit) for i in range(size)])]
  transfers between devices with their start and end apart: 23 -> 23, of which waited for: 11 -> 13; matrix products, arithmetic and copies ran while one was open for 0% -> 0% of each run, Pallas kernels for 19% -> 19%
where the time goes in v9:
time: 74.7 us; the launch traced here: 74.5 us
  waiting for transfers between devices  30.5 us (41%)
  starting transfers between devices  24.7 us (33%)
  Pallas kernels  15.5 us (21%)
  between operations  1.47 us (2%)
  other arithmetic  1.38 us (2%)
  local copies, waits for them, and re-layouts  0.92 us (1%)
    ppermute x19, waiting for transfers between devices, swap(): return lax.ppermute(value, axis, [(i, i ^ bit) for i in range(size)])  23.5 us
    ppermute x19, starting transfers between devices, swap(): return lax.ppermute(value, axis, [(i, i ^ bit) for i in range(size)])  19.2 us
    pallas_call x1, Pallas kernels, first_of(): pl.pallas_call(functools.partial(first_kernel, picks), out_shape=[jax.Sha...  7.4 us
    ppermute x4, waiting for transfers between devices, across(): lax.ppermute(value, axis, [(i, i ^ first[1] ^ second[1]) for i in range(s...  7.01 us
    ppermute x4, starting transfers between devices, across(): lax.ppermute(value, axis, [(i, i ^ first[1] ^ second[1]) for i in range(s...  5.56 us
    pallas_call x1, Pallas kernels, attend(): pl.pallas_call(attend_kernel, out_shape=[jax.ShapeDtypeStruct((count, hea...  2.7 us
    pallas_call x1, Pallas kernels, expert_of(): pl.pallas_call(functools.partial(expert_kernel, picks, len(after)), out_s...  2.7 us
  transfers between devices with their start and end apart: 23, of which 13 were waited for; matrix products, arithmetic and copies ran while one was open for 0% of the time, Pallas kernels for 19%

profile of v9, /device:TPU:0, one launch (start us, length us, event | category | flops | bytes accessed | tf_op | source)
XLA Modules:
  0.0 74.5 jit_solution(12148485942775549712)
XLA Ops:
  2.0 0.9 %copy-done.2 = bf16[16,3584]{1,0:T(8,128)(2,1)S(1)} copy-done((bf16[16,3584]{1,0:T(8,128)(2,1)S(1)}, bf16[16,3584]{1,0:T(8,128)(2,1)}, u32[]{:S(2)}) %copy-start.2) | copy-done | bytes 114712
  3.1 3.0 %collective-permute-start = (bf16[16,3712]{1,0:T(8,128)(2,1)S(1)}, bf16[16,3712]{1,0:T(8,128)(2,1)S(1)}, u32[]{:S(2)}, u32[]{:S(2)}) collective-permute-start(bf16[16,3712]{1,0:T(8,128)(2,1)S(1)} %pack.1.refs_0_), channel_id=1, source_target_pairs={{0,8},{4,12},{8,0},{12,4},{16,24},{20,28},{24,16},{28,20},{1,9},{5... | collective-permute-start | bytes 356360 | tf_op jit(solution)/shard_map/ppermute | solution.py:82
  6.1 2.6 %collective-permute-start.3 = (bf16[16,3712]{1,0:T(8,128)(2,1)S(1)}, bf16[16,3712]{1,0:T(8,128)(2,1)S(1)}, u32[]{:S(2)}, u32[]{:S(2)}) collective-permute-start(bf16[16,3712]{1,0:T(8,128)(2,1)S(1)} %pack.1.refs_0_), channel_id=1, source_target_pairs={{0,16},{4,20},{8,24},{12,28},{16,0},{20,4},{24,8},{28,12},{1,17},{... | collective-permute-start | bytes 356360 | tf_op jit(solution)/shard_map/ppermute | solution.py:82
  8.7 1.9 %collective-permute-done.refs_1_ = bf16[16,3712]{1,0:T(8,128)(2,1)S(1)} collective-permute-done((bf16[16,3712]{1,0:T(8,128)(2,1)S(1)}, bf16[16,3712]{1,0:T(8,128)(2,1)S(1)}, u32[]{:S(2)}, u32[]{:S(2)}) %collective-permute-start) | collective-permute-done | bytes 118816 | tf_op jit(solution)/shard_map/ppermute | solution.py:82
  10.7 1.9 %collective-permute-start.1 = (bf16[32,3712]{1,0:T(8,128)(2,1)S(1)}, bf16[32,3712]{1,0:T(8,128)(2,1)S(1)}, u32[]{:S(2)}, u32[]{:S(2)}) collective-permute-start(bf16[32,3712]{1,0:T(8,128)(2,1)S(1)} %combine.9.refs_0_), channel_id=1, source_target_pairs={{0,1},{1,0},{2,3},{3,2},{4,5},{5,4},{6,7},{7,6},{8,9},{9,8},{10,11... | collective-permute-start | bytes 712712 | tf_op jit(solution)/shard_map/ppermute | solution.py:82
  12.6 1.5 %collective-permute-start.2 = (bf16[32,3712]{1,0:T(8,128)(2,1)S(1)}, bf16[32,3712]{1,0:T(8,128)(2,1)S(1)}, u32[]{:S(2)}, u32[]{:S(2)}) collective-permute-start(bf16[32,3712]{1,0:T(8,128)(2,1)S(1)} %combine.9.refs_0_), channel_id=1, source_target_pairs={{0,2},{1,3},{2,0},{3,1},{4,6},{5,7},{6,4},{7,5},{8,10},{9,11},{10,... | collective-permute-start | bytes 712712 | tf_op jit(solution)/shard_map/ppermute | solution.py:82
  14.7 4.4 %collective-permute-done.4.refs_4_ = bf16[16,3712]{1,0:T(8,128)(2,1)S(1)} collective-permute-done((bf16[16,3712]{1,0:T(8,128)(2,1)S(1)}, bf16[16,3712]{1,0:T(8,128)(2,1)S(1)}, u32[]{:S(2)}, u32[]{:S(2)}) %collective-permute-start.4) | collective-permute-done | bytes 118816 | tf_op jit(solution)/shard_map/ppermute | solution.py:82
  19.4 1.6 %collective-permute-start.5 = (bf16[48,3712]{1,0:T(8,128)(2,1)S(1)}, bf16[48,3712]{1,0:T(8,128)(2,1)S(1)}, u32[]{:S(2)}, u32[]{:S(2)}) collective-permute-start(bf16[48,3712]{1,0:T(8,128)(2,1)S(1)} %get-tuple-element.29), channel_id=1, source_target_pairs={{0,1},{1,0},{2,3},{3,2},{4,5},{5,4},{6,7},{7,6},{8,9},{9,8},{10,11... | collective-permute-start | bytes 1069064 | tf_op jit(solution)/shard_map/ppermute | solution.py:82
  20.9 1.5 %collective-permute-start.6 = (bf16[48,3712]{1,0:T(8,128)(2,1)S(1)}, bf16[48,3712]{1,0:T(8,128)(2,1)S(1)}, u32[]{:S(2)}, u32[]{:S(2)}) collective-permute-start(bf16[48,3712]{1,0:T(8,128)(2,1)S(1)} %get-tuple-element.30), channel_id=1, source_target_pairs={{0,2},{1,3},{2,0},{3,1},{4,6},{5,7},{6,4},{7,5},{8,10},{9,11},{10,... | collective-permute-start | bytes 1069064 | tf_op jit(solution)/shard_map/ppermute | solution.py:82
  22.9 7.4 %first.1 = (bf16[128,512]{1,0:T(8,128)(2,1)S(1)}, bf16[128,3584]{1,0:T(8,128)(2,1)S(1)}, bf16[1,3584,512]{2,1,0:T(8,128)(2,1)S(1)}, bf16[1,3584,512]{2,1,0:T(8,128)(2,1)S(1)}, bf16[1,512,3584]{2,1,0:T(8,128)(2,1)S(1)}) custom-call(bf16[128,3712]{1,0:T(8,128)(2,1)S(1)} %get-tuple-element.32.own, bf16[128,3712]{1,0:T(8,128)(2,1)S(1)} %collective-permute-done.8.other, ...), custom_call_target="tpu_custom_call" | custom-call | flops 2348810240 | bytes 11010048 | tf_op jit(solution)/shard_map/first/pallas_call | solution.py:365
  30.4 5.8 %collective-permute-done.7.refs_2_ = bf16[32,3712]{1,0:T(8,128)(2,1)S(1)} collective-permute-done((bf16[32,3712]{1,0:T(8,128)(2,1)S(1)}, bf16[32,3712]{1,0:T(8,128)(2,1)S(1)}, u32[]{:S(2)}, u32[]{:S(2)}) %collective-permute-start.7) | collective-permute-done | bytes 237600 | tf_op jit(solution)/shard_map/ppermute | solution.py:88
  37.2 1.3 %collective-permute-start.14 = (bf16[32,3584]{1,0:T(8,128)(2,1)S(1)}, bf16[32,3584]{1,0:T(8,128)(2,1)S(1)}, u32[]{:S(2)}, u32[]{:S(2)}) collective-permute-start(bf16[32,3584]{1,0:T(8,128)(2,1)S(1)} %get-tuple-element.43), channel_id=1, source_target_pairs={{0,1},{1,0},{2,3},{3,2},{4,5},{5,4},{6,7},{7,6},{8,9},{9,8},{10,11... | collective-permute-start | bytes 688136 | tf_op jit(solution)/shard_map/ppermute | solution.py:82
  39.3 2.7 %expert.1 = (bf16[128,512]{1,0:T(8,128)(2,1)S(1)}, bf16[32,3584]{1,0:T(8,128)(2,1)S(1)}, bf16[32,3584]{1,0:T(8,128)(2,1)S(1)}, bf16[64,3584]{1,0:T(8,128)(2,1)S(1)}) custom-call(bf16[128,3712]{1,0:T(8,128)(2,1)S(1)} %combine.11.own, bf16[128,3712]{1,0:T(8,128)(2,1)S(1)} %collective-permute-done.9.other, bf16[1,3584,512]{2,1,0:T(8,128)(2,1)S(1)} %get-tuple-element.34.w_gate, ...), custom_call_target="tpu_custom_call" | custom-call | flops 2348810240 | bytes 917504 | tf_op jit(solution)/shard_map/expert/pallas_call | solution.py:390
  42.7 2.6 %collective-permute-done.14.refs_1_ = bf16[32,3584]{1,0:T(8,128)(2,1)S(1)} collective-permute-done((bf16[32,3584]{1,0:T(8,128)(2,1)S(1)}, bf16[32,3584]{1,0:T(8,128)(2,1)S(1)}, u32[]{:S(2)}, u32[]{:S(2)}) %collective-permute-start.14) | collective-permute-done | bytes 229408 | tf_op jit(solution)/shard_map/ppermute | solution.py:82
  45.3 1.0 %collective-permute-done.15.refs_2_ = bf16[32,3584]{1,0:T(8,128)(2,1)S(1)} collective-permute-done((bf16[32,3584]{1,0:T(8,128)(2,1)S(1)}, bf16[32,3584]{1,0:T(8,128)(2,1)S(1)}, u32[]{:S(2)}, u32[]{:S(2)}) %collective-permute-start.15) | collective-permute-done | bytes 229408 | tf_op jit(solution)/shard_map/ppermute | solution.py:82
  47.0 1.8 %collective-permute-start.17 = (bf16[32,3584]{1,0:T(8,128)(2,1)S(1)}, bf16[32,3584]{1,0:T(8,128)(2,1)S(1)}, u32[]{:S(2)}, u32[]{:S(2)}) collective-permute-start(bf16[32,3584]{1,0:T(8,128)(2,1)S(1)} %get-tuple-element.50), channel_id=1, source_target_pairs={{0,3},{1,2},{2,1},{3,0},{4,7},{5,6},{6,5},{7,4},{8,11},{9,10},{10,... | collective-permute-start | bytes 688136 | tf_op jit(solution)/shard_map/ppermute | solution.py:88
  49.4 1.2 %collective-permute-start.19 = (bf16[32,3584]{1,0:T(8,128)(2,1)S(1)}, bf16[32,3584]{1,0:T(8,128)(2,1)S(1)}, u32[]{:S(2)}, u32[]{:S(2)}) collective-permute-start(bf16[32,3584]{1,0:T(8,128)(2,1)S(1)} %get-tuple-element.51), channel_id=1, source_target_pairs={{0,2},{1,3},{2,0},{3,1},{4,6},{5,7},{6,4},{7,5},{8,10},{9,11},{10,... | collective-permute-start | bytes 688136 | tf_op jit(solution)/shard_map/ppermute | solution.py:82
  51.3 2.7 %attend.1 = (bf16[4,64,512]{2,1,0:T(8,128)(2,1)}, f32[8,128]{1,0:T(8,128)S(1)}) custom-call(s32[4]{0:T(128)S(1)} %copy-done.3, s32[1]{0:T(128)S(6)} %copy.12.live_rows, bf16[4,64,576]{2,1,0:T(8,128)(2,1)S(1)} %copy-done.1, bf16[4,576,256]{2,1,0:T(8,128)(2,1)S(1)} %bitcast.4, bf16[32,3584]{1,0:T(8,128)(2,1)S(1)} %get-tuple-element.45.refs_0_), custom_call_target="tpu_custom_call" | custom-call | flops 150994944 | bytes 1179648 | tf_op jit(solution)/shard_map/attend/pallas_call | solution.py:55
  54.0 1.8 %collective-permute-start.16 = (bf16[32,3584]{1,0:T(8,128)(2,1)S(1)}, bf16[32,3584]{1,0:T(8,128)(2,1)S(1)}, u32[]{:S(2)}, u32[]{:S(2)}) collective-permute-start(bf16[32,3584]{1,0:T(8,128)(2,1)S(1)} %combine.13.refs_4_), channel_id=1, source_target_pairs={{0,3},{1,2},{2,1},{3,0},{4,7},{5,6},{6,5},{7,4},{8,11},{9,10},{10,... | collective-permute-start | bytes 688136 | tf_op jit(solution)/shard_map/ppermute | solution.py:88
  56.6 4.3 %collective-permute-done.18.refs_2_ = bf16[32,3584]{1,0:T(8,128)(2,1)S(1)} collective-permute-done((bf16[32,3584]{1,0:T(8,128)(2,1)S(1)}, bf16[32,3584]{1,0:T(8,128)(2,1)S(1)}, u32[]{:S(2)}, u32[]{:S(2)}) %collective-permute-start.18) | collective-permute-done | bytes 229408 | tf_op jit(solution)/shard_map/ppermute | solution.py:82
  61.5 1.4 %collective-permute-start.20 = (bf16[16,3584]{1,0:T(8,128)(2,1)S(1)}, bf16[16,3584]{1,0:T(8,128)(2,1)S(1)}, u32[]{:S(2)}, u32[]{:S(2)}) collective-permute-start(bf16[16,3584]{1,0:T(8,128)(2,1)S(1)} %get-tuple-element.52.refs_2_), channel_id=1, source_target_pairs={{0,16},{4,20},{8,24},{12,28},{16,0},{20,4},{24,8},{28,12},{1,17},{... | collective-permute-start | bytes 344072 | tf_op jit(solution)/shard_map/ppermute | solution.py:82
  62.9 1.5 %collective-permute-start.21 = (bf16[16,3584]{1,0:T(8,128)(2,1)S(1)}, bf16[16,3584]{1,0:T(8,128)(2,1)S(1)}, u32[]{:S(2)}, u32[]{:S(2)}) collective-permute-start(bf16[16,3584]{1,0:T(8,128)(2,1)S(1)} %get-tuple-element.54), channel_id=1, source_target_pairs={{0,24},{4,28},{8,16},{12,20},{16,8},{20,12},{24,0},{28,4},{1,25},{... | collective-permute-start | bytes 344072 | tf_op jit(solution)/shard_map/ppermute | solution.py:88
  65.3 7.1 %collective-permute-done.20.refs_0_ = bf16[16,3584]{1,0:T(8,128)(2,1)S(1)} collective-permute-done((bf16[16,3584]{1,0:T(8,128)(2,1)S(1)}, bf16[16,3584]{1,0:T(8,128)(2,1)S(1)}, u32[]{:S(2)}, u32[]{:S(2)}) %collective-permute-start.20) | collective-permute-done | bytes 114720 | tf_op jit(solution)/shard_map/ppermute | solution.py:82
  72.4 1.3 %collective-permute-done.22.refs_2_ = bf16[16,3584]{1,0:T(8,128)(2,1)S(1)} collective-permute-done((bf16[16,3584]{1,0:T(8,128)(2,1)S(1)}, bf16[16,3584]{1,0:T(8,128)(2,1)S(1)}, u32[]{:S(2)}, u32[]{:S(2)}) %collective-permute-start.22) | collective-permute-done | bytes 114720 | tf_op jit(solution)/shard_map/ppermute | solution.py:82
  (47 shorter events, 9.8 us)
Async XLA Ops:
  3.1 7.6 %collective-permute-start = (bf16[16,3712]{1,0:T(8,128)(2,1)S(1)}, bf16[16,3712]{1,0:T(8,128)(2,1)S(1)}, u32[]{:S(2)}, u32[]{:S(2)}) collective-permute-start(bf16[16,3712]{1,0:T(8,128)(2,1)S(1)} %pack.1.refs_0_), channel_id=1, source_target_pairs={{0,8},{4,12},{8,0},{12,4},{16,24},{20,28},{24,16},{28,20},{1,9},{5... | collective-permute-start | bytes 356360 | tf_op jit(solution)/shard_map/ppermute | solution.py:82
  6.1 8.2 %collective-permute-start.3 = (bf16[16,3712]{1,0:T(8,128)(2,1)S(1)}, bf16[16,3712]{1,0:T(8,128)(2,1)S(1)}, u32[]{:S(2)}, u32[]{:S(2)}) collective-permute-start(bf16[16,3712]{1,0:T(8,128)(2,1)S(1)} %pack.1.refs_0_), channel_id=1, source_target_pairs={{0,16},{4,20},{8,24},{12,28},{16,0},{20,4},{24,8},{28,12},{1,17},{... | collective-permute-start | bytes 356360 | tf_op jit(solution)/shard_map/ppermute | solution.py:82
  10.7 8.5 %collective-permute-start.1 = (bf16[32,3712]{1,0:T(8,128)(2,1)S(1)}, bf16[32,3712]{1,0:T(8,128)(2,1)S(1)}, u32[]{:S(2)}, u32[]{:S(2)}) collective-permute-start(bf16[32,3712]{1,0:T(8,128)(2,1)S(1)} %combine.9.refs_0_), channel_id=1, source_target_pairs={{0,1},{1,0},{2,3},{3,2},{4,5},{5,4},{6,7},{7,6},{8,9},{9,8},{10,11... | collective-permute-start | bytes 712712 | tf_op jit(solution)/shard_map/ppermute | solution.py:82
  12.6 6.6 %collective-permute-start.2 = (bf16[32,3712]{1,0:T(8,128)(2,1)S(1)}, bf16[32,3712]{1,0:T(8,128)(2,1)S(1)}, u32[]{:S(2)}, u32[]{:S(2)}) collective-permute-start(bf16[32,3712]{1,0:T(8,128)(2,1)S(1)} %combine.9.refs_0_), channel_id=1, source_target_pairs={{0,2},{1,3},{2,0},{3,1},{4,6},{5,7},{6,4},{7,5},{8,10},{9,11},{10,... | collective-permute-start | bytes 712712 | tf_op jit(solution)/shard_map/ppermute | solution.py:82
  14.3 4.8 %collective-permute-start.4 = (bf16[16,3712]{1,0:T(8,128)(2,1)S(1)}, bf16[16,3712]{1,0:T(8,128)(2,1)S(1)}, u32[]{:S(2)}, u32[]{:S(2)}) collective-permute-start(bf16[16,3712]{1,0:T(8,128)(2,1)S(1)} %collective-permute-done.3.refs_3_), channel_id=1, source_target_pairs={{0,8},{4,12},{8,0},{12,4},{16,24},{20,28},{24,16},{28,20},{1,9},{5... | collective-permute-start | bytes 356360 | tf_op jit(solution)/shard_map/ppermute | solution.py:82
  19.3 3.6 %collective-permute-start.8 = (bf16[128,3712]{1,0:T(8,128)(2,1)S(1)}, bf16[128,3712]{1,0:T(8,128)(2,1)S(1)}, u32[]{:S(2)}, u32[]{:S(2)}) collective-permute-start(bf16[128,3712]{1,0:T(8,128)(2,1)S(1)} %get-tuple-element.32.own), channel_id=1, source_target_pairs={{0,4},{4,0},{8,12},{12,8},{16,20},{20,16},{24,28},{28,24},{1,5},{5... | collective-permute-start | bytes 2850824 | tf_op jit(solution)/shard_map/ppermute | solution.py:82
  19.4 16.9 %collective-permute-start.5 = (bf16[48,3712]{1,0:T(8,128)(2,1)S(1)}, bf16[48,3712]{1,0:T(8,128)(2,1)S(1)}, u32[]{:S(2)}, u32[]{:S(2)}) collective-permute-start(bf16[48,3712]{1,0:T(8,128)(2,1)S(1)} %get-tuple-element.29), channel_id=1, source_target_pairs={{0,1},{1,0},{2,3},{3,2},{4,5},{5,4},{6,7},{7,6},{8,9},{9,8},{10,11... | collective-permute-start | bytes 1069064 | tf_op jit(solution)/shard_map/ppermute | solution.py:82
  20.9 15.5 %collective-permute-start.6 = (bf16[48,3712]{1,0:T(8,128)(2,1)S(1)}, bf16[48,3712]{1,0:T(8,128)(2,1)S(1)}, u32[]{:S(2)}, u32[]{:S(2)}) collective-permute-start(bf16[48,3712]{1,0:T(8,128)(2,1)S(1)} %get-tuple-element.30), channel_id=1, source_target_pairs={{0,2},{1,3},{2,0},{3,1},{4,6},{5,7},{6,4},{7,5},{8,10},{9,11},{10,... | collective-permute-start | bytes 1069064 | tf_op jit(solution)/shard_map/ppermute | solution.py:82
  22.4 13.8 %collective-permute-start.7 = (bf16[32,3712]{1,0:T(8,128)(2,1)S(1)}, bf16[32,3712]{1,0:T(8,128)(2,1)S(1)}, u32[]{:S(2)}, u32[]{:S(2)}) collective-permute-start(bf16[32,3712]{1,0:T(8,128)(2,1)S(1)} %get-tuple-element.31), channel_id=1, source_target_pairs={{0,3},{1,2},{2,1},{3,0},{4,7},{5,6},{6,5},{7,4},{8,11},{9,10},{10,... | collective-permute-start | bytes 712712 | tf_op jit(solution)/shard_map/ppermute | solution.py:88
  30.3 6.2 %collective-permute-start.10 = (bf16[128,3584]{1,0:T(8,128)(2,1)S(1)}, bf16[128,3584]{1,0:T(8,128)(2,1)S(1)}, u32[]{:S(2)}, u32[]{:S(2)}) collective-permute-start(bf16[128,3584]{1,0:T(8,128)(2,1)S(1)} %get-tuple-element.33.refs_3_), channel_id=1, source_target_pairs={{0,4},{4,0},{8,12},{12,8},{16,20},{20,16},{24,28},{28,24},{1,5},{5... | collective-permute-start | bytes 2752520 | tf_op jit(solution)/shard_map/ppermute | solution.py:82
  36.5 2.9 %collective-permute-start.9 = (bf16[128,3712]{1,0:T(8,128)(2,1)S(1)}, bf16[128,3712]{1,0:T(8,128)(2,1)S(1)}, u32[]{:S(2)}, u32[]{:S(2)}) collective-permute-start(bf16[128,3712]{1,0:T(8,128)(2,1)S(1)} %combine.11.own), channel_id=1, source_target_pairs={{0,4},{4,0},{8,12},{12,8},{16,20},{20,16},{24,28},{28,24},{1,5},{5... | collective-permute-start | bytes 2850824 | tf_op jit(solution)/shard_map/ppermute | solution.py:82
  37.2 8.1 %collective-permute-start.14 = (bf16[32,3584]{1,0:T(8,128)(2,1)S(1)}, bf16[32,3584]{1,0:T(8,128)(2,1)S(1)}, u32[]{:S(2)}, u32[]{:S(2)}) collective-permute-start(bf16[32,3584]{1,0:T(8,128)(2,1)S(1)} %get-tuple-element.43), channel_id=1, source_target_pairs={{0,1},{1,0},{2,3},{3,2},{4,5},{5,4},{6,7},{7,6},{8,9},{9,8},{10,11... | collective-permute-start | bytes 688136 | tf_op jit(solution)/shard_map/ppermute | solution.py:82
  38.5 7.7 %collective-permute-start.15 = (bf16[32,3584]{1,0:T(8,128)(2,1)S(1)}, bf16[32,3584]{1,0:T(8,128)(2,1)S(1)}, u32[]{:S(2)}, u32[]{:S(2)}) collective-permute-start(bf16[32,3584]{1,0:T(8,128)(2,1)S(1)} %get-tuple-element.44), channel_id=1, source_target_pairs={{0,2},{1,3},{2,0},{3,1},{4,6},{5,7},{6,4},{7,5},{8,10},{9,11},{10,... | collective-permute-start | bytes 688136 | tf_op jit(solution)/shard_map/ppermute | solution.py:82
  42.0 4.3 %collective-permute-start.13 = (bf16[64,3584]{1,0:T(8,128)(2,1)S(1)}, bf16[64,3584]{1,0:T(8,128)(2,1)S(1)}, u32[]{:S(2)}, u32[]{:S(2)}) collective-permute-start(bf16[64,3584]{1,0:T(8,128)(2,1)S(1)} %get-tuple-element.42), channel_id=1, source_target_pairs={{0,4},{4,0},{8,12},{12,8},{16,20},{20,16},{24,28},{28,24},{1,5},{5... | collective-permute-start | bytes 1376264 | tf_op jit(solution)/shard_map/ppermute | solution.py:82
  42.1 4.2 %collective-permute-start.11 = (bf16[32,3584]{1,0:T(8,128)(2,1)S(1)}, bf16[32,3584]{1,0:T(8,128)(2,1)S(1)}, u32[]{:S(2)}, u32[]{:S(2)}) collective-permute-start(bf16[32,3584]{1,0:T(8,128)(2,1)S(1)} %get-tuple-element.40), channel_id=1, source_target_pairs={{0,4},{4,0},{8,12},{12,8},{16,20},{20,16},{24,28},{28,24},{1,5},{5... | collective-permute-start | bytes 688136 | tf_op jit(solution)/shard_map/ppermute | solution.py:82
  42.6 3.8 %collective-permute-start.12 = (bf16[32,3584]{1,0:T(8,128)(2,1)S(1)}, bf16[32,3584]{1,0:T(8,128)(2,1)S(1)}, u32[]{:S(2)}, u32[]{:S(2)}) collective-permute-start(bf16[32,3584]{1,0:T(8,128)(2,1)S(1)} %get-tuple-element.41), channel_id=1, source_target_pairs={{0,4},{4,0},{8,12},{12,8},{16,20},{20,16},{24,28},{28,24},{1,5},{5... | collective-permute-start | bytes 688136 | tf_op jit(solution)/shard_map/ppermute | solution.py:82
  46.3 4.9 %copy-start = (bf16[4,256,576]{1,2,0:T(8,128)(2,1)S(1)}, bf16[4,256,576]{1,2,0:T(8,128)(2,1)}, u32[]{:S(2)}) copy-start(bf16[4,256,576]{1,2,0:T(8,128)(2,1)} %param.11) | copy-start | bytes 3538948
  47.0 9.6 %collective-permute-start.17 = (bf16[32,3584]{1,0:T(8,128)(2,1)S(1)}, bf16[32,3584]{1,0:T(8,128)(2,1)S(1)}, u32[]{:S(2)}, u32[]{:S(2)}) collective-permute-start(bf16[32,3584]{1,0:T(8,128)(2,1)S(1)} %get-tuple-element.50), channel_id=1, source_target_pairs={{0,3},{1,2},{2,1},{3,0},{4,7},{5,6},{6,5},{7,4},{8,11},{9,10},{10,... | collective-permute-start | bytes 688136 | tf_op jit(solution)/shard_map/ppermute | solution.py:88
  48.9 12.0 %collective-permute-start.18 = (bf16[32,3584]{1,0:T(8,128)(2,1)S(1)}, bf16[32,3584]{1,0:T(8,128)(2,1)S(1)}, u32[]{:S(2)}, u32[]{:S(2)}) collective-permute-start(bf16[32,3584]{1,0:T(8,128)(2,1)S(1)} %get-tuple-element.45.refs_0_), channel_id=1, source_target_pairs={{0,1},{1,0},{2,3},{3,2},{4,5},{5,4},{6,7},{7,6},{8,9},{9,8},{10,11... | collective-permute-start | bytes 688136 | tf_op jit(solution)/shard_map/ppermute | solution.py:82
  49.4 12.0 %collective-permute-start.19 = (bf16[32,3584]{1,0:T(8,128)(2,1)S(1)}, bf16[32,3584]{1,0:T(8,128)(2,1)S(1)}, u32[]{:S(2)}, u32[]{:S(2)}) collective-permute-start(bf16[32,3584]{1,0:T(8,128)(2,1)S(1)} %get-tuple-element.51), channel_id=1, source_target_pairs={{0,2},{1,3},{2,0},{3,1},{4,6},{5,7},{6,4},{7,5},{8,10},{9,11},{10,... | collective-permute-start | bytes 688136 | tf_op jit(solution)/shard_map/ppermute | solution.py:82
  54.0 10.8 %collective-permute-start.16 = (bf16[32,3584]{1,0:T(8,128)(2,1)S(1)}, bf16[32,3584]{1,0:T(8,128)(2,1)S(1)}, u32[]{:S(2)}, u32[]{:S(2)}) collective-permute-start(bf16[32,3584]{1,0:T(8,128)(2,1)S(1)} %combine.13.refs_4_), channel_id=1, source_target_pairs={{0,3},{1,2},{2,1},{3,0},{4,7},{5,6},{6,5},{7,4},{8,11},{9,10},{10,... | collective-permute-start | bytes 688136 | tf_op jit(solution)/shard_map/ppermute | solution.py:88
  61.5 10.9 %collective-permute-start.20 = (bf16[16,3584]{1,0:T(8,128)(2,1)S(1)}, bf16[16,3584]{1,0:T(8,128)(2,1)S(1)}, u32[]{:S(2)}, u32[]{:S(2)}) collective-permute-start(bf16[16,3584]{1,0:T(8,128)(2,1)S(1)} %get-tuple-element.52.refs_2_), channel_id=1, source_target_pairs={{0,16},{4,20},{8,24},{12,28},{16,0},{20,4},{24,8},{28,12},{1,17},{... | collective-permute-start | bytes 344072 | tf_op jit(solution)/shard_map/ppermute | solution.py:82
  62.9 9.5 %collective-permute-start.21 = (bf16[16,3584]{1,0:T(8,128)(2,1)S(1)}, bf16[16,3584]{1,0:T(8,128)(2,1)S(1)}, u32[]{:S(2)}, u32[]{:S(2)}) collective-permute-start(bf16[16,3584]{1,0:T(8,128)(2,1)S(1)} %get-tuple-element.54), channel_id=1, source_target_pairs={{0,24},{4,28},{8,16},{12,20},{16,8},{20,12},{24,0},{28,4},{1,25},{... | collective-permute-start | bytes 344072 | tf_op jit(solution)/shard_map/ppermute | solution.py:88
  64.8 8.9 %collective-permute-start.22 = (bf16[16,3584]{1,0:T(8,128)(2,1)S(1)}, bf16[16,3584]{1,0:T(8,128)(2,1)S(1)}, u32[]{:S(2)}, u32[]{:S(2)}) collective-permute-start(bf16[16,3584]{1,0:T(8,128)(2,1)S(1)} %get-tuple-element.55), channel_id=1, source_target_pairs={{0,8},{4,12},{8,0},{12,4},{16,24},{20,28},{24,16},{28,20},{1,9},{5... | collective-permute-start | bytes 344072 | tf_op jit(solution)/shard_map/ppermute | solution.py:82
  (3 other events, 10.8 us)

commit v10 on v9

--- a/solution.py
+++ b/solution.py
@@ -407,29 +407,28 @@
     )(own, other, w_gate, w_up, w_down, *after)
 
 
-def sums_kernel(parts, groups, hidden, w_down, *refs):
-    arrived, outs = refs[:parts], refs[len(refs) - groups :]
+def sums_kernel(parts, cuts, hidden, w_down, *refs):
+    arrived, outs = refs[:parts], refs[len(refs) - len(cuts) :]
     feature = w_down.shape[2]
-    cut = hidden.shape[0] // groups
-    places = [(term, top) for term in arrived for top in range(0, term.shape[0], cut)]
     for column in range(0, feature, 2 * TILE):
         span = slice(column, column + 2 * TILE)
         part = jnp.dot(hidden[...], w_down[0, :, span], preferred_element_type=jnp.float32)
-        for number, ((term, top), out) in enumerate(zip(places, outs)):
-            own = part[number * cut : (number + 1) * cut, :]
-            other = term[top : top + cut, span].astype(jnp.float32)
-            out[:, span] = (own + other).astype(jnp.bfloat16)
-
-
-def sums_of(hidden, w_down, arrived, cut, after=()):
+        other = jnp.concatenate([term[:, span] for term in arrived], axis=0)
+        part = (part + other.astype(jnp.float32)).astype(jnp.bfloat16)
+        top = 0
+        for cut, out in zip(cuts, outs):
+            out[:, span] = part[top : top + cut, :]
+            top += cut
+
+
+def sums_of(hidden, w_down, arrived, cuts, after=()):
     count, half = hidden.shape
     feature = w_down.shape[2]
-    groups = count // cut
-    return pl.pallas_call(
-        functools.partial(sums_kernel, len(arrived), groups),
-        out_shape=[jax.ShapeDtypeStruct((cut, feature), jnp.bfloat16)] * groups,
+    return pl.pallas_call(
+        functools.partial(sums_kernel, len(arrived), cuts),
+        out_shape=[jax.ShapeDtypeStruct((cut, feature), jnp.bfloat16) for cut in cuts],
         in_specs=[whole] * (2 + len(arrived)) + [pl.BlockSpec(memory_space=pl.ANY)] * len(after),
-        out_specs=[whole] * groups,
+        out_specs=[whole] * len(cuts),
         compiler_params=pltpu.CompilerParams(vmem_limit_bytes=SMALL_BYTES),
         cost_estimate=pl.CostEstimate(
             flops=2 * count * feature * half,
@@ -503,7 +502,9 @@
         [first_out],
     )
     second_other = swap(second_own, core)
-    near, near_x, near_y, far = sums_of(first_h, w_down, [first_in], 2 * n)
+    near, near_x, near_y, far_sum, both_sum = sums_of(
+        first_h, w_down, [first_in], [2 * n] * 3 + [n] * 2
+    )
     to_near = [swap(near_x, x), swap(near_y, y)]
     second_h, *second_out = expert_of(
         second_own, second_other, *weights, picks, [2 * n, 2 * n, 4 * n], [near]
@@ -514,18 +515,24 @@
         return [(count, [(index, start) for index in range(terms)])]
 
     (near,) = combine([near, *to_near], [all_of(3, 0, 2 * n)], flops=NEAR_FLOPS)
-    far_x, far_y, far_xy, near_xy = sums_of(second_h, w_down, second_in, 2 * n, [near])
-
+    far_x, both_x, far_y, both_y, far_xy, both_xy, near_xy = sums_of(
+        second_h, w_down, second_in, [n] * 6 + [2 * n], [near]
+    )
+
+    to_both = [across(both_xy, x, y), swap(both_x, x), swap(both_y, y)]
     to_far = [across(far_xy, x, y), swap(far_x, x), swap(far_y, y)]
-    context, done = attention([far_x])
-    (near_xy,) = combine([near_xy], [rows_of((0, 0, 2 * n))], [done])
+    context, done = attention([both_x])
+    (both_sum,) = combine([both_sum, *to_both], [all_of(4, 0)], [done])
+    (near_xy,) = combine([near_xy], [rows_of((0, 0, 2 * n))], [both_sum])
     to_near = across(near_xy, x, y)
-    far_sum, both_sum = combine([far, *to_far], [all_of(4, 0), all_of(4, n)], [near_xy])
-    own_sum, near_sum = combine([near, to_near], [all_of(2, 0), all_of(2, n)], [far_sum])
-    (far_sum,) = combine(
-        [swap(far_sum, z_far), across(both_sum, z_far, z_near)], [all_of(2, 0)], flops=FAR_FLOPS
-    )
-    (mixed,) = combine([own_sum, far_sum, swap(near_sum, z_near)], [all_of(3, 0)])
+    (far_sum,) = combine([far_sum, *to_far], [all_of(4, 0)], [near_xy], flops=FAR_FLOPS)
+    from_both = across(both_sum, z_far, z_near)
+    own_sum, near_sum = combine(
+        [near, to_near, from_both], [all_of(3, 0), all_of(2, n)], [far_sum]
+    )
+    (mixed,) = combine(
+        [own_sum, swap(far_sum, z_far), swap(near_sum, z_near)], [all_of(3, 0)]
+    )
     return mixed, context
 
 

time: 74.7 us -> 74.5 us (level)
  waiting for transfers between devices: 30.5 us -> 27.8 us
  starting transfers between devices: 24.7 us -> 27.3 us
    ppermute x19 -> x21, waiting for transfers between devices: 23.5 us -> 15.1 us  [swap(): return lax.ppermute(value, axis, [(i, i ^ bit) for i in range(size)])]
    ppermute x4 -> x5, waiting for transfers between devices: 7.01 us -> 12.7 us  [across(): lax.ppermute(value, axis, [(i, i ^ first[1] ^ second[1]) for i in range(s...]
    ppermute x4 -> x5, starting transfers between devices: 5.56 us -> 8.57 us  [across(): lax.ppermute(value, axis, [(i, i ^ first[1] ^ second[1]) for i in range(s...]
    ppermute x19 -> x21, starting transfers between devices: 19.2 us -> 18.7 us  [swap(): return lax.ppermute(value, axis, [(i, i ^ bit) for i in range(size)])]
  transfers between devices with their start and end apart: 23 -> 26, of which waited for: 13 -> 12; matrix products, arithmetic and copies ran while one was open for 0% -> 0% of each run, Pallas kernels for 19% -> 19%
where the time goes in v10:
time: 74.5 us; the launch traced here: 74.3 us
  waiting for transfers between devices  27.8 us (37%)
  starting transfers between devices  27.3 us (37%)
  Pallas kernels  15.5 us (21%)
  between operations  1.5 us (2%)
  other arithmetic  1.38 us (2%)
  local copies, waits for them, and re-layouts  0.92 us (1%)
    ppermute x21, starting transfers between devices, swap(): return lax.ppermute(value, axis, [(i, i ^ bit) for i in range(size)])  18.7 us
    ppermute x21, waiting for transfers between devices, swap(): return lax.ppermute(value, axis, [(i, i ^ bit) for i in range(size)])  15.1 us
    ppermute x5, waiting for transfers between devices, across(): lax.ppermute(value, axis, [(i, i ^ first[1] ^ second[1]) for i in range(s...  12.7 us
    ppermute x5, starting transfers between devices, across(): lax.ppermute(value, axis, [(i, i ^ first[1] ^ second[1]) for i in range(s...  8.57 us
    pallas_call x1, Pallas kernels, first_of(): pl.pallas_call(functools.partial(first_kernel, picks), out_shape=[jax.Sha...  7.4 us
    pallas_call x1, Pallas kernels, attend(): pl.pallas_call(attend_kernel, out_shape=[jax.ShapeDtypeStruct((count, hea...  2.71 us
    pallas_call x1, Pallas kernels, expert_of(): pl.pallas_call(functools.partial(expert_kernel, picks, len(after)), out_s...  2.7 us
  transfers between devices with their start and end apart: 26, of which 12 were waited for; matrix products, arithmetic and copies ran while one was open for 0% of the time, Pallas kernels for 19%

profile of v10, /device:TPU:0, one launch (start us, length us, event | category | flops | bytes accessed | tf_op | source)
XLA Modules:
  0.0 74.3 jit_solution(605795820277512385)
XLA Ops:
  3.1 3.0 %collective-permute-start = (bf16[16,3712]{1,0:T(8,128)(2,1)S(1)}, bf16[16,3712]{1,0:T(8,128)(2,1)S(1)}, u32[]{:S(2)}, u32[]{:S(2)}) collective-permute-start(bf16[16,3712]{1,0:T(8,128)(2,1)S(1)} %pack.1.refs_0_), channel_id=1, source_target_pairs={{0,8},{4,12},{8,0},{12,4},{16,24},{20,28},{24,16},{28,20},{1,9},{5... | collective-permute-start | bytes 356360 | tf_op jit(solution)/shard_map/ppermute | solution.py:82
  6.1 2.6 %collective-permute-start.3 = (bf16[16,3712]{1,0:T(8,128)(2,1)S(1)}, bf16[16,3712]{1,0:T(8,128)(2,1)S(1)}, u32[]{:S(2)}, u32[]{:S(2)}) collective-permute-start(bf16[16,3712]{1,0:T(8,128)(2,1)S(1)} %pack.1.refs_0_), channel_id=1, source_target_pairs={{0,16},{4,20},{8,24},{12,28},{16,0},{20,4},{24,8},{28,12},{1,17},{... | collective-permute-start | bytes 356360 | tf_op jit(solution)/shard_map/ppermute | solution.py:82
  8.7 1.9 %collective-permute-done.refs_1_ = bf16[16,3712]{1,0:T(8,128)(2,1)S(1)} collective-permute-done((bf16[16,3712]{1,0:T(8,128)(2,1)S(1)}, bf16[16,3712]{1,0:T(8,128)(2,1)S(1)}, u32[]{:S(2)}, u32[]{:S(2)}) %collective-permute-start) | collective-permute-done | bytes 118816 | tf_op jit(solution)/shard_map/ppermute | solution.py:82
  10.7 1.9 %collective-permute-start.1 = (bf16[32,3712]{1,0:T(8,128)(2,1)S(1)}, bf16[32,3712]{1,0:T(8,128)(2,1)S(1)}, u32[]{:S(2)}, u32[]{:S(2)}) collective-permute-start(bf16[32,3712]{1,0:T(8,128)(2,1)S(1)} %combine.9.refs_0_), channel_id=1, source_target_pairs={{0,1},{1,0},{2,3},{3,2},{4,5},{5,4},{6,7},{7,6},{8,9},{9,8},{10,11... | collective-permute-start | bytes 712712 | tf_op jit(solution)/shard_map/ppermute | solution.py:82
  12.6 1.5 %collective-permute-start.2 = (bf16[32,3712]{1,0:T(8,128)(2,1)S(1)}, bf16[32,3712]{1,0:T(8,128)(2,1)S(1)}, u32[]{:S(2)}, u32[]{:S(2)}) collective-permute-start(bf16[32,3712]{1,0:T(8,128)(2,1)S(1)} %combine.9.refs_0_), channel_id=1, source_target_pairs={{0,2},{1,3},{2,0},{3,1},{4,6},{5,7},{6,4},{7,5},{8,10},{9,11},{10,... | collective-permute-start | bytes 712712 | tf_op jit(solution)/shard_map/ppermute | solution.py:82
  14.7 4.4 %collective-permute-done.4.refs_4_ = bf16[16,3712]{1,0:T(8,128)(2,1)S(1)} collective-permute-done((bf16[16,3712]{1,0:T(8,128)(2,1)S(1)}, bf16[16,3712]{1,0:T(8,128)(2,1)S(1)}, u32[]{:S(2)}, u32[]{:S(2)}) %collective-permute-start.4) | collective-permute-done | bytes 118816 | tf_op jit(solution)/shard_map/ppermute | solution.py:82
  19.4 1.6 %collective-permute-start.5 = (bf16[48,3712]{1,0:T(8,128)(2,1)S(1)}, bf16[48,3712]{1,0:T(8,128)(2,1)S(1)}, u32[]{:S(2)}, u32[]{:S(2)}) collective-permute-start(bf16[48,3712]{1,0:T(8,128)(2,1)S(1)} %get-tuple-element.31), channel_id=1, source_target_pairs={{0,1},{1,0},{2,3},{3,2},{4,5},{5,4},{6,7},{7,6},{8,9},{9,8},{10,11... | collective-permute-start | bytes 1069064 | tf_op jit(solution)/shard_map/ppermute | solution.py:82
  20.9 1.5 %collective-permute-start.6 = (bf16[48,3712]{1,0:T(8,128)(2,1)S(1)}, bf16[48,3712]{1,0:T(8,128)(2,1)S(1)}, u32[]{:S(2)}, u32[]{:S(2)}) collective-permute-start(bf16[48,3712]{1,0:T(8,128)(2,1)S(1)} %get-tuple-element.32), channel_id=1, source_target_pairs={{0,2},{1,3},{2,0},{3,1},{4,6},{5,7},{6,4},{7,5},{8,10},{9,11},{10,... | collective-permute-start | bytes 1069064 | tf_op jit(solution)/shard_map/ppermute | solution.py:82
  22.9 7.4 %first.1 = (bf16[128,512]{1,0:T(8,128)(2,1)S(1)}, bf16[128,3584]{1,0:T(8,128)(2,1)S(1)}, bf16[1,3584,512]{2,1,0:T(8,128)(2,1)S(1)}, bf16[1,3584,512]{2,1,0:T(8,128)(2,1)S(1)}, bf16[1,512,3584]{2,1,0:T(8,128)(2,1)S(1)}) custom-call(bf16[128,3712]{1,0:T(8,128)(2,1)S(1)} %get-tuple-element.34.own, bf16[128,3712]{1,0:T(8,128)(2,1)S(1)} %collective-permute-done.8.other, ...), custom_call_target="tpu_custom_call" | custom-call | flops 2348810240 | bytes 11010048 | tf_op jit(solution)/shard_map/first/pallas_call | solution.py:365
  30.4 5.8 %collective-permute-done.7.refs_2_ = bf16[32,3712]{1,0:T(8,128)(2,1)S(1)} collective-permute-done((bf16[32,3712]{1,0:T(8,128)(2,1)S(1)}, bf16[32,3712]{1,0:T(8,128)(2,1)S(1)}, u32[]{:S(2)}, u32[]{:S(2)}) %collective-permute-start.7) | collective-permute-done | bytes 237600 | tf_op jit(solution)/shard_map/ppermute | solution.py:88
  37.2 1.3 %collective-permute-start.14 = (bf16[32,3584]{1,0:T(8,128)(2,1)S(1)}, bf16[32,3584]{1,0:T(8,128)(2,1)S(1)}, u32[]{:S(2)}, u32[]{:S(2)}) collective-permute-start(bf16[32,3584]{1,0:T(8,128)(2,1)S(1)} %get-tuple-element.45), channel_id=1, source_target_pairs={{0,1},{1,0},{2,3},{3,2},{4,5},{5,4},{6,7},{7,6},{8,9},{9,8},{10,11... | collective-permute-start | bytes 688136 | tf_op jit(solution)/shard_map/ppermute | solution.py:82
  39.3 2.7 %expert.1 = (bf16[128,512]{1,0:T(8,128)(2,1)S(1)}, bf16[32,3584]{1,0:T(8,128)(2,1)S(1)}, bf16[32,3584]{1,0:T(8,128)(2,1)S(1)}, bf16[64,3584]{1,0:T(8,128)(2,1)S(1)}) custom-call(bf16[128,3712]{1,0:T(8,128)(2,1)S(1)} %combine.11.own, bf16[128,3712]{1,0:T(8,128)(2,1)S(1)} %collective-permute-done.9.other, bf16[1,3584,512]{2,1,0:T(8,128)(2,1)S(1)} %get-tuple-element.36.w_gate, ...), custom_call_target="tpu_custom_call" | custom-call | flops 2348810240 | bytes 917504 | tf_op jit(solution)/shard_map/expert/pallas_call | solution.py:390
  42.7 2.6 %collective-permute-done.14.refs_1_ = bf16[32,3584]{1,0:T(8,128)(2,1)S(1)} collective-permute-done((bf16[32,3584]{1,0:T(8,128)(2,1)S(1)}, bf16[32,3584]{1,0:T(8,128)(2,1)S(1)}, u32[]{:S(2)}, u32[]{:S(2)}) %collective-permute-start.14) | collective-permute-done | bytes 229408 | tf_op jit(solution)/shard_map/ppermute | solution.py:82
  45.3 1.0 %collective-permute-done.15.refs_2_ = bf16[32,3584]{1,0:T(8,128)(2,1)S(1)} collective-permute-done((bf16[32,3584]{1,0:T(8,128)(2,1)S(1)}, bf16[32,3584]{1,0:T(8,128)(2,1)S(1)}, u32[]{:S(2)}, u32[]{:S(2)}) %collective-permute-start.15) | collective-permute-done | bytes 229408 | tf_op jit(solution)/shard_map/ppermute | solution.py:82
  47.0 1.8 %collective-permute-start.16 = (bf16[16,3584]{1,0:T(8,128)(2,1)S(1)}, bf16[16,3584]{1,0:T(8,128)(2,1)S(1)}, u32[]{:S(2)}, u32[]{:S(2)}) collective-permute-start(bf16[16,3584]{1,0:T(8,128)(2,1)S(1)} %get-tuple-element.51), channel_id=1, source_target_pairs={{0,3},{1,2},{2,1},{3,0},{4,7},{5,6},{6,5},{7,4},{8,11},{9,10},{10,... | collective-permute-start | bytes 344072 | tf_op jit(solution)/shard_map/ppermute | solution.py:88
  49.4 1.2 %collective-permute-start.18 = (bf16[16,3584]{1,0:T(8,128)(2,1)S(1)}, bf16[16,3584]{1,0:T(8,128)(2,1)S(1)}, u32[]{:S(2)}, u32[]{:S(2)}) collective-permute-start(bf16[16,3584]{1,0:T(8,128)(2,1)S(1)} %get-tuple-element.52), channel_id=1, source_target_pairs={{0,2},{1,3},{2,0},{3,1},{4,6},{5,7},{6,4},{7,5},{8,10},{9,11},{10,... | collective-permute-start | bytes 344072 | tf_op jit(solution)/shard_map/ppermute | solution.py:82
  50.6 1.7 %collective-permute-start.21 = (bf16[16,3584]{1,0:T(8,128)(2,1)S(1)}, bf16[16,3584]{1,0:T(8,128)(2,1)S(1)}, u32[]{:S(2)}, u32[]{:S(2)}) collective-permute-start(bf16[16,3584]{1,0:T(8,128)(2,1)S(1)} %get-tuple-element.55), channel_id=1, source_target_pairs={{0,3},{1,2},{2,1},{3,0},{4,7},{5,6},{6,5},{7,4},{8,11},{9,10},{10,... | collective-permute-start | bytes 344072 | tf_op jit(solution)/shard_map/ppermute | solution.py:88
  52.9 1.3 %collective-permute-done.16.refs_1_ = bf16[16,3584]{1,0:T(8,128)(2,1)S(1)} collective-permute-done((bf16[16,3584]{1,0:T(8,128)(2,1)S(1)}, bf16[16,3584]{1,0:T(8,128)(2,1)S(1)}, u32[]{:S(2)}, u32[]{:S(2)}) %collective-permute-start.16) | collective-permute-done | bytes 114720 | tf_op jit(solution)/shard_map/ppermute | solution.py:88
  55.6 2.7 %attend.1 = (bf16[4,64,512]{2,1,0:T(8,128)(2,1)}, f32[8,128]{1,0:T(8,128)S(1)}) custom-call(s32[4]{0:T(128)S(1)} %copy-done.3, s32[1]{0:T(128)S(6)} %copy.12.live_rows, bf16[4,64,576]{2,1,0:T(8,128)(2,1)S(1)} %copy-done.1, bf16[4,576,256]{2,1,0:T(8,128)(2,1)S(1)} %bitcast.4, bf16[16,3584]{1,0:T(8,128)(2,1)S(1)} %get-tuple-element.47.refs_0_), custom_call_target="tpu_custom_call" | custom-call | flops 150994944 | bytes 1179648 | tf_op jit(solution)/shard_map/attend/pallas_call | solution.py:55
  58.4 3.3 %collective-permute-start.20 = (bf16[16,3584]{1,0:T(8,128)(2,1)S(1)}, bf16[16,3584]{1,0:T(8,128)(2,1)S(1)}, u32[]{:S(2)}, u32[]{:S(2)}) collective-permute-start(bf16[16,3584]{1,0:T(8,128)(2,1)S(1)} %combine.13.refs_1_), channel_id=1, source_target_pairs={{0,24},{4,28},{8,16},{12,20},{16,8},{20,12},{24,0},{28,4},{1,25},{... | collective-permute-start | bytes 344072 | tf_op jit(solution)/shard_map/ppermute | solution.py:88
  61.7 1.3 %collective-permute-start.19 = (bf16[32,3584]{1,0:T(8,128)(2,1)S(1)}, bf16[32,3584]{1,0:T(8,128)(2,1)S(1)}, u32[]{:S(2)}, u32[]{:S(2)}) collective-permute-start(bf16[32,3584]{1,0:T(8,128)(2,1)S(1)} %combine.14.refs_4_), channel_id=1, source_target_pairs={{0,3},{1,2},{2,1},{3,0},{4,7},{5,6},{6,5},{7,4},{8,11},{9,10},{10,... | collective-permute-start | bytes 688136 | tf_op jit(solution)/shard_map/ppermute | solution.py:88
  63.1 2.0 %collective-permute-done.20.refs_2_ = bf16[16,3584]{1,0:T(8,128)(2,1)S(1)} collective-permute-done((bf16[16,3584]{1,0:T(8,128)(2,1)S(1)}, bf16[16,3584]{1,0:T(8,128)(2,1)S(1)}, u32[]{:S(2)}, u32[]{:S(2)}) %collective-permute-start.20) | collective-permute-done | bytes 114720 | tf_op jit(solution)/shard_map/ppermute | solution.py:88
  65.2 3.5 %collective-permute-done.19.refs_1_ = bf16[32,3584]{1,0:T(8,128)(2,1)S(1)} collective-permute-done((bf16[32,3584]{1,0:T(8,128)(2,1)S(1)}, bf16[32,3584]{1,0:T(8,128)(2,1)S(1)}, u32[]{:S(2)}, u32[]{:S(2)}) %collective-permute-start.19) | collective-permute-done | bytes 229408 | tf_op jit(solution)/shard_map/ppermute | solution.py:88
  69.5 4.1 %collective-permute-done.25.refs_2_ = bf16[16,3584]{1,0:T(8,128)(2,1)S(1)} collective-permute-done((bf16[16,3584]{1,0:T(8,128)(2,1)S(1)}, bf16[16,3584]{1,0:T(8,128)(2,1)S(1)}, u32[]{:S(2)}, u32[]{:S(2)}) %collective-permute-start.25) | collective-permute-done | bytes 114720 | tf_op jit(solution)/shard_map/ppermute | solution.py:82
  (53 shorter events, 10.6 us)
Async XLA Ops:
  3.1 7.6 %collective-permute-start = (bf16[16,3712]{1,0:T(8,128)(2,1)S(1)}, bf16[16,3712]{1,0:T(8,128)(2,1)S(1)}, u32[]{:S(2)}, u32[]{:S(2)}) collective-permute-start(bf16[16,3712]{1,0:T(8,128)(2,1)S(1)} %pack.1.refs_0_), channel_id=1, source_target_pairs={{0,8},{4,12},{8,0},{12,4},{16,24},{20,28},{24,16},{28,20},{1,9},{5... | collective-permute-start | bytes 356360 | tf_op jit(solution)/shard_map/ppermute | solution.py:82
  6.1 8.2 %collective-permute-start.3 = (bf16[16,3712]{1,0:T(8,128)(2,1)S(1)}, bf16[16,3712]{1,0:T(8,128)(2,1)S(1)}, u32[]{:S(2)}, u32[]{:S(2)}) collective-permute-start(bf16[16,3712]{1,0:T(8,128)(2,1)S(1)} %pack.1.refs_0_), channel_id=1, source_target_pairs={{0,16},{4,20},{8,24},{12,28},{16,0},{20,4},{24,8},{28,12},{1,17},{... | collective-permute-start | bytes 356360 | tf_op jit(solution)/shard_map/ppermute | solution.py:82
  10.7 8.5 %collective-permute-start.1 = (bf16[32,3712]{1,0:T(8,128)(2,1)S(1)}, bf16[32,3712]{1,0:T(8,128)(2,1)S(1)}, u32[]{:S(2)}, u32[]{:S(2)}) collective-permute-start(bf16[32,3712]{1,0:T(8,128)(2,1)S(1)} %combine.9.refs_0_), channel_id=1, source_target_pairs={{0,1},{1,0},{2,3},{3,2},{4,5},{5,4},{6,7},{7,6},{8,9},{9,8},{10,11... | collective-permute-start | bytes 712712 | tf_op jit(solution)/shard_map/ppermute | solution.py:82
  12.6 6.6 %collective-permute-start.2 = (bf16[32,3712]{1,0:T(8,128)(2,1)S(1)}, bf16[32,3712]{1,0:T(8,128)(2,1)S(1)}, u32[]{:S(2)}, u32[]{:S(2)}) collective-permute-start(bf16[32,3712]{1,0:T(8,128)(2,1)S(1)} %combine.9.refs_0_), channel_id=1, source_target_pairs={{0,2},{1,3},{2,0},{3,1},{4,6},{5,7},{6,4},{7,5},{8,10},{9,11},{10,... | collective-permute-start | bytes 712712 | tf_op jit(solution)/shard_map/ppermute | solution.py:82
  14.3 4.8 %collective-permute-start.4 = (bf16[16,3712]{1,0:T(8,128)(2,1)S(1)}, bf16[16,3712]{1,0:T(8,128)(2,1)S(1)}, u32[]{:S(2)}, u32[]{:S(2)}) collective-permute-start(bf16[16,3712]{1,0:T(8,128)(2,1)S(1)} %collective-permute-done.3.refs_3_), channel_id=1, source_target_pairs={{0,8},{4,12},{8,0},{12,4},{16,24},{20,28},{24,16},{28,20},{1,9},{5... | collective-permute-start | bytes 356360 | tf_op jit(solution)/shard_map/ppermute | solution.py:82
  19.4 16.9 %collective-permute-start.5 = (bf16[48,3712]{1,0:T(8,128)(2,1)S(1)}, bf16[48,3712]{1,0:T(8,128)(2,1)S(1)}, u32[]{:S(2)}, u32[]{:S(2)}) collective-permute-start(bf16[48,3712]{1,0:T(8,128)(2,1)S(1)} %get-tuple-element.31), channel_id=1, source_target_pairs={{0,1},{1,0},{2,3},{3,2},{4,5},{5,4},{6,7},{7,6},{8,9},{9,8},{10,11... | collective-permute-start | bytes 1069064 | tf_op jit(solution)/shard_map/ppermute | solution.py:82
  20.9 15.5 %collective-permute-start.6 = (bf16[48,3712]{1,0:T(8,128)(2,1)S(1)}, bf16[48,3712]{1,0:T(8,128)(2,1)S(1)}, u32[]{:S(2)}, u32[]{:S(2)}) collective-permute-start(bf16[48,3712]{1,0:T(8,128)(2,1)S(1)} %get-tuple-element.32), channel_id=1, source_target_pairs={{0,2},{1,3},{2,0},{3,1},{4,6},{5,7},{6,4},{7,5},{8,10},{9,11},{10,... | collective-permute-start | bytes 1069064 | tf_op jit(solution)/shard_map/ppermute | solution.py:82
  22.4 13.8 %collective-permute-start.7 = (bf16[32,3712]{1,0:T(8,128)(2,1)S(1)}, bf16[32,3712]{1,0:T(8,128)(2,1)S(1)}, u32[]{:S(2)}, u32[]{:S(2)}) collective-permute-start(bf16[32,3712]{1,0:T(8,128)(2,1)S(1)} %get-tuple-element.33), channel_id=1, source_target_pairs={{0,3},{1,2},{2,1},{3,0},{4,7},{5,6},{6,5},{7,4},{8,11},{9,10},{10,... | collective-permute-start | bytes 712712 | tf_op jit(solution)/shard_map/ppermute | solution.py:88
  30.3 6.2 %collective-permute-start.10 = (bf16[128,3584]{1,0:T(8,128)(2,1)S(1)}, bf16[128,3584]{1,0:T(8,128)(2,1)S(1)}, u32[]{:S(2)}, u32[]{:S(2)}) collective-permute-start(bf16[128,3584]{1,0:T(8,128)(2,1)S(1)} %get-tuple-element.35.refs_3_), channel_id=1, source_target_pairs={{0,4},{4,0},{8,12},{12,8},{16,20},{20,16},{24,28},{28,24},{1,5},{5... | collective-permute-start | bytes 2752520 | tf_op jit(solution)/shard_map/ppermute | solution.py:82
  37.2 8.1 %collective-permute-start.14 = (bf16[32,3584]{1,0:T(8,128)(2,1)S(1)}, bf16[32,3584]{1,0:T(8,128)(2,1)S(1)}, u32[]{:S(2)}, u32[]{:S(2)}) collective-permute-start(bf16[32,3584]{1,0:T(8,128)(2,1)S(1)} %get-tuple-element.45), channel_id=1, source_target_pairs={{0,1},{1,0},{2,3},{3,2},{4,5},{5,4},{6,7},{7,6},{8,9},{9,8},{10,11... | collective-permute-start | bytes 688136 | tf_op jit(solution)/shard_map/ppermute | solution.py:82
  38.5 7.7 %collective-permute-start.15 = (bf16[32,3584]{1,0:T(8,128)(2,1)S(1)}, bf16[32,3584]{1,0:T(8,128)(2,1)S(1)}, u32[]{:S(2)}, u32[]{:S(2)}) collective-permute-start(bf16[32,3584]{1,0:T(8,128)(2,1)S(1)} %get-tuple-element.46), channel_id=1, source_target_pairs={{0,2},{1,3},{2,0},{3,1},{4,6},{5,7},{6,4},{7,5},{8,10},{9,11},{10,... | collective-permute-start | bytes 688136 | tf_op jit(solution)/shard_map/ppermute | solution.py:82
  42.0 4.3 %collective-permute-start.13 = (bf16[64,3584]{1,0:T(8,128)(2,1)S(1)}, bf16[64,3584]{1,0:T(8,128)(2,1)S(1)}, u32[]{:S(2)}, u32[]{:S(2)}) collective-permute-start(bf16[64,3584]{1,0:T(8,128)(2,1)S(1)} %get-tuple-element.44), channel_id=1, source_target_pairs={{0,4},{4,0},{8,12},{12,8},{16,20},{20,16},{24,28},{28,24},{1,5},{5... | collective-permute-start | bytes 1376264 | tf_op jit(solution)/shard_map/ppermute | solution.py:82
  42.1 4.2 %collective-permute-start.11 = (bf16[32,3584]{1,0:T(8,128)(2,1)S(1)}, bf16[32,3584]{1,0:T(8,128)(2,1)S(1)}, u32[]{:S(2)}, u32[]{:S(2)}) collective-permute-start(bf16[32,3584]{1,0:T(8,128)(2,1)S(1)} %get-tuple-element.42), channel_id=1, source_target_pairs={{0,4},{4,0},{8,12},{12,8},{16,20},{20,16},{24,28},{28,24},{1,5},{5... | collective-permute-start | bytes 688136 | tf_op jit(solution)/shard_map/ppermute | solution.py:82
  42.6 3.8 %collective-permute-start.12 = (bf16[32,3584]{1,0:T(8,128)(2,1)S(1)}, bf16[32,3584]{1,0:T(8,128)(2,1)S(1)}, u32[]{:S(2)}, u32[]{:S(2)}) collective-permute-start(bf16[32,3584]{1,0:T(8,128)(2,1)S(1)} %get-tuple-element.43), channel_id=1, source_target_pairs={{0,4},{4,0},{8,12},{12,8},{16,20},{20,16},{24,28},{28,24},{1,5},{5... | collective-permute-start | bytes 688136 | tf_op jit(solution)/shard_map/ppermute | solution.py:82
  47.0 7.1 %collective-permute-start.16 = (bf16[16,3584]{1,0:T(8,128)(2,1)S(1)}, bf16[16,3584]{1,0:T(8,128)(2,1)S(1)}, u32[]{:S(2)}, u32[]{:S(2)}) collective-permute-start(bf16[16,3584]{1,0:T(8,128)(2,1)S(1)} %get-tuple-element.51), channel_id=1, source_target_pairs={{0,3},{1,2},{2,1},{3,0},{4,7},{5,6},{6,5},{7,4},{8,11},{9,10},{10,... | collective-permute-start | bytes 344072 | tf_op jit(solution)/shard_map/ppermute | solution.py:88
  48.9 9.5 %collective-permute-start.17 = (bf16[16,3584]{1,0:T(8,128)(2,1)S(1)}, bf16[16,3584]{1,0:T(8,128)(2,1)S(1)}, u32[]{:S(2)}, u32[]{:S(2)}) collective-permute-start(bf16[16,3584]{1,0:T(8,128)(2,1)S(1)} %get-tuple-element.47.refs_0_), channel_id=1, source_target_pairs={{0,1},{1,0},{2,3},{3,2},{4,5},{5,4},{6,7},{7,6},{8,9},{9,8},{10,11... | collective-permute-start | bytes 344072 | tf_op jit(solution)/shard_map/ppermute | solution.py:82
  49.4 9.0 %collective-permute-start.18 = (bf16[16,3584]{1,0:T(8,128)(2,1)S(1)}, bf16[16,3584]{1,0:T(8,128)(2,1)S(1)}, u32[]{:S(2)}, u32[]{:S(2)}) collective-permute-start(bf16[16,3584]{1,0:T(8,128)(2,1)S(1)} %get-tuple-element.52), channel_id=1, source_target_pairs={{0,2},{1,3},{2,0},{3,1},{4,6},{5,7},{6,4},{7,5},{8,10},{9,11},{10,... | collective-permute-start | bytes 344072 | tf_op jit(solution)/shard_map/ppermute | solution.py:82
  50.6 12.4 %collective-permute-start.21 = (bf16[16,3584]{1,0:T(8,128)(2,1)S(1)}, bf16[16,3584]{1,0:T(8,128)(2,1)S(1)}, u32[]{:S(2)}, u32[]{:S(2)}) collective-permute-start(bf16[16,3584]{1,0:T(8,128)(2,1)S(1)} %get-tuple-element.55), channel_id=1, source_target_pairs={{0,3},{1,2},{2,1},{3,0},{4,7},{5,6},{6,5},{7,4},{8,11},{9,10},{10,... | collective-permute-start | bytes 344072 | tf_op jit(solution)/shard_map/ppermute | solution.py:88
  52.3 10.7 %collective-permute-start.22 = (bf16[16,3584]{1,0:T(8,128)(2,1)S(1)}, bf16[16,3584]{1,0:T(8,128)(2,1)S(1)}, u32[]{:S(2)}, u32[]{:S(2)}) collective-permute-start(bf16[16,3584]{1,0:T(8,128)(2,1)S(1)} %get-tuple-element.56), channel_id=1, source_target_pairs={{0,1},{1,0},{2,3},{3,2},{4,5},{5,4},{6,7},{7,6},{8,9},{9,8},{10,11... | collective-permute-start | bytes 344072 | tf_op jit(solution)/shard_map/ppermute | solution.py:82
  54.2 8.8 %collective-permute-start.23 = (bf16[16,3584]{1,0:T(8,128)(2,1)S(1)}, bf16[16,3584]{1,0:T(8,128)(2,1)S(1)}, u32[]{:S(2)}, u32[]{:S(2)}) collective-permute-start(bf16[16,3584]{1,0:T(8,128)(2,1)S(1)} %get-tuple-element.57), channel_id=1, source_target_pairs={{0,2},{1,3},{2,0},{3,1},{4,6},{5,7},{6,4},{7,5},{8,10},{9,11},{10,... | collective-permute-start | bytes 344072 | tf_op jit(solution)/shard_map/ppermute | solution.py:82
  58.4 6.8 %collective-permute-start.20 = (bf16[16,3584]{1,0:T(8,128)(2,1)S(1)}, bf16[16,3584]{1,0:T(8,128)(2,1)S(1)}, u32[]{:S(2)}, u32[]{:S(2)}) collective-permute-start(bf16[16,3584]{1,0:T(8,128)(2,1)S(1)} %combine.13.refs_1_), channel_id=1, source_target_pairs={{0,24},{4,28},{8,16},{12,20},{16,8},{20,12},{24,0},{28,4},{1,25},{... | collective-permute-start | bytes 344072 | tf_op jit(solution)/shard_map/ppermute | solution.py:88
  61.7 7.0 %collective-permute-start.19 = (bf16[32,3584]{1,0:T(8,128)(2,1)S(1)}, bf16[32,3584]{1,0:T(8,128)(2,1)S(1)}, u32[]{:S(2)}, u32[]{:S(2)}) collective-permute-start(bf16[32,3584]{1,0:T(8,128)(2,1)S(1)} %combine.14.refs_4_), channel_id=1, source_target_pairs={{0,3},{1,2},{2,1},{3,0},{4,7},{5,6},{6,5},{7,4},{8,11},{9,10},{10,... | collective-permute-start | bytes 688136 | tf_op jit(solution)/shard_map/ppermute | solution.py:88
  63.1 6.4 %collective-permute-start.24 = (bf16[16,3584]{1,0:T(8,128)(2,1)S(1)}, bf16[16,3584]{1,0:T(8,128)(2,1)S(1)}, u32[]{:S(2)}, u32[]{:S(2)}) collective-permute-start(bf16[16,3584]{1,0:T(8,128)(2,1)S(1)} %combine.15.refs_3_), channel_id=1, source_target_pairs={{0,16},{4,20},{8,24},{12,28},{16,0},{20,4},{24,8},{28,12},{1,17},{... | collective-permute-start | bytes 344072 | tf_op jit(solution)/shard_map/ppermute | solution.py:82
  68.8 4.9 %collective-permute-start.25 = (bf16[16,3584]{1,0:T(8,128)(2,1)S(1)}, bf16[16,3584]{1,0:T(8,128)(2,1)S(1)}, u32[]{:S(2)}, u32[]{:S(2)}) collective-permute-start(bf16[16,3584]{1,0:T(8,128)(2,1)S(1)} %get-tuple-element.59), channel_id=1, source_target_pairs={{0,8},{4,12},{8,0},{12,4},{16,24},{20,28},{24,16},{28,20},{1,9},{5... | collective-permute-start | bytes 344072 | tf_op jit(solution)/shard_map/ppermute | solution.py:82
  (6 other events, 35.3 us)

commit v11 on v10

--- a/solution.py
+++ b/solution.py
@@ -496,10 +496,11 @@
     first_h, first_out, *weights = first_of(first_own, first_other, *weights, picks, [8 * n])
     w_down = weights[2]
     first_in = swap(first_out, core)
+    context, done = attention([first_out])
     (second_own,) = combine(
         [far_x, far_y, far_xy],
         [rows_of((0, 0, 2 * n), (1, 0, 2 * n), (2, 0, 2 * n), (1, 2 * n, n), (0, 2 * n, n))],
-        [first_out],
+        [done],
     )
     second_other = swap(second_own, core)
     near, near_x, near_y, far_sum, both_sum = sums_of(
@@ -521,8 +522,7 @@
 
     to_both = [across(both_xy, x, y), swap(both_x, x), swap(both_y, y)]
     to_far = [across(far_xy, x, y), swap(far_x, x), swap(far_y, y)]
-    context, done = attention([both_x])
-    (both_sum,) = combine([both_sum, *to_both], [all_of(4, 0)], [done])
+    (both_sum,) = combine([both_sum, *to_both], [all_of(4, 0)])
     (near_xy,) = combine([near_xy], [rows_of((0, 0, 2 * n))], [both_sum])
     to_near = across(near_xy, x, y)
     (far_sum,) = combine([far_sum, *to_far], [all_of(4, 0)], [near_xy], flops=FAR_FLOPS)

time: 74.5 us -> 73.7 us (0.989)
  waiting for transfers between devices: 27.8 us -> 26.8 us
    ppermute x5, waiting for transfers between devices: 12.7 us -> 8.73 us  [across(): lax.ppermute(value, axis, [(i, i ^ first[1] ^ second[1]) for i in range(s...]
    ppermute x21, waiting for transfers between devices: 15.1 us -> 18.1 us  [swap(): return lax.ppermute(value, axis, [(i, i ^ bit) for i in range(size)])]
  transfers between devices with their start and end apart: 26 -> 26, of which waited for: 12 -> 14; matrix products, arithmetic and copies ran while one was open for 0% -> 0% of each run, Pallas kernels for 19% -> 19%
where the time goes in v11:
time: 73.7 us; the launch traced here: 73.5 us
  starting transfers between devices  27.3 us (37%)
  waiting for transfers between devices  26.8 us (36%)
  Pallas kernels  15.6 us (21%)
  between operations  1.5 us (2%)
  other arithmetic  1.38 us (2%)
  local copies, waits for them, and re-layouts  0.92 us (1%)
    ppermute x21, starting transfers between devices, swap(): return lax.ppermute(value, axis, [(i, i ^ bit) for i in range(size)])  18.7 us
    ppermute x21, waiting for transfers between devices, swap(): return lax.ppermute(value, axis, [(i, i ^ bit) for i in range(size)])  18.1 us
    ppermute x5, waiting for transfers between devices, across(): lax.ppermute(value, axis, [(i, i ^ first[1] ^ second[1]) for i in range(s...  8.73 us
    ppermute x5, starting transfers between devices, across(): lax.ppermute(value, axis, [(i, i ^ first[1] ^ second[1]) for i in range(s...  8.57 us
    pallas_call x1, Pallas kernels, first_of(): pl.pallas_call(functools.partial(first_kernel, picks), out_shape=[jax.Sha...  7.48 us
    pallas_call x1, Pallas kernels, attend(): pl.pallas_call(attend_kernel, out_shape=[jax.ShapeDtypeStruct((count, hea...  2.7 us
    pallas_call x1, Pallas kernels, expert_of(): pl.pallas_call(functools.partial(expert_kernel, picks, len(after)), out_s...  2.7 us
  transfers between devices with their start and end apart: 26, of which 14 were waited for; matrix products, arithmetic and copies ran while one was open for 0% of the time, Pallas kernels for 19%

profile of v11, /device:TPU:0, one launch (start us, length us, event | category | flops | bytes accessed | tf_op | source)
XLA Modules:
  0.0 73.5 jit_solution(11485460405961419973)
XLA Ops:
  3.1 3.0 %collective-permute-start = (bf16[16,3712]{1,0:T(8,128)(2,1)S(1)}, bf16[16,3712]{1,0:T(8,128)(2,1)S(1)}, u32[]{:S(2)}, u32[]{:S(2)}) collective-permute-start(bf16[16,3712]{1,0:T(8,128)(2,1)S(1)} %pack.1.refs_0_), channel_id=1, source_target_pairs={{0,8},{4,12},{8,0},{12,4},{16,24},{20,28},{24,16},{28,20},{1,9},{5... | collective-permute-start | bytes 356360 | tf_op jit(solution)/shard_map/ppermute | solution.py:82
  6.1 2.6 %collective-permute-start.3 = (bf16[16,3712]{1,0:T(8,128)(2,1)S(1)}, bf16[16,3712]{1,0:T(8,128)(2,1)S(1)}, u32[]{:S(2)}, u32[]{:S(2)}) collective-permute-start(bf16[16,3712]{1,0:T(8,128)(2,1)S(1)} %pack.1.refs_0_), channel_id=1, source_target_pairs={{0,16},{4,20},{8,24},{12,28},{16,0},{20,4},{24,8},{28,12},{1,17},{... | collective-permute-start | bytes 356360 | tf_op jit(solution)/shard_map/ppermute | solution.py:82
  8.7 1.9 %collective-permute-done.refs_1_ = bf16[16,3712]{1,0:T(8,128)(2,1)S(1)} collective-permute-done((bf16[16,3712]{1,0:T(8,128)(2,1)S(1)}, bf16[16,3712]{1,0:T(8,128)(2,1)S(1)}, u32[]{:S(2)}, u32[]{:S(2)}) %collective-permute-start) | collective-permute-done | bytes 118816 | tf_op jit(solution)/shard_map/ppermute | solution.py:82
  10.7 1.9 %collective-permute-start.2 = (bf16[32,3712]{1,0:T(8,128)(2,1)S(1)}, bf16[32,3712]{1,0:T(8,128)(2,1)S(1)}, u32[]{:S(2)}, u32[]{:S(2)}) collective-permute-start(bf16[32,3712]{1,0:T(8,128)(2,1)S(1)} %combine.9.refs_0_), channel_id=1, source_target_pairs={{0,2},{1,3},{2,0},{3,1},{4,6},{5,7},{6,4},{7,5},{8,10},{9,11},{10,... | collective-permute-start | bytes 712712 | tf_op jit(solution)/shard_map/ppermute | solution.py:82
  12.6 1.5 %collective-permute-start.1 = (bf16[32,3712]{1,0:T(8,128)(2,1)S(1)}, bf16[32,3712]{1,0:T(8,128)(2,1)S(1)}, u32[]{:S(2)}, u32[]{:S(2)}) collective-permute-start(bf16[32,3712]{1,0:T(8,128)(2,1)S(1)} %combine.9.refs_0_), channel_id=1, source_target_pairs={{0,1},{1,0},{2,3},{3,2},{4,5},{5,4},{6,7},{7,6},{8,9},{9,8},{10,11... | collective-permute-start | bytes 712712 | tf_op jit(solution)/shard_map/ppermute | solution.py:82
  14.7 4.4 %collective-permute-done.4.refs_4_ = bf16[16,3712]{1,0:T(8,128)(2,1)S(1)} collective-permute-done((bf16[16,3712]{1,0:T(8,128)(2,1)S(1)}, bf16[16,3712]{1,0:T(8,128)(2,1)S(1)}, u32[]{:S(2)}, u32[]{:S(2)}) %collective-permute-start.4) | collective-permute-done | bytes 118816 | tf_op jit(solution)/shard_map/ppermute | solution.py:82
  19.4 1.6 %collective-permute-start.9 = (bf16[48,3712]{1,0:T(8,128)(2,1)S(1)}, bf16[48,3712]{1,0:T(8,128)(2,1)S(1)}, u32[]{:S(2)}, u32[]{:S(2)}) collective-permute-start(bf16[48,3712]{1,0:T(8,128)(2,1)S(1)} %get-tuple-element.39), channel_id=1, source_target_pairs={{0,1},{1,0},{2,3},{3,2},{4,5},{5,4},{6,7},{7,6},{8,9},{9,8},{10,11... | collective-permute-start | bytes 1069064 | tf_op jit(solution)/shard_map/ppermute | solution.py:82
  20.9 1.5 %collective-permute-start.10 = (bf16[48,3712]{1,0:T(8,128)(2,1)S(1)}, bf16[48,3712]{1,0:T(8,128)(2,1)S(1)}, u32[]{:S(2)}, u32[]{:S(2)}) collective-permute-start(bf16[48,3712]{1,0:T(8,128)(2,1)S(1)} %get-tuple-element.40), channel_id=1, source_target_pairs={{0,2},{1,3},{2,0},{3,1},{4,6},{5,7},{6,4},{7,5},{8,10},{9,11},{10,... | collective-permute-start | bytes 1069064 | tf_op jit(solution)/shard_map/ppermute | solution.py:82
  23.6 7.5 %first.1 = (bf16[128,512]{1,0:T(8,128)(2,1)S(1)}, bf16[128,3584]{1,0:T(8,128)(2,1)S(1)}, bf16[1,3584,512]{2,1,0:T(8,128)(2,1)S(1)}, bf16[1,3584,512]{2,1,0:T(8,128)(2,1)S(1)}, bf16[1,512,3584]{2,1,0:T(8,128)(2,1)S(1)}) custom-call(bf16[128,3712]{1,0:T(8,128)(2,1)S(1)} %get-tuple-element.31.own, bf16[128,3712]{1,0:T(8,128)(2,1)S(1)} %collective-permute-done.5.other, ...), custom_call_target="tpu_custom_call" | custom-call | flops 2348810240 | bytes 11010048 | tf_op jit(solution)/shard_map/first/pallas_call | solution.py:365
  31.2 2.7 %attend.1 = (bf16[4,64,512]{2,1,0:T(8,128)(2,1)}, f32[8,128]{1,0:T(8,128)S(1)}) custom-call(s32[4]{0:T(128)S(1)} %copy-done.3, s32[1]{0:T(128)S(6)} %copy.12.live_rows, bf16[4,64,576]{2,1,0:T(8,128)(2,1)S(1)} %copy-done.1, bf16[4,576,256]{2,1,0:T(8,128)(2,1)S(1)} %bitcast.4, bf16[128,3584]{1,0:T(8,128)(2,1)S(1)} %get-tuple-element.32.refs_0_), custom_call_target="tpu_custom_call" | custom-call | flops 150994944 | bytes 1179648 | tf_op jit(solution)/shard_map/attend/pallas_call | solution.py:55
  33.9 2.3 %collective-permute-done.11.refs_2_ = bf16[32,3712]{1,0:T(8,128)(2,1)S(1)} collective-permute-done((bf16[32,3712]{1,0:T(8,128)(2,1)S(1)}, bf16[32,3712]{1,0:T(8,128)(2,1)S(1)}, u32[]{:S(2)}, u32[]{:S(2)}) %collective-permute-start.11) | collective-permute-done | bytes 237600 | tf_op jit(solution)/shard_map/ppermute | solution.py:88
  37.2 1.3 %collective-permute-start.7 = (bf16[32,3584]{1,0:T(8,128)(2,1)S(1)}, bf16[32,3584]{1,0:T(8,128)(2,1)S(1)}, u32[]{:S(2)}, u32[]{:S(2)}) collective-permute-start(bf16[32,3584]{1,0:T(8,128)(2,1)S(1)} %get-tuple-element.37), channel_id=1, source_target_pairs={{0,1},{1,0},{2,3},{3,2},{4,5},{5,4},{6,7},{7,6},{8,9},{9,8},{10,11... | collective-permute-start | bytes 688136 | tf_op jit(solution)/shard_map/ppermute | solution.py:82
  39.3 2.7 %expert.1 = (bf16[128,512]{1,0:T(8,128)(2,1)S(1)}, bf16[32,3584]{1,0:T(8,128)(2,1)S(1)}, bf16[32,3584]{1,0:T(8,128)(2,1)S(1)}, bf16[64,3584]{1,0:T(8,128)(2,1)S(1)}) custom-call(bf16[128,3712]{1,0:T(8,128)(2,1)S(1)} %combine.12.own, bf16[128,3712]{1,0:T(8,128)(2,1)S(1)} %collective-permute-done.12.other, bf16[1,3584,512]{2,1,0:T(8,128)(2,1)S(1)} %get-tuple-element.43.w_gate, ...), custom_call_target="tpu_custom_call" | custom-call | flops 2348810240 | bytes 917504 | tf_op jit(solution)/shard_map/expert/pallas_call | solution.py:390
  42.7 2.6 %collective-permute-done.7.refs_1_ = bf16[32,3584]{1,0:T(8,128)(2,1)S(1)} collective-permute-done((bf16[32,3584]{1,0:T(8,128)(2,1)S(1)}, bf16[32,3584]{1,0:T(8,128)(2,1)S(1)}, u32[]{:S(2)}, u32[]{:S(2)}) %collective-permute-start.7) | collective-permute-done | bytes 229408 | tf_op jit(solution)/shard_map/ppermute | solution.py:82
  47.0 1.8 %collective-permute-start.16 = (bf16[16,3584]{1,0:T(8,128)(2,1)S(1)}, bf16[16,3584]{1,0:T(8,128)(2,1)S(1)}, u32[]{:S(2)}, u32[]{:S(2)}) collective-permute-start(bf16[16,3584]{1,0:T(8,128)(2,1)S(1)} %get-tuple-element.51), channel_id=1, source_target_pairs={{0,3},{1,2},{2,1},{3,0},{4,7},{5,6},{6,5},{7,4},{8,11},{9,10},{10,... | collective-permute-start | bytes 344072 | tf_op jit(solution)/shard_map/ppermute | solution.py:88
  49.4 1.2 %collective-permute-start.18 = (bf16[16,3584]{1,0:T(8,128)(2,1)S(1)}, bf16[16,3584]{1,0:T(8,128)(2,1)S(1)}, u32[]{:S(2)}, u32[]{:S(2)}) collective-permute-start(bf16[16,3584]{1,0:T(8,128)(2,1)S(1)} %get-tuple-element.53), channel_id=1, source_target_pairs={{0,2},{1,3},{2,0},{3,1},{4,6},{5,7},{6,4},{7,5},{8,10},{9,11},{10,... | collective-permute-start | bytes 344072 | tf_op jit(solution)/shard_map/ppermute | solution.py:82
  50.6 1.7 %collective-permute-start.21 = (bf16[16,3584]{1,0:T(8,128)(2,1)S(1)}, bf16[16,3584]{1,0:T(8,128)(2,1)S(1)}, u32[]{:S(2)}, u32[]{:S(2)}) collective-permute-start(bf16[16,3584]{1,0:T(8,128)(2,1)S(1)} %get-tuple-element.55), channel_id=1, source_target_pairs={{0,3},{1,2},{2,1},{3,0},{4,7},{5,6},{6,5},{7,4},{8,11},{9,10},{10,... | collective-permute-start | bytes 344072 | tf_op jit(solution)/shard_map/ppermute | solution.py:88
  52.8 1.3 %collective-permute-done.16.refs_1_ = bf16[16,3584]{1,0:T(8,128)(2,1)S(1)} collective-permute-done((bf16[16,3584]{1,0:T(8,128)(2,1)S(1)}, bf16[16,3584]{1,0:T(8,128)(2,1)S(1)}, u32[]{:S(2)}, u32[]{:S(2)}) %collective-permute-start.16) | collective-permute-done | bytes 114720 | tf_op jit(solution)/shard_map/ppermute | solution.py:88
  55.9 2.1 %collective-permute-done.18.refs_3_ = bf16[16,3584]{1,0:T(8,128)(2,1)S(1)} collective-permute-done((bf16[16,3584]{1,0:T(8,128)(2,1)S(1)}, bf16[16,3584]{1,0:T(8,128)(2,1)S(1)}, u32[]{:S(2)}, u32[]{:S(2)}) %collective-permute-start.18) | collective-permute-done | bytes 114720 | tf_op jit(solution)/shard_map/ppermute | solution.py:82
  58.0 2.8 %collective-permute-start.20 = (bf16[16,3584]{1,0:T(8,128)(2,1)S(1)}, bf16[16,3584]{1,0:T(8,128)(2,1)S(1)}, u32[]{:S(2)}, u32[]{:S(2)}) collective-permute-start(bf16[16,3584]{1,0:T(8,128)(2,1)S(1)} %combine.13.refs_1_), channel_id=1, source_target_pairs={{0,24},{4,28},{8,16},{12,20},{16,8},{20,12},{24,0},{28,4},{1,25},{... | collective-permute-start | bytes 344072 | tf_op jit(solution)/shard_map/ppermute | solution.py:88
  60.9 1.7 %collective-permute-start.19 = (bf16[32,3584]{1,0:T(8,128)(2,1)S(1)}, bf16[32,3584]{1,0:T(8,128)(2,1)S(1)}, u32[]{:S(2)}, u32[]{:S(2)}) collective-permute-start(bf16[32,3584]{1,0:T(8,128)(2,1)S(1)} %combine.14.refs_4_), channel_id=1, source_target_pairs={{0,3},{1,2},{2,1},{3,0},{4,7},{5,6},{6,5},{7,4},{8,11},{9,10},{10,... | collective-permute-start | bytes 688136 | tf_op jit(solution)/shard_map/ppermute | solution.py:88
  62.8 1.9 %collective-permute-done.20.refs_2_ = bf16[16,3584]{1,0:T(8,128)(2,1)S(1)} collective-permute-done((bf16[16,3584]{1,0:T(8,128)(2,1)S(1)}, bf16[16,3584]{1,0:T(8,128)(2,1)S(1)}, u32[]{:S(2)}, u32[]{:S(2)}) %collective-permute-start.20) | collective-permute-done | bytes 114720 | tf_op jit(solution)/shard_map/ppermute | solution.py:88
  64.7 3.2 %collective-permute-done.19.refs_1_ = bf16[32,3584]{1,0:T(8,128)(2,1)S(1)} collective-permute-done((bf16[32,3584]{1,0:T(8,128)(2,1)S(1)}, bf16[32,3584]{1,0:T(8,128)(2,1)S(1)}, u32[]{:S(2)}, u32[]{:S(2)}) %collective-permute-start.19) | collective-permute-done | bytes 229408 | tf_op jit(solution)/shard_map/ppermute | solution.py:88
  68.9 3.9 %collective-permute-done.25.refs_2_ = bf16[16,3584]{1,0:T(8,128)(2,1)S(1)} collective-permute-done((bf16[16,3584]{1,0:T(8,128)(2,1)S(1)}, bf16[16,3584]{1,0:T(8,128)(2,1)S(1)}, u32[]{:S(2)}, u32[]{:S(2)}) %collective-permute-start.25) | collective-permute-done | bytes 114720 | tf_op jit(solution)/shard_map/ppermute | solution.py:82
  (53 shorter events, 12.8 us)
Async XLA Ops:
  3.1 7.6 %collective-permute-start = (bf16[16,3712]{1,0:T(8,128)(2,1)S(1)}, bf16[16,3712]{1,0:T(8,128)(2,1)S(1)}, u32[]{:S(2)}, u32[]{:S(2)}) collective-permute-start(bf16[16,3712]{1,0:T(8,128)(2,1)S(1)} %pack.1.refs_0_), channel_id=1, source_target_pairs={{0,8},{4,12},{8,0},{12,4},{16,24},{20,28},{24,16},{28,20},{1,9},{5... | collective-permute-start | bytes 356360 | tf_op jit(solution)/shard_map/ppermute | solution.py:82
  6.1 8.2 %collective-permute-start.3 = (bf16[16,3712]{1,0:T(8,128)(2,1)S(1)}, bf16[16,3712]{1,0:T(8,128)(2,1)S(1)}, u32[]{:S(2)}, u32[]{:S(2)}) collective-permute-start(bf16[16,3712]{1,0:T(8,128)(2,1)S(1)} %pack.1.refs_0_), channel_id=1, source_target_pairs={{0,16},{4,20},{8,24},{12,28},{16,0},{20,4},{24,8},{28,12},{1,17},{... | collective-permute-start | bytes 356360 | tf_op jit(solution)/shard_map/ppermute | solution.py:82
  10.7 8.5 %collective-permute-start.2 = (bf16[32,3712]{1,0:T(8,128)(2,1)S(1)}, bf16[32,3712]{1,0:T(8,128)(2,1)S(1)}, u32[]{:S(2)}, u32[]{:S(2)}) collective-permute-start(bf16[32,3712]{1,0:T(8,128)(2,1)S(1)} %combine.9.refs_0_), channel_id=1, source_target_pairs={{0,2},{1,3},{2,0},{3,1},{4,6},{5,7},{6,4},{7,5},{8,10},{9,11},{10,... | collective-permute-start | bytes 712712 | tf_op jit(solution)/shard_map/ppermute | solution.py:82
  12.6 6.6 %collective-permute-start.1 = (bf16[32,3712]{1,0:T(8,128)(2,1)S(1)}, bf16[32,3712]{1,0:T(8,128)(2,1)S(1)}, u32[]{:S(2)}, u32[]{:S(2)}) collective-permute-start(bf16[32,3712]{1,0:T(8,128)(2,1)S(1)} %combine.9.refs_0_), channel_id=1, source_target_pairs={{0,1},{1,0},{2,3},{3,2},{4,5},{5,4},{6,7},{7,6},{8,9},{9,8},{10,11... | collective-permute-start | bytes 712712 | tf_op jit(solution)/shard_map/ppermute | solution.py:82
  14.3 4.8 %collective-permute-start.4 = (bf16[16,3712]{1,0:T(8,128)(2,1)S(1)}, bf16[16,3712]{1,0:T(8,128)(2,1)S(1)}, u32[]{:S(2)}, u32[]{:S(2)}) collective-permute-start(bf16[16,3712]{1,0:T(8,128)(2,1)S(1)} %collective-permute-done.3.refs_3_), channel_id=1, source_target_pairs={{0,8},{4,12},{8,0},{12,4},{16,24},{20,28},{24,16},{28,20},{1,9},{5... | collective-permute-start | bytes 356360 | tf_op jit(solution)/shard_map/ppermute | solution.py:82
  19.3 4.3 %collective-permute-start.5 = (bf16[128,3712]{1,0:T(8,128)(2,1)S(1)}, bf16[128,3712]{1,0:T(8,128)(2,1)S(1)}, u32[]{:S(2)}, u32[]{:S(2)}) collective-permute-start(bf16[128,3712]{1,0:T(8,128)(2,1)S(1)} %get-tuple-element.31.own), channel_id=1, source_target_pairs={{0,4},{4,0},{8,12},{12,8},{16,20},{20,16},{24,28},{28,24},{1,5},{5... | collective-permute-start | bytes 2850824 | tf_op jit(solution)/shard_map/ppermute | solution.py:82
  19.4 16.9 %collective-permute-start.9 = (bf16[48,3712]{1,0:T(8,128)(2,1)S(1)}, bf16[48,3712]{1,0:T(8,128)(2,1)S(1)}, u32[]{:S(2)}, u32[]{:S(2)}) collective-permute-start(bf16[48,3712]{1,0:T(8,128)(2,1)S(1)} %get-tuple-element.39), channel_id=1, source_target_pairs={{0,1},{1,0},{2,3},{3,2},{4,5},{5,4},{6,7},{7,6},{8,9},{9,8},{10,11... | collective-permute-start | bytes 1069064 | tf_op jit(solution)/shard_map/ppermute | solution.py:82
  20.9 15.5 %collective-permute-start.10 = (bf16[48,3712]{1,0:T(8,128)(2,1)S(1)}, bf16[48,3712]{1,0:T(8,128)(2,1)S(1)}, u32[]{:S(2)}, u32[]{:S(2)}) collective-permute-start(bf16[48,3712]{1,0:T(8,128)(2,1)S(1)} %get-tuple-element.40), channel_id=1, source_target_pairs={{0,2},{1,3},{2,0},{3,1},{4,6},{5,7},{6,4},{7,5},{8,10},{9,11},{10,... | collective-permute-start | bytes 1069064 | tf_op jit(solution)/shard_map/ppermute | solution.py:82
  22.4 13.8 %collective-permute-start.11 = (bf16[32,3712]{1,0:T(8,128)(2,1)S(1)}, bf16[32,3712]{1,0:T(8,128)(2,1)S(1)}, u32[]{:S(2)}, u32[]{:S(2)}) collective-permute-start(bf16[32,3712]{1,0:T(8,128)(2,1)S(1)} %get-tuple-element.41), channel_id=1, source_target_pairs={{0,3},{1,2},{2,1},{3,0},{4,7},{5,6},{6,5},{7,4},{8,11},{9,10},{10,... | collective-permute-start | bytes 712712 | tf_op jit(solution)/shard_map/ppermute | solution.py:88
  31.1 5.5 %collective-permute-start.6 = (bf16[128,3584]{1,0:T(8,128)(2,1)S(1)}, bf16[128,3584]{1,0:T(8,128)(2,1)S(1)}, u32[]{:S(2)}, u32[]{:S(2)}) collective-permute-start(bf16[128,3584]{1,0:T(8,128)(2,1)S(1)} %get-tuple-element.32.refs_0_), channel_id=1, source_target_pairs={{0,4},{4,0},{8,12},{12,8},{16,20},{20,16},{24,28},{28,24},{1,5},{5... | collective-permute-start | bytes 2752520 | tf_op jit(solution)/shard_map/ppermute | solution.py:82
  37.2 8.1 %collective-permute-start.7 = (bf16[32,3584]{1,0:T(8,128)(2,1)S(1)}, bf16[32,3584]{1,0:T(8,128)(2,1)S(1)}, u32[]{:S(2)}, u32[]{:S(2)}) collective-permute-start(bf16[32,3584]{1,0:T(8,128)(2,1)S(1)} %get-tuple-element.37), channel_id=1, source_target_pairs={{0,1},{1,0},{2,3},{3,2},{4,5},{5,4},{6,7},{7,6},{8,9},{9,8},{10,11... | collective-permute-start | bytes 688136 | tf_op jit(solution)/shard_map/ppermute | solution.py:82
  38.5 7.7 %collective-permute-start.8 = (bf16[32,3584]{1,0:T(8,128)(2,1)S(1)}, bf16[32,3584]{1,0:T(8,128)(2,1)S(1)}, u32[]{:S(2)}, u32[]{:S(2)}) collective-permute-start(bf16[32,3584]{1,0:T(8,128)(2,1)S(1)} %get-tuple-element.38), channel_id=1, source_target_pairs={{0,2},{1,3},{2,0},{3,1},{4,6},{5,7},{6,4},{7,5},{8,10},{9,11},{10,... | collective-permute-start | bytes 688136 | tf_op jit(solution)/shard_map/ppermute | solution.py:82
  42.0 4.3 %collective-permute-start.15 = (bf16[64,3584]{1,0:T(8,128)(2,1)S(1)}, bf16[64,3584]{1,0:T(8,128)(2,1)S(1)}, u32[]{:S(2)}, u32[]{:S(2)}) collective-permute-start(bf16[64,3584]{1,0:T(8,128)(2,1)S(1)} %get-tuple-element.48), channel_id=1, source_target_pairs={{0,4},{4,0},{8,12},{12,8},{16,20},{20,16},{24,28},{28,24},{1,5},{5... | collective-permute-start | bytes 1376264 | tf_op jit(solution)/shard_map/ppermute | solution.py:82
  42.1 4.2 %collective-permute-start.13 = (bf16[32,3584]{1,0:T(8,128)(2,1)S(1)}, bf16[32,3584]{1,0:T(8,128)(2,1)S(1)}, u32[]{:S(2)}, u32[]{:S(2)}) collective-permute-start(bf16[32,3584]{1,0:T(8,128)(2,1)S(1)} %get-tuple-element.46), channel_id=1, source_target_pairs={{0,4},{4,0},{8,12},{12,8},{16,20},{20,16},{24,28},{28,24},{1,5},{5... | collective-permute-start | bytes 688136 | tf_op jit(solution)/shard_map/ppermute | solution.py:82
  47.0 7.1 %collective-permute-start.16 = (bf16[16,3584]{1,0:T(8,128)(2,1)S(1)}, bf16[16,3584]{1,0:T(8,128)(2,1)S(1)}, u32[]{:S(2)}, u32[]{:S(2)}) collective-permute-start(bf16[16,3584]{1,0:T(8,128)(2,1)S(1)} %get-tuple-element.51), channel_id=1, source_target_pairs={{0,3},{1,2},{2,1},{3,0},{4,7},{5,6},{6,5},{7,4},{8,11},{9,10},{10,... | collective-permute-start | bytes 344072 | tf_op jit(solution)/shard_map/ppermute | solution.py:88
  48.8 7.0 %collective-permute-start.17 = (bf16[16,3584]{1,0:T(8,128)(2,1)S(1)}, bf16[16,3584]{1,0:T(8,128)(2,1)S(1)}, u32[]{:S(2)}, u32[]{:S(2)}) collective-permute-start(bf16[16,3584]{1,0:T(8,128)(2,1)S(1)} %get-tuple-element.52), channel_id=1, source_target_pairs={{0,1},{1,0},{2,3},{3,2},{4,5},{5,4},{6,7},{7,6},{8,9},{9,8},{10,11... | collective-permute-start | bytes 344072 | tf_op jit(solution)/shard_map/ppermute | solution.py:82
  49.4 8.6 %collective-permute-start.18 = (bf16[16,3584]{1,0:T(8,128)(2,1)S(1)}, bf16[16,3584]{1,0:T(8,128)(2,1)S(1)}, u32[]{:S(2)}, u32[]{:S(2)}) collective-permute-start(bf16[16,3584]{1,0:T(8,128)(2,1)S(1)} %get-tuple-element.53), channel_id=1, source_target_pairs={{0,2},{1,3},{2,0},{3,1},{4,6},{5,7},{6,4},{7,5},{8,10},{9,11},{10,... | collective-permute-start | bytes 344072 | tf_op jit(solution)/shard_map/ppermute | solution.py:82
  50.6 12.0 %collective-permute-start.21 = (bf16[16,3584]{1,0:T(8,128)(2,1)S(1)}, bf16[16,3584]{1,0:T(8,128)(2,1)S(1)}, u32[]{:S(2)}, u32[]{:S(2)}) collective-permute-start(bf16[16,3584]{1,0:T(8,128)(2,1)S(1)} %get-tuple-element.55), channel_id=1, source_target_pairs={{0,3},{1,2},{2,1},{3,0},{4,7},{5,6},{6,5},{7,4},{8,11},{9,10},{10,... | collective-permute-start | bytes 344072 | tf_op jit(solution)/shard_map/ppermute | solution.py:88
  52.3 10.3 %collective-permute-start.22 = (bf16[16,3584]{1,0:T(8,128)(2,1)S(1)}, bf16[16,3584]{1,0:T(8,128)(2,1)S(1)}, u32[]{:S(2)}, u32[]{:S(2)}) collective-permute-start(bf16[16,3584]{1,0:T(8,128)(2,1)S(1)} %get-tuple-element.56), channel_id=1, source_target_pairs={{0,1},{1,0},{2,3},{3,2},{4,5},{5,4},{6,7},{7,6},{8,9},{9,8},{10,11... | collective-permute-start | bytes 344072 | tf_op jit(solution)/shard_map/ppermute | solution.py:82
  54.1 8.5 %collective-permute-start.23 = (bf16[16,3584]{1,0:T(8,128)(2,1)S(1)}, bf16[16,3584]{1,0:T(8,128)(2,1)S(1)}, u32[]{:S(2)}, u32[]{:S(2)}) collective-permute-start(bf16[16,3584]{1,0:T(8,128)(2,1)S(1)} %get-tuple-element.57), channel_id=1, source_target_pairs={{0,2},{1,3},{2,0},{3,1},{4,6},{5,7},{6,4},{7,5},{8,10},{9,11},{10,... | collective-permute-start | bytes 344072 | tf_op jit(solution)/shard_map/ppermute | solution.py:82
  58.0 6.7 %collective-permute-start.20 = (bf16[16,3584]{1,0:T(8,128)(2,1)S(1)}, bf16[16,3584]{1,0:T(8,128)(2,1)S(1)}, u32[]{:S(2)}, u32[]{:S(2)}) collective-permute-start(bf16[16,3584]{1,0:T(8,128)(2,1)S(1)} %combine.13.refs_1_), channel_id=1, source_target_pairs={{0,24},{4,28},{8,16},{12,20},{16,8},{20,12},{24,0},{28,4},{1,25},{... | collective-permute-start | bytes 344072 | tf_op jit(solution)/shard_map/ppermute | solution.py:88
  60.9 7.0 %collective-permute-start.19 = (bf16[32,3584]{1,0:T(8,128)(2,1)S(1)}, bf16[32,3584]{1,0:T(8,128)(2,1)S(1)}, u32[]{:S(2)}, u32[]{:S(2)}) collective-permute-start(bf16[32,3584]{1,0:T(8,128)(2,1)S(1)} %combine.14.refs_4_), channel_id=1, source_target_pairs={{0,3},{1,2},{2,1},{3,0},{4,7},{5,6},{6,5},{7,4},{8,11},{9,10},{10,... | collective-permute-start | bytes 688136 | tf_op jit(solution)/shard_map/ppermute | solution.py:88
  62.7 6.3 %collective-permute-start.24 = (bf16[16,3584]{1,0:T(8,128)(2,1)S(1)}, bf16[16,3584]{1,0:T(8,128)(2,1)S(1)}, u32[]{:S(2)}, u32[]{:S(2)}) collective-permute-start(bf16[16,3584]{1,0:T(8,128)(2,1)S(1)} %combine.15.refs_3_), channel_id=1, source_target_pairs={{0,16},{4,20},{8,24},{12,28},{16,0},{20,4},{24,8},{28,12},{1,17},{... | collective-permute-start | bytes 344072 | tf_op jit(solution)/shard_map/ppermute | solution.py:82
  67.9 4.9 %collective-permute-start.25 = (bf16[16,3584]{1,0:T(8,128)(2,1)S(1)}, bf16[16,3584]{1,0:T(8,128)(2,1)S(1)}, u32[]{:S(2)}, u32[]{:S(2)}) collective-permute-start(bf16[16,3584]{1,0:T(8,128)(2,1)S(1)} %get-tuple-element.59), channel_id=1, source_target_pairs={{0,8},{4,12},{8,0},{12,4},{16,24},{20,28},{24,16},{28,20},{1,9},{5... | collective-permute-start | bytes 344072 | tf_op jit(solution)/shard_map/ppermute | solution.py:82
  (6 other events, 30.3 us)

commit v12 on v11

--- a/solution.py
+++ b/solution.py
@@ -499,7 +499,11 @@
     context, done = attention([first_out])
     (second_own,) = combine(
         [far_x, far_y, far_xy],
-        [rows_of((0, 0, 2 * n), (1, 0, 2 * n), (2, 0, 2 * n), (1, 2 * n, n), (0, 2 * n, n))],
+        [
+            rows_of(
+                (0, 0, 2 * n), (1, 0, 2 * n), (2, n, n), (2, 0, n), (1, 2 * n, n), (0, 2 * n, n)
+            )
+        ],
         [done],
     )
     second_other = swap(second_own, core)
@@ -516,19 +520,22 @@
         return [(count, [(index, start) for index in range(terms)])]
 
     (near,) = combine([near, *to_near], [all_of(3, 0, 2 * n)], flops=NEAR_FLOPS)
-    far_x, both_x, far_y, both_y, far_xy, both_xy, near_xy = sums_of(
-        second_h, w_down, second_in, [n] * 6 + [2 * n], [near]
+    far_x, both_x, far_y, both_y, both_xy, corner = sums_of(
+        second_h, w_down, second_in, [n] * 5 + [3 * n], [near]
     )
 
     to_both = [across(both_xy, x, y), swap(both_x, x), swap(both_y, y)]
-    to_far = [across(far_xy, x, y), swap(far_x, x), swap(far_y, y)]
+    to_rest = [across(corner, x, y), swap(far_x, x), swap(far_y, y)]
     (both_sum,) = combine([both_sum, *to_both], [all_of(4, 0)])
-    (near_xy,) = combine([near_xy], [rows_of((0, 0, 2 * n))], [both_sum])
-    to_near = across(near_xy, x, y)
-    (far_sum,) = combine([far_sum, *to_far], [all_of(4, 0)], [near_xy], flops=FAR_FLOPS)
+    far_sum, near_sum = combine(
+        [far_sum, *to_rest, near], [all_of(4, 0), [(n, [(1, 2 * n), (4, n)])]], [both_sum]
+    )
     from_both = across(both_sum, z_far, z_near)
-    own_sum, near_sum = combine(
-        [near, to_near, from_both], [all_of(3, 0), all_of(2, n)], [far_sum]
+    (own_sum,) = combine(
+        [near, to_rest[0], from_both],
+        [[(n, [(0, 0), (1, n), (2, 0)])]],
+        [near_sum],
+        flops=FAR_FLOPS,
     )
     (mixed,) = combine(
         [own_sum, swap(far_sum, z_far), swap(near_sum, z_near)], [all_of(3, 0)]

time: 73.7 us -> 76 us (1.031)
  starting transfers between devices: 27.3 us -> 28.7 us
  waiting for transfers between devices: 26.8 us -> 27.8 us
    ppermute x5 -> x4, waiting for transfers between devices: 8.73 us -> 12.4 us  [across(): lax.ppermute(value, axis, [(i, i ^ first[1] ^ second[1]) for i in range(s...]
    ppermute x21, starting transfers between devices: 18.7 us -> 22.3 us  [swap(): return lax.ppermute(value, axis, [(i, i ^ bit) for i in range(size)])]
    ppermute x21, waiting for transfers between devices: 18.1 us -> 15.4 us  [swap(): return lax.ppermute(value, axis, [(i, i ^ bit) for i in range(size)])]
    ppermute x5 -> x4, starting transfers between devices: 8.57 us -> 6.41 us  [across(): lax.ppermute(value, axis, [(i, i ^ first[1] ^ second[1]) for i in range(s...]
  transfers between devices with their start and end apart: 26 -> 25, of which waited for: 14 -> 12; matrix products, arithmetic and copies ran while one was open for 0% -> 0% of each run, Pallas kernels for 19% -> 18%
where the time goes in v12:
time: 76 us; the launch traced here: 75.8 us
  starting transfers between devices  28.7 us (38%)
  waiting for transfers between devices  27.8 us (37%)
  Pallas kernels  15.5 us (20%)
  between operations  1.48 us (2%)
  other arithmetic  1.38 us (2%)
  local copies, waits for them, and re-layouts  0.92 us (1%)
    ppermute x21, starting transfers between devices, swap(): return lax.ppermute(value, axis, [(i, i ^ bit) for i in range(size)])  22.3 us
    ppermute x21, waiting for transfers between devices, swap(): return lax.ppermute(value, axis, [(i, i ^ bit) for i in range(size)])  15.4 us
    ppermute x4, waiting for transfers between devices, across(): lax.ppermute(value, axis, [(i, i ^ first[1] ^ second[1]) for i in range(s...  12.4 us
    pallas_call x1, Pallas kernels, first_of(): pl.pallas_call(functools.partial(first_kernel, picks), out_shape=[jax.Sha...  7.48 us
    ppermute x4, starting transfers between devices, across(): lax.ppermute(value, axis, [(i, i ^ first[1] ^ second[1]) for i in range(s...  6.41 us
    pallas_call x1, Pallas kernels, attend(): pl.pallas_call(attend_kernel, out_shape=[jax.ShapeDtypeStruct((count, hea...  2.7 us
    pallas_call x1, Pallas kernels, expert_of(): pl.pallas_call(functools.partial(expert_kernel, picks, len(after)), out_s...  2.7 us
  transfers between devices with their start and end apart: 25, of which 12 were waited for; matrix products, arithmetic and copies ran while one was open for 0% of the time, Pallas kernels for 18%

profile of v12, /device:TPU:0, one launch (start us, length us, event | category | flops | bytes accessed | tf_op | source)
XLA Modules:
  0.0 75.8 jit_solution(14157357866690013883)
XLA Ops:
  3.1 3.0 %collective-permute-start = (bf16[16,3712]{1,0:T(8,128)(2,1)S(1)}, bf16[16,3712]{1,0:T(8,128)(2,1)S(1)}, u32[]{:S(2)}, u32[]{:S(2)}) collective-permute-start(bf16[16,3712]{1,0:T(8,128)(2,1)S(1)} %pack.1.refs_0_), channel_id=1, source_target_pairs={{0,8},{4,12},{8,0},{12,4},{16,24},{20,28},{24,16},{28,20},{1,9},{5... | collective-permute-start | bytes 356360 | tf_op jit(solution)/shard_map/ppermute | solution.py:82
  6.1 2.6 %collective-permute-start.3 = (bf16[16,3712]{1,0:T(8,128)(2,1)S(1)}, bf16[16,3712]{1,0:T(8,128)(2,1)S(1)}, u32[]{:S(2)}, u32[]{:S(2)}) collective-permute-start(bf16[16,3712]{1,0:T(8,128)(2,1)S(1)} %pack.1.refs_0_), channel_id=1, source_target_pairs={{0,16},{4,20},{8,24},{12,28},{16,0},{20,4},{24,8},{28,12},{1,17},{... | collective-permute-start | bytes 356360 | tf_op jit(solution)/shard_map/ppermute | solution.py:82
  8.7 1.9 %collective-permute-done.refs_1_ = bf16[16,3712]{1,0:T(8,128)(2,1)S(1)} collective-permute-done((bf16[16,3712]{1,0:T(8,128)(2,1)S(1)}, bf16[16,3712]{1,0:T(8,128)(2,1)S(1)}, u32[]{:S(2)}, u32[]{:S(2)}) %collective-permute-start) | collective-permute-done | bytes 118816 | tf_op jit(solution)/shard_map/ppermute | solution.py:82
  10.7 1.9 %collective-permute-start.2 = (bf16[32,3712]{1,0:T(8,128)(2,1)S(1)}, bf16[32,3712]{1,0:T(8,128)(2,1)S(1)}, u32[]{:S(2)}, u32[]{:S(2)}) collective-permute-start(bf16[32,3712]{1,0:T(8,128)(2,1)S(1)} %combine.8.refs_0_), channel_id=1, source_target_pairs={{0,2},{1,3},{2,0},{3,1},{4,6},{5,7},{6,4},{7,5},{8,10},{9,11},{10,... | collective-permute-start | bytes 712712 | tf_op jit(solution)/shard_map/ppermute | solution.py:82
  12.6 1.5 %collective-permute-start.1 = (bf16[32,3712]{1,0:T(8,128)(2,1)S(1)}, bf16[32,3712]{1,0:T(8,128)(2,1)S(1)}, u32[]{:S(2)}, u32[]{:S(2)}) collective-permute-start(bf16[32,3712]{1,0:T(8,128)(2,1)S(1)} %combine.8.refs_0_), channel_id=1, source_target_pairs={{0,1},{1,0},{2,3},{3,2},{4,5},{5,4},{6,7},{7,6},{8,9},{9,8},{10,11... | collective-permute-start | bytes 712712 | tf_op jit(solution)/shard_map/ppermute | solution.py:82
  14.7 4.4 %collective-permute-done.4.refs_4_ = bf16[16,3712]{1,0:T(8,128)(2,1)S(1)} collective-permute-done((bf16[16,3712]{1,0:T(8,128)(2,1)S(1)}, bf16[16,3712]{1,0:T(8,128)(2,1)S(1)}, u32[]{:S(2)}, u32[]{:S(2)}) %collective-permute-start.4) | collective-permute-done | bytes 118816 | tf_op jit(solution)/shard_map/ppermute | solution.py:82
  19.4 1.6 %collective-permute-start.9 = (bf16[48,3712]{1,0:T(8,128)(2,1)S(1)}, bf16[48,3712]{1,0:T(8,128)(2,1)S(1)}, u32[]{:S(2)}, u32[]{:S(2)}) collective-permute-start(bf16[48,3712]{1,0:T(8,128)(2,1)S(1)} %get-tuple-element.38), channel_id=1, source_target_pairs={{0,1},{1,0},{2,3},{3,2},{4,5},{5,4},{6,7},{7,6},{8,9},{9,8},{10,11... | collective-permute-start | bytes 1069064 | tf_op jit(solution)/shard_map/ppermute | solution.py:82
  20.9 1.5 %collective-permute-start.10 = (bf16[48,3712]{1,0:T(8,128)(2,1)S(1)}, bf16[48,3712]{1,0:T(8,128)(2,1)S(1)}, u32[]{:S(2)}, u32[]{:S(2)}) collective-permute-start(bf16[48,3712]{1,0:T(8,128)(2,1)S(1)} %get-tuple-element.39), channel_id=1, source_target_pairs={{0,2},{1,3},{2,0},{3,1},{4,6},{5,7},{6,4},{7,5},{8,10},{9,11},{10,... | collective-permute-start | bytes 1069064 | tf_op jit(solution)/shard_map/ppermute | solution.py:82
  23.6 7.5 %first.1 = (bf16[128,512]{1,0:T(8,128)(2,1)S(1)}, bf16[128,3584]{1,0:T(8,128)(2,1)S(1)}, bf16[1,3584,512]{2,1,0:T(8,128)(2,1)S(1)}, bf16[1,3584,512]{2,1,0:T(8,128)(2,1)S(1)}, bf16[1,512,3584]{2,1,0:T(8,128)(2,1)S(1)}) custom-call(bf16[128,3712]{1,0:T(8,128)(2,1)S(1)} %get-tuple-element.30.own, bf16[128,3712]{1,0:T(8,128)(2,1)S(1)} %collective-permute-done.5.other, ...), custom_call_target="tpu_custom_call" | custom-call | flops 2348810240 | bytes 11010048 | tf_op jit(solution)/shard_map/first/pallas_call | solution.py:365
  31.2 2.7 %attend.1 = (bf16[4,64,512]{2,1,0:T(8,128)(2,1)}, f32[8,128]{1,0:T(8,128)S(1)}) custom-call(s32[4]{0:T(128)S(1)} %copy-done.3, s32[1]{0:T(128)S(6)} %copy.12.live_rows, bf16[4,64,576]{2,1,0:T(8,128)(2,1)S(1)} %copy-done.1, bf16[4,576,256]{2,1,0:T(8,128)(2,1)S(1)} %bitcast.4, bf16[128,3584]{1,0:T(8,128)(2,1)S(1)} %get-tuple-element.31.refs_0_), custom_call_target="tpu_custom_call" | custom-call | flops 150994944 | bytes 1179648 | tf_op jit(solution)/shard_map/attend/pallas_call | solution.py:55
  33.9 2.3 %collective-permute-done.11.refs_2_ = bf16[32,3712]{1,0:T(8,128)(2,1)S(1)} collective-permute-done((bf16[32,3712]{1,0:T(8,128)(2,1)S(1)}, bf16[32,3712]{1,0:T(8,128)(2,1)S(1)}, u32[]{:S(2)}, u32[]{:S(2)}) %collective-permute-start.11) | collective-permute-done | bytes 237600 | tf_op jit(solution)/shard_map/ppermute | solution.py:88
  37.2 1.3 %collective-permute-start.7 = (bf16[32,3584]{1,0:T(8,128)(2,1)S(1)}, bf16[32,3584]{1,0:T(8,128)(2,1)S(1)}, u32[]{:S(2)}, u32[]{:S(2)}) collective-permute-start(bf16[32,3584]{1,0:T(8,128)(2,1)S(1)} %get-tuple-element.36), channel_id=1, source_target_pairs={{0,1},{1,0},{2,3},{3,2},{4,5},{5,4},{6,7},{7,6},{8,9},{9,8},{10,11... | collective-permute-start | bytes 688136 | tf_op jit(solution)/shard_map/ppermute | solution.py:82
  39.3 2.7 %expert.1 = (bf16[128,512]{1,0:T(8,128)(2,1)S(1)}, bf16[32,3584]{1,0:T(8,128)(2,1)S(1)}, bf16[32,3584]{1,0:T(8,128)(2,1)S(1)}, bf16[64,3584]{1,0:T(8,128)(2,1)S(1)}) custom-call(bf16[128,3712]{1,0:T(8,128)(2,1)S(1)} %combine.11.own, bf16[128,3712]{1,0:T(8,128)(2,1)S(1)} %collective-permute-done.12.other, bf16[1,3584,512]{2,1,0:T(8,128)(2,1)S(1)} %get-tuple-element.42.w_gate, ...), custom_call_target="tpu_custom_call" | custom-call | flops 2348810240 | bytes 917504 | tf_op jit(solution)/shard_map/expert/pallas_call | solution.py:390
  42.7 2.6 %collective-permute-done.7.refs_1_ = bf16[32,3584]{1,0:T(8,128)(2,1)S(1)} collective-permute-done((bf16[32,3584]{1,0:T(8,128)(2,1)S(1)}, bf16[32,3584]{1,0:T(8,128)(2,1)S(1)}, u32[]{:S(2)}, u32[]{:S(2)}) %collective-permute-start.7) | collective-permute-done | bytes 229408 | tf_op jit(solution)/shard_map/ppermute | solution.py:82
  45.3 1.0 %collective-permute-done.8.refs_2_ = bf16[32,3584]{1,0:T(8,128)(2,1)S(1)} collective-permute-done((bf16[32,3584]{1,0:T(8,128)(2,1)S(1)}, bf16[32,3584]{1,0:T(8,128)(2,1)S(1)}, u32[]{:S(2)}, u32[]{:S(2)}) %collective-permute-start.8) | collective-permute-done | bytes 229408 | tf_op jit(solution)/shard_map/ppermute | solution.py:82
  47.0 1.8 %collective-permute-start.16 = (bf16[48,3584]{1,0:T(8,128)(2,1)S(1)}, bf16[48,3584]{1,0:T(8,128)(2,1)S(1)}, u32[]{:S(2)}, u32[]{:S(2)}) collective-permute-start(bf16[48,3584]{1,0:T(8,128)(2,1)S(1)} %get-tuple-element.48), channel_id=1, source_target_pairs={{0,3},{1,2},{2,1},{3,0},{4,7},{5,6},{6,5},{7,4},{8,11},{9,10},{10,... | collective-permute-start | bytes 1032200 | tf_op jit(solution)/shard_map/ppermute | solution.py:88
  48.8 1.2 %collective-permute-start.17 = (bf16[16,3584]{1,0:T(8,128)(2,1)S(1)}, bf16[16,3584]{1,0:T(8,128)(2,1)S(1)}, u32[]{:S(2)}, u32[]{:S(2)}) collective-permute-start(bf16[16,3584]{1,0:T(8,128)(2,1)S(1)} %get-tuple-element.50), channel_id=1, source_target_pairs={{0,3},{1,2},{2,1},{3,0},{4,7},{5,6},{6,5},{7,4},{8,11},{9,10},{10,... | collective-permute-start | bytes 344072 | tf_op jit(solution)/shard_map/ppermute | solution.py:88
  50.8 1.5 %collective-permute-start.19 = (bf16[16,3584]{1,0:T(8,128)(2,1)S(1)}, bf16[16,3584]{1,0:T(8,128)(2,1)S(1)}, u32[]{:S(2)}, u32[]{:S(2)}) collective-permute-start(bf16[16,3584]{1,0:T(8,128)(2,1)S(1)} %get-tuple-element.52), channel_id=1, source_target_pairs={{0,2},{1,3},{2,0},{3,1},{4,6},{5,7},{6,4},{7,5},{8,10},{9,11},{10,... | collective-permute-start | bytes 344072 | tf_op jit(solution)/shard_map/ppermute | solution.py:82
  52.8 8.6 %collective-permute-done.17.refs_1_ = bf16[16,3584]{1,0:T(8,128)(2,1)S(1)} collective-permute-done((bf16[16,3584]{1,0:T(8,128)(2,1)S(1)}, bf16[16,3584]{1,0:T(8,128)(2,1)S(1)}, u32[]{:S(2)}, u32[]{:S(2)}) %collective-permute-start.17) | collective-permute-done | bytes 114720 | tf_op jit(solution)/shard_map/ppermute | solution.py:88
  63.0 2.9 %collective-permute-start.20 = (bf16[16,3584]{1,0:T(8,128)(2,1)S(1)}, bf16[16,3584]{1,0:T(8,128)(2,1)S(1)}, u32[]{:S(2)}, u32[]{:S(2)}) collective-permute-start(bf16[16,3584]{1,0:T(8,128)(2,1)S(1)} %combine.12.refs_5_), channel_id=1, source_target_pairs={{0,24},{4,28},{8,16},{12,20},{16,8},{20,12},{24,0},{28,4},{1,25},{... | collective-permute-start | bytes 344072 | tf_op jit(solution)/shard_map/ppermute | solution.py:88
  66.4 1.4 %collective-permute-start.23 = (bf16[16,3584]{1,0:T(8,128)(2,1)S(1)}, bf16[16,3584]{1,0:T(8,128)(2,1)S(1)}, u32[]{:S(2)}, u32[]{:S(2)}) collective-permute-start(bf16[16,3584]{1,0:T(8,128)(2,1)S(1)} %get-tuple-element.57), channel_id=1, source_target_pairs={{0,16},{4,20},{8,24},{12,28},{16,0},{20,4},{24,8},{28,12},{1,17},{... | collective-permute-start | bytes 344072 | tf_op jit(solution)/shard_map/ppermute | solution.py:82
  67.8 1.8 %collective-permute-start.24 = (bf16[16,3584]{1,0:T(8,128)(2,1)S(1)}, bf16[16,3584]{1,0:T(8,128)(2,1)S(1)}, u32[]{:S(2)}, u32[]{:S(2)}) collective-permute-start(bf16[16,3584]{1,0:T(8,128)(2,1)S(1)} %get-tuple-element.56.refs_3_), channel_id=1, source_target_pairs={{0,8},{4,12},{8,0},{12,4},{16,24},{20,28},{24,16},{28,20},{1,9},{5... | collective-permute-start | bytes 344072 | tf_op jit(solution)/shard_map/ppermute | solution.py:82
  69.6 1.4 %collective-permute-done.20.refs_2_ = bf16[16,3584]{1,0:T(8,128)(2,1)S(1)} collective-permute-done((bf16[16,3584]{1,0:T(8,128)(2,1)S(1)}, bf16[16,3584]{1,0:T(8,128)(2,1)S(1)}, u32[]{:S(2)}, u32[]{:S(2)}) %collective-permute-start.20) | collective-permute-done | bytes 114720 | tf_op jit(solution)/shard_map/ppermute | solution.py:88
  71.0 4.1 %collective-permute-done.23.refs_1_ = bf16[16,3584]{1,0:T(8,128)(2,1)S(1)} collective-permute-done((bf16[16,3584]{1,0:T(8,128)(2,1)S(1)}, bf16[16,3584]{1,0:T(8,128)(2,1)S(1)}, u32[]{:S(2)}, u32[]{:S(2)}) %collective-permute-start.23) | collective-permute-done | bytes 114720 | tf_op jit(solution)/shard_map/ppermute | solution.py:82
  (50 shorter events, 11.1 us)
Async XLA Ops:
  3.1 7.6 %collective-permute-start = (bf16[16,3712]{1,0:T(8,128)(2,1)S(1)}, bf16[16,3712]{1,0:T(8,128)(2,1)S(1)}, u32[]{:S(2)}, u32[]{:S(2)}) collective-permute-start(bf16[16,3712]{1,0:T(8,128)(2,1)S(1)} %pack.1.refs_0_), channel_id=1, source_target_pairs={{0,8},{4,12},{8,0},{12,4},{16,24},{20,28},{24,16},{28,20},{1,9},{5... | collective-permute-start | bytes 356360 | tf_op jit(solution)/shard_map/ppermute | solution.py:82
  6.1 8.2 %collective-permute-start.3 = (bf16[16,3712]{1,0:T(8,128)(2,1)S(1)}, bf16[16,3712]{1,0:T(8,128)(2,1)S(1)}, u32[]{:S(2)}, u32[]{:S(2)}) collective-permute-start(bf16[16,3712]{1,0:T(8,128)(2,1)S(1)} %pack.1.refs_0_), channel_id=1, source_target_pairs={{0,16},{4,20},{8,24},{12,28},{16,0},{20,4},{24,8},{28,12},{1,17},{... | collective-permute-start | bytes 356360 | tf_op jit(solution)/shard_map/ppermute | solution.py:82
  10.7 8.5 %collective-permute-start.2 = (bf16[32,3712]{1,0:T(8,128)(2,1)S(1)}, bf16[32,3712]{1,0:T(8,128)(2,1)S(1)}, u32[]{:S(2)}, u32[]{:S(2)}) collective-permute-start(bf16[32,3712]{1,0:T(8,128)(2,1)S(1)} %combine.8.refs_0_), channel_id=1, source_target_pairs={{0,2},{1,3},{2,0},{3,1},{4,6},{5,7},{6,4},{7,5},{8,10},{9,11},{10,... | collective-permute-start | bytes 712712 | tf_op jit(solution)/shard_map/ppermute | solution.py:82
  12.6 6.6 %collective-permute-start.1 = (bf16[32,3712]{1,0:T(8,128)(2,1)S(1)}, bf16[32,3712]{1,0:T(8,128)(2,1)S(1)}, u32[]{:S(2)}, u32[]{:S(2)}) collective-permute-start(bf16[32,3712]{1,0:T(8,128)(2,1)S(1)} %combine.8.refs_0_), channel_id=1, source_target_pairs={{0,1},{1,0},{2,3},{3,2},{4,5},{5,4},{6,7},{7,6},{8,9},{9,8},{10,11... | collective-permute-start | bytes 712712 | tf_op jit(solution)/shard_map/ppermute | solution.py:82
  14.3 4.8 %collective-permute-start.4 = (bf16[16,3712]{1,0:T(8,128)(2,1)S(1)}, bf16[16,3712]{1,0:T(8,128)(2,1)S(1)}, u32[]{:S(2)}, u32[]{:S(2)}) collective-permute-start(bf16[16,3712]{1,0:T(8,128)(2,1)S(1)} %collective-permute-done.3.refs_3_), channel_id=1, source_target_pairs={{0,8},{4,12},{8,0},{12,4},{16,24},{20,28},{24,16},{28,20},{1,9},{5... | collective-permute-start | bytes 356360 | tf_op jit(solution)/shard_map/ppermute | solution.py:82
  19.3 4.3 %collective-permute-start.5 = (bf16[128,3712]{1,0:T(8,128)(2,1)S(1)}, bf16[128,3712]{1,0:T(8,128)(2,1)S(1)}, u32[]{:S(2)}, u32[]{:S(2)}) collective-permute-start(bf16[128,3712]{1,0:T(8,128)(2,1)S(1)} %get-tuple-element.30.own), channel_id=1, source_target_pairs={{0,4},{4,0},{8,12},{12,8},{16,20},{20,16},{24,28},{28,24},{1,5},{5... | collective-permute-start | bytes 2850824 | tf_op jit(solution)/shard_map/ppermute | solution.py:82
  19.4 16.9 %collective-permute-start.9 = (bf16[48,3712]{1,0:T(8,128)(2,1)S(1)}, bf16[48,3712]{1,0:T(8,128)(2,1)S(1)}, u32[]{:S(2)}, u32[]{:S(2)}) collective-permute-start(bf16[48,3712]{1,0:T(8,128)(2,1)S(1)} %get-tuple-element.38), channel_id=1, source_target_pairs={{0,1},{1,0},{2,3},{3,2},{4,5},{5,4},{6,7},{7,6},{8,9},{9,8},{10,11... | collective-permute-start | bytes 1069064 | tf_op jit(solution)/shard_map/ppermute | solution.py:82
  20.9 15.5 %collective-permute-start.10 = (bf16[48,3712]{1,0:T(8,128)(2,1)S(1)}, bf16[48,3712]{1,0:T(8,128)(2,1)S(1)}, u32[]{:S(2)}, u32[]{:S(2)}) collective-permute-start(bf16[48,3712]{1,0:T(8,128)(2,1)S(1)} %get-tuple-element.39), channel_id=1, source_target_pairs={{0,2},{1,3},{2,0},{3,1},{4,6},{5,7},{6,4},{7,5},{8,10},{9,11},{10,... | collective-permute-start | bytes 1069064 | tf_op jit(solution)/shard_map/ppermute | solution.py:82
  22.4 13.8 %collective-permute-start.11 = (bf16[32,3712]{1,0:T(8,128)(2,1)S(1)}, bf16[32,3712]{1,0:T(8,128)(2,1)S(1)}, u32[]{:S(2)}, u32[]{:S(2)}) collective-permute-start(bf16[32,3712]{1,0:T(8,128)(2,1)S(1)} %get-tuple-element.40), channel_id=1, source_target_pairs={{0,3},{1,2},{2,1},{3,0},{4,7},{5,6},{6,5},{7,4},{8,11},{9,10},{10,... | collective-permute-start | bytes 712712 | tf_op jit(solution)/shard_map/ppermute | solution.py:88
  31.1 5.5 %collective-permute-start.6 = (bf16[128,3584]{1,0:T(8,128)(2,1)S(1)}, bf16[128,3584]{1,0:T(8,128)(2,1)S(1)}, u32[]{:S(2)}, u32[]{:S(2)}) collective-permute-start(bf16[128,3584]{1,0:T(8,128)(2,1)S(1)} %get-tuple-element.31.refs_0_), channel_id=1, source_target_pairs={{0,4},{4,0},{8,12},{12,8},{16,20},{20,16},{24,28},{28,24},{1,5},{5... | collective-permute-start | bytes 2752520 | tf_op jit(solution)/shard_map/ppermute | solution.py:82
  37.2 8.1 %collective-permute-start.7 = (bf16[32,3584]{1,0:T(8,128)(2,1)S(1)}, bf16[32,3584]{1,0:T(8,128)(2,1)S(1)}, u32[]{:S(2)}, u32[]{:S(2)}) collective-permute-start(bf16[32,3584]{1,0:T(8,128)(2,1)S(1)} %get-tuple-element.36), channel_id=1, source_target_pairs={{0,1},{1,0},{2,3},{3,2},{4,5},{5,4},{6,7},{7,6},{8,9},{9,8},{10,11... | collective-permute-start | bytes 688136 | tf_op jit(solution)/shard_map/ppermute | solution.py:82
  38.5 7.7 %collective-permute-start.8 = (bf16[32,3584]{1,0:T(8,128)(2,1)S(1)}, bf16[32,3584]{1,0:T(8,128)(2,1)S(1)}, u32[]{:S(2)}, u32[]{:S(2)}) collective-permute-start(bf16[32,3584]{1,0:T(8,128)(2,1)S(1)} %get-tuple-element.37), channel_id=1, source_target_pairs={{0,2},{1,3},{2,0},{3,1},{4,6},{5,7},{6,4},{7,5},{8,10},{9,11},{10,... | collective-permute-start | bytes 688136 | tf_op jit(solution)/shard_map/ppermute | solution.py:82
  42.0 4.3 %collective-permute-start.15 = (bf16[64,3584]{1,0:T(8,128)(2,1)S(1)}, bf16[64,3584]{1,0:T(8,128)(2,1)S(1)}, u32[]{:S(2)}, u32[]{:S(2)}) collective-permute-start(bf16[64,3584]{1,0:T(8,128)(2,1)S(1)} %get-tuple-element.47), channel_id=1, source_target_pairs={{0,4},{4,0},{8,12},{12,8},{16,20},{20,16},{24,28},{28,24},{1,5},{5... | collective-permute-start | bytes 1376264 | tf_op jit(solution)/shard_map/ppermute | solution.py:82
  42.1 4.2 %collective-permute-start.13 = (bf16[32,3584]{1,0:T(8,128)(2,1)S(1)}, bf16[32,3584]{1,0:T(8,128)(2,1)S(1)}, u32[]{:S(2)}, u32[]{:S(2)}) collective-permute-start(bf16[32,3584]{1,0:T(8,128)(2,1)S(1)} %get-tuple-element.45), channel_id=1, source_target_pairs={{0,4},{4,0},{8,12},{12,8},{16,20},{20,16},{24,28},{28,24},{1,5},{5... | collective-permute-start | bytes 688136 | tf_op jit(solution)/shard_map/ppermute | solution.py:82
  42.6 3.7 %collective-permute-start.14 = (bf16[32,3584]{1,0:T(8,128)(2,1)S(1)}, bf16[32,3584]{1,0:T(8,128)(2,1)S(1)}, u32[]{:S(2)}, u32[]{:S(2)}) collective-permute-start(bf16[32,3584]{1,0:T(8,128)(2,1)S(1)} %get-tuple-element.46), channel_id=1, source_target_pairs={{0,4},{4,0},{8,12},{12,8},{16,20},{20,16},{24,28},{28,24},{1,5},{5... | collective-permute-start | bytes 688136 | tf_op jit(solution)/shard_map/ppermute | solution.py:82
  47.0 19.3 %collective-permute-start.16 = (bf16[48,3584]{1,0:T(8,128)(2,1)S(1)}, bf16[48,3584]{1,0:T(8,128)(2,1)S(1)}, u32[]{:S(2)}, u32[]{:S(2)}) collective-permute-start(bf16[48,3584]{1,0:T(8,128)(2,1)S(1)} %get-tuple-element.48), channel_id=1, source_target_pairs={{0,3},{1,2},{2,1},{3,0},{4,7},{5,6},{6,5},{7,4},{8,11},{9,10},{10,... | collective-permute-start | bytes 1032200 | tf_op jit(solution)/shard_map/ppermute | solution.py:88
  48.8 12.7 %collective-permute-start.17 = (bf16[16,3584]{1,0:T(8,128)(2,1)S(1)}, bf16[16,3584]{1,0:T(8,128)(2,1)S(1)}, u32[]{:S(2)}, u32[]{:S(2)}) collective-permute-start(bf16[16,3584]{1,0:T(8,128)(2,1)S(1)} %get-tuple-element.50), channel_id=1, source_target_pairs={{0,3},{1,2},{2,1},{3,0},{4,7},{5,6},{6,5},{7,4},{8,11},{9,10},{10,... | collective-permute-start | bytes 344072 | tf_op jit(solution)/shard_map/ppermute | solution.py:88
  50.0 12.9 %collective-permute-start.18 = (bf16[16,3584]{1,0:T(8,128)(2,1)S(1)}, bf16[16,3584]{1,0:T(8,128)(2,1)S(1)}, u32[]{:S(2)}, u32[]{:S(2)}) collective-permute-start(bf16[16,3584]{1,0:T(8,128)(2,1)S(1)} %get-tuple-element.51), channel_id=1, source_target_pairs={{0,1},{1,0},{2,3},{3,2},{4,5},{5,4},{6,7},{7,6},{8,9},{9,8},{10,11... | collective-permute-start | bytes 344072 | tf_op jit(solution)/shard_map/ppermute | solution.py:82
  50.8 12.1 %collective-permute-start.19 = (bf16[16,3584]{1,0:T(8,128)(2,1)S(1)}, bf16[16,3584]{1,0:T(8,128)(2,1)S(1)}, u32[]{:S(2)}, u32[]{:S(2)}) collective-permute-start(bf16[16,3584]{1,0:T(8,128)(2,1)S(1)} %get-tuple-element.52), channel_id=1, source_target_pairs={{0,2},{1,3},{2,0},{3,1},{4,6},{5,7},{6,4},{7,5},{8,10},{9,11},{10,... | collective-permute-start | bytes 344072 | tf_op jit(solution)/shard_map/ppermute | solution.py:82
  52.3 13.6 %collective-permute-start.21 = (bf16[16,3584]{1,0:T(8,128)(2,1)S(1)}, bf16[16,3584]{1,0:T(8,128)(2,1)S(1)}, u32[]{:S(2)}, u32[]{:S(2)}) collective-permute-start(bf16[16,3584]{1,0:T(8,128)(2,1)S(1)} %get-tuple-element.54), channel_id=1, source_target_pairs={{0,1},{1,0},{2,3},{3,2},{4,5},{5,4},{6,7},{7,6},{8,9},{9,8},{10,11... | collective-permute-start | bytes 344072 | tf_op jit(solution)/shard_map/ppermute | solution.py:82
  61.5 4.8 %collective-permute-start.22 = (bf16[16,3584]{1,0:T(8,128)(2,1)S(1)}, bf16[16,3584]{1,0:T(8,128)(2,1)S(1)}, u32[]{:S(2)}, u32[]{:S(2)}) collective-permute-start(bf16[16,3584]{1,0:T(8,128)(2,1)S(1)} %get-tuple-element.55), channel_id=1, source_target_pairs={{0,2},{1,3},{2,0},{3,1},{4,6},{5,7},{6,4},{7,5},{8,10},{9,11},{10,... | collective-permute-start | bytes 344072 | tf_op jit(solution)/shard_map/ppermute | solution.py:82
  63.0 7.9 %collective-permute-start.20 = (bf16[16,3584]{1,0:T(8,128)(2,1)S(1)}, bf16[16,3584]{1,0:T(8,128)(2,1)S(1)}, u32[]{:S(2)}, u32[]{:S(2)}) collective-permute-start(bf16[16,3584]{1,0:T(8,128)(2,1)S(1)} %combine.12.refs_5_), channel_id=1, source_target_pairs={{0,24},{4,28},{8,16},{12,20},{16,8},{20,12},{24,0},{28,4},{1,25},{... | collective-permute-start | bytes 344072 | tf_op jit(solution)/shard_map/ppermute | solution.py:88
  66.4 8.7 %collective-permute-start.23 = (bf16[16,3584]{1,0:T(8,128)(2,1)S(1)}, bf16[16,3584]{1,0:T(8,128)(2,1)S(1)}, u32[]{:S(2)}, u32[]{:S(2)}) collective-permute-start(bf16[16,3584]{1,0:T(8,128)(2,1)S(1)} %get-tuple-element.57), channel_id=1, source_target_pairs={{0,16},{4,20},{8,24},{12,28},{16,0},{20,4},{24,8},{28,12},{1,17},{... | collective-permute-start | bytes 344072 | tf_op jit(solution)/shard_map/ppermute | solution.py:82
  67.8 7.3 %collective-permute-start.24 = (bf16[16,3584]{1,0:T(8,128)(2,1)S(1)}, bf16[16,3584]{1,0:T(8,128)(2,1)S(1)}, u32[]{:S(2)}, u32[]{:S(2)}) collective-permute-start(bf16[16,3584]{1,0:T(8,128)(2,1)S(1)} %get-tuple-element.56.refs_3_), channel_id=1, source_target_pairs={{0,8},{4,12},{8,0},{12,4},{16,24},{20,28},{24,16},{28,20},{1,9},{5... | collective-permute-start | bytes 344072 | tf_op jit(solution)/shard_map/ppermute | solution.py:82
  (5 other events, 26.6 us)

commit v13 on v11

--- a/solution.py
+++ b/solution.py
@@ -136,6 +136,9 @@
 
 
 def pack(tokens, ids, gates):
+    picks = ids.shape[1]
+    chosen = lax.pad(ids.T, 0, ((0, picks, 0), (0, 0, 0))).astype(jnp.float32)
+    chosen = chosen + lax.pad(gates.T, 0.0, ((picks, 0, 0), (0, 0, 0)))
     return pl.pallas_call(
         pack_kernel,
         out_shape=jax.ShapeDtypeStruct((tokens.shape[0], tokens.shape[1] + EXTRA), jnp.bfloat16),
@@ -143,7 +146,7 @@
         out_specs=whole,
         compiler_params=pltpu.CompilerParams(vmem_limit_bytes=SMALL_BYTES),
         name="pack",
-    )(tokens, jnp.concatenate([ids.T.astype(jnp.float32), gates.T], axis=0))
+    )(tokens, chosen)
 
 
 def expert_index():
@@ -523,9 +526,8 @@
     to_both = [across(both_xy, x, y), swap(both_x, x), swap(both_y, y)]
     to_far = [across(far_xy, x, y), swap(far_x, x), swap(far_y, y)]
     (both_sum,) = combine([both_sum, *to_both], [all_of(4, 0)])
-    (near_xy,) = combine([near_xy], [rows_of((0, 0, 2 * n))], [both_sum])
     to_near = across(near_xy, x, y)
-    (far_sum,) = combine([far_sum, *to_far], [all_of(4, 0)], [near_xy], flops=FAR_FLOPS)
+    (far_sum,) = combine([far_sum, *to_far], [all_of(4, 0)], [both_sum], flops=FAR_FLOPS)
     from_both = across(both_sum, z_far, z_near)
     own_sum, near_sum = combine(
         [near, to_near, from_both], [all_of(3, 0), all_of(2, n)], [far_sum]

time: 73.7 us -> 70.8 us (0.961)
  waiting for transfers between devices: 26.8 us -> 20.7 us
  starting transfers between devices: 27.3 us -> 31.3 us
    ppermute x21, starting transfers between devices: 18.7 us -> 23 us  [swap(): return lax.ppermute(value, axis, [(i, i ^ bit) for i in range(size)])]
    ppermute x5, waiting for transfers between devices: 8.73 us -> 5.45 us  [across(): lax.ppermute(value, axis, [(i, i ^ first[1] ^ second[1]) for i in range(s...]
    ppermute x21, waiting for transfers between devices: 18.1 us -> 15.2 us  [swap(): return lax.ppermute(value, axis, [(i, i ^ bit) for i in range(size)])]
  transfers between devices with their start and end apart: 26 -> 26, of which waited for: 14 -> 14; matrix products, arithmetic and copies ran while one was open for 0% -> 0% of each run, Pallas kernels for 19% -> 20%
where the time goes in v13:
time: 70.8 us; the launch traced here: 70.6 us
  starting transfers between devices  31.3 us (44%)
  waiting for transfers between devices  20.7 us (29%)
  Pallas kernels  15.5 us (22%)
  between operations  1.48 us (2%)
  local copies, waits for them, and re-layouts  0.92 us (1%)
  other arithmetic  0.71 us (1%)
    ppermute x21, starting transfers between devices, swap(): return lax.ppermute(value, axis, [(i, i ^ bit) for i in range(size)])  23 us
    ppermute x21, waiting for transfers between devices, swap(): return lax.ppermute(value, axis, [(i, i ^ bit) for i in range(size)])  15.2 us
    ppermute x5, starting transfers between devices, across(): lax.ppermute(value, axis, [(i, i ^ first[1] ^ second[1]) for i in range(s...  8.28 us
    pallas_call x1, Pallas kernels, first_of(): pl.pallas_call(functools.partial(first_kernel, picks), out_shape=[jax.Sha...  7.47 us
    ppermute x5, waiting for transfers between devices, across(): lax.ppermute(value, axis, [(i, i ^ first[1] ^ second[1]) for i in range(s...  5.45 us
    pallas_call x1, Pallas kernels, attend(): pl.pallas_call(attend_kernel, out_shape=[jax.ShapeDtypeStruct((count, hea...  2.7 us
    pallas_call x1, Pallas kernels, expert_of(): pl.pallas_call(functools.partial(expert_kernel, picks, len(after)), out_s...  2.7 us
  transfers between devices with their start and end apart: 26, of which 14 were waited for; matrix products, arithmetic and copies ran while one was open for 0% of the time, Pallas kernels for 20%

profile of v13, /device:TPU:0, one launch (start us, length us, event | category | flops | bytes accessed | tf_op | source)
XLA Modules:
  0.0 70.6 jit_solution(14775311158480904244)
XLA Ops:
  2.4 3.0 %collective-permute-start = (bf16[16,3712]{1,0:T(8,128)(2,1)S(1)}, bf16[16,3712]{1,0:T(8,128)(2,1)S(1)}, u32[]{:S(2)}, u32[]{:S(2)}) collective-permute-start(bf16[16,3712]{1,0:T(8,128)(2,1)S(1)} %pack.1.refs_0_), channel_id=1, source_target_pairs={{0,8},{4,12},{8,0},{12,4},{16,24},{20,28},{24,16},{28,20},{1,9},{5... | collective-permute-start | bytes 356360 | tf_op jit(solution)/shard_map/ppermute | solution.py:82
  5.4 2.6 %collective-permute-start.3 = (bf16[16,3712]{1,0:T(8,128)(2,1)S(1)}, bf16[16,3712]{1,0:T(8,128)(2,1)S(1)}, u32[]{:S(2)}, u32[]{:S(2)}) collective-permute-start(bf16[16,3712]{1,0:T(8,128)(2,1)S(1)} %pack.1.refs_0_), channel_id=1, source_target_pairs={{0,16},{4,20},{8,24},{12,28},{16,0},{20,4},{24,8},{28,12},{1,17},{... | collective-permute-start | bytes 356360 | tf_op jit(solution)/shard_map/ppermute | solution.py:82
  8.0 1.9 %collective-permute-done.refs_1_ = bf16[16,3712]{1,0:T(8,128)(2,1)S(1)} collective-permute-done((bf16[16,3712]{1,0:T(8,128)(2,1)S(1)}, bf16[16,3712]{1,0:T(8,128)(2,1)S(1)}, u32[]{:S(2)}, u32[]{:S(2)}) %collective-permute-start) | collective-permute-done | bytes 118816 | tf_op jit(solution)/shard_map/ppermute | solution.py:82
  10.0 1.9 %collective-permute-start.2 = (bf16[32,3712]{1,0:T(8,128)(2,1)S(1)}, bf16[32,3712]{1,0:T(8,128)(2,1)S(1)}, u32[]{:S(2)}, u32[]{:S(2)}) collective-permute-start(bf16[32,3712]{1,0:T(8,128)(2,1)S(1)} %combine.8.refs_0_), channel_id=1, source_target_pairs={{0,2},{1,3},{2,0},{3,1},{4,6},{5,7},{6,4},{7,5},{8,10},{9,11},{10,... | collective-permute-start | bytes 712712 | tf_op jit(solution)/shard_map/ppermute | solution.py:82
  11.9 1.5 %collective-permute-start.1 = (bf16[32,3712]{1,0:T(8,128)(2,1)S(1)}, bf16[32,3712]{1,0:T(8,128)(2,1)S(1)}, u32[]{:S(2)}, u32[]{:S(2)}) collective-permute-start(bf16[32,3712]{1,0:T(8,128)(2,1)S(1)} %combine.8.refs_0_), channel_id=1, source_target_pairs={{0,1},{1,0},{2,3},{3,2},{4,5},{5,4},{6,7},{7,6},{8,9},{9,8},{10,11... | collective-permute-start | bytes 712712 | tf_op jit(solution)/shard_map/ppermute | solution.py:82
  14.1 4.4 %collective-permute-done.4.refs_4_ = bf16[16,3712]{1,0:T(8,128)(2,1)S(1)} collective-permute-done((bf16[16,3712]{1,0:T(8,128)(2,1)S(1)}, bf16[16,3712]{1,0:T(8,128)(2,1)S(1)}, u32[]{:S(2)}, u32[]{:S(2)}) %collective-permute-start.4) | collective-permute-done | bytes 118816 | tf_op jit(solution)/shard_map/ppermute | solution.py:82
  18.7 1.6 %collective-permute-start.9 = (bf16[48,3712]{1,0:T(8,128)(2,1)S(1)}, bf16[48,3712]{1,0:T(8,128)(2,1)S(1)}, u32[]{:S(2)}, u32[]{:S(2)}) collective-permute-start(bf16[48,3712]{1,0:T(8,128)(2,1)S(1)} %get-tuple-element.39), channel_id=1, source_target_pairs={{0,1},{1,0},{2,3},{3,2},{4,5},{5,4},{6,7},{7,6},{8,9},{9,8},{10,11... | collective-permute-start | bytes 1069064 | tf_op jit(solution)/shard_map/ppermute | solution.py:82
  20.2 1.5 %collective-permute-start.10 = (bf16[48,3712]{1,0:T(8,128)(2,1)S(1)}, bf16[48,3712]{1,0:T(8,128)(2,1)S(1)}, u32[]{:S(2)}, u32[]{:S(2)}) collective-permute-start(bf16[48,3712]{1,0:T(8,128)(2,1)S(1)} %get-tuple-element.40), channel_id=1, source_target_pairs={{0,2},{1,3},{2,0},{3,1},{4,6},{5,7},{6,4},{7,5},{8,10},{9,11},{10,... | collective-permute-start | bytes 1069064 | tf_op jit(solution)/shard_map/ppermute | solution.py:82
  22.9 7.5 %first.1 = (bf16[128,512]{1,0:T(8,128)(2,1)S(1)}, bf16[128,3584]{1,0:T(8,128)(2,1)S(1)}, bf16[1,3584,512]{2,1,0:T(8,128)(2,1)S(1)}, bf16[1,3584,512]{2,1,0:T(8,128)(2,1)S(1)}, bf16[1,512,3584]{2,1,0:T(8,128)(2,1)S(1)}) custom-call(bf16[128,3712]{1,0:T(8,128)(2,1)S(1)} %get-tuple-element.31.own, bf16[128,3712]{1,0:T(8,128)(2,1)S(1)} %collective-permute-done.5.other, ...), custom_call_target="tpu_custom_call" | custom-call | flops 2348810240 | bytes 11010048 | tf_op jit(solution)/shard_map/first/pallas_call | solution.py:368
  30.5 2.7 %attend.1 = (bf16[4,64,512]{2,1,0:T(8,128)(2,1)}, f32[8,128]{1,0:T(8,128)S(1)}) custom-call(s32[4]{0:T(128)S(1)} %copy-done.3, s32[1]{0:T(128)S(6)} %copy.12.live_rows, bf16[4,64,576]{2,1,0:T(8,128)(2,1)S(1)} %copy-done.1, bf16[4,576,256]{2,1,0:T(8,128)(2,1)S(1)} %bitcast.3, bf16[128,3584]{1,0:T(8,128)(2,1)S(1)} %get-tuple-element.32.refs_0_), custom_call_target="tpu_custom_call" | custom-call | flops 150994944 | bytes 1179648 | tf_op jit(solution)/shard_map/attend/pallas_call | solution.py:55
  33.2 2.3 %collective-permute-done.11.refs_2_ = bf16[32,3712]{1,0:T(8,128)(2,1)S(1)} collective-permute-done((bf16[32,3712]{1,0:T(8,128)(2,1)S(1)}, bf16[32,3712]{1,0:T(8,128)(2,1)S(1)}, u32[]{:S(2)}, u32[]{:S(2)}) %collective-permute-start.11) | collective-permute-done | bytes 237600 | tf_op jit(solution)/shard_map/ppermute | solution.py:88
  36.5 1.3 %collective-permute-start.7 = (bf16[32,3584]{1,0:T(8,128)(2,1)S(1)}, bf16[32,3584]{1,0:T(8,128)(2,1)S(1)}, u32[]{:S(2)}, u32[]{:S(2)}) collective-permute-start(bf16[32,3584]{1,0:T(8,128)(2,1)S(1)} %get-tuple-element.37), channel_id=1, source_target_pairs={{0,1},{1,0},{2,3},{3,2},{4,5},{5,4},{6,7},{7,6},{8,9},{9,8},{10,11... | collective-permute-start | bytes 688136 | tf_op jit(solution)/shard_map/ppermute | solution.py:82
  38.7 2.7 %expert.1 = (bf16[128,512]{1,0:T(8,128)(2,1)S(1)}, bf16[32,3584]{1,0:T(8,128)(2,1)S(1)}, bf16[32,3584]{1,0:T(8,128)(2,1)S(1)}, bf16[64,3584]{1,0:T(8,128)(2,1)S(1)}) custom-call(bf16[128,3712]{1,0:T(8,128)(2,1)S(1)} %combine.11.own, bf16[128,3712]{1,0:T(8,128)(2,1)S(1)} %collective-permute-done.12.other, bf16[1,3584,512]{2,1,0:T(8,128)(2,1)S(1)} %get-tuple-element.43.w_gate, ...), custom_call_target="tpu_custom_call" | custom-call | flops 2348810240 | bytes 917504 | tf_op jit(solution)/shard_map/expert/pallas_call | solution.py:393
  42.0 2.6 %collective-permute-done.7.refs_1_ = bf16[32,3584]{1,0:T(8,128)(2,1)S(1)} collective-permute-done((bf16[32,3584]{1,0:T(8,128)(2,1)S(1)}, bf16[32,3584]{1,0:T(8,128)(2,1)S(1)}, u32[]{:S(2)}, u32[]{:S(2)}) %collective-permute-start.7) | collective-permute-done | bytes 229408 | tf_op jit(solution)/shard_map/ppermute | solution.py:82
  46.4 1.8 %collective-permute-start.17 = (bf16[16,3584]{1,0:T(8,128)(2,1)S(1)}, bf16[16,3584]{1,0:T(8,128)(2,1)S(1)}, u32[]{:S(2)}, u32[]{:S(2)}) collective-permute-start(bf16[16,3584]{1,0:T(8,128)(2,1)S(1)} %get-tuple-element.51), channel_id=1, source_target_pairs={{0,3},{1,2},{2,1},{3,0},{4,7},{5,6},{6,5},{7,4},{8,11},{9,10},{10,... | collective-permute-start | bytes 344072 | tf_op jit(solution)/shard_map/ppermute | solution.py:88
  48.7 1.2 %collective-permute-start.19 = (bf16[16,3584]{1,0:T(8,128)(2,1)S(1)}, bf16[16,3584]{1,0:T(8,128)(2,1)S(1)}, u32[]{:S(2)}, u32[]{:S(2)}) collective-permute-start(bf16[16,3584]{1,0:T(8,128)(2,1)S(1)} %get-tuple-element.53), channel_id=1, source_target_pairs={{0,2},{1,3},{2,0},{3,1},{4,6},{5,7},{6,4},{7,5},{8,10},{9,11},{10,... | collective-permute-start | bytes 344072 | tf_op jit(solution)/shard_map/ppermute | solution.py:82
  49.9 1.7 %collective-permute-start.21 = (bf16[16,3584]{1,0:T(8,128)(2,1)S(1)}, bf16[16,3584]{1,0:T(8,128)(2,1)S(1)}, u32[]{:S(2)}, u32[]{:S(2)}) collective-permute-start(bf16[16,3584]{1,0:T(8,128)(2,1)S(1)} %get-tuple-element.55), channel_id=1, source_target_pairs={{0,3},{1,2},{2,1},{3,0},{4,7},{5,6},{6,5},{7,4},{8,11},{9,10},{10,... | collective-permute-start | bytes 344072 | tf_op jit(solution)/shard_map/ppermute | solution.py:88
  52.2 1.3 %collective-permute-done.17.refs_1_ = bf16[16,3584]{1,0:T(8,128)(2,1)S(1)} collective-permute-done((bf16[16,3584]{1,0:T(8,128)(2,1)S(1)}, bf16[16,3584]{1,0:T(8,128)(2,1)S(1)}, u32[]{:S(2)}, u32[]{:S(2)}) %collective-permute-start.17) | collective-permute-done | bytes 114720 | tf_op jit(solution)/shard_map/ppermute | solution.py:88
  55.2 1.4 %collective-permute-start.16 = (bf16[32,3584]{1,0:T(8,128)(2,1)S(1)}, bf16[32,3584]{1,0:T(8,128)(2,1)S(1)}, u32[]{:S(2)}, u32[]{:S(2)}) collective-permute-start(bf16[32,3584]{1,0:T(8,128)(2,1)S(1)} %get-tuple-element.49), channel_id=1, source_target_pairs={{0,3},{1,2},{2,1},{3,0},{4,7},{5,6},{6,5},{7,4},{8,11},{9,10},{10,... | collective-permute-start | bytes 688136 | tf_op jit(solution)/shard_map/ppermute | solution.py:88
  57.4 2.8 %collective-permute-start.20 = (bf16[16,3584]{1,0:T(8,128)(2,1)S(1)}, bf16[16,3584]{1,0:T(8,128)(2,1)S(1)}, u32[]{:S(2)}, u32[]{:S(2)}) collective-permute-start(bf16[16,3584]{1,0:T(8,128)(2,1)S(1)} %combine.12.refs_4_), channel_id=1, source_target_pairs={{0,24},{4,28},{8,16},{12,20},{16,8},{20,12},{24,0},{28,4},{1,25},{... | collective-permute-start | bytes 344072 | tf_op jit(solution)/shard_map/ppermute | solution.py:88
  60.8 1.4 %collective-permute-start.24 = (bf16[16,3584]{1,0:T(8,128)(2,1)S(1)}, bf16[16,3584]{1,0:T(8,128)(2,1)S(1)}, u32[]{:S(2)}, u32[]{:S(2)}) collective-permute-start(bf16[16,3584]{1,0:T(8,128)(2,1)S(1)} %combine.13.refs_3_), channel_id=1, source_target_pairs={{0,16},{4,20},{8,24},{12,28},{16,0},{20,4},{24,8},{28,12},{1,17},{... | collective-permute-start | bytes 344072 | tf_op jit(solution)/shard_map/ppermute | solution.py:82
  62.2 1.8 %collective-permute-done.16.refs_1_ = bf16[32,3584]{1,0:T(8,128)(2,1)S(1)} collective-permute-done((bf16[32,3584]{1,0:T(8,128)(2,1)S(1)}, bf16[32,3584]{1,0:T(8,128)(2,1)S(1)}, u32[]{:S(2)}, u32[]{:S(2)}) %collective-permute-start.16) | collective-permute-done | bytes 229408 | tf_op jit(solution)/shard_map/ppermute | solution.py:88
  64.1 3.0 %collective-permute-start.25 = (bf16[16,3584]{1,0:T(8,128)(2,1)S(1)}, bf16[16,3584]{1,0:T(8,128)(2,1)S(1)}, u32[]{:S(2)}, u32[]{:S(2)}) collective-permute-start(bf16[16,3584]{1,0:T(8,128)(2,1)S(1)} %get-tuple-element.59), channel_id=1, source_target_pairs={{0,8},{4,12},{8,0},{12,4},{16,24},{20,28},{24,16},{28,20},{1,9},{5... | collective-permute-start | bytes 344072 | tf_op jit(solution)/shard_map/ppermute | solution.py:82
  68.2 1.6 %collective-permute-done.25.refs_2_ = bf16[16,3584]{1,0:T(8,128)(2,1)S(1)} collective-permute-done((bf16[16,3584]{1,0:T(8,128)(2,1)S(1)}, bf16[16,3584]{1,0:T(8,128)(2,1)S(1)}, u32[]{:S(2)}, u32[]{:S(2)}) %collective-permute-start.25) | collective-permute-done | bytes 114720 | tf_op jit(solution)/shard_map/ppermute | solution.py:82
  (51 shorter events, 13.4 us)
Async XLA Ops:
  2.4 7.6 %collective-permute-start = (bf16[16,3712]{1,0:T(8,128)(2,1)S(1)}, bf16[16,3712]{1,0:T(8,128)(2,1)S(1)}, u32[]{:S(2)}, u32[]{:S(2)}) collective-permute-start(bf16[16,3712]{1,0:T(8,128)(2,1)S(1)} %pack.1.refs_0_), channel_id=1, source_target_pairs={{0,8},{4,12},{8,0},{12,4},{16,24},{20,28},{24,16},{28,20},{1,9},{5... | collective-permute-start | bytes 356360 | tf_op jit(solution)/shard_map/ppermute | solution.py:82
  5.4 8.2 %collective-permute-start.3 = (bf16[16,3712]{1,0:T(8,128)(2,1)S(1)}, bf16[16,3712]{1,0:T(8,128)(2,1)S(1)}, u32[]{:S(2)}, u32[]{:S(2)}) collective-permute-start(bf16[16,3712]{1,0:T(8,128)(2,1)S(1)} %pack.1.refs_0_), channel_id=1, source_target_pairs={{0,16},{4,20},{8,24},{12,28},{16,0},{20,4},{24,8},{28,12},{1,17},{... | collective-permute-start | bytes 356360 | tf_op jit(solution)/shard_map/ppermute | solution.py:82
  10.0 8.5 %collective-permute-start.2 = (bf16[32,3712]{1,0:T(8,128)(2,1)S(1)}, bf16[32,3712]{1,0:T(8,128)(2,1)S(1)}, u32[]{:S(2)}, u32[]{:S(2)}) collective-permute-start(bf16[32,3712]{1,0:T(8,128)(2,1)S(1)} %combine.8.refs_0_), channel_id=1, source_target_pairs={{0,2},{1,3},{2,0},{3,1},{4,6},{5,7},{6,4},{7,5},{8,10},{9,11},{10,... | collective-permute-start | bytes 712712 | tf_op jit(solution)/shard_map/ppermute | solution.py:82
  11.9 6.6 %collective-permute-start.1 = (bf16[32,3712]{1,0:T(8,128)(2,1)S(1)}, bf16[32,3712]{1,0:T(8,128)(2,1)S(1)}, u32[]{:S(2)}, u32[]{:S(2)}) collective-permute-start(bf16[32,3712]{1,0:T(8,128)(2,1)S(1)} %combine.8.refs_0_), channel_id=1, source_target_pairs={{0,1},{1,0},{2,3},{3,2},{4,5},{5,4},{6,7},{7,6},{8,9},{9,8},{10,11... | collective-permute-start | bytes 712712 | tf_op jit(solution)/shard_map/ppermute | solution.py:82
  13.6 4.8 %collective-permute-start.4 = (bf16[16,3712]{1,0:T(8,128)(2,1)S(1)}, bf16[16,3712]{1,0:T(8,128)(2,1)S(1)}, u32[]{:S(2)}, u32[]{:S(2)}) collective-permute-start(bf16[16,3712]{1,0:T(8,128)(2,1)S(1)} %collective-permute-done.3.refs_3_), channel_id=1, source_target_pairs={{0,8},{4,12},{8,0},{12,4},{16,24},{20,28},{24,16},{28,20},{1,9},{5... | collective-permute-start | bytes 356360 | tf_op jit(solution)/shard_map/ppermute | solution.py:82
  18.6 4.3 %collective-permute-start.5 = (bf16[128,3712]{1,0:T(8,128)(2,1)S(1)}, bf16[128,3712]{1,0:T(8,128)(2,1)S(1)}, u32[]{:S(2)}, u32[]{:S(2)}) collective-permute-start(bf16[128,3712]{1,0:T(8,128)(2,1)S(1)} %get-tuple-element.31.own), channel_id=1, source_target_pairs={{0,4},{4,0},{8,12},{12,8},{16,20},{20,16},{24,28},{28,24},{1,5},{5... | collective-permute-start | bytes 2850824 | tf_op jit(solution)/shard_map/ppermute | solution.py:82
  18.7 16.9 %collective-permute-start.9 = (bf16[48,3712]{1,0:T(8,128)(2,1)S(1)}, bf16[48,3712]{1,0:T(8,128)(2,1)S(1)}, u32[]{:S(2)}, u32[]{:S(2)}) collective-permute-start(bf16[48,3712]{1,0:T(8,128)(2,1)S(1)} %get-tuple-element.39), channel_id=1, source_target_pairs={{0,1},{1,0},{2,3},{3,2},{4,5},{5,4},{6,7},{7,6},{8,9},{9,8},{10,11... | collective-permute-start | bytes 1069064 | tf_op jit(solution)/shard_map/ppermute | solution.py:82
  20.2 15.5 %collective-permute-start.10 = (bf16[48,3712]{1,0:T(8,128)(2,1)S(1)}, bf16[48,3712]{1,0:T(8,128)(2,1)S(1)}, u32[]{:S(2)}, u32[]{:S(2)}) collective-permute-start(bf16[48,3712]{1,0:T(8,128)(2,1)S(1)} %get-tuple-element.40), channel_id=1, source_target_pairs={{0,2},{1,3},{2,0},{3,1},{4,6},{5,7},{6,4},{7,5},{8,10},{9,11},{10,... | collective-permute-start | bytes 1069064 | tf_op jit(solution)/shard_map/ppermute | solution.py:82
  21.8 13.8 %collective-permute-start.11 = (bf16[32,3712]{1,0:T(8,128)(2,1)S(1)}, bf16[32,3712]{1,0:T(8,128)(2,1)S(1)}, u32[]{:S(2)}, u32[]{:S(2)}) collective-permute-start(bf16[32,3712]{1,0:T(8,128)(2,1)S(1)} %get-tuple-element.41), channel_id=1, source_target_pairs={{0,3},{1,2},{2,1},{3,0},{4,7},{5,6},{6,5},{7,4},{8,11},{9,10},{10,... | collective-permute-start | bytes 712712 | tf_op jit(solution)/shard_map/ppermute | solution.py:88
  30.4 5.5 %collective-permute-start.6 = (bf16[128,3584]{1,0:T(8,128)(2,1)S(1)}, bf16[128,3584]{1,0:T(8,128)(2,1)S(1)}, u32[]{:S(2)}, u32[]{:S(2)}) collective-permute-start(bf16[128,3584]{1,0:T(8,128)(2,1)S(1)} %get-tuple-element.32.refs_0_), channel_id=1, source_target_pairs={{0,4},{4,0},{8,12},{12,8},{16,20},{20,16},{24,28},{28,24},{1,5},{5... | collective-permute-start | bytes 2752520 | tf_op jit(solution)/shard_map/ppermute | solution.py:82
  36.5 8.1 %collective-permute-start.7 = (bf16[32,3584]{1,0:T(8,128)(2,1)S(1)}, bf16[32,3584]{1,0:T(8,128)(2,1)S(1)}, u32[]{:S(2)}, u32[]{:S(2)}) collective-permute-start(bf16[32,3584]{1,0:T(8,128)(2,1)S(1)} %get-tuple-element.37), channel_id=1, source_target_pairs={{0,1},{1,0},{2,3},{3,2},{4,5},{5,4},{6,7},{7,6},{8,9},{9,8},{10,11... | collective-permute-start | bytes 688136 | tf_op jit(solution)/shard_map/ppermute | solution.py:82
  37.9 7.7 %collective-permute-start.8 = (bf16[32,3584]{1,0:T(8,128)(2,1)S(1)}, bf16[32,3584]{1,0:T(8,128)(2,1)S(1)}, u32[]{:S(2)}, u32[]{:S(2)}) collective-permute-start(bf16[32,3584]{1,0:T(8,128)(2,1)S(1)} %get-tuple-element.38), channel_id=1, source_target_pairs={{0,2},{1,3},{2,0},{3,1},{4,6},{5,7},{6,4},{7,5},{8,10},{9,11},{10,... | collective-permute-start | bytes 688136 | tf_op jit(solution)/shard_map/ppermute | solution.py:82
  41.4 4.3 %collective-permute-start.15 = (bf16[64,3584]{1,0:T(8,128)(2,1)S(1)}, bf16[64,3584]{1,0:T(8,128)(2,1)S(1)}, u32[]{:S(2)}, u32[]{:S(2)}) collective-permute-start(bf16[64,3584]{1,0:T(8,128)(2,1)S(1)} %get-tuple-element.48), channel_id=1, source_target_pairs={{0,4},{4,0},{8,12},{12,8},{16,20},{20,16},{24,28},{28,24},{1,5},{5... | collective-permute-start | bytes 1376264 | tf_op jit(solution)/shard_map/ppermute | solution.py:82
  41.5 4.2 %collective-permute-start.13 = (bf16[32,3584]{1,0:T(8,128)(2,1)S(1)}, bf16[32,3584]{1,0:T(8,128)(2,1)S(1)}, u32[]{:S(2)}, u32[]{:S(2)}) collective-permute-start(bf16[32,3584]{1,0:T(8,128)(2,1)S(1)} %get-tuple-element.46), channel_id=1, source_target_pairs={{0,4},{4,0},{8,12},{12,8},{16,20},{20,16},{24,28},{28,24},{1,5},{5... | collective-permute-start | bytes 688136 | tf_op jit(solution)/shard_map/ppermute | solution.py:82
  46.4 7.1 %collective-permute-start.17 = (bf16[16,3584]{1,0:T(8,128)(2,1)S(1)}, bf16[16,3584]{1,0:T(8,128)(2,1)S(1)}, u32[]{:S(2)}, u32[]{:S(2)}) collective-permute-start(bf16[16,3584]{1,0:T(8,128)(2,1)S(1)} %get-tuple-element.51), channel_id=1, source_target_pairs={{0,3},{1,2},{2,1},{3,0},{4,7},{5,6},{6,5},{7,4},{8,11},{9,10},{10,... | collective-permute-start | bytes 344072 | tf_op jit(solution)/shard_map/ppermute | solution.py:88
  48.1 7.1 %collective-permute-start.18 = (bf16[16,3584]{1,0:T(8,128)(2,1)S(1)}, bf16[16,3584]{1,0:T(8,128)(2,1)S(1)}, u32[]{:S(2)}, u32[]{:S(2)}) collective-permute-start(bf16[16,3584]{1,0:T(8,128)(2,1)S(1)} %get-tuple-element.52), channel_id=1, source_target_pairs={{0,1},{1,0},{2,3},{3,2},{4,5},{5,4},{6,7},{7,6},{8,9},{9,8},{10,11... | collective-permute-start | bytes 344072 | tf_op jit(solution)/shard_map/ppermute | solution.py:82
  48.7 8.6 %collective-permute-start.19 = (bf16[16,3584]{1,0:T(8,128)(2,1)S(1)}, bf16[16,3584]{1,0:T(8,128)(2,1)S(1)}, u32[]{:S(2)}, u32[]{:S(2)}) collective-permute-start(bf16[16,3584]{1,0:T(8,128)(2,1)S(1)} %get-tuple-element.53), channel_id=1, source_target_pairs={{0,2},{1,3},{2,0},{3,1},{4,6},{5,7},{6,4},{7,5},{8,10},{9,11},{10,... | collective-permute-start | bytes 344072 | tf_op jit(solution)/shard_map/ppermute | solution.py:82
  49.9 10.3 %collective-permute-start.21 = (bf16[16,3584]{1,0:T(8,128)(2,1)S(1)}, bf16[16,3584]{1,0:T(8,128)(2,1)S(1)}, u32[]{:S(2)}, u32[]{:S(2)}) collective-permute-start(bf16[16,3584]{1,0:T(8,128)(2,1)S(1)} %get-tuple-element.55), channel_id=1, source_target_pairs={{0,3},{1,2},{2,1},{3,0},{4,7},{5,6},{6,5},{7,4},{8,11},{9,10},{10,... | collective-permute-start | bytes 344072 | tf_op jit(solution)/shard_map/ppermute | solution.py:88
  51.6 8.6 %collective-permute-start.22 = (bf16[16,3584]{1,0:T(8,128)(2,1)S(1)}, bf16[16,3584]{1,0:T(8,128)(2,1)S(1)}, u32[]{:S(2)}, u32[]{:S(2)}) collective-permute-start(bf16[16,3584]{1,0:T(8,128)(2,1)S(1)} %get-tuple-element.56), channel_id=1, source_target_pairs={{0,1},{1,0},{2,3},{3,2},{4,5},{5,4},{6,7},{7,6},{8,9},{9,8},{10,11... | collective-permute-start | bytes 344072 | tf_op jit(solution)/shard_map/ppermute | solution.py:82
  53.5 7.3 %collective-permute-start.23 = (bf16[16,3584]{1,0:T(8,128)(2,1)S(1)}, bf16[16,3584]{1,0:T(8,128)(2,1)S(1)}, u32[]{:S(2)}, u32[]{:S(2)}) collective-permute-start(bf16[16,3584]{1,0:T(8,128)(2,1)S(1)} %get-tuple-element.57), channel_id=1, source_target_pairs={{0,2},{1,3},{2,0},{3,1},{4,6},{5,7},{6,4},{7,5},{8,10},{9,11},{10,... | collective-permute-start | bytes 344072 | tf_op jit(solution)/shard_map/ppermute | solution.py:82
  55.2 8.8 %collective-permute-start.16 = (bf16[32,3584]{1,0:T(8,128)(2,1)S(1)}, bf16[32,3584]{1,0:T(8,128)(2,1)S(1)}, u32[]{:S(2)}, u32[]{:S(2)}) collective-permute-start(bf16[32,3584]{1,0:T(8,128)(2,1)S(1)} %get-tuple-element.49), channel_id=1, source_target_pairs={{0,3},{1,2},{2,1},{3,0},{4,7},{5,6},{6,5},{7,4},{8,11},{9,10},{10,... | collective-permute-start | bytes 688136 | tf_op jit(solution)/shard_map/ppermute | solution.py:88
  57.4 6.7 %collective-permute-start.20 = (bf16[16,3584]{1,0:T(8,128)(2,1)S(1)}, bf16[16,3584]{1,0:T(8,128)(2,1)S(1)}, u32[]{:S(2)}, u32[]{:S(2)}) collective-permute-start(bf16[16,3584]{1,0:T(8,128)(2,1)S(1)} %combine.12.refs_4_), channel_id=1, source_target_pairs={{0,24},{4,28},{8,16},{12,20},{16,8},{20,12},{24,0},{28,4},{1,25},{... | collective-permute-start | bytes 344072 | tf_op jit(solution)/shard_map/ppermute | solution.py:88
  60.8 7.4 %collective-permute-start.24 = (bf16[16,3584]{1,0:T(8,128)(2,1)S(1)}, bf16[16,3584]{1,0:T(8,128)(2,1)S(1)}, u32[]{:S(2)}, u32[]{:S(2)}) collective-permute-start(bf16[16,3584]{1,0:T(8,128)(2,1)S(1)} %combine.13.refs_3_), channel_id=1, source_target_pairs={{0,16},{4,20},{8,24},{12,28},{16,0},{20,4},{24,8},{28,12},{1,17},{... | collective-permute-start | bytes 344072 | tf_op jit(solution)/shard_map/ppermute | solution.py:82
  64.1 5.7 %collective-permute-start.25 = (bf16[16,3584]{1,0:T(8,128)(2,1)S(1)}, bf16[16,3584]{1,0:T(8,128)(2,1)S(1)}, u32[]{:S(2)}, u32[]{:S(2)}) collective-permute-start(bf16[16,3584]{1,0:T(8,128)(2,1)S(1)} %get-tuple-element.59), channel_id=1, source_target_pairs={{0,8},{4,12},{8,0},{12,4},{16,24},{20,28},{24,16},{28,20},{1,9},{5... | collective-permute-start | bytes 344072 | tf_op jit(solution)/shard_map/ppermute | solution.py:82
  (6 other events, 30.3 us)

commit v14 on v13

--- a/solution.py
+++ b/solution.py
@@ -13,7 +13,7 @@
 BLOCKS = 4
 TILE = 256
 WIDE = 512
-NEAR_FLOPS = 4 * 10**9
+NEAR_FLOPS = 16 * 10**9
 FAR_FLOPS = 4 * 10**9
 VMEM_BYTES = 48 * 1024 * 1024
 LARGE_BYTES = 16 * 1024 * 1024
@@ -511,7 +511,7 @@
     )
     to_near = [swap(near_x, x), swap(near_y, y)]
     second_h, *second_out = expert_of(
-        second_own, second_other, *weights, picks, [2 * n, 2 * n, 4 * n], [near]
+        second_own, second_other, *weights, picks, [8 * n], [near]
     )
     second_in = [swap(part, core) for part in second_out]
 

time: 70.8 us -> 70.9 us (level)
    ppermute x21 -> x19, waiting for transfers between devices: 15.2 us -> 15.8 us  [swap(): return lax.ppermute(value, axis, [(i, i ^ bit) for i in range(size)])]
    ppermute x21 -> x19, starting transfers between devices: 23 us -> 22.5 us  [swap(): return lax.ppermute(value, axis, [(i, i ^ bit) for i in range(size)])]
  transfers between devices with their start and end apart: 26 -> 24, of which waited for: 14 -> 14; matrix products, arithmetic and copies ran while one was open for 0% -> 0% of each run, Pallas kernels for 20% -> 20%
where the time goes in v14:
time: 70.9 us; the launch traced here: 70.7 us
  starting transfers between devices  30.8 us (43%)
  waiting for transfers between devices  21.3 us (30%)
  Pallas kernels  15.5 us (22%)
  between operations  1.43 us (2%)
  local copies, waits for them, and re-layouts  0.91 us (1%)
  other arithmetic  0.71 us (1%)
    ppermute x19, starting transfers between devices, swap(): return lax.ppermute(value, axis, [(i, i ^ bit) for i in range(size)])  22.5 us
    ppermute x19, waiting for transfers between devices, swap(): return lax.ppermute(value, axis, [(i, i ^ bit) for i in range(size)])  15.8 us
    ppermute x5, starting transfers between devices, across(): lax.ppermute(value, axis, [(i, i ^ first[1] ^ second[1]) for i in range(s...  8.25 us
    pallas_call x1, Pallas kernels, first_of(): pl.pallas_call(functools.partial(first_kernel, picks), out_shape=[jax.Sha...  7.4 us
    ppermute x5, waiting for transfers between devices, across(): lax.ppermute(value, axis, [(i, i ^ first[1] ^ second[1]) for i in range(s...  5.55 us
    pallas_call x1, Pallas kernels, attend(): pl.pallas_call(attend_kernel, out_shape=[jax.ShapeDtypeStruct((count, hea...  2.7 us
    pallas_call x1, Pallas kernels, expert_of(): pl.pallas_call(functools.partial(expert_kernel, picks, len(after)), out_s...  2.7 us
  transfers between devices with their start and end apart: 24, of which 14 were waited for; matrix products, arithmetic and copies ran while one was open for 0% of the time, Pallas kernels for 20%

profile of v14, /device:TPU:0, one launch (start us, length us, event | category | flops | bytes accessed | tf_op | source)
XLA Modules:
  0.0 70.7 jit_solution(2637636425562593535)
XLA Ops:
  2.4 3.0 %collective-permute-start = (bf16[16,3712]{1,0:T(8,128)(2,1)S(1)}, bf16[16,3712]{1,0:T(8,128)(2,1)S(1)}, u32[]{:S(2)}, u32[]{:S(2)}) collective-permute-start(bf16[16,3712]{1,0:T(8,128)(2,1)S(1)} %pack.1.refs_0_), channel_id=1, source_target_pairs={{0,8},{4,12},{8,0},{12,4},{16,24},{20,28},{24,16},{28,20},{1,9},{5... | collective-permute-start | bytes 356360 | tf_op jit(solution)/shard_map/ppermute | solution.py:82
  5.4 2.6 %collective-permute-start.3 = (bf16[16,3712]{1,0:T(8,128)(2,1)S(1)}, bf16[16,3712]{1,0:T(8,128)(2,1)S(1)}, u32[]{:S(2)}, u32[]{:S(2)}) collective-permute-start(bf16[16,3712]{1,0:T(8,128)(2,1)S(1)} %pack.1.refs_0_), channel_id=1, source_target_pairs={{0,16},{4,20},{8,24},{12,28},{16,0},{20,4},{24,8},{28,12},{1,17},{... | collective-permute-start | bytes 356360 | tf_op jit(solution)/shard_map/ppermute | solution.py:82
  8.0 1.9 %collective-permute-done.refs_1_ = bf16[16,3712]{1,0:T(8,128)(2,1)S(1)} collective-permute-done((bf16[16,3712]{1,0:T(8,128)(2,1)S(1)}, bf16[16,3712]{1,0:T(8,128)(2,1)S(1)}, u32[]{:S(2)}, u32[]{:S(2)}) %collective-permute-start) | collective-permute-done | bytes 118816 | tf_op jit(solution)/shard_map/ppermute | solution.py:82
  10.0 1.9 %collective-permute-start.2 = (bf16[32,3712]{1,0:T(8,128)(2,1)S(1)}, bf16[32,3712]{1,0:T(8,128)(2,1)S(1)}, u32[]{:S(2)}, u32[]{:S(2)}) collective-permute-start(bf16[32,3712]{1,0:T(8,128)(2,1)S(1)} %combine.8.refs_0_), channel_id=1, source_target_pairs={{0,2},{1,3},{2,0},{3,1},{4,6},{5,7},{6,4},{7,5},{8,10},{9,11},{10,... | collective-permute-start | bytes 712712 | tf_op jit(solution)/shard_map/ppermute | solution.py:82
  11.9 1.5 %collective-permute-start.1 = (bf16[32,3712]{1,0:T(8,128)(2,1)S(1)}, bf16[32,3712]{1,0:T(8,128)(2,1)S(1)}, u32[]{:S(2)}, u32[]{:S(2)}) collective-permute-start(bf16[32,3712]{1,0:T(8,128)(2,1)S(1)} %combine.8.refs_0_), channel_id=1, source_target_pairs={{0,1},{1,0},{2,3},{3,2},{4,5},{5,4},{6,7},{7,6},{8,9},{9,8},{10,11... | collective-permute-start | bytes 712712 | tf_op jit(solution)/shard_map/ppermute | solution.py:82
  14.1 4.4 %collective-permute-done.4.refs_4_ = bf16[16,3712]{1,0:T(8,128)(2,1)S(1)} collective-permute-done((bf16[16,3712]{1,0:T(8,128)(2,1)S(1)}, bf16[16,3712]{1,0:T(8,128)(2,1)S(1)}, u32[]{:S(2)}, u32[]{:S(2)}) %collective-permute-start.4) | collective-permute-done | bytes 118816 | tf_op jit(solution)/shard_map/ppermute | solution.py:82
  18.7 1.6 %collective-permute-start.9 = (bf16[48,3712]{1,0:T(8,128)(2,1)S(1)}, bf16[48,3712]{1,0:T(8,128)(2,1)S(1)}, u32[]{:S(2)}, u32[]{:S(2)}) collective-permute-start(bf16[48,3712]{1,0:T(8,128)(2,1)S(1)} %get-tuple-element.37), channel_id=1, source_target_pairs={{0,1},{1,0},{2,3},{3,2},{4,5},{5,4},{6,7},{7,6},{8,9},{9,8},{10,11... | collective-permute-start | bytes 1069064 | tf_op jit(solution)/shard_map/ppermute | solution.py:82
  20.2 1.5 %collective-permute-start.10 = (bf16[48,3712]{1,0:T(8,128)(2,1)S(1)}, bf16[48,3712]{1,0:T(8,128)(2,1)S(1)}, u32[]{:S(2)}, u32[]{:S(2)}) collective-permute-start(bf16[48,3712]{1,0:T(8,128)(2,1)S(1)} %get-tuple-element.38), channel_id=1, source_target_pairs={{0,2},{1,3},{2,0},{3,1},{4,6},{5,7},{6,4},{7,5},{8,10},{9,11},{10,... | collective-permute-start | bytes 1069064 | tf_op jit(solution)/shard_map/ppermute | solution.py:82
  22.2 7.4 %first.1 = (bf16[128,512]{1,0:T(8,128)(2,1)S(1)}, bf16[128,3584]{1,0:T(8,128)(2,1)S(1)}, bf16[1,3584,512]{2,1,0:T(8,128)(2,1)S(1)}, bf16[1,3584,512]{2,1,0:T(8,128)(2,1)S(1)}, bf16[1,512,3584]{2,1,0:T(8,128)(2,1)S(1)}) custom-call(bf16[128,3712]{1,0:T(8,128)(2,1)S(1)} %get-tuple-element.29.own, bf16[128,3712]{1,0:T(8,128)(2,1)S(1)} %collective-permute-done.5.other, ...), custom_call_target="tpu_custom_call" | custom-call | flops 2348810240 | bytes 11010048 | tf_op jit(solution)/shard_map/first/pallas_call | solution.py:368
  30.4 2.7 %attend.1 = (bf16[4,64,512]{2,1,0:T(8,128)(2,1)}, f32[8,128]{1,0:T(8,128)S(1)}) custom-call(s32[4]{0:T(128)S(1)} %copy-done.3, s32[1]{0:T(128)S(6)} %copy.12.live_rows, bf16[4,64,576]{2,1,0:T(8,128)(2,1)S(1)} %copy-done.1, bf16[4,576,256]{2,1,0:T(8,128)(2,1)S(1)} %bitcast.3, bf16[128,3584]{1,0:T(8,128)(2,1)S(1)} %get-tuple-element.30.refs_0_), custom_call_target="tpu_custom_call" | custom-call | flops 150994944 | bytes 1179648 | tf_op jit(solution)/shard_map/attend/pallas_call | solution.py:55
  33.1 2.5 %collective-permute-done.11.refs_2_ = bf16[32,3712]{1,0:T(8,128)(2,1)S(1)} collective-permute-done((bf16[32,3712]{1,0:T(8,128)(2,1)S(1)}, bf16[32,3712]{1,0:T(8,128)(2,1)S(1)}, u32[]{:S(2)}, u32[]{:S(2)}) %collective-permute-start.11) | collective-permute-done | bytes 237600 | tf_op jit(solution)/shard_map/ppermute | solution.py:88
  36.5 1.3 %collective-permute-start.7 = (bf16[32,3584]{1,0:T(8,128)(2,1)S(1)}, bf16[32,3584]{1,0:T(8,128)(2,1)S(1)}, u32[]{:S(2)}, u32[]{:S(2)}) collective-permute-start(bf16[32,3584]{1,0:T(8,128)(2,1)S(1)} %get-tuple-element.35), channel_id=1, source_target_pairs={{0,1},{1,0},{2,3},{3,2},{4,5},{5,4},{6,7},{7,6},{8,9},{9,8},{10,11... | collective-permute-start | bytes 688136 | tf_op jit(solution)/shard_map/ppermute | solution.py:82
  38.7 2.7 %expert.1 = (bf16[128,512]{1,0:T(8,128)(2,1)S(1)}, bf16[128,3584]{1,0:T(8,128)(2,1)S(1)}) custom-call(bf16[128,3712]{1,0:T(8,128)(2,1)S(1)} %combine.11.own, bf16[128,3712]{1,0:T(8,128)(2,1)S(1)} %collective-permute-done.12.other, bf16[1,3584,512]{2,1,0:T(8,128)(2,1)S(1)} %get-tuple-element.41.w_gate, bf16[1,3584,512]{2,1,0:T(8,128)(2,1)S(1)} %get-tuple-element.42.w_up, ...), custom_call_target="tpu_custom_call" | custom-call | flops 2348810240 | bytes 917504 | tf_op jit(solution)/shard_map/expert/pallas_call | solution.py:393
  41.5 3.1 %collective-permute-done.7.refs_1_ = bf16[32,3584]{1,0:T(8,128)(2,1)S(1)} collective-permute-done((bf16[32,3584]{1,0:T(8,128)(2,1)S(1)}, bf16[32,3584]{1,0:T(8,128)(2,1)S(1)}, u32[]{:S(2)}, u32[]{:S(2)}) %collective-permute-start.7) | collective-permute-done | bytes 229408 | tf_op jit(solution)/shard_map/ppermute | solution.py:82
  46.3 1.8 %collective-permute-start.15 = (bf16[16,3584]{1,0:T(8,128)(2,1)S(1)}, bf16[16,3584]{1,0:T(8,128)(2,1)S(1)}, u32[]{:S(2)}, u32[]{:S(2)}) collective-permute-start(bf16[16,3584]{1,0:T(8,128)(2,1)S(1)} %get-tuple-element.47), channel_id=1, source_target_pairs={{0,3},{1,2},{2,1},{3,0},{4,7},{5,6},{6,5},{7,4},{8,11},{9,10},{10,... | collective-permute-start | bytes 344072 | tf_op jit(solution)/shard_map/ppermute | solution.py:88
  48.7 1.2 %collective-permute-start.17 = (bf16[16,3584]{1,0:T(8,128)(2,1)S(1)}, bf16[16,3584]{1,0:T(8,128)(2,1)S(1)}, u32[]{:S(2)}, u32[]{:S(2)}) collective-permute-start(bf16[16,3584]{1,0:T(8,128)(2,1)S(1)} %get-tuple-element.49), channel_id=1, source_target_pairs={{0,2},{1,3},{2,0},{3,1},{4,6},{5,7},{6,4},{7,5},{8,10},{9,11},{10,... | collective-permute-start | bytes 344072 | tf_op jit(solution)/shard_map/ppermute | solution.py:82
  49.9 1.7 %collective-permute-start.19 = (bf16[16,3584]{1,0:T(8,128)(2,1)S(1)}, bf16[16,3584]{1,0:T(8,128)(2,1)S(1)}, u32[]{:S(2)}, u32[]{:S(2)}) collective-permute-start(bf16[16,3584]{1,0:T(8,128)(2,1)S(1)} %get-tuple-element.51), channel_id=1, source_target_pairs={{0,3},{1,2},{2,1},{3,0},{4,7},{5,6},{6,5},{7,4},{8,11},{9,10},{10,... | collective-permute-start | bytes 344072 | tf_op jit(solution)/shard_map/ppermute | solution.py:88
  52.2 1.3 %collective-permute-done.15.refs_1_ = bf16[16,3584]{1,0:T(8,128)(2,1)S(1)} collective-permute-done((bf16[16,3584]{1,0:T(8,128)(2,1)S(1)}, bf16[16,3584]{1,0:T(8,128)(2,1)S(1)}, u32[]{:S(2)}, u32[]{:S(2)}) %collective-permute-start.15) | collective-permute-done | bytes 114720 | tf_op jit(solution)/shard_map/ppermute | solution.py:88
  55.2 1.4 %collective-permute-start.14 = (bf16[32,3584]{1,0:T(8,128)(2,1)S(1)}, bf16[32,3584]{1,0:T(8,128)(2,1)S(1)}, u32[]{:S(2)}, u32[]{:S(2)}) collective-permute-start(bf16[32,3584]{1,0:T(8,128)(2,1)S(1)} %get-tuple-element.45), channel_id=1, source_target_pairs={{0,3},{1,2},{2,1},{3,0},{4,7},{5,6},{6,5},{7,4},{8,11},{9,10},{10,... | collective-permute-start | bytes 688136 | tf_op jit(solution)/shard_map/ppermute | solution.py:88
  57.3 2.8 %collective-permute-start.18 = (bf16[16,3584]{1,0:T(8,128)(2,1)S(1)}, bf16[16,3584]{1,0:T(8,128)(2,1)S(1)}, u32[]{:S(2)}, u32[]{:S(2)}) collective-permute-start(bf16[16,3584]{1,0:T(8,128)(2,1)S(1)} %combine.12.refs_4_), channel_id=1, source_target_pairs={{0,24},{4,28},{8,16},{12,20},{16,8},{20,12},{24,0},{28,4},{1,25},{... | collective-permute-start | bytes 344072 | tf_op jit(solution)/shard_map/ppermute | solution.py:88
  60.8 1.4 %collective-permute-start.22 = (bf16[16,3584]{1,0:T(8,128)(2,1)S(1)}, bf16[16,3584]{1,0:T(8,128)(2,1)S(1)}, u32[]{:S(2)}, u32[]{:S(2)}) collective-permute-start(bf16[16,3584]{1,0:T(8,128)(2,1)S(1)} %combine.13.refs_3_), channel_id=1, source_target_pairs={{0,16},{4,20},{8,24},{12,28},{16,0},{20,4},{24,8},{28,12},{1,17},{... | collective-permute-start | bytes 344072 | tf_op jit(solution)/shard_map/ppermute | solution.py:82
  62.2 1.8 %collective-permute-done.18.refs_2_ = bf16[16,3584]{1,0:T(8,128)(2,1)S(1)} collective-permute-done((bf16[16,3584]{1,0:T(8,128)(2,1)S(1)}, bf16[16,3584]{1,0:T(8,128)(2,1)S(1)}, u32[]{:S(2)}, u32[]{:S(2)}) %collective-permute-start.18) | collective-permute-done | bytes 114720 | tf_op jit(solution)/shard_map/ppermute | solution.py:88
  64.1 3.1 %collective-permute-start.23 = (bf16[16,3584]{1,0:T(8,128)(2,1)S(1)}, bf16[16,3584]{1,0:T(8,128)(2,1)S(1)}, u32[]{:S(2)}, u32[]{:S(2)}) collective-permute-start(bf16[16,3584]{1,0:T(8,128)(2,1)S(1)} %get-tuple-element.55), channel_id=1, source_target_pairs={{0,8},{4,12},{8,0},{12,4},{16,24},{20,28},{24,16},{28,20},{1,9},{5... | collective-permute-start | bytes 344072 | tf_op jit(solution)/shard_map/ppermute | solution.py:82
  68.2 1.7 %collective-permute-done.23.refs_2_ = bf16[16,3584]{1,0:T(8,128)(2,1)S(1)} collective-permute-done((bf16[16,3584]{1,0:T(8,128)(2,1)S(1)}, bf16[16,3584]{1,0:T(8,128)(2,1)S(1)}, u32[]{:S(2)}, u32[]{:S(2)}) %collective-permute-start.23) | collective-permute-done | bytes 114720 | tf_op jit(solution)/shard_map/ppermute | solution.py:82
  (47 shorter events, 12.8 us)
Async XLA Ops:
  2.4 7.6 %collective-permute-start = (bf16[16,3712]{1,0:T(8,128)(2,1)S(1)}, bf16[16,3712]{1,0:T(8,128)(2,1)S(1)}, u32[]{:S(2)}, u32[]{:S(2)}) collective-permute-start(bf16[16,3712]{1,0:T(8,128)(2,1)S(1)} %pack.1.refs_0_), channel_id=1, source_target_pairs={{0,8},{4,12},{8,0},{12,4},{16,24},{20,28},{24,16},{28,20},{1,9},{5... | collective-permute-start | bytes 356360 | tf_op jit(solution)/shard_map/ppermute | solution.py:82
  5.4 8.2 %collective-permute-start.3 = (bf16[16,3712]{1,0:T(8,128)(2,1)S(1)}, bf16[16,3712]{1,0:T(8,128)(2,1)S(1)}, u32[]{:S(2)}, u32[]{:S(2)}) collective-permute-start(bf16[16,3712]{1,0:T(8,128)(2,1)S(1)} %pack.1.refs_0_), channel_id=1, source_target_pairs={{0,16},{4,20},{8,24},{12,28},{16,0},{20,4},{24,8},{28,12},{1,17},{... | collective-permute-start | bytes 356360 | tf_op jit(solution)/shard_map/ppermute | solution.py:82
  10.0 8.5 %collective-permute-start.2 = (bf16[32,3712]{1,0:T(8,128)(2,1)S(1)}, bf16[32,3712]{1,0:T(8,128)(2,1)S(1)}, u32[]{:S(2)}, u32[]{:S(2)}) collective-permute-start(bf16[32,3712]{1,0:T(8,128)(2,1)S(1)} %combine.8.refs_0_), channel_id=1, source_target_pairs={{0,2},{1,3},{2,0},{3,1},{4,6},{5,7},{6,4},{7,5},{8,10},{9,11},{10,... | collective-permute-start | bytes 712712 | tf_op jit(solution)/shard_map/ppermute | solution.py:82
  11.9 6.6 %collective-permute-start.1 = (bf16[32,3712]{1,0:T(8,128)(2,1)S(1)}, bf16[32,3712]{1,0:T(8,128)(2,1)S(1)}, u32[]{:S(2)}, u32[]{:S(2)}) collective-permute-start(bf16[32,3712]{1,0:T(8,128)(2,1)S(1)} %combine.8.refs_0_), channel_id=1, source_target_pairs={{0,1},{1,0},{2,3},{3,2},{4,5},{5,4},{6,7},{7,6},{8,9},{9,8},{10,11... | collective-permute-start | bytes 712712 | tf_op jit(solution)/shard_map/ppermute | solution.py:82
  13.6 4.8 %collective-permute-start.4 = (bf16[16,3712]{1,0:T(8,128)(2,1)S(1)}, bf16[16,3712]{1,0:T(8,128)(2,1)S(1)}, u32[]{:S(2)}, u32[]{:S(2)}) collective-permute-start(bf16[16,3712]{1,0:T(8,128)(2,1)S(1)} %collective-permute-done.3.refs_3_), channel_id=1, source_target_pairs={{0,8},{4,12},{8,0},{12,4},{16,24},{20,28},{24,16},{28,20},{1,9},{5... | collective-permute-start | bytes 356360 | tf_op jit(solution)/shard_map/ppermute | solution.py:82
  18.6 3.6 %collective-permute-start.5 = (bf16[128,3712]{1,0:T(8,128)(2,1)S(1)}, bf16[128,3712]{1,0:T(8,128)(2,1)S(1)}, u32[]{:S(2)}, u32[]{:S(2)}) collective-permute-start(bf16[128,3712]{1,0:T(8,128)(2,1)S(1)} %get-tuple-element.29.own), channel_id=1, source_target_pairs={{0,4},{4,0},{8,12},{12,8},{16,20},{20,16},{24,28},{28,24},{1,5},{5... | collective-permute-start | bytes 2850824 | tf_op jit(solution)/shard_map/ppermute | solution.py:82
  18.7 16.9 %collective-permute-start.9 = (bf16[48,3712]{1,0:T(8,128)(2,1)S(1)}, bf16[48,3712]{1,0:T(8,128)(2,1)S(1)}, u32[]{:S(2)}, u32[]{:S(2)}) collective-permute-start(bf16[48,3712]{1,0:T(8,128)(2,1)S(1)} %get-tuple-element.37), channel_id=1, source_target_pairs={{0,1},{1,0},{2,3},{3,2},{4,5},{5,4},{6,7},{7,6},{8,9},{9,8},{10,11... | collective-permute-start | bytes 1069064 | tf_op jit(solution)/shard_map/ppermute | solution.py:82
  20.2 15.5 %collective-permute-start.10 = (bf16[48,3712]{1,0:T(8,128)(2,1)S(1)}, bf16[48,3712]{1,0:T(8,128)(2,1)S(1)}, u32[]{:S(2)}, u32[]{:S(2)}) collective-permute-start(bf16[48,3712]{1,0:T(8,128)(2,1)S(1)} %get-tuple-element.38), channel_id=1, source_target_pairs={{0,2},{1,3},{2,0},{3,1},{4,6},{5,7},{6,4},{7,5},{8,10},{9,11},{10,... | collective-permute-start | bytes 1069064 | tf_op jit(solution)/shard_map/ppermute | solution.py:82
  21.8 13.8 %collective-permute-start.11 = (bf16[32,3712]{1,0:T(8,128)(2,1)S(1)}, bf16[32,3712]{1,0:T(8,128)(2,1)S(1)}, u32[]{:S(2)}, u32[]{:S(2)}) collective-permute-start(bf16[32,3712]{1,0:T(8,128)(2,1)S(1)} %get-tuple-element.39), channel_id=1, source_target_pairs={{0,3},{1,2},{2,1},{3,0},{4,7},{5,6},{6,5},{7,4},{8,11},{9,10},{10,... | collective-permute-start | bytes 712712 | tf_op jit(solution)/shard_map/ppermute | solution.py:88
  29.7 6.2 %collective-permute-start.6 = (bf16[128,3584]{1,0:T(8,128)(2,1)S(1)}, bf16[128,3584]{1,0:T(8,128)(2,1)S(1)}, u32[]{:S(2)}, u32[]{:S(2)}) collective-permute-start(bf16[128,3584]{1,0:T(8,128)(2,1)S(1)} %get-tuple-element.30.refs_0_), channel_id=1, source_target_pairs={{0,4},{4,0},{8,12},{12,8},{16,20},{20,16},{24,28},{28,24},{1,5},{5... | collective-permute-start | bytes 2752520 | tf_op jit(solution)/shard_map/ppermute | solution.py:82
  35.8 2.9 %collective-permute-start.12 = (bf16[128,3712]{1,0:T(8,128)(2,1)S(1)}, bf16[128,3712]{1,0:T(8,128)(2,1)S(1)}, u32[]{:S(2)}, u32[]{:S(2)}) collective-permute-start(bf16[128,3712]{1,0:T(8,128)(2,1)S(1)} %combine.11.own), channel_id=1, source_target_pairs={{0,4},{4,0},{8,12},{12,8},{16,20},{20,16},{24,28},{28,24},{1,5},{5... | collective-permute-start | bytes 2850824 | tf_op jit(solution)/shard_map/ppermute | solution.py:82
  36.5 8.1 %collective-permute-start.7 = (bf16[32,3584]{1,0:T(8,128)(2,1)S(1)}, bf16[32,3584]{1,0:T(8,128)(2,1)S(1)}, u32[]{:S(2)}, u32[]{:S(2)}) collective-permute-start(bf16[32,3584]{1,0:T(8,128)(2,1)S(1)} %get-tuple-element.35), channel_id=1, source_target_pairs={{0,1},{1,0},{2,3},{3,2},{4,5},{5,4},{6,7},{7,6},{8,9},{9,8},{10,11... | collective-permute-start | bytes 688136 | tf_op jit(solution)/shard_map/ppermute | solution.py:82
  37.9 7.7 %collective-permute-start.8 = (bf16[32,3584]{1,0:T(8,128)(2,1)S(1)}, bf16[32,3584]{1,0:T(8,128)(2,1)S(1)}, u32[]{:S(2)}, u32[]{:S(2)}) collective-permute-start(bf16[32,3584]{1,0:T(8,128)(2,1)S(1)} %get-tuple-element.36), channel_id=1, source_target_pairs={{0,2},{1,3},{2,0},{3,1},{4,6},{5,7},{6,4},{7,5},{8,10},{9,11},{10,... | collective-permute-start | bytes 688136 | tf_op jit(solution)/shard_map/ppermute | solution.py:82
  41.4 4.3 %collective-permute-start.13 = (bf16[128,3584]{1,0:T(8,128)(2,1)S(1)}, bf16[128,3584]{1,0:T(8,128)(2,1)S(1)}, u32[]{:S(2)}, u32[]{:S(2)}) collective-permute-start(bf16[128,3584]{1,0:T(8,128)(2,1)S(1)} %get-tuple-element.44), channel_id=1, source_target_pairs={{0,4},{4,0},{8,12},{12,8},{16,20},{20,16},{24,28},{28,24},{1,5},{5... | collective-permute-start | bytes 2752520 | tf_op jit(solution)/shard_map/ppermute | solution.py:82
  46.3 7.1 %collective-permute-start.15 = (bf16[16,3584]{1,0:T(8,128)(2,1)S(1)}, bf16[16,3584]{1,0:T(8,128)(2,1)S(1)}, u32[]{:S(2)}, u32[]{:S(2)}) collective-permute-start(bf16[16,3584]{1,0:T(8,128)(2,1)S(1)} %get-tuple-element.47), channel_id=1, source_target_pairs={{0,3},{1,2},{2,1},{3,0},{4,7},{5,6},{6,5},{7,4},{8,11},{9,10},{10,... | collective-permute-start | bytes 344072 | tf_op jit(solution)/shard_map/ppermute | solution.py:88
  48.1 7.1 %collective-permute-start.16 = (bf16[16,3584]{1,0:T(8,128)(2,1)S(1)}, bf16[16,3584]{1,0:T(8,128)(2,1)S(1)}, u32[]{:S(2)}, u32[]{:S(2)}) collective-permute-start(bf16[16,3584]{1,0:T(8,128)(2,1)S(1)} %get-tuple-element.48), channel_id=1, source_target_pairs={{0,1},{1,0},{2,3},{3,2},{4,5},{5,4},{6,7},{7,6},{8,9},{9,8},{10,11... | collective-permute-start | bytes 344072 | tf_op jit(solution)/shard_map/ppermute | solution.py:82
  48.7 8.6 %collective-permute-start.17 = (bf16[16,3584]{1,0:T(8,128)(2,1)S(1)}, bf16[16,3584]{1,0:T(8,128)(2,1)S(1)}, u32[]{:S(2)}, u32[]{:S(2)}) collective-permute-start(bf16[16,3584]{1,0:T(8,128)(2,1)S(1)} %get-tuple-element.49), channel_id=1, source_target_pairs={{0,2},{1,3},{2,0},{3,1},{4,6},{5,7},{6,4},{7,5},{8,10},{9,11},{10,... | collective-permute-start | bytes 344072 | tf_op jit(solution)/shard_map/ppermute | solution.py:82
  49.9 10.3 %collective-permute-start.19 = (bf16[16,3584]{1,0:T(8,128)(2,1)S(1)}, bf16[16,3584]{1,0:T(8,128)(2,1)S(1)}, u32[]{:S(2)}, u32[]{:S(2)}) collective-permute-start(bf16[16,3584]{1,0:T(8,128)(2,1)S(1)} %get-tuple-element.51), channel_id=1, source_target_pairs={{0,3},{1,2},{2,1},{3,0},{4,7},{5,6},{6,5},{7,4},{8,11},{9,10},{10,... | collective-permute-start | bytes 344072 | tf_op jit(solution)/shard_map/ppermute | solution.py:88
  51.6 8.6 %collective-permute-start.20 = (bf16[16,3584]{1,0:T(8,128)(2,1)S(1)}, bf16[16,3584]{1,0:T(8,128)(2,1)S(1)}, u32[]{:S(2)}, u32[]{:S(2)}) collective-permute-start(bf16[16,3584]{1,0:T(8,128)(2,1)S(1)} %get-tuple-element.52), channel_id=1, source_target_pairs={{0,1},{1,0},{2,3},{3,2},{4,5},{5,4},{6,7},{7,6},{8,9},{9,8},{10,11... | collective-permute-start | bytes 344072 | tf_op jit(solution)/shard_map/ppermute | solution.py:82
  53.4 7.3 %collective-permute-start.21 = (bf16[16,3584]{1,0:T(8,128)(2,1)S(1)}, bf16[16,3584]{1,0:T(8,128)(2,1)S(1)}, u32[]{:S(2)}, u32[]{:S(2)}) collective-permute-start(bf16[16,3584]{1,0:T(8,128)(2,1)S(1)} %get-tuple-element.53), channel_id=1, source_target_pairs={{0,2},{1,3},{2,0},{3,1},{4,6},{5,7},{6,4},{7,5},{8,10},{9,11},{10,... | collective-permute-start | bytes 344072 | tf_op jit(solution)/shard_map/ppermute | solution.py:82
  55.2 8.8 %collective-permute-start.14 = (bf16[32,3584]{1,0:T(8,128)(2,1)S(1)}, bf16[32,3584]{1,0:T(8,128)(2,1)S(1)}, u32[]{:S(2)}, u32[]{:S(2)}) collective-permute-start(bf16[32,3584]{1,0:T(8,128)(2,1)S(1)} %get-tuple-element.45), channel_id=1, source_target_pairs={{0,3},{1,2},{2,1},{3,0},{4,7},{5,6},{6,5},{7,4},{8,11},{9,10},{10,... | collective-permute-start | bytes 688136 | tf_op jit(solution)/shard_map/ppermute | solution.py:88
  57.3 6.7 %collective-permute-start.18 = (bf16[16,3584]{1,0:T(8,128)(2,1)S(1)}, bf16[16,3584]{1,0:T(8,128)(2,1)S(1)}, u32[]{:S(2)}, u32[]{:S(2)}) collective-permute-start(bf16[16,3584]{1,0:T(8,128)(2,1)S(1)} %combine.12.refs_4_), channel_id=1, source_target_pairs={{0,24},{4,28},{8,16},{12,20},{16,8},{20,12},{24,0},{28,4},{1,25},{... | collective-permute-start | bytes 344072 | tf_op jit(solution)/shard_map/ppermute | solution.py:88
  60.8 7.4 %collective-permute-start.22 = (bf16[16,3584]{1,0:T(8,128)(2,1)S(1)}, bf16[16,3584]{1,0:T(8,128)(2,1)S(1)}, u32[]{:S(2)}, u32[]{:S(2)}) collective-permute-start(bf16[16,3584]{1,0:T(8,128)(2,1)S(1)} %combine.13.refs_3_), channel_id=1, source_target_pairs={{0,16},{4,20},{8,24},{12,28},{16,0},{20,4},{24,8},{28,12},{1,17},{... | collective-permute-start | bytes 344072 | tf_op jit(solution)/shard_map/ppermute | solution.py:82
  64.1 5.9 %collective-permute-start.23 = (bf16[16,3584]{1,0:T(8,128)(2,1)S(1)}, bf16[16,3584]{1,0:T(8,128)(2,1)S(1)}, u32[]{:S(2)}, u32[]{:S(2)}) collective-permute-start(bf16[16,3584]{1,0:T(8,128)(2,1)S(1)} %get-tuple-element.55), channel_id=1, source_target_pairs={{0,8},{4,12},{8,0},{12,4},{16,24},{20,28},{24,16},{28,20},{1,9},{5... | collective-permute-start | bytes 344072 | tf_op jit(solution)/shard_map/ppermute | solution.py:82
  (4 other events, 26.8 us)

commit v15 on v14

--- a/solution.py
+++ b/solution.py
@@ -530,10 +530,10 @@
     (far_sum,) = combine([far_sum, *to_far], [all_of(4, 0)], [both_sum], flops=FAR_FLOPS)
     from_both = across(both_sum, z_far, z_near)
     own_sum, near_sum = combine(
-        [near, to_near, from_both], [all_of(3, 0), all_of(2, n)], [far_sum]
+        [near, to_near], [all_of(2, 0), all_of(2, n)], [far_sum]
     )
     (mixed,) = combine(
-        [own_sum, swap(far_sum, z_far), swap(near_sum, z_near)], [all_of(3, 0)]
+        [own_sum, from_both, swap(far_sum, z_far), swap(near_sum, z_near)], [all_of(4, 0)]
     )
     return mixed, context
 

time: 70.9 us -> 70.4 us (level)
  starting transfers between devices: 30.8 us -> 28.2 us
  waiting for transfers between devices: 21.3 us -> 23.4 us
    ppermute x19, starting transfers between devices: 22.5 us -> 19.9 us  [swap(): return lax.ppermute(value, axis, [(i, i ^ bit) for i in range(size)])]
    ppermute x19, waiting for transfers between devices: 15.8 us -> 17.9 us  [swap(): return lax.ppermute(value, axis, [(i, i ^ bit) for i in range(size)])]
where the time goes in v15:
time: 70.4 us; the launch traced here: 70.2 us
  starting transfers between devices  28.2 us (40%)
  waiting for transfers between devices  23.4 us (33%)
  Pallas kernels  15.5 us (22%)
  between operations  1.43 us (2%)
  local copies, waits for them, and re-layouts  0.91 us (1%)
  other arithmetic  0.71 us (1%)
    ppermute x19, starting transfers between devices, swap(): return lax.ppermute(value, axis, [(i, i ^ bit) for i in range(size)])  19.9 us
    ppermute x19, waiting for transfers between devices, swap(): return lax.ppermute(value, axis, [(i, i ^ bit) for i in range(size)])  17.9 us
    ppermute x5, starting transfers between devices, across(): lax.ppermute(value, axis, [(i, i ^ first[1] ^ second[1]) for i in range(s...  8.25 us
    pallas_call x1, Pallas kernels, first_of(): pl.pallas_call(functools.partial(first_kernel, picks), out_shape=[jax.Sha...  7.4 us
    ppermute x5, waiting for transfers between devices, across(): lax.ppermute(value, axis, [(i, i ^ first[1] ^ second[1]) for i in range(s...  5.56 us
    pallas_call x1, Pallas kernels, attend(): pl.pallas_call(attend_kernel, out_shape=[jax.ShapeDtypeStruct((count, hea...  2.7 us
    pallas_call x1, Pallas kernels, expert_of(): pl.pallas_call(functools.partial(expert_kernel, picks, len(after)), out_s...  2.7 us
  transfers between devices with their start and end apart: 24, of which 14 were waited for; matrix products, arithmetic and copies ran while one was open for 0% of the time, Pallas kernels for 20%

profile of v15, /device:TPU:0, one launch (start us, length us, event | category | flops | bytes accessed | tf_op | source)
XLA Modules:
  0.0 70.2 jit_solution(15568923897359029087)
XLA Ops:
  2.4 3.0 %collective-permute-start = (bf16[16,3712]{1,0:T(8,128)(2,1)S(1)}, bf16[16,3712]{1,0:T(8,128)(2,1)S(1)}, u32[]{:S(2)}, u32[]{:S(2)}) collective-permute-start(bf16[16,3712]{1,0:T(8,128)(2,1)S(1)} %pack.1.refs_0_), channel_id=1, source_target_pairs={{0,8},{4,12},{8,0},{12,4},{16,24},{20,28},{24,16},{28,20},{1,9},{5... | collective-permute-start | bytes 356360 | tf_op jit(solution)/shard_map/ppermute | solution.py:82
  5.4 2.6 %collective-permute-start.3 = (bf16[16,3712]{1,0:T(8,128)(2,1)S(1)}, bf16[16,3712]{1,0:T(8,128)(2,1)S(1)}, u32[]{:S(2)}, u32[]{:S(2)}) collective-permute-start(bf16[16,3712]{1,0:T(8,128)(2,1)S(1)} %pack.1.refs_0_), channel_id=1, source_target_pairs={{0,16},{4,20},{8,24},{12,28},{16,0},{20,4},{24,8},{28,12},{1,17},{... | collective-permute-start | bytes 356360 | tf_op jit(solution)/shard_map/ppermute | solution.py:82
  8.0 1.9 %collective-permute-done.refs_1_ = bf16[16,3712]{1,0:T(8,128)(2,1)S(1)} collective-permute-done((bf16[16,3712]{1,0:T(8,128)(2,1)S(1)}, bf16[16,3712]{1,0:T(8,128)(2,1)S(1)}, u32[]{:S(2)}, u32[]{:S(2)}) %collective-permute-start) | collective-permute-done | bytes 118816 | tf_op jit(solution)/shard_map/ppermute | solution.py:82
  10.0 1.9 %collective-permute-start.2 = (bf16[32,3712]{1,0:T(8,128)(2,1)S(1)}, bf16[32,3712]{1,0:T(8,128)(2,1)S(1)}, u32[]{:S(2)}, u32[]{:S(2)}) collective-permute-start(bf16[32,3712]{1,0:T(8,128)(2,1)S(1)} %combine.8.refs_0_), channel_id=1, source_target_pairs={{0,2},{1,3},{2,0},{3,1},{4,6},{5,7},{6,4},{7,5},{8,10},{9,11},{10,... | collective-permute-start | bytes 712712 | tf_op jit(solution)/shard_map/ppermute | solution.py:82
  11.9 1.5 %collective-permute-start.1 = (bf16[32,3712]{1,0:T(8,128)(2,1)S(1)}, bf16[32,3712]{1,0:T(8,128)(2,1)S(1)}, u32[]{:S(2)}, u32[]{:S(2)}) collective-permute-start(bf16[32,3712]{1,0:T(8,128)(2,1)S(1)} %combine.8.refs_0_), channel_id=1, source_target_pairs={{0,1},{1,0},{2,3},{3,2},{4,5},{5,4},{6,7},{7,6},{8,9},{9,8},{10,11... | collective-permute-start | bytes 712712 | tf_op jit(solution)/shard_map/ppermute | solution.py:82
  14.1 4.4 %collective-permute-done.4.refs_4_ = bf16[16,3712]{1,0:T(8,128)(2,1)S(1)} collective-permute-done((bf16[16,3712]{1,0:T(8,128)(2,1)S(1)}, bf16[16,3712]{1,0:T(8,128)(2,1)S(1)}, u32[]{:S(2)}, u32[]{:S(2)}) %collective-permute-start.4) | collective-permute-done | bytes 118816 | tf_op jit(solution)/shard_map/ppermute | solution.py:82
  18.7 1.6 %collective-permute-start.9 = (bf16[48,3712]{1,0:T(8,128)(2,1)S(1)}, bf16[48,3712]{1,0:T(8,128)(2,1)S(1)}, u32[]{:S(2)}, u32[]{:S(2)}) collective-permute-start(bf16[48,3712]{1,0:T(8,128)(2,1)S(1)} %get-tuple-element.37), channel_id=1, source_target_pairs={{0,1},{1,0},{2,3},{3,2},{4,5},{5,4},{6,7},{7,6},{8,9},{9,8},{10,11... | collective-permute-start | bytes 1069064 | tf_op jit(solution)/shard_map/ppermute | solution.py:82
  20.2 1.5 %collective-permute-start.10 = (bf16[48,3712]{1,0:T(8,128)(2,1)S(1)}, bf16[48,3712]{1,0:T(8,128)(2,1)S(1)}, u32[]{:S(2)}, u32[]{:S(2)}) collective-permute-start(bf16[48,3712]{1,0:T(8,128)(2,1)S(1)} %get-tuple-element.38), channel_id=1, source_target_pairs={{0,2},{1,3},{2,0},{3,1},{4,6},{5,7},{6,4},{7,5},{8,10},{9,11},{10,... | collective-permute-start | bytes 1069064 | tf_op jit(solution)/shard_map/ppermute | solution.py:82
  22.2 7.4 %first.1 = (bf16[128,512]{1,0:T(8,128)(2,1)S(1)}, bf16[128,3584]{1,0:T(8,128)(2,1)S(1)}, bf16[1,3584,512]{2,1,0:T(8,128)(2,1)S(1)}, bf16[1,3584,512]{2,1,0:T(8,128)(2,1)S(1)}, bf16[1,512,3584]{2,1,0:T(8,128)(2,1)S(1)}) custom-call(bf16[128,3712]{1,0:T(8,128)(2,1)S(1)} %get-tuple-element.29.own, bf16[128,3712]{1,0:T(8,128)(2,1)S(1)} %collective-permute-done.5.other, ...), custom_call_target="tpu_custom_call" | custom-call | flops 2348810240 | bytes 11010048 | tf_op jit(solution)/shard_map/first/pallas_call | solution.py:368
  30.4 2.7 %attend.1 = (bf16[4,64,512]{2,1,0:T(8,128)(2,1)}, f32[8,128]{1,0:T(8,128)S(1)}) custom-call(s32[4]{0:T(128)S(1)} %copy-done.3, s32[1]{0:T(128)S(6)} %copy.12.live_rows, bf16[4,64,576]{2,1,0:T(8,128)(2,1)S(1)} %copy-done.1, bf16[4,576,256]{2,1,0:T(8,128)(2,1)S(1)} %bitcast.3, bf16[128,3584]{1,0:T(8,128)(2,1)S(1)} %get-tuple-element.30.refs_0_), custom_call_target="tpu_custom_call" | custom-call | flops 150994944 | bytes 1179648 | tf_op jit(solution)/shard_map/attend/pallas_call | solution.py:55
  33.1 2.5 %collective-permute-done.11.refs_2_ = bf16[32,3712]{1,0:T(8,128)(2,1)S(1)} collective-permute-done((bf16[32,3712]{1,0:T(8,128)(2,1)S(1)}, bf16[32,3712]{1,0:T(8,128)(2,1)S(1)}, u32[]{:S(2)}, u32[]{:S(2)}) %collective-permute-start.11) | collective-permute-done | bytes 237600 | tf_op jit(solution)/shard_map/ppermute | solution.py:88
  36.5 1.3 %collective-permute-start.7 = (bf16[32,3584]{1,0:T(8,128)(2,1)S(1)}, bf16[32,3584]{1,0:T(8,128)(2,1)S(1)}, u32[]{:S(2)}, u32[]{:S(2)}) collective-permute-start(bf16[32,3584]{1,0:T(8,128)(2,1)S(1)} %get-tuple-element.35), channel_id=1, source_target_pairs={{0,1},{1,0},{2,3},{3,2},{4,5},{5,4},{6,7},{7,6},{8,9},{9,8},{10,11... | collective-permute-start | bytes 688136 | tf_op jit(solution)/shard_map/ppermute | solution.py:82
  38.7 2.7 %expert.1 = (bf16[128,512]{1,0:T(8,128)(2,1)S(1)}, bf16[128,3584]{1,0:T(8,128)(2,1)S(1)}) custom-call(bf16[128,3712]{1,0:T(8,128)(2,1)S(1)} %combine.11.own, bf16[128,3712]{1,0:T(8,128)(2,1)S(1)} %collective-permute-done.12.other, bf16[1,3584,512]{2,1,0:T(8,128)(2,1)S(1)} %get-tuple-element.41.w_gate, bf16[1,3584,512]{2,1,0:T(8,128)(2,1)S(1)} %get-tuple-element.42.w_up, ...), custom_call_target="tpu_custom_call" | custom-call | flops 2348810240 | bytes 917504 | tf_op jit(solution)/shard_map/expert/pallas_call | solution.py:393
  41.5 3.1 %collective-permute-done.7.refs_1_ = bf16[32,3584]{1,0:T(8,128)(2,1)S(1)} collective-permute-done((bf16[32,3584]{1,0:T(8,128)(2,1)S(1)}, bf16[32,3584]{1,0:T(8,128)(2,1)S(1)}, u32[]{:S(2)}, u32[]{:S(2)}) %collective-permute-start.7) | collective-permute-done | bytes 229408 | tf_op jit(solution)/shard_map/ppermute | solution.py:82
  46.3 1.8 %collective-permute-start.18 = (bf16[16,3584]{1,0:T(8,128)(2,1)S(1)}, bf16[16,3584]{1,0:T(8,128)(2,1)S(1)}, u32[]{:S(2)}, u32[]{:S(2)}) collective-permute-start(bf16[16,3584]{1,0:T(8,128)(2,1)S(1)} %get-tuple-element.51), channel_id=1, source_target_pairs={{0,3},{1,2},{2,1},{3,0},{4,7},{5,6},{6,5},{7,4},{8,11},{9,10},{10,... | collective-permute-start | bytes 344072 | tf_op jit(solution)/shard_map/ppermute | solution.py:88
  48.7 1.2 %collective-permute-start.20 = (bf16[16,3584]{1,0:T(8,128)(2,1)S(1)}, bf16[16,3584]{1,0:T(8,128)(2,1)S(1)}, u32[]{:S(2)}, u32[]{:S(2)}) collective-permute-start(bf16[16,3584]{1,0:T(8,128)(2,1)S(1)} %get-tuple-element.53), channel_id=1, source_target_pairs={{0,2},{1,3},{2,0},{3,1},{4,6},{5,7},{6,4},{7,5},{8,10},{9,11},{10,... | collective-permute-start | bytes 344072 | tf_op jit(solution)/shard_map/ppermute | solution.py:82
  49.9 1.7 %collective-permute-start.15 = (bf16[16,3584]{1,0:T(8,128)(2,1)S(1)}, bf16[16,3584]{1,0:T(8,128)(2,1)S(1)}, u32[]{:S(2)}, u32[]{:S(2)}) collective-permute-start(bf16[16,3584]{1,0:T(8,128)(2,1)S(1)} %get-tuple-element.47), channel_id=1, source_target_pairs={{0,3},{1,2},{2,1},{3,0},{4,7},{5,6},{6,5},{7,4},{8,11},{9,10},{10,... | collective-permute-start | bytes 344072 | tf_op jit(solution)/shard_map/ppermute | solution.py:88
  52.2 1.3 %collective-permute-done.18.refs_1_ = bf16[16,3584]{1,0:T(8,128)(2,1)S(1)} collective-permute-done((bf16[16,3584]{1,0:T(8,128)(2,1)S(1)}, bf16[16,3584]{1,0:T(8,128)(2,1)S(1)}, u32[]{:S(2)}, u32[]{:S(2)}) %collective-permute-start.18) | collective-permute-done | bytes 114720 | tf_op jit(solution)/shard_map/ppermute | solution.py:88
  55.2 1.4 %collective-permute-start.14 = (bf16[32,3584]{1,0:T(8,128)(2,1)S(1)}, bf16[32,3584]{1,0:T(8,128)(2,1)S(1)}, u32[]{:S(2)}, u32[]{:S(2)}) collective-permute-start(bf16[32,3584]{1,0:T(8,128)(2,1)S(1)} %get-tuple-element.45), channel_id=1, source_target_pairs={{0,3},{1,2},{2,1},{3,0},{4,7},{5,6},{6,5},{7,4},{8,11},{9,10},{10,... | collective-permute-start | bytes 688136 | tf_op jit(solution)/shard_map/ppermute | solution.py:88
  57.3 2.8 %collective-permute-start.21 = (bf16[16,3584]{1,0:T(8,128)(2,1)S(1)}, bf16[16,3584]{1,0:T(8,128)(2,1)S(1)}, u32[]{:S(2)}, u32[]{:S(2)}) collective-permute-start(bf16[16,3584]{1,0:T(8,128)(2,1)S(1)} %combine.12.refs_4_), channel_id=1, source_target_pairs={{0,24},{4,28},{8,16},{12,20},{16,8},{20,12},{24,0},{28,4},{1,25},{... | collective-permute-start | bytes 344072 | tf_op jit(solution)/shard_map/ppermute | solution.py:88
  60.8 1.4 %collective-permute-start.22 = (bf16[16,3584]{1,0:T(8,128)(2,1)S(1)}, bf16[16,3584]{1,0:T(8,128)(2,1)S(1)}, u32[]{:S(2)}, u32[]{:S(2)}) collective-permute-start(bf16[16,3584]{1,0:T(8,128)(2,1)S(1)} %combine.13.refs_2_), channel_id=1, source_target_pairs={{0,16},{4,20},{8,24},{12,28},{16,0},{20,4},{24,8},{28,12},{1,17},{... | collective-permute-start | bytes 344072 | tf_op jit(solution)/shard_map/ppermute | solution.py:82
  62.2 1.8 %collective-permute-done.14.refs_1_ = bf16[32,3584]{1,0:T(8,128)(2,1)S(1)} collective-permute-done((bf16[32,3584]{1,0:T(8,128)(2,1)S(1)}, bf16[32,3584]{1,0:T(8,128)(2,1)S(1)}, u32[]{:S(2)}, u32[]{:S(2)}) %collective-permute-start.14) | collective-permute-done | bytes 229408 | tf_op jit(solution)/shard_map/ppermute | solution.py:88
  64.6 3.7 %collective-permute-done.22.refs_2_ = bf16[16,3584]{1,0:T(8,128)(2,1)S(1)} collective-permute-done((bf16[16,3584]{1,0:T(8,128)(2,1)S(1)}, bf16[16,3584]{1,0:T(8,128)(2,1)S(1)}, u32[]{:S(2)}, u32[]{:S(2)}) %collective-permute-start.22) | collective-permute-done | bytes 114720 | tf_op jit(solution)/shard_map/ppermute | solution.py:82
  68.3 1.2 %collective-permute-done.23.refs_3_ = bf16[16,3584]{1,0:T(8,128)(2,1)S(1)} collective-permute-done((bf16[16,3584]{1,0:T(8,128)(2,1)S(1)}, bf16[16,3584]{1,0:T(8,128)(2,1)S(1)}, u32[]{:S(2)}, u32[]{:S(2)}) %collective-permute-start.23) | collective-permute-done | bytes 114720 | tf_op jit(solution)/shard_map/ppermute | solution.py:82
  (47 shorter events, 12.2 us)
Async XLA Ops:
  2.4 7.6 %collective-permute-start = (bf16[16,3712]{1,0:T(8,128)(2,1)S(1)}, bf16[16,3712]{1,0:T(8,128)(2,1)S(1)}, u32[]{:S(2)}, u32[]{:S(2)}) collective-permute-start(bf16[16,3712]{1,0:T(8,128)(2,1)S(1)} %pack.1.refs_0_), channel_id=1, source_target_pairs={{0,8},{4,12},{8,0},{12,4},{16,24},{20,28},{24,16},{28,20},{1,9},{5... | collective-permute-start | bytes 356360 | tf_op jit(solution)/shard_map/ppermute | solution.py:82
  5.4 8.2 %collective-permute-start.3 = (bf16[16,3712]{1,0:T(8,128)(2,1)S(1)}, bf16[16,3712]{1,0:T(8,128)(2,1)S(1)}, u32[]{:S(2)}, u32[]{:S(2)}) collective-permute-start(bf16[16,3712]{1,0:T(8,128)(2,1)S(1)} %pack.1.refs_0_), channel_id=1, source_target_pairs={{0,16},{4,20},{8,24},{12,28},{16,0},{20,4},{24,8},{28,12},{1,17},{... | collective-permute-start | bytes 356360 | tf_op jit(solution)/shard_map/ppermute | solution.py:82
  10.0 8.5 %collective-permute-start.2 = (bf16[32,3712]{1,0:T(8,128)(2,1)S(1)}, bf16[32,3712]{1,0:T(8,128)(2,1)S(1)}, u32[]{:S(2)}, u32[]{:S(2)}) collective-permute-start(bf16[32,3712]{1,0:T(8,128)(2,1)S(1)} %combine.8.refs_0_), channel_id=1, source_target_pairs={{0,2},{1,3},{2,0},{3,1},{4,6},{5,7},{6,4},{7,5},{8,10},{9,11},{10,... | collective-permute-start | bytes 712712 | tf_op jit(solution)/shard_map/ppermute | solution.py:82
  11.9 6.6 %collective-permute-start.1 = (bf16[32,3712]{1,0:T(8,128)(2,1)S(1)}, bf16[32,3712]{1,0:T(8,128)(2,1)S(1)}, u32[]{:S(2)}, u32[]{:S(2)}) collective-permute-start(bf16[32,3712]{1,0:T(8,128)(2,1)S(1)} %combine.8.refs_0_), channel_id=1, source_target_pairs={{0,1},{1,0},{2,3},{3,2},{4,5},{5,4},{6,7},{7,6},{8,9},{9,8},{10,11... | collective-permute-start | bytes 712712 | tf_op jit(solution)/shard_map/ppermute | solution.py:82
  13.6 4.8 %collective-permute-start.4 = (bf16[16,3712]{1,0:T(8,128)(2,1)S(1)}, bf16[16,3712]{1,0:T(8,128)(2,1)S(1)}, u32[]{:S(2)}, u32[]{:S(2)}) collective-permute-start(bf16[16,3712]{1,0:T(8,128)(2,1)S(1)} %collective-permute-done.3.refs_3_), channel_id=1, source_target_pairs={{0,8},{4,12},{8,0},{12,4},{16,24},{20,28},{24,16},{28,20},{1,9},{5... | collective-permute-start | bytes 356360 | tf_op jit(solution)/shard_map/ppermute | solution.py:82
  18.6 3.6 %collective-permute-start.5 = (bf16[128,3712]{1,0:T(8,128)(2,1)S(1)}, bf16[128,3712]{1,0:T(8,128)(2,1)S(1)}, u32[]{:S(2)}, u32[]{:S(2)}) collective-permute-start(bf16[128,3712]{1,0:T(8,128)(2,1)S(1)} %get-tuple-element.29.own), channel_id=1, source_target_pairs={{0,4},{4,0},{8,12},{12,8},{16,20},{20,16},{24,28},{28,24},{1,5},{5... | collective-permute-start | bytes 2850824 | tf_op jit(solution)/shard_map/ppermute | solution.py:82
  18.7 16.9 %collective-permute-start.9 = (bf16[48,3712]{1,0:T(8,128)(2,1)S(1)}, bf16[48,3712]{1,0:T(8,128)(2,1)S(1)}, u32[]{:S(2)}, u32[]{:S(2)}) collective-permute-start(bf16[48,3712]{1,0:T(8,128)(2,1)S(1)} %get-tuple-element.37), channel_id=1, source_target_pairs={{0,1},{1,0},{2,3},{3,2},{4,5},{5,4},{6,7},{7,6},{8,9},{9,8},{10,11... | collective-permute-start | bytes 1069064 | tf_op jit(solution)/shard_map/ppermute | solution.py:82
  20.2 15.5 %collective-permute-start.10 = (bf16[48,3712]{1,0:T(8,128)(2,1)S(1)}, bf16[48,3712]{1,0:T(8,128)(2,1)S(1)}, u32[]{:S(2)}, u32[]{:S(2)}) collective-permute-start(bf16[48,3712]{1,0:T(8,128)(2,1)S(1)} %get-tuple-element.38), channel_id=1, source_target_pairs={{0,2},{1,3},{2,0},{3,1},{4,6},{5,7},{6,4},{7,5},{8,10},{9,11},{10,... | collective-permute-start | bytes 1069064 | tf_op jit(solution)/shard_map/ppermute | solution.py:82
  21.8 13.8 %collective-permute-start.11 = (bf16[32,3712]{1,0:T(8,128)(2,1)S(1)}, bf16[32,3712]{1,0:T(8,128)(2,1)S(1)}, u32[]{:S(2)}, u32[]{:S(2)}) collective-permute-start(bf16[32,3712]{1,0:T(8,128)(2,1)S(1)} %get-tuple-element.39), channel_id=1, source_target_pairs={{0,3},{1,2},{2,1},{3,0},{4,7},{5,6},{6,5},{7,4},{8,11},{9,10},{10,... | collective-permute-start | bytes 712712 | tf_op jit(solution)/shard_map/ppermute | solution.py:88
  29.7 6.2 %collective-permute-start.6 = (bf16[128,3584]{1,0:T(8,128)(2,1)S(1)}, bf16[128,3584]{1,0:T(8,128)(2,1)S(1)}, u32[]{:S(2)}, u32[]{:S(2)}) collective-permute-start(bf16[128,3584]{1,0:T(8,128)(2,1)S(1)} %get-tuple-element.30.refs_0_), channel_id=1, source_target_pairs={{0,4},{4,0},{8,12},{12,8},{16,20},{20,16},{24,28},{28,24},{1,5},{5... | collective-permute-start | bytes 2752520 | tf_op jit(solution)/shard_map/ppermute | solution.py:82
  35.8 2.9 %collective-permute-start.12 = (bf16[128,3712]{1,0:T(8,128)(2,1)S(1)}, bf16[128,3712]{1,0:T(8,128)(2,1)S(1)}, u32[]{:S(2)}, u32[]{:S(2)}) collective-permute-start(bf16[128,3712]{1,0:T(8,128)(2,1)S(1)} %combine.11.own), channel_id=1, source_target_pairs={{0,4},{4,0},{8,12},{12,8},{16,20},{20,16},{24,28},{28,24},{1,5},{5... | collective-permute-start | bytes 2850824 | tf_op jit(solution)/shard_map/ppermute | solution.py:82
  36.5 8.1 %collective-permute-start.7 = (bf16[32,3584]{1,0:T(8,128)(2,1)S(1)}, bf16[32,3584]{1,0:T(8,128)(2,1)S(1)}, u32[]{:S(2)}, u32[]{:S(2)}) collective-permute-start(bf16[32,3584]{1,0:T(8,128)(2,1)S(1)} %get-tuple-element.35), channel_id=1, source_target_pairs={{0,1},{1,0},{2,3},{3,2},{4,5},{5,4},{6,7},{7,6},{8,9},{9,8},{10,11... | collective-permute-start | bytes 688136 | tf_op jit(solution)/shard_map/ppermute | solution.py:82
  37.9 7.7 %collective-permute-start.8 = (bf16[32,3584]{1,0:T(8,128)(2,1)S(1)}, bf16[32,3584]{1,0:T(8,128)(2,1)S(1)}, u32[]{:S(2)}, u32[]{:S(2)}) collective-permute-start(bf16[32,3584]{1,0:T(8,128)(2,1)S(1)} %get-tuple-element.36), channel_id=1, source_target_pairs={{0,2},{1,3},{2,0},{3,1},{4,6},{5,7},{6,4},{7,5},{8,10},{9,11},{10,... | collective-permute-start | bytes 688136 | tf_op jit(solution)/shard_map/ppermute | solution.py:82
  41.4 4.3 %collective-permute-start.13 = (bf16[128,3584]{1,0:T(8,128)(2,1)S(1)}, bf16[128,3584]{1,0:T(8,128)(2,1)S(1)}, u32[]{:S(2)}, u32[]{:S(2)}) collective-permute-start(bf16[128,3584]{1,0:T(8,128)(2,1)S(1)} %get-tuple-element.44), channel_id=1, source_target_pairs={{0,4},{4,0},{8,12},{12,8},{16,20},{20,16},{24,28},{28,24},{1,5},{5... | collective-permute-start | bytes 2752520 | tf_op jit(solution)/shard_map/ppermute | solution.py:82
  46.3 7.1 %collective-permute-start.18 = (bf16[16,3584]{1,0:T(8,128)(2,1)S(1)}, bf16[16,3584]{1,0:T(8,128)(2,1)S(1)}, u32[]{:S(2)}, u32[]{:S(2)}) collective-permute-start(bf16[16,3584]{1,0:T(8,128)(2,1)S(1)} %get-tuple-element.51), channel_id=1, source_target_pairs={{0,3},{1,2},{2,1},{3,0},{4,7},{5,6},{6,5},{7,4},{8,11},{9,10},{10,... | collective-permute-start | bytes 344072 | tf_op jit(solution)/shard_map/ppermute | solution.py:88
  48.1 7.1 %collective-permute-start.19 = (bf16[16,3584]{1,0:T(8,128)(2,1)S(1)}, bf16[16,3584]{1,0:T(8,128)(2,1)S(1)}, u32[]{:S(2)}, u32[]{:S(2)}) collective-permute-start(bf16[16,3584]{1,0:T(8,128)(2,1)S(1)} %get-tuple-element.52), channel_id=1, source_target_pairs={{0,1},{1,0},{2,3},{3,2},{4,5},{5,4},{6,7},{7,6},{8,9},{9,8},{10,11... | collective-permute-start | bytes 344072 | tf_op jit(solution)/shard_map/ppermute | solution.py:82
  48.7 8.6 %collective-permute-start.20 = (bf16[16,3584]{1,0:T(8,128)(2,1)S(1)}, bf16[16,3584]{1,0:T(8,128)(2,1)S(1)}, u32[]{:S(2)}, u32[]{:S(2)}) collective-permute-start(bf16[16,3584]{1,0:T(8,128)(2,1)S(1)} %get-tuple-element.53), channel_id=1, source_target_pairs={{0,2},{1,3},{2,0},{3,1},{4,6},{5,7},{6,4},{7,5},{8,10},{9,11},{10,... | collective-permute-start | bytes 344072 | tf_op jit(solution)/shard_map/ppermute | solution.py:82
  49.9 10.3 %collective-permute-start.15 = (bf16[16,3584]{1,0:T(8,128)(2,1)S(1)}, bf16[16,3584]{1,0:T(8,128)(2,1)S(1)}, u32[]{:S(2)}, u32[]{:S(2)}) collective-permute-start(bf16[16,3584]{1,0:T(8,128)(2,1)S(1)} %get-tuple-element.47), channel_id=1, source_target_pairs={{0,3},{1,2},{2,1},{3,0},{4,7},{5,6},{6,5},{7,4},{8,11},{9,10},{10,... | collective-permute-start | bytes 344072 | tf_op jit(solution)/shard_map/ppermute | solution.py:88
  51.6 8.6 %collective-permute-start.16 = (bf16[16,3584]{1,0:T(8,128)(2,1)S(1)}, bf16[16,3584]{1,0:T(8,128)(2,1)S(1)}, u32[]{:S(2)}, u32[]{:S(2)}) collective-permute-start(bf16[16,3584]{1,0:T(8,128)(2,1)S(1)} %get-tuple-element.48), channel_id=1, source_target_pairs={{0,1},{1,0},{2,3},{3,2},{4,5},{5,4},{6,7},{7,6},{8,9},{9,8},{10,11... | collective-permute-start | bytes 344072 | tf_op jit(solution)/shard_map/ppermute | solution.py:82
  53.4 7.3 %collective-permute-start.17 = (bf16[16,3584]{1,0:T(8,128)(2,1)S(1)}, bf16[16,3584]{1,0:T(8,128)(2,1)S(1)}, u32[]{:S(2)}, u32[]{:S(2)}) collective-permute-start(bf16[16,3584]{1,0:T(8,128)(2,1)S(1)} %get-tuple-element.49), channel_id=1, source_target_pairs={{0,2},{1,3},{2,0},{3,1},{4,6},{5,7},{6,4},{7,5},{8,10},{9,11},{10,... | collective-permute-start | bytes 344072 | tf_op jit(solution)/shard_map/ppermute | solution.py:82
  55.2 8.8 %collective-permute-start.14 = (bf16[32,3584]{1,0:T(8,128)(2,1)S(1)}, bf16[32,3584]{1,0:T(8,128)(2,1)S(1)}, u32[]{:S(2)}, u32[]{:S(2)}) collective-permute-start(bf16[32,3584]{1,0:T(8,128)(2,1)S(1)} %get-tuple-element.45), channel_id=1, source_target_pairs={{0,3},{1,2},{2,1},{3,0},{4,7},{5,6},{6,5},{7,4},{8,11},{9,10},{10,... | collective-permute-start | bytes 688136 | tf_op jit(solution)/shard_map/ppermute | solution.py:88
  57.3 10.9 %collective-permute-start.21 = (bf16[16,3584]{1,0:T(8,128)(2,1)S(1)}, bf16[16,3584]{1,0:T(8,128)(2,1)S(1)}, u32[]{:S(2)}, u32[]{:S(2)}) collective-permute-start(bf16[16,3584]{1,0:T(8,128)(2,1)S(1)} %combine.12.refs_4_), channel_id=1, source_target_pairs={{0,24},{4,28},{8,16},{12,20},{16,8},{20,12},{24,0},{28,4},{1,25},{... | collective-permute-start | bytes 344072 | tf_op jit(solution)/shard_map/ppermute | solution.py:88
  60.8 7.4 %collective-permute-start.22 = (bf16[16,3584]{1,0:T(8,128)(2,1)S(1)}, bf16[16,3584]{1,0:T(8,128)(2,1)S(1)}, u32[]{:S(2)}, u32[]{:S(2)}) collective-permute-start(bf16[16,3584]{1,0:T(8,128)(2,1)S(1)} %combine.13.refs_2_), channel_id=1, source_target_pairs={{0,16},{4,20},{8,24},{12,28},{16,0},{20,4},{24,8},{28,12},{1,17},{... | collective-permute-start | bytes 344072 | tf_op jit(solution)/shard_map/ppermute | solution.py:82
  64.1 5.4 %collective-permute-start.23 = (bf16[16,3584]{1,0:T(8,128)(2,1)S(1)}, bf16[16,3584]{1,0:T(8,128)(2,1)S(1)}, u32[]{:S(2)}, u32[]{:S(2)}) collective-permute-start(bf16[16,3584]{1,0:T(8,128)(2,1)S(1)} %get-tuple-element.55), channel_id=1, source_target_pairs={{0,8},{4,12},{8,0},{12,4},{16,24},{20,28},{24,16},{28,20},{1,9},{5... | collective-permute-start | bytes 344072 | tf_op jit(solution)/shard_map/ppermute | solution.py:82
  (4 other events, 26.8 us)
